TPU v7x, 32 devices: a whole 2x2x4 slice. The times are simulated.
32 devices in a mesh: rep: 2 (over x), seq: 16 (over z, y, core).
Axes of the slice: x: 2, y: 2, z: 4, core: 2. Of those that a mesh axis runs over, the one named last changes fastest.
Arguments:
- keys: bfloat16 [2048, 5120], P(('rep', 'seq')), parts along dimension 0, may hold values from -36 to 36
- values: bfloat16 [2048, 5120], P(('rep', 'seq')), parts along dimension 0, may hold values from -6 to 6
- queries: bfloat16 [2, 1024, 5120], P(None, ('rep', 'seq')), parts along dimension 1, may hold values from -6 to 6
Outputs:
- attended: bfloat16 [2, 1024, 5120], P(None, ('rep', 'seq')), parts along dimension 1
There are 2 independent parts, one for each index of `rep`. A program takes and returns all parts, laid end to end along the dimension named above; each array names one. Nothing has to cross between parts.
All inputs are finite; a program needn't handle non-finite values.
Results may differ from a plain program's by a relative error of at most 0.0038.
Values may be sent and summed in bfloat16 or wider, within the bound.
No kernel may reach another device: no remote copies, remote signals or barrier semaphores. Data moves between devices by JAX's collectives and lax.ppermute only.
A program may use at most 128 MiB of HBM per device.

v0:
```python
import functools
import math

import jax
import jax.numpy as jnp
from jax import lax
from jax.experimental import pallas as pl
from jax.experimental.pallas import tpu as pltpu
from jax.sharding import Mesh, PartitionSpec as P

HEAD_DIM = 128
GROUPS = 8
SUB = 128
F32 = jnp.float32
BF16 = jnp.bfloat16
VMEM = pl.BlockSpec(memory_space=pltpu.VMEM)
HBM = pl.BlockSpec(memory_space=pltpu.HBM)
SMEM = pl.BlockSpec(memory_space=pltpu.SMEM)
FREE = pl.CostEstimate(flops=0, bytes_accessed=0, transcendentals=0)
PARAMS = pltpu.CompilerParams(vmem_limit_bytes=40 * 2**20)


def softmax_rows(q, ka, va, kb, vb):
    factor = math.log2(math.e) / math.sqrt(HEAD_DIM)
    nt = (((1,), (1,)), ((), ()))
    sa = lax.dot_general(q, ka, nt, preferred_element_type=F32)
    sb = lax.dot_general(q, kb, nt, preferred_element_type=F32)
    peak = jnp.max(jnp.maximum(sa, sb), axis=1, keepdims=True)
    ea = jnp.exp2((sa - peak) * factor).astype(BF16)
    eb = jnp.exp2((sb - peak) * factor).astype(BF16)
    both = jnp.dot(ea, va, preferred_element_type=F32) + jnp.dot(eb, vb, preferred_element_type=F32)
    return both[:, :HEAD_DIM], peak * factor, both[:, HEAD_DIM:]


def beside_ones(v):
    return jnp.concatenate([v, jnp.ones_like(v)], axis=1)


FIRST = (6, 2, 7)
REST = (4, 3, 1, 5, 0)
LAST = (6, 7)
NEAR = (2, 3, 1)


def pack_body(rows, gw, layout, chip_ref, *refs):
    arrays, out_refs, sems = refs[:3], refs[3:-1], refs[-1]
    copies = []
    for out_ref, (k, parts) in zip(out_refs, layout):
        col = pl.ds(pl.multiple_of((chip_ref[0] ^ k) * gw, HEAD_DIM), gw)
        for at, n in enumerate(parts):
            to = out_ref.at[at * rows : (at + 1) * rows]
            copies.append(pltpu.make_async_copy(arrays[n].at[:, col], to, sems.at[len(copies)]))
    for copy in copies:
        copy.start()
    for copy in copies:
        copy.wait()


def merge_body(rows, *refs):
    out_ref = refs[-1]
    for n, piece in enumerate(refs[:-1]):
        for which in range(2):
            out_ref[which, n * rows : (n + 1) * rows] = piece[which * rows : (which + 1) * rows]


def unpack_body(gw, order, chip_ref, *refs):
    pieces, out_ref, sems = refs[: len(order)], refs[-2], refs[-1]
    copies = []
    for n, k in enumerate(order):
        col = pl.ds(pl.multiple_of((chip_ref[0] ^ k) * gw, HEAD_DIM), gw)
        copies.append(pltpu.make_async_copy(pieces[n], out_ref.at[:, col], sems.at[n]))
    for copy in copies:
        copy.start()
    for copy in copies:
        copy.wait()


def attend_body(count, rows, own, other, *refs):
    queries, outs = refs[:count], refs[count:]
    for h in range(own.shape[2] // HEAD_DIM):
        col = slice(h * HEAD_DIM, (h + 1) * HEAD_DIM)
        q = jnp.concatenate([r[r.shape[0] - rows :, col] for r in queries], axis=0)
        va, vb = beside_ones(own[1, :, col]), beside_ones(other[1, :, col])
        acc, _, total = softmax_rows(q, own[0, :, col], va, other[0, :, col], vb)
        acc = (acc / total).astype(BF16)
        for n, out in enumerate(outs):
            out[:, col] = acc[n * rows : (n + 1) * rows]


def local_permutes(keys, values, queries):
    chips = lax.axis_size("chip")
    rows, width = keys.shape
    gw = width // chips
    layers, tok_rows, _ = queries.shape
    rows_q = layers * tok_rows
    assert rows_q == rows
    chip = lax.axis_index("chip").reshape(1).astype(jnp.int32)

    def across(piece, k):
        return lax.ppermute(piece, "chip", [(i, i ^ k) for i in range(chips)]) if k else piece

    def call(body, n_in, out_shape, smem=0, **more):
        return pl.pallas_call(
            body,
            in_specs=[SMEM] * smem + [VMEM] * n_in,
            out_specs=jax.tree.map(lambda _: VMEM, out_shape),
            out_shape=out_shape,
            compiler_params=PARAMS,
            cost_estimate=FREE,
            **more,
        )

    def shape(*dims):
        return jax.ShapeDtypeStruct(dims, BF16)

    sources = [keys, values, queries.reshape(rows_q, width)]
    sources = [pltpu.with_memory_space_constraint(a, pltpu.HBM) for a in sources]

    def pack(layout, after=()):
        arrays = lax.optimization_barrier((*sources, *after))[:3] if after else sources
        return pl.pallas_call(
            functools.partial(pack_body, rows, gw, layout),
            in_specs=[SMEM, HBM, HBM, HBM],
            out_specs=[VMEM] * len(layout),
            out_shape=[shape(len(parts) * rows, gw) for _, parts in layout],
            scratch_shapes=[pltpu.SemaphoreType.DMA((sum(len(parts) for _, parts in layout),))],
            compiler_params=PARAMS,
            cost_estimate=FREE,
        )(chip, *arrays)

    layout = [(k, (0, 1) if k in LAST else (0, 1, 2)) for k in FIRST + REST]
    layout += [(k, (2,)) for k in LAST]
    packed = pack(layout[: len(FIRST)])
    packed += pack(layout[len(FIRST) :], packed[:1])
    got = [across(piece, k) for piece, (k, _) in zip(packed, layout)]
    late = dict(zip(LAST, got[chips:]))
    got = {k: piece for piece, (k, _) in zip(got[:chips], layout)}
    own = call(functools.partial(merge_body, rows), chips, shape(2, chips * rows, gw))(*got.values())
    other = lax.ppermute(own, "core", [(0, 1), (1, 0)])

    def attend(ks, after=()):
        pieces = [late.get(k, got[k]) for k in ks]
        if after:
            pieces = lax.optimization_barrier((*pieces, *after))[: len(pieces)]
        body = functools.partial(attend_body, len(ks), rows)
        outs = call(body, 2 + len(ks), [shape(rows, gw)] * len(ks))(own, other, *pieces)
        return dict(zip(ks, outs))

    outs = attend((4, 5))
    outs |= attend(NEAR + (0,), (outs[4],))
    outs |= attend(LAST, (outs[0],))
    back = {k: across(outs[k], k) for k in (4, 5) + LAST + (0,)}
    back[2] = across(lax.optimization_barrier((outs[2], outs[LAST[0]]))[0], 2)
    for k, before in ((3, 5), (1, 4)):
        back[k] = across(lax.optimization_barrier((outs[k], outs[LAST[0]], back[before]))[0], k)

    def unpack(order, so_far=()):
        return pl.pallas_call(
            functools.partial(unpack_body, gw, order),
            in_specs=[SMEM] + [VMEM] * len(order) + [HBM] * len(so_far),
            out_specs=HBM,
            out_shape=shape(rows_q, width),
            scratch_shapes=[pltpu.SemaphoreType.DMA((len(order),))],
            input_output_aliases={1 + len(order): 0} if so_far else {},
            compiler_params=PARAMS,
            cost_estimate=FREE,
        )(chip, *[back[k] for k in order], *so_far)

    result = unpack(LAST + (3, 1), (unpack((0, 4, 5, 2)),))
    return result.reshape(layers, tok_rows, width)


def partial_head(q_ref, ka_ref, va_ref, kb_ref, vb_ref, o_ref, peak_ref, total_ref):
    src, rows, _ = q_ref.shape
    q = q_ref[...].reshape(src * rows, HEAD_DIM)
    ka, va, kb, vb = (r[...].reshape(-1, HEAD_DIM) for r in (ka_ref, va_ref, kb_ref, vb_ref))
    kv = ka, beside_ones(va), kb, beside_ones(vb)
    outs = []
    for at in range(0, src * rows, SUB):
        acc, peak, total = softmax_rows(q[at : at + SUB], *kv)
        outs.append(acc)
        peak_ref[at : at + SUB] = jnp.broadcast_to(peak, (SUB, HEAD_DIM))
        total_ref[at : at + SUB] = total
    o_ref[...] = jnp.concatenate(outs, axis=0).reshape(o_ref.shape)


def partial_attend(got, other, rows_kv, rows_q):
    chips, _, width = got.shape
    heads = width // HEAD_DIM
    own_kv = got[:, : 2 * rows_kv].reshape(chips, 2, rows_kv, width)
    own_q = got[:, 2 * rows_kv :]
    other = other.reshape(chips, 2, rows_kv, width)

    def kv(which):
        return pl.BlockSpec((chips, None, rows_kv, HEAD_DIM), lambda h: (0, which, 0, h))

    q_spec = pl.BlockSpec((chips, rows_q, HEAD_DIM), lambda h: (0, 0, h))
    stat_spec = pl.BlockSpec((None, chips * rows_q, HEAD_DIM), lambda h: (h, 0, 0))
    stat = jax.ShapeDtypeStruct((heads, chips * rows_q, HEAD_DIM), F32)
    return pl.pallas_call(
        partial_head,
        grid=(heads,),
        in_specs=[q_spec, kv(0), kv(1), kv(0), kv(1)],
        out_specs=[q_spec, stat_spec, stat_spec],
        out_shape=[jax.ShapeDtypeStruct((chips, rows_q, width), F32), stat, stat],
        compiler_params=PARAMS,
    )(own_q, own_kv, own_kv, other, other)


def local_blocks(keys, values, queries):
    chips = lax.axis_size("chip")
    blocks = chips // GROUPS
    ctx_rows, width = keys.shape
    gw = width // GROUPS
    heads = gw // HEAD_DIM
    layers, tok_rows, _ = queries.shape
    rows_q = layers * tok_rows
    rows_kv = ctx_rows // blocks

    def by_chip(array):
        return jnp.swapaxes(array.reshape(rows_kv, chips, gw), 0, 1)

    q = jnp.swapaxes(queries.reshape(rows_q, GROUPS, gw), 0, 1)
    q = jnp.broadcast_to(q[None], (blocks, GROUPS, rows_q, gw)).reshape(chips, rows_q, gw)
    packed = jnp.concatenate([by_chip(keys), by_chip(values), q], axis=1)
    got = lax.all_to_all(packed, "chip", split_axis=0, concat_axis=0, tiled=True)
    other = lax.ppermute(got[:, : 2 * rows_kv], "core", [(0, 1), (1, 0)])
    outs = partial_attend(got, other, rows_kv, rows_q)
    stats = [jnp.moveaxis(s[:, :, 0].reshape(heads, chips, rows_q), 0, 2) for s in outs[1:]]
    stats = jnp.concatenate(stats, axis=2)
    stats = jnp.pad(stats, ((0, 0), (0, 0), (0, -2 * heads % HEAD_DIM)))
    sent = jnp.concatenate([outs[0], stats], axis=2)
    back = lax.all_to_all(sent, "chip", split_axis=0, concat_axis=0, tiled=True)
    back = back.reshape(blocks, GROUPS, rows_q, -1)
    summed = back[..., :gw].reshape(blocks, GROUPS, rows_q, heads, HEAD_DIM)
    peak = back[..., gw : gw + heads]
    total = back[..., gw + heads : gw + 2 * heads]
    share = jnp.exp2(peak - jnp.max(peak, axis=0))
    denom = jnp.sum(share * total, axis=0)
    numer = jnp.sum(share[..., None] * summed, axis=0)
    result = (numer / denom[..., None]).astype(BF16)
    return jnp.swapaxes(result.reshape(GROUPS, rows_q, gw), 0, 1).reshape(layers, tok_rows, width)


def solution(mesh):
    rep, seq = mesh.shape["rep"], mesh.shape["seq"]
    chips = seq // 2
    by_core = Mesh(mesh.devices.reshape(rep, chips, 2), ("rep", "chip", "core"))
    rows = ("rep", "chip", "core")
    return jax.shard_map(
        local_permutes if chips == GROUPS else local_blocks,
        mesh=by_core,
        in_specs=(P(rows, None), P(rows, None), P(None, rows, None)),
        out_specs=P(None, rows, None),
        check_vma=False,
    )
```

profile of v0, /device:TPU:0, one launch (start us, length us, event | category | flops | bytes accessed | tf_op | source)
XLA Modules:
  0.0 68.0 jit_solution(8800661495590200193)
XLA Ops:
  0.0 1.2 %shard_map.37 = (bf16[128,640]{1,0:T(8,128)(2,1)S(1)}, bf16[192,640]{1,0:T(8,128)(2,1)S(1)}, bf16[128,640]{1,0:T(8,128)(2,1)S(1)}) custom-call(s32[1]{0:T(128)} %bitcast.chip_ref, bf16[64,5120]{1,0:T(8,128)(2,1)} %refs_0_.2, bf16[64,5120]{1,0:T(8,128)(2,1)} %refs_1_.2, bf16[64,5120]{1,0:T(8,128)(2,1)} %bitcast.3), custom_call_target="tpu_custom_call" | custom-call | tf_op jit(solution)/shard_map/pallas_call | solution.py:121
  1.2 6.1 %collective-permute-start.2 = (bf16[128,640]{1,0:T(8,128)(2,1)S(1)}, bf16[128,640]{1,0:T(8,128)(2,1)S(1)}, u32[]{:S(2)}, u32[]{:S(2)}) collective-permute-start(bf16[128,640]{1,0:T(8,128)(2,1)S(1)} %get-tuple-element.37), channel_id=1, source_target_pairs={{0,14},{2,12},{4,10},{6,8},{8,6},{10,4},{12,2},{14,0},{1,15},{3,13... | collective-permute-start | bytes 491528 | tf_op jit(solution)/shard_map/ppermute | solution.py:100
  7.5 1.5 %shard_map.38 = (bf16[192,640]{1,0:T(8,128)(2,1)S(1)}, bf16[192,640]{1,0:T(8,128)(2,1)S(1)}, bf16[192,640]{1,0:T(8,128)(2,1)S(1)}, bf16[192,640]{1,0:T(8,128)(2,...) custom-call(s32[1]{0:T(128)} %bitcast.chip_ref, ...), custom_call_target="tpu_custom_call" | custom-call | tf_op jit(solution)/shard_map/pallas_call | solution.py:121
  9.0 4.2 %collective-permute-start.3 = (bf16[192,640]{1,0:T(8,128)(2,1)S(1)}, bf16[192,640]{1,0:T(8,128)(2,1)S(1)}, u32[]{:S(2)}, u32[]{:S(2)}) collective-permute-start(bf16[192,640]{1,0:T(8,128)(2,1)S(1)} %get-tuple-element.41), channel_id=1, source_target_pairs={{0,8},{2,10},{4,12},{6,14},{8,0},{10,2},{12,4},{14,6},{1,9},{3,11}... | collective-permute-start | bytes 737288 | tf_op jit(solution)/shard_map/ppermute | solution.py:100
  13.3 1.5 %collective-permute-start.5 = (bf16[192,640]{1,0:T(8,128)(2,1)S(1)}, bf16[192,640]{1,0:T(8,128)(2,1)S(1)}, u32[]{:S(2)}, u32[]{:S(2)}) collective-permute-start(bf16[192,640]{1,0:T(8,128)(2,1)S(1)} %get-tuple-element.43), channel_id=1, source_target_pairs={{0,2},{2,0},{4,6},{6,4},{8,10},{10,8},{12,14},{14,12},{1,3},{3,1},... | collective-permute-start | bytes 737288 | tf_op jit(solution)/shard_map/ppermute | solution.py:100
  14.7 1.4 %collective-permute-done.refs_0_ = bf16[128,640]{1,0:T(8,128)(2,1)S(1)} collective-permute-done((bf16[128,640]{1,0:T(8,128)(2,1)S(1)}, bf16[128,640]{1,0:T(8,128)(2,1)S(1)}, u32[]{:S(2)}, u32[]{:S(2)}) %collective-permute-start) | collective-permute-done | bytes 163872 | tf_op jit(solution)/shard_map/ppermute | solution.py:100
  16.2 12.6 %collective-permute-start.6 = (bf16[192,640]{1,0:T(8,128)(2,1)S(1)}, bf16[192,640]{1,0:T(8,128)(2,1)S(1)}, u32[]{:S(2)}, u32[]{:S(2)}) collective-permute-start(bf16[192,640]{1,0:T(8,128)(2,1)S(1)} %get-tuple-element.44), channel_id=1, source_target_pairs={{0,10},{2,8},{4,14},{6,12},{8,2},{10,0},{12,6},{14,4},{1,11},{3,9}... | collective-permute-start | bytes 737288 | tf_op jit(solution)/shard_map/ppermute | solution.py:100
  28.8 9.0 %collective-permute-done.3.refs_3_.refs_0_ = bf16[192,640]{1,0:T(8,128)(2,1)S(1)} collective-permute-done((bf16[192,640]{1,0:T(8,128)(2,1)S(1)}, bf16[192,640]{1,0:T(8,128)(2,1)S(1)}, u32[]{:S(2)}, u32[]{:S(2)}) %collective-permute-start.3) | collective-permute-done | bytes 245792 | tf_op jit(solution)/shard_map/ppermute | solution.py:100
  37.9 4.3 %collective-permute-done.6.refs_6_.refs_1_ = bf16[192,640]{1,0:T(8,128)(2,1)S(1)} collective-permute-done((bf16[192,640]{1,0:T(8,128)(2,1)S(1)}, bf16[192,640]{1,0:T(8,128)(2,1)S(1)}, u32[]{:S(2)}, u32[]{:S(2)}) %collective-permute-start.6) | collective-permute-done | bytes 245792 | tf_op jit(solution)/shard_map/ppermute | solution.py:100
  42.3 2.6 %collective-permute-start.8 = (bf16[64,640]{1,0:T(8,128)(2,1)S(1)}, bf16[64,640]{1,0:T(8,128)(2,1)S(1)}, u32[]{:S(2)}, u32[]{:S(2)}) collective-permute-start(bf16[64,640]{1,0:T(8,128)(2,1)S(1)} %get-tuple-element.46), channel_id=1, source_target_pairs={{0,12},{2,14},{4,8},{6,10},{8,4},{10,6},{12,0},{14,2},{1,13},{3,15... | collective-permute-start | bytes 245768 | tf_op jit(solution)/shard_map/ppermute | solution.py:100
  44.9 2.3 %collective-permute-start.9 = (bf16[64,640]{1,0:T(8,128)(2,1)S(1)}, bf16[64,640]{1,0:T(8,128)(2,1)S(1)}, u32[]{:S(2)}, u32[]{:S(2)}) collective-permute-start(bf16[64,640]{1,0:T(8,128)(2,1)S(1)} %get-tuple-element.47), channel_id=1, source_target_pairs={{0,14},{2,12},{4,10},{6,8},{8,6},{10,4},{12,2},{14,0},{1,15},{3,13... | collective-permute-start | bytes 245768 | tf_op jit(solution)/shard_map/ppermute | solution.py:100
  47.2 1.2 %shard_map.40 = (bf16[64,640]{1,0:T(8,128)(2,1)S(1)}, bf16[64,640]{1,0:T(8,128)(2,1)S(1)}) custom-call(bf16[2,512,640]{2,1,0:T(8,128)(2,1)S(1)} %shard_map.39.own, bf16[2,512,640]{2,1,0:T(8,128)(2,1)S(1)} %collective-permute-done.7.other, bf16[192,640]{1,0:T(8,128)(2,1)S(1)} %collective-permute-done.3.refs_3_.refs_0_, ...), custom_call_target="tpu_custom_call" | custom-call | tf_op jit(solution)/shard_map/pallas_call | solution.py:146
  48.4 2.9 %collective-permute-start.14 = (bf16[64,640]{1,0:T(8,128)(2,1)S(1)}, bf16[64,640]{1,0:T(8,128)(2,1)S(1)}, u32[]{:S(2)}, u32[]{:S(2)}) collective-permute-start(bf16[64,640]{1,0:T(8,128)(2,1)S(1)} %get-tuple-element.48), channel_id=1, source_target_pairs={{0,8},{2,10},{4,12},{6,14},{8,0},{10,2},{12,4},{14,6},{1,9},{3,11}... | collective-permute-start | bytes 245768 | tf_op jit(solution)/shard_map/ppermute | solution.py:100
  51.3 2.0 %shard_map.41 = (bf16[64,640]{1,0:T(8,128)(2,1)S(1)}, bf16[64,640]{1,0:T(8,128)(2,1)S(1)}, bf16[64,640]{1,0:T(8,128)(2,1)S(1)}, bf16[64,640]{1,0:T(8,128)(2,1)S(1)}) custom-call(bf16[2,512,640]{2,1,0:T(8,128)(2,1)S(1)} %shard_map.39.own, bf16[2,512,640]{2,1,0:T(8,128)(2,1)S(1)} %collective-permute-done.7.other, ...), custom_call_target="tpu_custom_call" | custom-call | tf_op jit(solution)/shard_map/pallas_call | solution.py:146
  53.3 1.2 %shard_map.42 = (bf16[64,640]{1,0:T(8,128)(2,1)S(1)}, bf16[64,640]{1,0:T(8,128)(2,1)S(1)}) custom-call(bf16[2,512,640]{2,1,0:T(8,128)(2,1)S(1)} %shard_map.39.own, bf16[2,512,640]{2,1,0:T(8,128)(2,1)S(1)} %collective-permute-done.7.other, bf16[64,640]{1,0:T(8,128)(2,1)S(1)} %collective-permute-done.8.refs_0_, bf16[64,640]{1,0:T(8,128)(2,1)S(1)} %collective-permute-done.9.refs_1_), custom_call_target="tpu_custom_call" | custom-call | tf_op jit(solution)/shard_map/pallas_call | solution.py:146
  54.5 2.6 %collective-permute-start.10 = (bf16[64,640]{1,0:T(8,128)(2,1)S(1)}, bf16[64,640]{1,0:T(8,128)(2,1)S(1)}, u32[]{:S(2)}, u32[]{:S(2)}) collective-permute-start(bf16[64,640]{1,0:T(8,128)(2,1)S(1)} %get-tuple-element.56), channel_id=1, source_target_pairs={{0,12},{2,14},{4,8},{6,10},{8,4},{10,6},{12,0},{14,2},{1,13},{3,15... | collective-permute-start | bytes 245768 | tf_op jit(solution)/shard_map/ppermute | solution.py:100
  57.1 2.3 %collective-permute-start.11 = (bf16[64,640]{1,0:T(8,128)(2,1)S(1)}, bf16[64,640]{1,0:T(8,128)(2,1)S(1)}, u32[]{:S(2)}, u32[]{:S(2)}) collective-permute-start(bf16[64,640]{1,0:T(8,128)(2,1)S(1)} %get-tuple-element.57), channel_id=1, source_target_pairs={{0,14},{2,12},{4,10},{6,8},{8,6},{10,4},{12,2},{14,0},{1,15},{3,13... | collective-permute-start | bytes 245768 | tf_op jit(solution)/shard_map/ppermute | solution.py:100
  59.3 1.1 %collective-permute-start.13 = (bf16[64,640]{1,0:T(8,128)(2,1)S(1)}, bf16[64,640]{1,0:T(8,128)(2,1)S(1)}, u32[]{:S(2)}, u32[]{:S(2)}) collective-permute-start(bf16[64,640]{1,0:T(8,128)(2,1)S(1)} %get-tuple-element.60), channel_id=1, source_target_pairs={{0,6},{2,4},{4,2},{6,0},{8,14},{10,12},{12,10},{14,8},{1,7},{3,5},... | collective-permute-start | bytes 245768 | tf_op jit(solution)/shard_map/ppermute | solution.py:100
  61.1 0.8 %collective-permute-start.15 = (bf16[64,640]{1,0:T(8,128)(2,1)S(1)}, bf16[64,640]{1,0:T(8,128)(2,1)S(1)}, u32[]{:S(2)}, u32[]{:S(2)}) collective-permute-start(bf16[64,640]{1,0:T(8,128)(2,1)S(1)} %get-tuple-element.62), channel_id=1, source_target_pairs={{0,2},{2,0},{4,6},{6,4},{8,10},{10,8},{12,14},{14,12},{1,3},{3,1},... | collective-permute-start | bytes 245768 | tf_op jit(solution)/shard_map/ppermute | solution.py:100
  61.9 2.7 %collective-permute-done.16.refs_3_ = bf16[64,640]{1,0:T(8,128)(2,1)S(1)} collective-permute-done((bf16[64,640]{1,0:T(8,128)(2,1)S(1)}, bf16[64,640]{1,0:T(8,128)(2,1)S(1)}, u32[]{:S(2)}, u32[]{:S(2)}) %collective-permute-start.16) | collective-permute-done | bytes 81952 | tf_op jit(solution)/shard_map/ppermute | solution.py:100
  64.6 0.8 %shard_map.43.refs_4_ = bf16[64,5120]{1,0:T(8,128)(2,1)} custom-call(s32[1]{0:T(128)} %bitcast.chip_ref, bf16[64,640]{1,0:T(8,128)(2,1)S(1)} %get-tuple-element.53.refs_0_, bf16[64,640]{1,0:T(8,128)(2,1)S(1)} %collective-permute-done.14.refs_1_, bf16[64,640]{1,0:T(8,128)(2,1)S(1)} %collective-permute-done.12.refs_2_, ...), custom_call_target="tpu_custom_call" | custom-call | tf_op jit(solution)/shard_map/pallas_call | solution.py:158
  65.6 0.8 %collective-permute-done.13.refs_2_ = bf16[64,640]{1,0:T(8,128)(2,1)S(1)} collective-permute-done((bf16[64,640]{1,0:T(8,128)(2,1)S(1)}, bf16[64,640]{1,0:T(8,128)(2,1)S(1)}, u32[]{:S(2)}, u32[]{:S(2)}) %collective-permute-start.13) | collective-permute-done | bytes 81952 | tf_op jit(solution)/shard_map/ppermute | solution.py:100
  66.4 0.9 %collective-permute-done.15.refs_3_ = bf16[64,640]{1,0:T(8,128)(2,1)S(1)} collective-permute-done((bf16[64,640]{1,0:T(8,128)(2,1)S(1)}, bf16[64,640]{1,0:T(8,128)(2,1)S(1)}, u32[]{:S(2)}, u32[]{:S(2)}) %collective-permute-start.15) | collective-permute-done | bytes 81952 | tf_op jit(solution)/shard_map/ppermute | solution.py:100
  67.3 0.8 %shard_map.44 = bf16[64,5120]{1,0:T(8,128)(2,1)} custom-call(s32[1]{0:T(128)} %bitcast.chip_ref, bf16[64,640]{1,0:T(8,128)(2,1)S(1)} %collective-permute-done.10.refs_0_, bf16[64,640]{1,0:T(8,128)(2,1)S(1)} %collective-permute-done.11.refs_1_, bf16[64,640]{1,0:T(8,128)(2,1)S(1)} %collective-permute-done.13.refs_2_, ...), custom_call_target="tpu_custom_call", output_to_operand_aliasing={{}: (5, {})} | custom-call | tf_op jit(solution)/shard_map/pallas_call | solution.py:158
  (18 shorter events, 1.4 us)
Async XLA Ops:
  1.2 12.1 %collective-permute-start.2 = (bf16[128,640]{1,0:T(8,128)(2,1)S(1)}, bf16[128,640]{1,0:T(8,128)(2,1)S(1)}, u32[]{:S(2)}, u32[]{:S(2)}) collective-permute-start(bf16[128,640]{1,0:T(8,128)(2,1)S(1)} %get-tuple-element.37), channel_id=1, source_target_pairs={{0,14},{2,12},{4,10},{6,8},{8,6},{10,4},{12,2},{14,0},{1,15},{3,13... | collective-permute-start | bytes 491528 | tf_op jit(solution)/shard_map/ppermute | solution.py:100
  7.3 8.9 %collective-permute-start = (bf16[128,640]{1,0:T(8,128)(2,1)S(1)}, bf16[128,640]{1,0:T(8,128)(2,1)S(1)}, u32[]{:S(2)}, u32[]{:S(2)}) collective-permute-start(bf16[128,640]{1,0:T(8,128)(2,1)S(1)} %get-tuple-element.35), channel_id=1, source_target_pairs={{0,12},{2,14},{4,8},{6,10},{8,4},{10,6},{12,0},{14,2},{1,13},{3,15... | collective-permute-start | bytes 491528 | tf_op jit(solution)/shard_map/ppermute | solution.py:100
  7.5 21.3 %collective-permute-start.1 = (bf16[192,640]{1,0:T(8,128)(2,1)S(1)}, bf16[192,640]{1,0:T(8,128)(2,1)S(1)}, u32[]{:S(2)}, u32[]{:S(2)}) collective-permute-start(bf16[192,640]{1,0:T(8,128)(2,1)S(1)} %get-tuple-element.36), channel_id=1, source_target_pairs={{0,4},{2,6},{4,0},{6,2},{8,12},{10,14},{12,8},{14,10},{1,5},{3,7},... | collective-permute-start | bytes 737288 | tf_op jit(solution)/shard_map/ppermute | solution.py:100
  9.0 28.8 %collective-permute-start.3 = (bf16[192,640]{1,0:T(8,128)(2,1)S(1)}, bf16[192,640]{1,0:T(8,128)(2,1)S(1)}, u32[]{:S(2)}, u32[]{:S(2)}) collective-permute-start(bf16[192,640]{1,0:T(8,128)(2,1)S(1)} %get-tuple-element.41), channel_id=1, source_target_pairs={{0,8},{2,10},{4,12},{6,14},{8,0},{10,2},{12,4},{14,6},{1,9},{3,11}... | collective-permute-start | bytes 737288 | tf_op jit(solution)/shard_map/ppermute | solution.py:100
  13.3 24.6 %collective-permute-start.4 = (bf16[192,640]{1,0:T(8,128)(2,1)S(1)}, bf16[192,640]{1,0:T(8,128)(2,1)S(1)}, u32[]{:S(2)}, u32[]{:S(2)}) collective-permute-start(bf16[192,640]{1,0:T(8,128)(2,1)S(1)} %get-tuple-element.42), channel_id=1, source_target_pairs={{0,6},{2,4},{4,2},{6,0},{8,14},{10,12},{12,10},{14,8},{1,7},{3,5},... | collective-permute-start | bytes 737288 | tf_op jit(solution)/shard_map/ppermute | solution.py:100
  13.3 24.6 %collective-permute-start.5 = (bf16[192,640]{1,0:T(8,128)(2,1)S(1)}, bf16[192,640]{1,0:T(8,128)(2,1)S(1)}, u32[]{:S(2)}, u32[]{:S(2)}) collective-permute-start(bf16[192,640]{1,0:T(8,128)(2,1)S(1)} %get-tuple-element.43), channel_id=1, source_target_pairs={{0,2},{2,0},{4,6},{6,4},{8,10},{10,8},{12,14},{14,12},{1,3},{3,1},... | collective-permute-start | bytes 737288 | tf_op jit(solution)/shard_map/ppermute | solution.py:100
  16.2 26.0 %collective-permute-start.6 = (bf16[192,640]{1,0:T(8,128)(2,1)S(1)}, bf16[192,640]{1,0:T(8,128)(2,1)S(1)}, u32[]{:S(2)}, u32[]{:S(2)}) collective-permute-start(bf16[192,640]{1,0:T(8,128)(2,1)S(1)} %get-tuple-element.44), channel_id=1, source_target_pairs={{0,10},{2,8},{4,14},{6,12},{8,2},{10,0},{12,6},{14,4},{1,11},{3,9}... | collective-permute-start | bytes 737288 | tf_op jit(solution)/shard_map/ppermute | solution.py:100
  42.3 4.9 %collective-permute-start.7 = (bf16[2,512,640]{2,1,0:T(8,128)(2,1)S(1)}, bf16[2,512,640]{2,1,0:T(8,128)(2,1)S(1)}, u32[]{:S(2)}, u32[]{:S(2)}) collective-permute-start(bf16[2,512,640]{2,1,0:T(8,128)(2,1)S(1)} %shard_map.39.own), channel_id=1, source_target_pairs={{0,1},{1,0},{2,3},{3,2},{4,5},{5,4},{6,7},{7,6},{8,9},{9,8},{10,11... | collective-permute-start | bytes 3932168 | tf_op jit(solution)/shard_map/ppermute | solution.py:139
  42.3 11.0 %collective-permute-start.8 = (bf16[64,640]{1,0:T(8,128)(2,1)S(1)}, bf16[64,640]{1,0:T(8,128)(2,1)S(1)}, u32[]{:S(2)}, u32[]{:S(2)}) collective-permute-start(bf16[64,640]{1,0:T(8,128)(2,1)S(1)} %get-tuple-element.46), channel_id=1, source_target_pairs={{0,12},{2,14},{4,8},{6,10},{8,4},{10,6},{12,0},{14,2},{1,13},{3,15... | collective-permute-start | bytes 245768 | tf_op jit(solution)/shard_map/ppermute | solution.py:100
  44.9 8.4 %collective-permute-start.9 = (bf16[64,640]{1,0:T(8,128)(2,1)S(1)}, bf16[64,640]{1,0:T(8,128)(2,1)S(1)}, u32[]{:S(2)}, u32[]{:S(2)}) collective-permute-start(bf16[64,640]{1,0:T(8,128)(2,1)S(1)} %get-tuple-element.47), channel_id=1, source_target_pairs={{0,14},{2,12},{4,10},{6,8},{8,6},{10,4},{12,2},{14,0},{1,15},{3,13... | collective-permute-start | bytes 245768 | tf_op jit(solution)/shard_map/ppermute | solution.py:100
  48.4 11.0 %collective-permute-start.12 = (bf16[64,640]{1,0:T(8,128)(2,1)S(1)}, bf16[64,640]{1,0:T(8,128)(2,1)S(1)}, u32[]{:S(2)}, u32[]{:S(2)}) collective-permute-start(bf16[64,640]{1,0:T(8,128)(2,1)S(1)} %get-tuple-element.59), channel_id=1, source_target_pairs={{0,10},{2,8},{4,14},{6,12},{8,2},{10,0},{12,6},{14,4},{1,11},{3,9}... | collective-permute-start | bytes 245768 | tf_op jit(solution)/shard_map/ppermute | solution.py:100
  48.4 12.7 %collective-permute-start.14 = (bf16[64,640]{1,0:T(8,128)(2,1)S(1)}, bf16[64,640]{1,0:T(8,128)(2,1)S(1)}, u32[]{:S(2)}, u32[]{:S(2)}) collective-permute-start(bf16[64,640]{1,0:T(8,128)(2,1)S(1)} %get-tuple-element.48), channel_id=1, source_target_pairs={{0,8},{2,10},{4,12},{6,14},{8,0},{10,2},{12,4},{14,6},{1,9},{3,11}... | collective-permute-start | bytes 245768 | tf_op jit(solution)/shard_map/ppermute | solution.py:100
  54.5 11.1 %collective-permute-start.10 = (bf16[64,640]{1,0:T(8,128)(2,1)S(1)}, bf16[64,640]{1,0:T(8,128)(2,1)S(1)}, u32[]{:S(2)}, u32[]{:S(2)}) collective-permute-start(bf16[64,640]{1,0:T(8,128)(2,1)S(1)} %get-tuple-element.56), channel_id=1, source_target_pairs={{0,12},{2,14},{4,8},{6,10},{8,4},{10,6},{12,0},{14,2},{1,13},{3,15... | collective-permute-start | bytes 245768 | tf_op jit(solution)/shard_map/ppermute | solution.py:100
  57.1 7.5 %collective-permute-start.16 = (bf16[64,640]{1,0:T(8,128)(2,1)S(1)}, bf16[64,640]{1,0:T(8,128)(2,1)S(1)}, u32[]{:S(2)}, u32[]{:S(2)}) collective-permute-start(bf16[64,640]{1,0:T(8,128)(2,1)S(1)} %get-tuple-element.64), channel_id=1, source_target_pairs={{0,4},{2,6},{4,0},{6,2},{8,12},{10,14},{12,8},{14,10},{1,5},{3,7},... | collective-permute-start | bytes 245768 | tf_op jit(solution)/shard_map/ppermute | solution.py:100
  57.1 8.5 %collective-permute-start.11 = (bf16[64,640]{1,0:T(8,128)(2,1)S(1)}, bf16[64,640]{1,0:T(8,128)(2,1)S(1)}, u32[]{:S(2)}, u32[]{:S(2)}) collective-permute-start(bf16[64,640]{1,0:T(8,128)(2,1)S(1)} %get-tuple-element.57), channel_id=1, source_target_pairs={{0,14},{2,12},{4,10},{6,8},{8,6},{10,4},{12,2},{14,0},{1,15},{3,13... | collective-permute-start | bytes 245768 | tf_op jit(solution)/shard_map/ppermute | solution.py:100
  59.3 7.1 %collective-permute-start.13 = (bf16[64,640]{1,0:T(8,128)(2,1)S(1)}, bf16[64,640]{1,0:T(8,128)(2,1)S(1)}, u32[]{:S(2)}, u32[]{:S(2)}) collective-permute-start(bf16[64,640]{1,0:T(8,128)(2,1)S(1)} %get-tuple-element.60), channel_id=1, source_target_pairs={{0,6},{2,4},{4,2},{6,0},{8,14},{10,12},{12,10},{14,8},{1,7},{3,5},... | collective-permute-start | bytes 245768 | tf_op jit(solution)/shard_map/ppermute | solution.py:100
  61.1 6.2 %collective-permute-start.15 = (bf16[64,640]{1,0:T(8,128)(2,1)S(1)}, bf16[64,640]{1,0:T(8,128)(2,1)S(1)}, u32[]{:S(2)}, u32[]{:S(2)}) collective-permute-start(bf16[64,640]{1,0:T(8,128)(2,1)S(1)} %get-tuple-element.62), channel_id=1, source_target_pairs={{0,2},{2,0},{4,6},{6,4},{8,10},{10,8},{12,14},{14,12},{1,3},{3,1},... | collective-permute-start | bytes 245768 | tf_op jit(solution)/shard_map/ppermute | solution.py:100
where the time goes:
time: 68.2 us; the launch traced here: 68 us
  starting transfers between devices  39.2 us (57%)
  waiting for transfers between devices  20.1 us (29%)
  Pallas kernels  8.66 us (13%)
    ppermute x16, starting transfers between devices, across(): lax.ppermute(piece, 'chip', [(i, i ^ k) for i in range(chips)])  39.2 us
    ppermute x16, waiting for transfers between devices, across(): lax.ppermute(piece, 'chip', [(i, i ^ k) for i in range(chips)])  20 us
    pallas_call x3, Pallas kernels, attend(): call(body, 2 + len(ks), [shape(rows, gw)] * len(ks))(own, other, *pieces)  4.33 us
    pallas_call x2, Pallas kernels, pack(): pl.pallas_call(functools.partial(pack_body, rows, gw, layout), in_specs=[...  2.73 us
    pallas_call x2, Pallas kernels, unpack(): pl.pallas_call(functools.partial(unpack_body, gw, order), in_specs=[SMEM]...  1.5 us
  transfers between devices with their start and end apart: 17, of which 8 were waited for; matrix products, arithmetic and copies ran while one was open for 0% of the time, Pallas kernels for 10%

commit v1 on v0

--- a/solution.py
+++ b/solution.py
@@ -149,10 +149,12 @@
     outs = attend((4, 5))
     outs |= attend(NEAR + (0,), (outs[4],))
     outs |= attend(LAST, (outs[0],))
-    back = {k: across(outs[k], k) for k in (4, 5) + LAST + (0,)}
-    back[2] = across(lax.optimization_barrier((outs[2], outs[LAST[0]]))[0], 2)
-    for k, before in ((3, 5), (1, 4)):
-        back[k] = across(lax.optimization_barrier((outs[k], outs[LAST[0]], back[before]))[0], k)
+    def send(k, *after):
+        return across(lax.optimization_barrier((outs[k], *after))[0], k)
+
+    back = {k: across(outs[k], k) for k in NEAR + (0,)}
+    back |= {k: send(k, outs[0]) for k in (4, 5)}
+    back |= {7: send(7, back[2]), 6: send(6, back[3])}
 
     def unpack(order, so_far=()):
         return pl.pallas_call(
@@ -166,7 +168,7 @@
             cost_estimate=FREE,
         )(chip, *[back[k] for k in order], *so_far)
 
-    result = unpack(LAST + (3, 1), (unpack((0, 4, 5, 2)),))
+    result = unpack((4, 5) + LAST, (unpack((0,) + NEAR),))
     return result.reshape(layers, tok_rows, width)
 
 

time: 68.2 us -> 68.8 us (level)
  starting transfers between devices: 39.2 us -> 40.8 us
  waiting for transfers between devices: 20.1 us -> 19 us
    ppermute x16, starting transfers between devices: 39.2 us -> 40.7 us  [across(): lax.ppermute(piece, 'chip', [(i, i ^ k) for i in range(chips)])]
    ppermute x16, waiting for transfers between devices: 20 us -> 19 us  [across(): lax.ppermute(piece, 'chip', [(i, i ^ k) for i in range(chips)])]
  transfers between devices with their start and end apart: 17 -> 17, of which waited for: 8 -> 5; matrix products, arithmetic and copies ran while one was open for 0% -> 0% of each run, Pallas kernels for 10% -> 10%
where the time goes in v1:
time: 68.8 us; the launch traced here: 68.6 us
  starting transfers between devices  40.8 us (59%)
  waiting for transfers between devices  19 us (28%)
  Pallas kernels  8.66 us (13%)
    ppermute x16, starting transfers between devices, across(): lax.ppermute(piece, 'chip', [(i, i ^ k) for i in range(chips)])  40.7 us
    ppermute x16, waiting for transfers between devices, across(): lax.ppermute(piece, 'chip', [(i, i ^ k) for i in range(chips)])  19 us
    pallas_call x3, Pallas kernels, attend(): call(body, 2 + len(ks), [shape(rows, gw)] * len(ks))(own, other, *pieces)  4.33 us
    pallas_call x2, Pallas kernels, pack(): pl.pallas_call(functools.partial(pack_body, rows, gw, layout), in_specs=[...  2.73 us
    pallas_call x2, Pallas kernels, unpack(): pl.pallas_call(functools.partial(unpack_body, gw, order), in_specs=[SMEM]...  1.5 us
  transfers between devices with their start and end apart: 17, of which 5 were waited for; matrix products, arithmetic and copies ran while one was open for 0% of the time, Pallas kernels for 10%

profile of v1, /device:TPU:0, one launch (start us, length us, event | category | flops | bytes accessed | tf_op | source)
XLA Modules:
  0.0 68.6 jit_solution(6670216862102889328)
XLA Ops:
  0.0 1.2 %shard_map.37 = (bf16[128,640]{1,0:T(8,128)(2,1)S(1)}, bf16[192,640]{1,0:T(8,128)(2,1)S(1)}, bf16[128,640]{1,0:T(8,128)(2,1)S(1)}) custom-call(s32[1]{0:T(128)} %bitcast.chip_ref, bf16[64,5120]{1,0:T(8,128)(2,1)} %refs_0_.2, bf16[64,5120]{1,0:T(8,128)(2,1)} %refs_1_.2, bf16[64,5120]{1,0:T(8,128)(2,1)} %bitcast.3), custom_call_target="tpu_custom_call" | custom-call | tf_op jit(solution)/shard_map/pallas_call | solution.py:121
  1.2 6.1 %collective-permute-start.2 = (bf16[128,640]{1,0:T(8,128)(2,1)S(1)}, bf16[128,640]{1,0:T(8,128)(2,1)S(1)}, u32[]{:S(2)}, u32[]{:S(2)}) collective-permute-start(bf16[128,640]{1,0:T(8,128)(2,1)S(1)} %get-tuple-element.38), channel_id=1, source_target_pairs={{0,14},{2,12},{4,10},{6,8},{8,6},{10,4},{12,2},{14,0},{1,15},{3,13... | collective-permute-start | bytes 491528 | tf_op jit(solution)/shard_map/ppermute | solution.py:100
  7.5 1.5 %shard_map.38 = (bf16[192,640]{1,0:T(8,128)(2,1)S(1)}, bf16[192,640]{1,0:T(8,128)(2,1)S(1)}, bf16[192,640]{1,0:T(8,128)(2,1)S(1)}, bf16[192,640]{1,0:T(8,128)(2,...) custom-call(s32[1]{0:T(128)} %bitcast.chip_ref, ...), custom_call_target="tpu_custom_call" | custom-call | tf_op jit(solution)/shard_map/pallas_call | solution.py:121
  9.0 4.2 %collective-permute-start.3 = (bf16[192,640]{1,0:T(8,128)(2,1)S(1)}, bf16[192,640]{1,0:T(8,128)(2,1)S(1)}, u32[]{:S(2)}, u32[]{:S(2)}) collective-permute-start(bf16[192,640]{1,0:T(8,128)(2,1)S(1)} %get-tuple-element.42), channel_id=1, source_target_pairs={{0,8},{2,10},{4,12},{6,14},{8,0},{10,2},{12,4},{14,6},{1,9},{3,11}... | collective-permute-start | bytes 737288 | tf_op jit(solution)/shard_map/ppermute | solution.py:100
  13.3 1.5 %collective-permute-start.5 = (bf16[192,640]{1,0:T(8,128)(2,1)S(1)}, bf16[192,640]{1,0:T(8,128)(2,1)S(1)}, u32[]{:S(2)}, u32[]{:S(2)}) collective-permute-start(bf16[192,640]{1,0:T(8,128)(2,1)S(1)} %get-tuple-element.44), channel_id=1, source_target_pairs={{0,2},{2,0},{4,6},{6,4},{8,10},{10,8},{12,14},{14,12},{1,3},{3,1},... | collective-permute-start | bytes 737288 | tf_op jit(solution)/shard_map/ppermute | solution.py:100
  14.7 1.4 %collective-permute-done.refs_0_ = bf16[128,640]{1,0:T(8,128)(2,1)S(1)} collective-permute-done((bf16[128,640]{1,0:T(8,128)(2,1)S(1)}, bf16[128,640]{1,0:T(8,128)(2,1)S(1)}, u32[]{:S(2)}, u32[]{:S(2)}) %collective-permute-start) | collective-permute-done | bytes 163872 | tf_op jit(solution)/shard_map/ppermute | solution.py:100
  16.2 12.6 %collective-permute-start.6 = (bf16[192,640]{1,0:T(8,128)(2,1)S(1)}, bf16[192,640]{1,0:T(8,128)(2,1)S(1)}, u32[]{:S(2)}, u32[]{:S(2)}) collective-permute-start(bf16[192,640]{1,0:T(8,128)(2,1)S(1)} %get-tuple-element.45), channel_id=1, source_target_pairs={{0,10},{2,8},{4,14},{6,12},{8,2},{10,0},{12,6},{14,4},{1,11},{3,9}... | collective-permute-start | bytes 737288 | tf_op jit(solution)/shard_map/ppermute | solution.py:100
  28.8 9.0 %collective-permute-done.3.refs_3_.refs_0_ = bf16[192,640]{1,0:T(8,128)(2,1)S(1)} collective-permute-done((bf16[192,640]{1,0:T(8,128)(2,1)S(1)}, bf16[192,640]{1,0:T(8,128)(2,1)S(1)}, u32[]{:S(2)}, u32[]{:S(2)}) %collective-permute-start.3) | collective-permute-done | bytes 245792 | tf_op jit(solution)/shard_map/ppermute | solution.py:100
  37.9 4.3 %collective-permute-done.6.refs_6_.refs_1_ = bf16[192,640]{1,0:T(8,128)(2,1)S(1)} collective-permute-done((bf16[192,640]{1,0:T(8,128)(2,1)S(1)}, bf16[192,640]{1,0:T(8,128)(2,1)S(1)}, u32[]{:S(2)}, u32[]{:S(2)}) %collective-permute-start.6) | collective-permute-done | bytes 245792 | tf_op jit(solution)/shard_map/ppermute | solution.py:100
  42.3 2.6 %collective-permute-start.10 = (bf16[64,640]{1,0:T(8,128)(2,1)S(1)}, bf16[64,640]{1,0:T(8,128)(2,1)S(1)}, u32[]{:S(2)}, u32[]{:S(2)}) collective-permute-start(bf16[64,640]{1,0:T(8,128)(2,1)S(1)} %get-tuple-element.56), channel_id=1, source_target_pairs={{0,12},{2,14},{4,8},{6,10},{8,4},{10,6},{12,0},{14,2},{1,13},{3,15... | collective-permute-start | bytes 245768 | tf_op jit(solution)/shard_map/ppermute | solution.py:100
  44.9 2.3 %collective-permute-start.11 = (bf16[64,640]{1,0:T(8,128)(2,1)S(1)}, bf16[64,640]{1,0:T(8,128)(2,1)S(1)}, u32[]{:S(2)}, u32[]{:S(2)}) collective-permute-start(bf16[64,640]{1,0:T(8,128)(2,1)S(1)} %get-tuple-element.57), channel_id=1, source_target_pairs={{0,14},{2,12},{4,10},{6,8},{8,6},{10,4},{12,2},{14,0},{1,15},{3,13... | collective-permute-start | bytes 245768 | tf_op jit(solution)/shard_map/ppermute | solution.py:100
  47.2 1.2 %shard_map.40 = (bf16[64,640]{1,0:T(8,128)(2,1)S(1)}, bf16[64,640]{1,0:T(8,128)(2,1)S(1)}) custom-call(bf16[2,512,640]{2,1,0:T(8,128)(2,1)S(1)} %shard_map.39.own, bf16[2,512,640]{2,1,0:T(8,128)(2,1)S(1)} %collective-permute-done.7.other, bf16[192,640]{1,0:T(8,128)(2,1)S(1)} %collective-permute-done.3.refs_3_.refs_0_, ...), custom_call_target="tpu_custom_call" | custom-call | tf_op jit(solution)/shard_map/pallas_call | solution.py:146
  48.4 2.0 %shard_map.41 = (bf16[64,640]{1,0:T(8,128)(2,1)S(1)}, bf16[64,640]{1,0:T(8,128)(2,1)S(1)}, bf16[64,640]{1,0:T(8,128)(2,1)S(1)}, bf16[64,640]{1,0:T(8,128)(2,1)S(1)}) custom-call(bf16[2,512,640]{2,1,0:T(8,128)(2,1)S(1)} %shard_map.39.own, bf16[2,512,640]{2,1,0:T(8,128)(2,1)S(1)} %collective-permute-done.7.other, ...), custom_call_target="tpu_custom_call" | custom-call | tf_op jit(solution)/shard_map/pallas_call | solution.py:146
  50.4 2.0 %collective-permute-start.14 = (bf16[64,640]{1,0:T(8,128)(2,1)S(1)}, bf16[64,640]{1,0:T(8,128)(2,1)S(1)}, u32[]{:S(2)}, u32[]{:S(2)}) collective-permute-start(bf16[64,640]{1,0:T(8,128)(2,1)S(1)} %get-tuple-element.64), channel_id=1, source_target_pairs={{0,4},{2,6},{4,0},{6,2},{8,12},{10,14},{12,8},{14,10},{1,5},{3,7},... | collective-permute-start | bytes 245768 | tf_op jit(solution)/shard_map/ppermute | solution.py:100
  52.4 1.2 %collective-permute-start.8 = (bf16[64,640]{1,0:T(8,128)(2,1)S(1)}, bf16[64,640]{1,0:T(8,128)(2,1)S(1)}, u32[]{:S(2)}, u32[]{:S(2)}) collective-permute-start(bf16[64,640]{1,0:T(8,128)(2,1)S(1)} %get-tuple-element.53), channel_id=1, source_target_pairs={{0,8},{2,10},{4,12},{6,14},{8,0},{10,2},{12,4},{14,6},{1,9},{3,11}... | collective-permute-start | bytes 245768 | tf_op jit(solution)/shard_map/ppermute | solution.py:100
  53.6 2.7 %collective-permute-start.9 = (bf16[64,640]{1,0:T(8,128)(2,1)S(1)}, bf16[64,640]{1,0:T(8,128)(2,1)S(1)}, u32[]{:S(2)}, u32[]{:S(2)}) collective-permute-start(bf16[64,640]{1,0:T(8,128)(2,1)S(1)} %get-tuple-element.55), channel_id=1, source_target_pairs={{0,10},{2,8},{4,14},{6,12},{8,2},{10,0},{12,6},{14,4},{1,11},{3,9}... | collective-permute-start | bytes 245768 | tf_op jit(solution)/shard_map/ppermute | solution.py:100
  56.3 0.5 collective-permute-start.16
  56.8 1.2 %shard_map.42 = (bf16[64,640]{1,0:T(8,128)(2,1)S(1)}, bf16[64,640]{1,0:T(8,128)(2,1)S(1)}) custom-call(bf16[2,512,640]{2,1,0:T(8,128)(2,1)S(1)} %shard_map.39.own, bf16[2,512,640]{2,1,0:T(8,128)(2,1)S(1)} %collective-permute-done.7.other, bf16[64,640]{1,0:T(8,128)(2,1)S(1)} %collective-permute-done.10.refs_0_, ...), custom_call_target="tpu_custom_call" | custom-call | tf_op jit(solution)/shard_map/pallas_call | solution.py:146
  58.0 2.6 %collective-permute-start.13 = (bf16[64,640]{1,0:T(8,128)(2,1)S(1)}, bf16[64,640]{1,0:T(8,128)(2,1)S(1)}, u32[]{:S(2)}, u32[]{:S(2)}) collective-permute-start(bf16[64,640]{1,0:T(8,128)(2,1)S(1)} %get-tuple-element.62), channel_id=1, source_target_pairs={{0,12},{2,14},{4,8},{6,10},{8,4},{10,6},{12,0},{14,2},{1,13},{3,15... | collective-permute-start | bytes 245768 | tf_op jit(solution)/shard_map/ppermute | solution.py:100
  60.6 2.3 %collective-permute-start.15 = (bf16[64,640]{1,0:T(8,128)(2,1)S(1)}, bf16[64,640]{1,0:T(8,128)(2,1)S(1)}, u32[]{:S(2)}, u32[]{:S(2)}) collective-permute-start(bf16[64,640]{1,0:T(8,128)(2,1)S(1)} %get-tuple-element.65), channel_id=1, source_target_pairs={{0,14},{2,12},{4,10},{6,8},{8,6},{10,4},{12,2},{14,0},{1,15},{3,13... | collective-permute-start | bytes 245768 | tf_op jit(solution)/shard_map/ppermute | solution.py:100
  62.8 0.8 %shard_map.43.refs_4_ = bf16[64,5120]{1,0:T(8,128)(2,1)} custom-call(s32[1]{0:T(128)} %bitcast.chip_ref, bf16[64,640]{1,0:T(8,128)(2,1)S(1)} %get-tuple-element.52.refs_0_, bf16[64,640]{1,0:T(8,128)(2,1)S(1)} %collective-permute-done.14.refs_1_, bf16[64,640]{1,0:T(8,128)(2,1)S(1)} %collective-permute-done.12.refs_2_, ...), custom_call_target="tpu_custom_call" | custom-call | tf_op jit(solution)/shard_map/pallas_call | solution.py:160
  63.6 3.2 %collective-permute-done.9.refs_1_ = bf16[64,640]{1,0:T(8,128)(2,1)S(1)} collective-permute-done((bf16[64,640]{1,0:T(8,128)(2,1)S(1)}, bf16[64,640]{1,0:T(8,128)(2,1)S(1)}, u32[]{:S(2)}, u32[]{:S(2)}) %collective-permute-start.9) | collective-permute-done | bytes 81952 | tf_op jit(solution)/shard_map/ppermute | solution.py:100
  66.8 1.0 %collective-permute-done.15.refs_3_ = bf16[64,640]{1,0:T(8,128)(2,1)S(1)} collective-permute-done((bf16[64,640]{1,0:T(8,128)(2,1)S(1)}, bf16[64,640]{1,0:T(8,128)(2,1)S(1)}, u32[]{:S(2)}, u32[]{:S(2)}) %collective-permute-start.15) | collective-permute-done | bytes 81952 | tf_op jit(solution)/shard_map/ppermute | solution.py:100
  67.8 0.8 %shard_map.44 = bf16[64,5120]{1,0:T(8,128)(2,1)} custom-call(s32[1]{0:T(128)} %bitcast.chip_ref, bf16[64,640]{1,0:T(8,128)(2,1)S(1)} %collective-permute-done.8.refs_0_, bf16[64,640]{1,0:T(8,128)(2,1)S(1)} %collective-permute-done.9.refs_1_, bf16[64,640]{1,0:T(8,128)(2,1)S(1)} %collective-permute-done.13.refs_2_, ...), custom_call_target="tpu_custom_call", output_to_operand_aliasing={{}: (5, {})} | custom-call | tf_op jit(solution)/shard_map/pallas_call | solution.py:160
  (18 shorter events, 0.5 us)
Async XLA Ops:
  1.2 12.1 %collective-permute-start.2 = (bf16[128,640]{1,0:T(8,128)(2,1)S(1)}, bf16[128,640]{1,0:T(8,128)(2,1)S(1)}, u32[]{:S(2)}, u32[]{:S(2)}) collective-permute-start(bf16[128,640]{1,0:T(8,128)(2,1)S(1)} %get-tuple-element.38), channel_id=1, source_target_pairs={{0,14},{2,12},{4,10},{6,8},{8,6},{10,4},{12,2},{14,0},{1,15},{3,13... | collective-permute-start | bytes 491528 | tf_op jit(solution)/shard_map/ppermute | solution.py:100
  7.3 8.9 %collective-permute-start = (bf16[128,640]{1,0:T(8,128)(2,1)S(1)}, bf16[128,640]{1,0:T(8,128)(2,1)S(1)}, u32[]{:S(2)}, u32[]{:S(2)}) collective-permute-start(bf16[128,640]{1,0:T(8,128)(2,1)S(1)} %get-tuple-element.36), channel_id=1, source_target_pairs={{0,12},{2,14},{4,8},{6,10},{8,4},{10,6},{12,0},{14,2},{1,13},{3,15... | collective-permute-start | bytes 491528 | tf_op jit(solution)/shard_map/ppermute | solution.py:100
  7.5 21.3 %collective-permute-start.1 = (bf16[192,640]{1,0:T(8,128)(2,1)S(1)}, bf16[192,640]{1,0:T(8,128)(2,1)S(1)}, u32[]{:S(2)}, u32[]{:S(2)}) collective-permute-start(bf16[192,640]{1,0:T(8,128)(2,1)S(1)} %get-tuple-element.37), channel_id=1, source_target_pairs={{0,4},{2,6},{4,0},{6,2},{8,12},{10,14},{12,8},{14,10},{1,5},{3,7},... | collective-permute-start | bytes 737288 | tf_op jit(solution)/shard_map/ppermute | solution.py:100
  9.0 28.8 %collective-permute-start.3 = (bf16[192,640]{1,0:T(8,128)(2,1)S(1)}, bf16[192,640]{1,0:T(8,128)(2,1)S(1)}, u32[]{:S(2)}, u32[]{:S(2)}) collective-permute-start(bf16[192,640]{1,0:T(8,128)(2,1)S(1)} %get-tuple-element.42), channel_id=1, source_target_pairs={{0,8},{2,10},{4,12},{6,14},{8,0},{10,2},{12,4},{14,6},{1,9},{3,11}... | collective-permute-start | bytes 737288 | tf_op jit(solution)/shard_map/ppermute | solution.py:100
  13.3 24.6 %collective-permute-start.4 = (bf16[192,640]{1,0:T(8,128)(2,1)S(1)}, bf16[192,640]{1,0:T(8,128)(2,1)S(1)}, u32[]{:S(2)}, u32[]{:S(2)}) collective-permute-start(bf16[192,640]{1,0:T(8,128)(2,1)S(1)} %get-tuple-element.43), channel_id=1, source_target_pairs={{0,6},{2,4},{4,2},{6,0},{8,14},{10,12},{12,10},{14,8},{1,7},{3,5},... | collective-permute-start | bytes 737288 | tf_op jit(solution)/shard_map/ppermute | solution.py:100
  13.3 24.6 %collective-permute-start.5 = (bf16[192,640]{1,0:T(8,128)(2,1)S(1)}, bf16[192,640]{1,0:T(8,128)(2,1)S(1)}, u32[]{:S(2)}, u32[]{:S(2)}) collective-permute-start(bf16[192,640]{1,0:T(8,128)(2,1)S(1)} %get-tuple-element.44), channel_id=1, source_target_pairs={{0,2},{2,0},{4,6},{6,4},{8,10},{10,8},{12,14},{14,12},{1,3},{3,1},... | collective-permute-start | bytes 737288 | tf_op jit(solution)/shard_map/ppermute | solution.py:100
  16.2 26.0 %collective-permute-start.6 = (bf16[192,640]{1,0:T(8,128)(2,1)S(1)}, bf16[192,640]{1,0:T(8,128)(2,1)S(1)}, u32[]{:S(2)}, u32[]{:S(2)}) collective-permute-start(bf16[192,640]{1,0:T(8,128)(2,1)S(1)} %get-tuple-element.45), channel_id=1, source_target_pairs={{0,10},{2,8},{4,14},{6,12},{8,2},{10,0},{12,6},{14,4},{1,11},{3,9}... | collective-permute-start | bytes 737288 | tf_op jit(solution)/shard_map/ppermute | solution.py:100
  42.3 4.9 %collective-permute-start.7 = (bf16[2,512,640]{2,1,0:T(8,128)(2,1)S(1)}, bf16[2,512,640]{2,1,0:T(8,128)(2,1)S(1)}, u32[]{:S(2)}, u32[]{:S(2)}) collective-permute-start(bf16[2,512,640]{2,1,0:T(8,128)(2,1)S(1)} %shard_map.39.own), channel_id=1, source_target_pairs={{0,1},{1,0},{2,3},{3,2},{4,5},{5,4},{6,7},{7,6},{8,9},{9,8},{10,11... | collective-permute-start | bytes 3932168 | tf_op jit(solution)/shard_map/ppermute | solution.py:139
  42.3 10.1 %collective-permute-start.10 = (bf16[64,640]{1,0:T(8,128)(2,1)S(1)}, bf16[64,640]{1,0:T(8,128)(2,1)S(1)}, u32[]{:S(2)}, u32[]{:S(2)}) collective-permute-start(bf16[64,640]{1,0:T(8,128)(2,1)S(1)} %get-tuple-element.56), channel_id=1, source_target_pairs={{0,12},{2,14},{4,8},{6,10},{8,4},{10,6},{12,0},{14,2},{1,13},{3,15... | collective-permute-start | bytes 245768 | tf_op jit(solution)/shard_map/ppermute | solution.py:100
  44.9 7.5 %collective-permute-start.11 = (bf16[64,640]{1,0:T(8,128)(2,1)S(1)}, bf16[64,640]{1,0:T(8,128)(2,1)S(1)}, u32[]{:S(2)}, u32[]{:S(2)}) collective-permute-start(bf16[64,640]{1,0:T(8,128)(2,1)S(1)} %get-tuple-element.57), channel_id=1, source_target_pairs={{0,14},{2,12},{4,10},{6,8},{8,6},{10,4},{12,2},{14,0},{1,15},{3,13... | collective-permute-start | bytes 245768 | tf_op jit(solution)/shard_map/ppermute | solution.py:100
  50.4 7.6 %collective-permute-start.12 = (bf16[64,640]{1,0:T(8,128)(2,1)S(1)}, bf16[64,640]{1,0:T(8,128)(2,1)S(1)}, u32[]{:S(2)}, u32[]{:S(2)}) collective-permute-start(bf16[64,640]{1,0:T(8,128)(2,1)S(1)} %get-tuple-element.61), channel_id=1, source_target_pairs={{0,6},{2,4},{4,2},{6,0},{8,14},{10,12},{12,10},{14,8},{1,7},{3,5},... | collective-permute-start | bytes 245768 | tf_op jit(solution)/shard_map/ppermute | solution.py:100
  50.4 10.1 %collective-permute-start.14 = (bf16[64,640]{1,0:T(8,128)(2,1)S(1)}, bf16[64,640]{1,0:T(8,128)(2,1)S(1)}, u32[]{:S(2)}, u32[]{:S(2)}) collective-permute-start(bf16[64,640]{1,0:T(8,128)(2,1)S(1)} %get-tuple-element.64), channel_id=1, source_target_pairs={{0,4},{2,6},{4,0},{6,2},{8,12},{10,14},{12,8},{14,10},{1,5},{3,7},... | collective-permute-start | bytes 245768 | tf_op jit(solution)/shard_map/ppermute | solution.py:100
  52.4 11.2 %collective-permute-start.8 = (bf16[64,640]{1,0:T(8,128)(2,1)S(1)}, bf16[64,640]{1,0:T(8,128)(2,1)S(1)}, u32[]{:S(2)}, u32[]{:S(2)}) collective-permute-start(bf16[64,640]{1,0:T(8,128)(2,1)S(1)} %get-tuple-element.53), channel_id=1, source_target_pairs={{0,8},{2,10},{4,12},{6,14},{8,0},{10,2},{12,4},{14,6},{1,9},{3,11}... | collective-permute-start | bytes 245768 | tf_op jit(solution)/shard_map/ppermute | solution.py:100
  53.6 13.2 %collective-permute-start.9 = (bf16[64,640]{1,0:T(8,128)(2,1)S(1)}, bf16[64,640]{1,0:T(8,128)(2,1)S(1)}, u32[]{:S(2)}, u32[]{:S(2)}) collective-permute-start(bf16[64,640]{1,0:T(8,128)(2,1)S(1)} %get-tuple-element.55), channel_id=1, source_target_pairs={{0,10},{2,8},{4,14},{6,12},{8,2},{10,0},{12,6},{14,4},{1,11},{3,9}... | collective-permute-start | bytes 245768 | tf_op jit(solution)/shard_map/ppermute | solution.py:100
  56.3 6.5 %collective-permute-start.16 = (bf16[64,640]{1,0:T(8,128)(2,1)S(1)}, bf16[64,640]{1,0:T(8,128)(2,1)S(1)}, u32[]{:S(2)}, u32[]{:S(2)}) collective-permute-start(bf16[64,640]{1,0:T(8,128)(2,1)S(1)} %get-tuple-element.66), channel_id=1, source_target_pairs={{0,2},{2,0},{4,6},{6,4},{8,10},{10,8},{12,14},{14,12},{1,3},{3,1},... | collective-permute-start | bytes 245768 | tf_op jit(solution)/shard_map/ppermute | solution.py:100
  58.0 8.8 %collective-permute-start.13 = (bf16[64,640]{1,0:T(8,128)(2,1)S(1)}, bf16[64,640]{1,0:T(8,128)(2,1)S(1)}, u32[]{:S(2)}, u32[]{:S(2)}) collective-permute-start(bf16[64,640]{1,0:T(8,128)(2,1)S(1)} %get-tuple-element.62), channel_id=1, source_target_pairs={{0,12},{2,14},{4,8},{6,10},{8,4},{10,6},{12,0},{14,2},{1,13},{3,15... | collective-permute-start | bytes 245768 | tf_op jit(solution)/shard_map/ppermute | solution.py:100
  60.6 7.2 %collective-permute-start.15 = (bf16[64,640]{1,0:T(8,128)(2,1)S(1)}, bf16[64,640]{1,0:T(8,128)(2,1)S(1)}, u32[]{:S(2)}, u32[]{:S(2)}) collective-permute-start(bf16[64,640]{1,0:T(8,128)(2,1)S(1)} %get-tuple-element.65), channel_id=1, source_target_pairs={{0,14},{2,12},{4,10},{6,8},{8,6},{10,4},{12,2},{14,0},{1,15},{3,13... | collective-permute-start | bytes 245768 | tf_op jit(solution)/shard_map/ppermute | solution.py:100

commit v2 on v1

--- a/solution.py
+++ b/solution.py
@@ -147,14 +147,15 @@
         return dict(zip(ks, outs))
 
     outs = attend((4, 5))
-    outs |= attend(NEAR + (0,), (outs[4],))
-    outs |= attend(LAST, (outs[0],))
+    outs |= attend(LAST, (outs[4],))
+    outs |= attend(NEAR + (0,), (outs[LAST[0]],))
+
     def send(k, *after):
         return across(lax.optimization_barrier((outs[k], *after))[0], k)
 
-    back = {k: across(outs[k], k) for k in NEAR + (0,)}
-    back |= {k: send(k, outs[0]) for k in (4, 5)}
-    back |= {7: send(7, back[2]), 6: send(6, back[3])}
+    back = {k: across(outs[k], k) for k in (0, 4, 5, 6)}
+    back[7] = send(7, outs[0])
+    back |= {k: send(k, outs[0], back[before]) for k, before in ((1, 5), (3, 4), (2, 4))}
 
     def unpack(order, so_far=()):
         return pl.pallas_call(
@@ -168,7 +169,7 @@
             cost_estimate=FREE,
         )(chip, *[back[k] for k in order], *so_far)
 
-    result = unpack((4, 5) + LAST, (unpack((0,) + NEAR),))
+    result = unpack((7, 3, 2, 1), (unpack((0, 4, 5, 6)),))
     return result.reshape(layers, tok_rows, width)
 
 

time: 68.8 us -> 68.8 us (level)
  transfers between devices with their start and end apart: 17 -> 17, of which waited for: 5 -> 6; matrix products, arithmetic and copies ran while one was open for 0% -> 0% of each run, Pallas kernels for 10% -> 10%
where the time goes in v2:
time: 68.8 us; the launch traced here: 68.6 us
  starting transfers between devices  41 us (60%)
  waiting for transfers between devices  18.9 us (27%)
  Pallas kernels  8.66 us (13%)
    ppermute x16, starting transfers between devices, across(): lax.ppermute(piece, 'chip', [(i, i ^ k) for i in range(chips)])  40.9 us
    ppermute x16, waiting for transfers between devices, across(): lax.ppermute(piece, 'chip', [(i, i ^ k) for i in range(chips)])  18.9 us
    pallas_call x3, Pallas kernels, attend(): call(body, 2 + len(ks), [shape(rows, gw)] * len(ks))(own, other, *pieces)  4.33 us
    pallas_call x2, Pallas kernels, pack(): pl.pallas_call(functools.partial(pack_body, rows, gw, layout), in_specs=[...  2.73 us
    pallas_call x2, Pallas kernels, unpack(): pl.pallas_call(functools.partial(unpack_body, gw, order), in_specs=[SMEM]...  1.5 us
  transfers between devices with their start and end apart: 17, of which 6 were waited for; matrix products, arithmetic and copies ran while one was open for 0% of the time, Pallas kernels for 10%

profile of v2, /device:TPU:0, one launch (start us, length us, event | category | flops | bytes accessed | tf_op | source)
XLA Modules:
  0.0 68.6 jit_solution(16143669896850081557)
XLA Ops:
  0.0 1.2 %shard_map.37 = (bf16[128,640]{1,0:T(8,128)(2,1)S(1)}, bf16[192,640]{1,0:T(8,128)(2,1)S(1)}, bf16[128,640]{1,0:T(8,128)(2,1)S(1)}) custom-call(s32[1]{0:T(128)} %bitcast.chip_ref, bf16[64,5120]{1,0:T(8,128)(2,1)} %refs_0_.2, bf16[64,5120]{1,0:T(8,128)(2,1)} %refs_1_.2, bf16[64,5120]{1,0:T(8,128)(2,1)} %bitcast.3), custom_call_target="tpu_custom_call" | custom-call | tf_op jit(solution)/shard_map/pallas_call | solution.py:121
  1.2 6.1 %collective-permute-start.2 = (bf16[128,640]{1,0:T(8,128)(2,1)S(1)}, bf16[128,640]{1,0:T(8,128)(2,1)S(1)}, u32[]{:S(2)}, u32[]{:S(2)}) collective-permute-start(bf16[128,640]{1,0:T(8,128)(2,1)S(1)} %get-tuple-element.38), channel_id=1, source_target_pairs={{0,14},{2,12},{4,10},{6,8},{8,6},{10,4},{12,2},{14,0},{1,15},{3,13... | collective-permute-start | bytes 491528 | tf_op jit(solution)/shard_map/ppermute | solution.py:100
  7.5 1.5 %shard_map.38 = (bf16[192,640]{1,0:T(8,128)(2,1)S(1)}, bf16[192,640]{1,0:T(8,128)(2,1)S(1)}, bf16[192,640]{1,0:T(8,128)(2,1)S(1)}, bf16[192,640]{1,0:T(8,128)(2,...) custom-call(s32[1]{0:T(128)} %bitcast.chip_ref, ...), custom_call_target="tpu_custom_call" | custom-call | tf_op jit(solution)/shard_map/pallas_call | solution.py:121
  9.0 4.2 %collective-permute-start.3 = (bf16[192,640]{1,0:T(8,128)(2,1)S(1)}, bf16[192,640]{1,0:T(8,128)(2,1)S(1)}, u32[]{:S(2)}, u32[]{:S(2)}) collective-permute-start(bf16[192,640]{1,0:T(8,128)(2,1)S(1)} %get-tuple-element.42), channel_id=1, source_target_pairs={{0,8},{2,10},{4,12},{6,14},{8,0},{10,2},{12,4},{14,6},{1,9},{3,11}... | collective-permute-start | bytes 737288 | tf_op jit(solution)/shard_map/ppermute | solution.py:100
  13.3 1.5 %collective-permute-start.5 = (bf16[192,640]{1,0:T(8,128)(2,1)S(1)}, bf16[192,640]{1,0:T(8,128)(2,1)S(1)}, u32[]{:S(2)}, u32[]{:S(2)}) collective-permute-start(bf16[192,640]{1,0:T(8,128)(2,1)S(1)} %get-tuple-element.44), channel_id=1, source_target_pairs={{0,2},{2,0},{4,6},{6,4},{8,10},{10,8},{12,14},{14,12},{1,3},{3,1},... | collective-permute-start | bytes 737288 | tf_op jit(solution)/shard_map/ppermute | solution.py:100
  14.7 1.4 %collective-permute-done.refs_0_ = bf16[128,640]{1,0:T(8,128)(2,1)S(1)} collective-permute-done((bf16[128,640]{1,0:T(8,128)(2,1)S(1)}, bf16[128,640]{1,0:T(8,128)(2,1)S(1)}, u32[]{:S(2)}, u32[]{:S(2)}) %collective-permute-start) | collective-permute-done | bytes 163872 | tf_op jit(solution)/shard_map/ppermute | solution.py:100
  16.2 12.6 %collective-permute-start.6 = (bf16[192,640]{1,0:T(8,128)(2,1)S(1)}, bf16[192,640]{1,0:T(8,128)(2,1)S(1)}, u32[]{:S(2)}, u32[]{:S(2)}) collective-permute-start(bf16[192,640]{1,0:T(8,128)(2,1)S(1)} %get-tuple-element.45), channel_id=1, source_target_pairs={{0,10},{2,8},{4,14},{6,12},{8,2},{10,0},{12,6},{14,4},{1,11},{3,9}... | collective-permute-start | bytes 737288 | tf_op jit(solution)/shard_map/ppermute | solution.py:100
  28.8 9.0 %collective-permute-done.3.refs_3_.refs_0_ = bf16[192,640]{1,0:T(8,128)(2,1)S(1)} collective-permute-done((bf16[192,640]{1,0:T(8,128)(2,1)S(1)}, bf16[192,640]{1,0:T(8,128)(2,1)S(1)}, u32[]{:S(2)}, u32[]{:S(2)}) %collective-permute-start.3) | collective-permute-done | bytes 245792 | tf_op jit(solution)/shard_map/ppermute | solution.py:100
  37.9 4.3 %collective-permute-done.6.refs_6_.refs_1_ = bf16[192,640]{1,0:T(8,128)(2,1)S(1)} collective-permute-done((bf16[192,640]{1,0:T(8,128)(2,1)S(1)}, bf16[192,640]{1,0:T(8,128)(2,1)S(1)}, u32[]{:S(2)}, u32[]{:S(2)}) %collective-permute-start.6) | collective-permute-done | bytes 245792 | tf_op jit(solution)/shard_map/ppermute | solution.py:100
  42.3 2.6 %collective-permute-start.8 = (bf16[64,640]{1,0:T(8,128)(2,1)S(1)}, bf16[64,640]{1,0:T(8,128)(2,1)S(1)}, u32[]{:S(2)}, u32[]{:S(2)}) collective-permute-start(bf16[64,640]{1,0:T(8,128)(2,1)S(1)} %get-tuple-element.47), channel_id=1, source_target_pairs={{0,12},{2,14},{4,8},{6,10},{8,4},{10,6},{12,0},{14,2},{1,13},{3,15... | collective-permute-start | bytes 245768 | tf_op jit(solution)/shard_map/ppermute | solution.py:100
  44.9 2.3 %collective-permute-start.9 = (bf16[64,640]{1,0:T(8,128)(2,1)S(1)}, bf16[64,640]{1,0:T(8,128)(2,1)S(1)}, u32[]{:S(2)}, u32[]{:S(2)}) collective-permute-start(bf16[64,640]{1,0:T(8,128)(2,1)S(1)} %get-tuple-element.48), channel_id=1, source_target_pairs={{0,14},{2,12},{4,10},{6,8},{8,6},{10,4},{12,2},{14,0},{1,15},{3,13... | collective-permute-start | bytes 245768 | tf_op jit(solution)/shard_map/ppermute | solution.py:100
  47.2 1.2 %shard_map.40 = (bf16[64,640]{1,0:T(8,128)(2,1)S(1)}, bf16[64,640]{1,0:T(8,128)(2,1)S(1)}) custom-call(bf16[2,512,640]{2,1,0:T(8,128)(2,1)S(1)} %shard_map.39.own, bf16[2,512,640]{2,1,0:T(8,128)(2,1)S(1)} %collective-permute-done.7.other, bf16[192,640]{1,0:T(8,128)(2,1)S(1)} %collective-permute-done.3.refs_3_.refs_0_, ...), custom_call_target="tpu_custom_call" | custom-call | tf_op jit(solution)/shard_map/pallas_call | solution.py:146
  48.4 2.9 %collective-permute-start.11 = (bf16[64,640]{1,0:T(8,128)(2,1)S(1)}, bf16[64,640]{1,0:T(8,128)(2,1)S(1)}, u32[]{:S(2)}, u32[]{:S(2)}) collective-permute-start(bf16[64,640]{1,0:T(8,128)(2,1)S(1)} %get-tuple-element.49), channel_id=1, source_target_pairs={{0,8},{2,10},{4,12},{6,14},{8,0},{10,2},{12,4},{14,6},{1,9},{3,11}... | collective-permute-start | bytes 245768 | tf_op jit(solution)/shard_map/ppermute | solution.py:100
  51.3 1.4 %collective-permute-done.9.refs_1_ = bf16[64,640]{1,0:T(8,128)(2,1)S(1)} collective-permute-done((bf16[64,640]{1,0:T(8,128)(2,1)S(1)}, bf16[64,640]{1,0:T(8,128)(2,1)S(1)}, u32[]{:S(2)}, u32[]{:S(2)}) %collective-permute-start.9) | collective-permute-done | bytes 81952 | tf_op jit(solution)/shard_map/ppermute | solution.py:100
  52.7 1.2 %shard_map.41 = (bf16[64,640]{1,0:T(8,128)(2,1)S(1)}, bf16[64,640]{1,0:T(8,128)(2,1)S(1)}) custom-call(bf16[2,512,640]{2,1,0:T(8,128)(2,1)S(1)} %shard_map.39.own, bf16[2,512,640]{2,1,0:T(8,128)(2,1)S(1)} %collective-permute-done.7.other, bf16[64,640]{1,0:T(8,128)(2,1)S(1)} %collective-permute-done.8.refs_0_, bf16[64,640]{1,0:T(8,128)(2,1)S(1)} %collective-permute-done.9.refs_1_), custom_call_target="tpu_custom_call" | custom-call | tf_op jit(solution)/shard_map/pallas_call | solution.py:146
  53.9 2.0 %collective-permute-start.16 = (bf16[64,640]{1,0:T(8,128)(2,1)S(1)}, bf16[64,640]{1,0:T(8,128)(2,1)S(1)}, u32[]{:S(2)}, u32[]{:S(2)}) collective-permute-start(bf16[64,640]{1,0:T(8,128)(2,1)S(1)} %get-tuple-element.53), channel_id=1, source_target_pairs={{0,12},{2,14},{4,8},{6,10},{8,4},{10,6},{12,0},{14,2},{1,13},{3,15... | collective-permute-start | bytes 245768 | tf_op jit(solution)/shard_map/ppermute | solution.py:100
  55.9 2.0 %shard_map.42 = (bf16[64,640]{1,0:T(8,128)(2,1)S(1)}, bf16[64,640]{1,0:T(8,128)(2,1)S(1)}, bf16[64,640]{1,0:T(8,128)(2,1)S(1)}, bf16[64,640]{1,0:T(8,128)(2,1)S(1)}) custom-call(bf16[2,512,640]{2,1,0:T(8,128)(2,1)S(1)} %shard_map.39.own, bf16[2,512,640]{2,1,0:T(8,128)(2,1)S(1)} %collective-permute-done.7.other, ...), custom_call_target="tpu_custom_call" | custom-call | tf_op jit(solution)/shard_map/pallas_call | solution.py:146
  57.9 3.0 %collective-permute-start.10 = (bf16[64,640]{1,0:T(8,128)(2,1)S(1)}, bf16[64,640]{1,0:T(8,128)(2,1)S(1)}, u32[]{:S(2)}, u32[]{:S(2)}) collective-permute-start(bf16[64,640]{1,0:T(8,128)(2,1)S(1)} %get-tuple-element.59), channel_id=1, source_target_pairs={{0,14},{2,12},{4,10},{6,8},{8,6},{10,4},{12,2},{14,0},{1,15},{3,13... | collective-permute-start | bytes 245768 | tf_op jit(solution)/shard_map/ppermute | solution.py:100
  60.9 0.4 collective-permute-start.15
  61.3 3.1 %collective-permute-start.13 = (bf16[64,640]{1,0:T(8,128)(2,1)S(1)}, bf16[64,640]{1,0:T(8,128)(2,1)S(1)}, u32[]{:S(2)}, u32[]{:S(2)}) collective-permute-start(bf16[64,640]{1,0:T(8,128)(2,1)S(1)} %get-tuple-element.63), channel_id=1, source_target_pairs={{0,4},{2,6},{4,0},{6,2},{8,12},{10,14},{12,8},{14,10},{1,5},{3,7},... | collective-permute-start | bytes 245768 | tf_op jit(solution)/shard_map/ppermute | solution.py:100
  64.4 0.8 %shard_map.43.refs_4_ = bf16[64,5120]{1,0:T(8,128)(2,1)} custom-call(s32[1]{0:T(128)} %bitcast.chip_ref, bf16[64,640]{1,0:T(8,128)(2,1)S(1)} %get-tuple-element.58.refs_0_, bf16[64,640]{1,0:T(8,128)(2,1)S(1)} %collective-permute-done.11.refs_1_, bf16[64,640]{1,0:T(8,128)(2,1)S(1)} %collective-permute-done.14.refs_2_, ...), custom_call_target="tpu_custom_call" | custom-call | tf_op jit(solution)/shard_map/pallas_call | solution.py:161
  65.2 0.9 %collective-permute-done.10.refs_0_ = bf16[64,640]{1,0:T(8,128)(2,1)S(1)} collective-permute-done((bf16[64,640]{1,0:T(8,128)(2,1)S(1)}, bf16[64,640]{1,0:T(8,128)(2,1)S(1)}, u32[]{:S(2)}, u32[]{:S(2)}) %collective-permute-start.10) | collective-permute-done | bytes 81952 | tf_op jit(solution)/shard_map/ppermute | solution.py:100
  66.0 1.8 %collective-permute-done.15.refs_3_ = bf16[64,640]{1,0:T(8,128)(2,1)S(1)} collective-permute-done((bf16[64,640]{1,0:T(8,128)(2,1)S(1)}, bf16[64,640]{1,0:T(8,128)(2,1)S(1)}, u32[]{:S(2)}, u32[]{:S(2)}) %collective-permute-start.15) | collective-permute-done | bytes 81952 | tf_op jit(solution)/shard_map/ppermute | solution.py:100
  67.9 0.8 %shard_map.44 = bf16[64,5120]{1,0:T(8,128)(2,1)} custom-call(s32[1]{0:T(128)} %bitcast.chip_ref, bf16[64,640]{1,0:T(8,128)(2,1)S(1)} %collective-permute-done.10.refs_0_, bf16[64,640]{1,0:T(8,128)(2,1)S(1)} %collective-permute-done.12.refs_1_, bf16[64,640]{1,0:T(8,128)(2,1)S(1)} %collective-permute-done.13.refs_2_, ...), custom_call_target="tpu_custom_call", output_to_operand_aliasing={{}: (5, {})} | custom-call | tf_op jit(solution)/shard_map/pallas_call | solution.py:161
  (18 shorter events, 0.5 us)
Async XLA Ops:
  1.2 12.1 %collective-permute-start.2 = (bf16[128,640]{1,0:T(8,128)(2,1)S(1)}, bf16[128,640]{1,0:T(8,128)(2,1)S(1)}, u32[]{:S(2)}, u32[]{:S(2)}) collective-permute-start(bf16[128,640]{1,0:T(8,128)(2,1)S(1)} %get-tuple-element.38), channel_id=1, source_target_pairs={{0,14},{2,12},{4,10},{6,8},{8,6},{10,4},{12,2},{14,0},{1,15},{3,13... | collective-permute-start | bytes 491528 | tf_op jit(solution)/shard_map/ppermute | solution.py:100
  7.3 8.9 %collective-permute-start = (bf16[128,640]{1,0:T(8,128)(2,1)S(1)}, bf16[128,640]{1,0:T(8,128)(2,1)S(1)}, u32[]{:S(2)}, u32[]{:S(2)}) collective-permute-start(bf16[128,640]{1,0:T(8,128)(2,1)S(1)} %get-tuple-element.36), channel_id=1, source_target_pairs={{0,12},{2,14},{4,8},{6,10},{8,4},{10,6},{12,0},{14,2},{1,13},{3,15... | collective-permute-start | bytes 491528 | tf_op jit(solution)/shard_map/ppermute | solution.py:100
  7.5 21.3 %collective-permute-start.1 = (bf16[192,640]{1,0:T(8,128)(2,1)S(1)}, bf16[192,640]{1,0:T(8,128)(2,1)S(1)}, u32[]{:S(2)}, u32[]{:S(2)}) collective-permute-start(bf16[192,640]{1,0:T(8,128)(2,1)S(1)} %get-tuple-element.37), channel_id=1, source_target_pairs={{0,4},{2,6},{4,0},{6,2},{8,12},{10,14},{12,8},{14,10},{1,5},{3,7},... | collective-permute-start | bytes 737288 | tf_op jit(solution)/shard_map/ppermute | solution.py:100
  9.0 28.8 %collective-permute-start.3 = (bf16[192,640]{1,0:T(8,128)(2,1)S(1)}, bf16[192,640]{1,0:T(8,128)(2,1)S(1)}, u32[]{:S(2)}, u32[]{:S(2)}) collective-permute-start(bf16[192,640]{1,0:T(8,128)(2,1)S(1)} %get-tuple-element.42), channel_id=1, source_target_pairs={{0,8},{2,10},{4,12},{6,14},{8,0},{10,2},{12,4},{14,6},{1,9},{3,11}... | collective-permute-start | bytes 737288 | tf_op jit(solution)/shard_map/ppermute | solution.py:100
  13.3 24.6 %collective-permute-start.4 = (bf16[192,640]{1,0:T(8,128)(2,1)S(1)}, bf16[192,640]{1,0:T(8,128)(2,1)S(1)}, u32[]{:S(2)}, u32[]{:S(2)}) collective-permute-start(bf16[192,640]{1,0:T(8,128)(2,1)S(1)} %get-tuple-element.43), channel_id=1, source_target_pairs={{0,6},{2,4},{4,2},{6,0},{8,14},{10,12},{12,10},{14,8},{1,7},{3,5},... | collective-permute-start | bytes 737288 | tf_op jit(solution)/shard_map/ppermute | solution.py:100
  13.3 24.6 %collective-permute-start.5 = (bf16[192,640]{1,0:T(8,128)(2,1)S(1)}, bf16[192,640]{1,0:T(8,128)(2,1)S(1)}, u32[]{:S(2)}, u32[]{:S(2)}) collective-permute-start(bf16[192,640]{1,0:T(8,128)(2,1)S(1)} %get-tuple-element.44), channel_id=1, source_target_pairs={{0,2},{2,0},{4,6},{6,4},{8,10},{10,8},{12,14},{14,12},{1,3},{3,1},... | collective-permute-start | bytes 737288 | tf_op jit(solution)/shard_map/ppermute | solution.py:100
  16.2 26.0 %collective-permute-start.6 = (bf16[192,640]{1,0:T(8,128)(2,1)S(1)}, bf16[192,640]{1,0:T(8,128)(2,1)S(1)}, u32[]{:S(2)}, u32[]{:S(2)}) collective-permute-start(bf16[192,640]{1,0:T(8,128)(2,1)S(1)} %get-tuple-element.45), channel_id=1, source_target_pairs={{0,10},{2,8},{4,14},{6,12},{8,2},{10,0},{12,6},{14,4},{1,11},{3,9}... | collective-permute-start | bytes 737288 | tf_op jit(solution)/shard_map/ppermute | solution.py:100
  42.3 4.9 %collective-permute-start.7 = (bf16[2,512,640]{2,1,0:T(8,128)(2,1)S(1)}, bf16[2,512,640]{2,1,0:T(8,128)(2,1)S(1)}, u32[]{:S(2)}, u32[]{:S(2)}) collective-permute-start(bf16[2,512,640]{2,1,0:T(8,128)(2,1)S(1)} %shard_map.39.own), channel_id=1, source_target_pairs={{0,1},{1,0},{2,3},{3,2},{4,5},{5,4},{6,7},{7,6},{8,9},{9,8},{10,11... | collective-permute-start | bytes 3932168 | tf_op jit(solution)/shard_map/ppermute | solution.py:139
  42.3 9.0 %collective-permute-start.8 = (bf16[64,640]{1,0:T(8,128)(2,1)S(1)}, bf16[64,640]{1,0:T(8,128)(2,1)S(1)}, u32[]{:S(2)}, u32[]{:S(2)}) collective-permute-start(bf16[64,640]{1,0:T(8,128)(2,1)S(1)} %get-tuple-element.47), channel_id=1, source_target_pairs={{0,12},{2,14},{4,8},{6,10},{8,4},{10,6},{12,0},{14,2},{1,13},{3,15... | collective-permute-start | bytes 245768 | tf_op jit(solution)/shard_map/ppermute | solution.py:100
  44.9 7.8 %collective-permute-start.9 = (bf16[64,640]{1,0:T(8,128)(2,1)S(1)}, bf16[64,640]{1,0:T(8,128)(2,1)S(1)}, u32[]{:S(2)}, u32[]{:S(2)}) collective-permute-start(bf16[64,640]{1,0:T(8,128)(2,1)S(1)} %get-tuple-element.48), channel_id=1, source_target_pairs={{0,14},{2,12},{4,10},{6,8},{8,6},{10,4},{12,2},{14,0},{1,15},{3,13... | collective-permute-start | bytes 245768 | tf_op jit(solution)/shard_map/ppermute | solution.py:100
  48.4 12.5 %collective-permute-start.14 = (bf16[64,640]{1,0:T(8,128)(2,1)S(1)}, bf16[64,640]{1,0:T(8,128)(2,1)S(1)}, u32[]{:S(2)}, u32[]{:S(2)}) collective-permute-start(bf16[64,640]{1,0:T(8,128)(2,1)S(1)} %get-tuple-element.65), channel_id=1, source_target_pairs={{0,10},{2,8},{4,14},{6,12},{8,2},{10,0},{12,6},{14,4},{1,11},{3,9}... | collective-permute-start | bytes 245768 | tf_op jit(solution)/shard_map/ppermute | solution.py:100
  48.4 12.9 %collective-permute-start.11 = (bf16[64,640]{1,0:T(8,128)(2,1)S(1)}, bf16[64,640]{1,0:T(8,128)(2,1)S(1)}, u32[]{:S(2)}, u32[]{:S(2)}) collective-permute-start(bf16[64,640]{1,0:T(8,128)(2,1)S(1)} %get-tuple-element.49), channel_id=1, source_target_pairs={{0,8},{2,10},{4,12},{6,14},{8,0},{10,2},{12,4},{14,6},{1,9},{3,11}... | collective-permute-start | bytes 245768 | tf_op jit(solution)/shard_map/ppermute | solution.py:100
  53.9 10.5 %collective-permute-start.16 = (bf16[64,640]{1,0:T(8,128)(2,1)S(1)}, bf16[64,640]{1,0:T(8,128)(2,1)S(1)}, u32[]{:S(2)}, u32[]{:S(2)}) collective-permute-start(bf16[64,640]{1,0:T(8,128)(2,1)S(1)} %get-tuple-element.53), channel_id=1, source_target_pairs={{0,12},{2,14},{4,8},{6,10},{8,4},{10,6},{12,0},{14,2},{1,13},{3,15... | collective-permute-start | bytes 245768 | tf_op jit(solution)/shard_map/ppermute | solution.py:100
  57.9 8.1 %collective-permute-start.10 = (bf16[64,640]{1,0:T(8,128)(2,1)S(1)}, bf16[64,640]{1,0:T(8,128)(2,1)S(1)}, u32[]{:S(2)}, u32[]{:S(2)}) collective-permute-start(bf16[64,640]{1,0:T(8,128)(2,1)S(1)} %get-tuple-element.59), channel_id=1, source_target_pairs={{0,14},{2,12},{4,10},{6,8},{8,6},{10,4},{12,2},{14,0},{1,15},{3,13... | collective-permute-start | bytes 245768 | tf_op jit(solution)/shard_map/ppermute | solution.py:100
  60.9 7.0 %collective-permute-start.15 = (bf16[64,640]{1,0:T(8,128)(2,1)S(1)}, bf16[64,640]{1,0:T(8,128)(2,1)S(1)}, u32[]{:S(2)}, u32[]{:S(2)}) collective-permute-start(bf16[64,640]{1,0:T(8,128)(2,1)S(1)} %get-tuple-element.66), channel_id=1, source_target_pairs={{0,2},{2,0},{4,6},{6,4},{8,10},{10,8},{12,14},{14,12},{1,3},{3,1},... | collective-permute-start | bytes 245768 | tf_op jit(solution)/shard_map/ppermute | solution.py:100
  61.3 6.5 %collective-permute-start.12 = (bf16[64,640]{1,0:T(8,128)(2,1)S(1)}, bf16[64,640]{1,0:T(8,128)(2,1)S(1)}, u32[]{:S(2)}, u32[]{:S(2)}) collective-permute-start(bf16[64,640]{1,0:T(8,128)(2,1)S(1)} %get-tuple-element.61), channel_id=1, source_target_pairs={{0,6},{2,4},{4,2},{6,0},{8,14},{10,12},{12,10},{14,8},{1,7},{3,5},... | collective-permute-start | bytes 245768 | tf_op jit(solution)/shard_map/ppermute | solution.py:100
  61.3 6.5 %collective-permute-start.13 = (bf16[64,640]{1,0:T(8,128)(2,1)S(1)}, bf16[64,640]{1,0:T(8,128)(2,1)S(1)}, u32[]{:S(2)}, u32[]{:S(2)}) collective-permute-start(bf16[64,640]{1,0:T(8,128)(2,1)S(1)} %get-tuple-element.63), channel_id=1, source_target_pairs={{0,4},{2,6},{4,0},{6,2},{8,12},{10,14},{12,8},{14,10},{1,5},{3,7},... | collective-permute-start | bytes 245768 | tf_op jit(solution)/shard_map/ppermute | solution.py:100

commit v3 on v0

--- a/solution.py
+++ b/solution.py
@@ -36,17 +36,23 @@
     return jnp.concatenate([v, jnp.ones_like(v)], axis=1)
 
 
-FIRST = (6, 2, 7)
-REST = (4, 3, 1, 5, 0)
-LAST = (6, 7)
-NEAR = (2, 3, 1)
-
-
-def pack_body(rows, gw, layout, chip_ref, *refs):
+LAST = 3
+JOINED_BY = (0, 0)
+UNPACK = (2,), (LAST, 1, 0)
+FIRST = ((3, 0), (1, 0), (3, 1))
+REST = ((2, 0), (1, 1), (0, 0), (2, 1), (0, 1))
+
+
+def columns(at_ref, dz, cross, gw):
+    group = at_ref[0] ^ (2 * dz + (at_ref[1] ^ cross))
+    return pl.ds(pl.multiple_of(group * gw, HEAD_DIM), gw)
+
+
+def pack_body(rows, gw, layout, at_ref, *refs):
     arrays, out_refs, sems = refs[:3], refs[3:-1], refs[-1]
     copies = []
-    for out_ref, (k, parts) in zip(out_refs, layout):
-        col = pl.ds(pl.multiple_of((chip_ref[0] ^ k) * gw, HEAD_DIM), gw)
+    for out_ref, (piece, parts) in zip(out_refs, layout):
+        col = columns(at_ref, *piece, gw)
         for at, n in enumerate(parts):
             to = out_ref.at[at * rows : (at + 1) * rows]
             copies.append(pltpu.make_async_copy(arrays[n].at[:, col], to, sems.at[len(copies)]))
@@ -63,12 +69,13 @@
             out_ref[which, n * rows : (n + 1) * rows] = piece[which * rows : (which + 1) * rows]
 
 
-def unpack_body(gw, order, chip_ref, *refs):
+def unpack_body(gw, order, at_ref, *refs):
     pieces, out_ref, sems = refs[: len(order)], refs[-2], refs[-1]
+    rows = out_ref.shape[0]
     copies = []
-    for n, k in enumerate(order):
-        col = pl.ds(pl.multiple_of((chip_ref[0] ^ k) * gw, HEAD_DIM), gw)
-        copies.append(pltpu.make_async_copy(pieces[n], out_ref.at[:, col], sems.at[n]))
+    for n, piece in enumerate(order):
+        to = out_ref.at[:, columns(at_ref, *piece, gw)]
+        copies.append(pltpu.make_async_copy(pieces[n].at[:rows], to, sems.at[n]))
     for copy in copies:
         copy.start()
     for copy in copies:
@@ -79,12 +86,12 @@
     queries, outs = refs[:count], refs[count:]
     for h in range(own.shape[2] // HEAD_DIM):
         col = slice(h * HEAD_DIM, (h + 1) * HEAD_DIM)
-        q = jnp.concatenate([r[r.shape[0] - rows :, col] for r in queries], axis=0)
+        q = [r[...][:, col] if r.shape[0] == 2 * rows else r[2 * rows :, col] for r in queries]
         va, vb = beside_ones(own[1, :, col]), beside_ones(other[1, :, col])
-        acc, _, total = softmax_rows(q, own[0, :, col], va, other[0, :, col], vb)
+        acc, _, total = softmax_rows(jnp.concatenate(q, axis=0), own[0, :, col], va, other[0, :, col], vb)
         acc = (acc / total).astype(BF16)
         for n, out in enumerate(outs):
-            out[:, col] = acc[n * rows : (n + 1) * rows]
+            out[:, col] = acc[n * 2 * rows : (n + 1) * 2 * rows]
 
 
 def local_permutes(keys, values, queries):
@@ -94,20 +101,28 @@
     layers, tok_rows, _ = queries.shape
     rows_q = layers * tok_rows
     assert rows_q == rows
-    chip = lax.axis_index("chip").reshape(1).astype(jnp.int32)
-
-    def across(piece, k):
-        return lax.ppermute(piece, "chip", [(i, i ^ k) for i in range(chips)]) if k else piece
-
-    def call(body, n_in, out_shape, smem=0, **more):
+    at = jnp.stack([lax.axis_index("chip"), lax.axis_index("core")]).astype(jnp.int32)
+
+    def across(array, dz, cross):
+        senders = [(chip, core) for chip in range(chips) for core in range(2)]
+        to = [(chip ^ (2 * dz + (core ^ cross)), core ^ cross) for chip, core in senders]
+        pairs = [(2 * a + b, 2 * c + d) for (a, b), (c, d) in zip(senders, to)]
+        return lax.ppermute(array, ("chip", "core"), pairs)
+
+    def swap(array):
+        return lax.ppermute(array, "core", [(0, 1), (1, 0)])
+
+    def after(array, *others):
+        return lax.optimization_barrier((array, *others))[0]
+
+    def call(body, n_in, out_shape):
         return pl.pallas_call(
             body,
-            in_specs=[SMEM] * smem + [VMEM] * n_in,
+            in_specs=[VMEM] * n_in,
             out_specs=jax.tree.map(lambda _: VMEM, out_shape),
             out_shape=out_shape,
             compiler_params=PARAMS,
             cost_estimate=FREE,
-            **more,
         )
 
     def shape(*dims):
@@ -116,8 +131,8 @@
     sources = [keys, values, queries.reshape(rows_q, width)]
     sources = [pltpu.with_memory_space_constraint(a, pltpu.HBM) for a in sources]
 
-    def pack(layout, after=()):
-        arrays = lax.optimization_barrier((*sources, *after))[:3] if after else sources
+    def pack(layout, *others):
+        arrays = lax.optimization_barrier((*sources, *others))[:3]
         return pl.pallas_call(
             functools.partial(pack_body, rows, gw, layout),
             in_specs=[SMEM, HBM, HBM, HBM],
@@ -126,35 +141,38 @@
             scratch_shapes=[pltpu.SemaphoreType.DMA((sum(len(parts) for _, parts in layout),))],
             compiler_params=PARAMS,
             cost_estimate=FREE,
-        )(chip, *arrays)
-
-    layout = [(k, (0, 1) if k in LAST else (0, 1, 2)) for k in FIRST + REST]
-    layout += [(k, (2,)) for k in LAST]
+        )(at, *arrays)
+
+    layout = [(p, (0, 1) if p[0] == LAST else (0, 1, 2)) for p in FIRST + REST]
+    layout += [((LAST, cross), (2,)) for cross in range(2)]
     packed = pack(layout[: len(FIRST)])
-    packed += pack(layout[len(FIRST) :], packed[:1])
-    got = [across(piece, k) for piece, (k, _) in zip(packed, layout)]
-    late = dict(zip(LAST, got[chips:]))
-    got = {k: piece for piece, (k, _) in zip(got[:chips], layout)}
+    packed += pack(layout[len(FIRST) :], packed[0])
+    late = jnp.concatenate([packed[-2], swap(packed[-1])], axis=0)
+    got = {}
+    for p, piece in zip(FIRST + REST, packed):
+        got[p] = across(after(piece, late) if p == JOINED_BY else piece, *p)
     own = call(functools.partial(merge_body, rows), chips, shape(2, chips * rows, gw))(*got.values())
-    other = lax.ppermute(own, "core", [(0, 1), (1, 0)])
-
-    def attend(ks, after=()):
-        pieces = [late.get(k, got[k]) for k in ks]
-        if after:
-            pieces = lax.optimization_barrier((*pieces, *after))[: len(pieces)]
-        body = functools.partial(attend_body, len(ks), rows)
-        outs = call(body, 2 + len(ks), [shape(rows, gw)] * len(ks))(own, other, *pieces)
-        return dict(zip(ks, outs))
-
-    outs = attend((4, 5))
-    outs |= attend(NEAR + (0,), (outs[4],))
-    outs |= attend(LAST, (outs[0],))
-    back = {k: across(outs[k], k) for k in (4, 5) + LAST + (0,)}
-    back[2] = across(lax.optimization_barrier((outs[2], outs[LAST[0]]))[0], 2)
-    for k, before in ((3, 5), (1, 4)):
-        back[k] = across(lax.optimization_barrier((outs[k], outs[LAST[0]], back[before]))[0], k)
-
-    def unpack(order, so_far=()):
+    other = swap(own)
+    late = across(late, LAST, 0)
+
+    def attend(dzs, *others):
+        pieces = [late] if dzs == (LAST,) else [got[dz, cross] for dz in dzs for cross in range(2)]
+        count = len(pieces)
+        pieces = lax.optimization_barrier((*pieces, *others))[:count] if others else pieces
+        body = functools.partial(attend_body, count, rows)
+        outs = call(body, 2 + count, [shape(2 * rows, gw)] * len(dzs))(own, other, *pieces)
+        return dict(zip(dzs, outs))
+
+    outs = attend((2,))
+    outs |= attend((LAST,), outs[2])
+    outs |= attend((1, 0), outs[LAST])
+    back = {dz: across(outs[dz], dz, 0) for dz in (2, LAST)}
+    back |= {dz: across(after(outs[dz], back[2]), dz, 0) for dz in (1, 0)}
+    handed = {dz: swap(back[dz][rows:]) for dz in (2, 1, 0)}
+
+    def unpack(dzs, *so_far):
+        order = [(dz, cross) for dz in dzs for cross in range(2)]
+        pieces = [handed[dz] if cross else back[dz] for dz, cross in order]
         return pl.pallas_call(
             functools.partial(unpack_body, gw, order),
             in_specs=[SMEM] + [VMEM] * len(order) + [HBM] * len(so_far),
@@ -164,9 +182,11 @@
             input_output_aliases={1 + len(order): 0} if so_far else {},
             compiler_params=PARAMS,
             cost_estimate=FREE,
-        )(chip, *[back[k] for k in order], *so_far)
-
-    result = unpack(LAST + (3, 1), (unpack((0, 4, 5, 2)),))
+        )(at, *pieces, *so_far)
+
+    result = unpack(UNPACK[0])
+    handed[LAST] = swap(after(back[LAST], result)[rows:])
+    result = unpack(UNPACK[1], result)
     return result.reshape(layers, tok_rows, width)
 
 

time: 68.2 us -> 74.1 us (1.087)
  waiting for transfers between devices: 20.1 us -> 29.5 us
  starting transfers between devices: 39.2 us -> 33.3 us
  Pallas kernels: 8.66 us -> 10.8 us
    ppermute x17 -> x19, waiting for transfers between devices: 20.1 us -> 29.5 us  [the longest x13 27.5 us: across(): return lax.ppermute(array, ('chip', 'core'), pairs)]
    ppermute x17 -> x19, starting transfers between devices: 39.2 us -> 33.3 us  [the longest x13 28.2 us: across(): return lax.ppermute(array, ('chip', 'core'), pairs)]
    pallas_call x2, Pallas kernels: 2.73 us -> 3.82 us  [pack(): pl.pallas_call(functools.partial(pack_body, rows, gw, layout), in_specs=[...]
    pallas_call x2, Pallas kernels: 1.5 us -> 2.59 us  [unpack(): pl.pallas_call(functools.partial(unpack_body, gw, order), in_specs=[SMEM]...]
  transfers between devices with their start and end apart: 17 -> 19, of which waited for: 8 -> 10; matrix products, arithmetic and copies ran while one was open for 0% -> 0% of each run, Pallas kernels for 10% -> 10%
where the time goes in v3:
time: 74.1 us; the launch traced here: 73.8 us
  starting transfers between devices  33.3 us (45%)
  waiting for transfers between devices  29.5 us (40%)
  Pallas kernels  10.8 us (15%)
    ppermute x13, starting transfers between devices, across(): return lax.ppermute(array, ('chip', 'core'), pairs)  28.2 us
    ppermute x13, waiting for transfers between devices, across(): return lax.ppermute(array, ('chip', 'core'), pairs)  27.5 us
    ppermute x6, starting transfers between devices, swap(): return lax.ppermute(array, 'core', [(0, 1), (1, 0)])  5.02 us
    pallas_call x3, Pallas kernels, attend(): call(body, 2 + count, [shape(2 * rows, gw)] * len(dzs))(own, other, *pieces)  4.33 us
    pallas_call x2, Pallas kernels, pack(): pl.pallas_call(functools.partial(pack_body, rows, gw, layout), in_specs=[...  3.82 us
    pallas_call x2, Pallas kernels, unpack(): pl.pallas_call(functools.partial(unpack_body, gw, order), in_specs=[SMEM]...  2.59 us
    ppermute x6, waiting for transfers between devices, swap(): return lax.ppermute(array, 'core', [(0, 1), (1, 0)])  1.97 us
  transfers between devices with their start and end apart: 19, of which 10 were waited for; matrix products, arithmetic and copies ran while one was open for 0% of the time, Pallas kernels for 10%

profile of v3, /device:TPU:0, one launch (start us, length us, event | category | flops | bytes accessed | tf_op | source)
XLA Modules:
  0.0 73.8 jit_solution(17588356499859699942)
XLA Ops:
  0.1 1.7 %shard_map.37 = (bf16[128,640]{1,0:T(8,128)(2,1)S(1)}, bf16[192,640]{1,0:T(8,128)(2,1)S(1)}, bf16[128,640]{1,0:T(8,128)(2,1)S(1)}) custom-call(s32[2]{0:T(128)S(1)} %pad_add_fusion.at_ref, bf16[64,5120]{1,0:T(8,128)(2,1)} %refs_0_.1, bf16[64,5120]{1,0:T(8,128)(2,1)} %refs_1_.1, bf16[64,5120]{1,0:T(8,128)(2,1)} %bitcast.4), custom_call_target="tpu_custom_call" | custom-call | tf_op jit(solution)/shard_map/pallas_call | solution.py:136
  1.8 3.1 %collective-permute-start.1 = (bf16[192,640]{1,0:T(8,128)(2,1)S(1)}, bf16[192,640]{1,0:T(8,128)(2,1)S(1)}, u32[]{:S(2)}, u32[]{:S(2)}) collective-permute-start(bf16[192,640]{1,0:T(8,128)(2,1)S(1)} %get-tuple-element.36), channel_id=1, source_target_pairs={{0,4},{1,7},{2,6},{3,5},{4,0},{5,3},{6,2},{7,1},{8,12},{9,15},{10,... | collective-permute-start | bytes 737288 | tf_op jit(solution)/shard_map/ppermute | solution.py:110
  4.9 2.5 %collective-permute-start.2 = (bf16[128,640]{1,0:T(8,128)(2,1)S(1)}, bf16[128,640]{1,0:T(8,128)(2,1)S(1)}, u32[]{:S(2)}, u32[]{:S(2)}) collective-permute-start(bf16[128,640]{1,0:T(8,128)(2,1)S(1)} %get-tuple-element.37), channel_id=1, source_target_pairs={{0,15},{1,12},{2,13},{3,14},{4,11},{5,8},{6,9},{7,10},{8,7},{9,4},... | collective-permute-start | bytes 491528 | tf_op jit(solution)/shard_map/ppermute | solution.py:110
  7.4 1.3 %collective-permute-start = (bf16[128,640]{1,0:T(8,128)(2,1)S(1)}, bf16[128,640]{1,0:T(8,128)(2,1)S(1)}, u32[]{:S(2)}, u32[]{:S(2)}) collective-permute-start(bf16[128,640]{1,0:T(8,128)(2,1)S(1)} %get-tuple-element.35), channel_id=1, source_target_pairs={{0,12},{1,15},{2,14},{3,13},{4,8},{5,11},{6,10},{7,9},{8,4},{9,7},... | collective-permute-start | bytes 491528 | tf_op jit(solution)/shard_map/ppermute | solution.py:110
  8.8 2.1 %shard_map.38 = (bf16[192,640]{1,0:T(8,128)(2,1)S(1)}, bf16[192,640]{1,0:T(8,128)(2,1)S(1)}, bf16[192,640]{1,0:T(8,128)(2,1)S(1)}, bf16[192,640]{1,0:T(8,128)(2,...) custom-call(s32[2]{0:T(128)S(1)} %pad_add_fusion.at_ref, ...), custom_call_target="tpu_custom_call" | custom-call | tf_op jit(solution)/shard_map/pallas_call | solution.py:136
  10.9 0.8 %collective-permute-start.5 = (bf16[64,640]{1,0:T(8,128)(2,1)S(1)}, bf16[64,640]{1,0:T(8,128)(2,1)S(1)}, u32[]{:S(2)}, u32[]{:S(2)}) collective-permute-start(bf16[64,640]{1,0:T(8,128)(2,1)S(1)} %get-tuple-element.45), channel_id=1, source_target_pairs={{0,1},{1,0},{2,3},{3,2},{4,5},{5,4},{6,7},{7,6},{8,9},{9,8},{10,11... | collective-permute-start | bytes 245768 | tf_op jit(solution)/shard_map/ppermute | solution.py:113
  11.7 0.8 %collective-permute-start.3 = (bf16[192,640]{1,0:T(8,128)(2,1)S(1)}, bf16[192,640]{1,0:T(8,128)(2,1)S(1)}, u32[]{:S(2)}, u32[]{:S(2)}) collective-permute-start(bf16[192,640]{1,0:T(8,128)(2,1)S(1)} %get-tuple-element.41), channel_id=1, source_target_pairs={{0,8},{1,11},{2,10},{3,9},{4,12},{5,15},{6,14},{7,13},{8,0},{9,3},... | collective-permute-start | bytes 737288 | tf_op jit(solution)/shard_map/ppermute | solution.py:110
  12.6 2.5 %collective-permute-start.4 = (bf16[192,640]{1,0:T(8,128)(2,1)S(1)}, bf16[192,640]{1,0:T(8,128)(2,1)S(1)}, u32[]{:S(2)}, u32[]{:S(2)}) collective-permute-start(bf16[192,640]{1,0:T(8,128)(2,1)S(1)} %get-tuple-element.42), channel_id=1, source_target_pairs={{0,7},{1,4},{2,5},{3,6},{4,3},{5,0},{6,1},{7,2},{8,15},{9,12},{10,... | collective-permute-start | bytes 737288 | tf_op jit(solution)/shard_map/ppermute | solution.py:110
  15.1 2.4 %collective-permute-done.2.refs_2_ = bf16[128,640]{1,0:T(8,128)(2,1)S(1)} collective-permute-done((bf16[128,640]{1,0:T(8,128)(2,1)S(1)}, bf16[128,640]{1,0:T(8,128)(2,1)S(1)}, u32[]{:S(2)}, u32[]{:S(2)}) %collective-permute-start.2) | collective-permute-done | bytes 163872 | tf_op jit(solution)/shard_map/ppermute | solution.py:110
  17.5 9.8 %collective-permute-start.7 = (bf16[192,640]{1,0:T(8,128)(2,1)S(1)}, bf16[192,640]{1,0:T(8,128)(2,1)S(1)}, u32[]{:S(2)}, u32[]{:S(2)}) collective-permute-start(bf16[192,640]{1,0:T(8,128)(2,1)S(1)} %get-tuple-element.47), channel_id=1, source_target_pairs={{0,11},{1,8},{2,9},{3,10},{4,15},{5,12},{6,13},{7,14},{8,3},{9,0},... | collective-permute-start | bytes 737288 | tf_op jit(solution)/shard_map/ppermute | solution.py:110
  28.1 10.8 %collective-permute-done.3.refs_3_.refs_0_ = bf16[192,640]{1,0:T(8,128)(2,1)S(1)} collective-permute-done((bf16[192,640]{1,0:T(8,128)(2,1)S(1)}, bf16[192,640]{1,0:T(8,128)(2,1)S(1)}, u32[]{:S(2)}, u32[]{:S(2)}) %collective-permute-start.3) | collective-permute-done | bytes 245792 | tf_op jit(solution)/shard_map/ppermute | solution.py:110
  38.9 4.9 %collective-permute-done.7.refs_6_.refs_1_ = bf16[192,640]{1,0:T(8,128)(2,1)S(1)} collective-permute-done((bf16[192,640]{1,0:T(8,128)(2,1)S(1)}, bf16[192,640]{1,0:T(8,128)(2,1)S(1)}, u32[]{:S(2)}, u32[]{:S(2)}) %collective-permute-start.7) | collective-permute-done | bytes 245792 | tf_op jit(solution)/shard_map/ppermute | solution.py:110
  44.1 3.3 %collective-permute-start.10 = (bf16[128,640]{1,0:T(8,128)(2,1)S(1)}, bf16[128,640]{1,0:T(8,128)(2,1)S(1)}, u32[]{:S(2)}, u32[]{:S(2)}) collective-permute-start(bf16[128,640]{1,0:T(8,128)(2,1)S(1)} %constant_dynamic-update-slice_fusion), channel_id=1, source_target_pairs={{0,12},{1,15},{2,14},{3,13},{4,8},{5,11},{6,10},{7,9},{8,4},{9,7},... | collective-permute-start | bytes 491528 | tf_op jit(solution)/shard_map/ppermute | solution.py:110
  47.5 1.2 %shard_map.40 = bf16[128,640]{1,0:T(8,128)(2,1)S(1)} custom-call(bf16[2,512,640]{2,1,0:T(8,128)(2,1)S(1)} %shard_map.39.own, bf16[2,512,640]{2,1,0:T(8,128)(2,1)S(1)} %collective-permute-done.9.other, bf16[192,640]{1,0:T(8,128)(2,1)S(1)} %collective-permute-done.3.refs_3_.refs_0_, bf16[192,640]{1,0:T(8,128)(2,1)S(1)} %collective-permute-done.7.refs_6_.refs_1_), custom_call_target="tpu_custom_call" | custom-call | tf_op jit(solution)/shard_map/pallas_call | solution.py:163
  48.7 4.4 %collective-permute-done.10.refs_0_ = bf16[128,640]{1,0:T(8,128)(2,1)S(1)} collective-permute-done((bf16[128,640]{1,0:T(8,128)(2,1)S(1)}, bf16[128,640]{1,0:T(8,128)(2,1)S(1)}, u32[]{:S(2)}, u32[]{:S(2)}) %collective-permute-start.10) | collective-permute-done | bytes 163872 | tf_op jit(solution)/shard_map/ppermute | solution.py:110
  53.1 1.2 %shard_map.41 = bf16[128,640]{1,0:T(8,128)(2,1)S(1)} custom-call(bf16[2,512,640]{2,1,0:T(8,128)(2,1)S(1)} %shard_map.39.own, bf16[2,512,640]{2,1,0:T(8,128)(2,1)S(1)} %collective-permute-done.9.other, bf16[128,640]{1,0:T(8,128)(2,1)S(1)} %collective-permute-done.10.refs_0_), custom_call_target="tpu_custom_call" | custom-call | tf_op jit(solution)/shard_map/pallas_call | solution.py:163
  54.2 3.4 %collective-permute-start.11 = (bf16[128,640]{1,0:T(8,128)(2,1)S(1)}, bf16[128,640]{1,0:T(8,128)(2,1)S(1)}, u32[]{:S(2)}, u32[]{:S(2)}) collective-permute-start(bf16[128,640]{1,0:T(8,128)(2,1)S(1)} %shard_map.41), channel_id=1, source_target_pairs={{0,12},{1,15},{2,14},{3,13},{4,8},{5,11},{6,10},{7,9},{8,4},{9,7},... | collective-permute-start | bytes 491528 | tf_op jit(solution)/shard_map/ppermute | solution.py:110
  57.6 2.0 %shard_map.43 = (bf16[128,640]{1,0:T(8,128)(2,1)S(1)}, bf16[128,640]{1,0:T(8,128)(2,1)S(1)}) custom-call(bf16[2,512,640]{2,1,0:T(8,128)(2,1)S(1)} %shard_map.39.own, bf16[2,512,640]{2,1,0:T(8,128)(2,1)S(1)} %collective-permute-done.9.other, bf16[192,640]{1,0:T(8,128)(2,1)S(1)} %collective-permute-done.1.refs_1_.refs_0_, ...), custom_call_target="tpu_custom_call" | custom-call | tf_op jit(solution)/shard_map/pallas_call | solution.py:163
  59.6 4.5 %collective-permute-done.12.refs_0_ = bf16[128,640]{1,0:T(8,128)(2,1)S(1)} collective-permute-done((bf16[128,640]{1,0:T(8,128)(2,1)S(1)}, bf16[128,640]{1,0:T(8,128)(2,1)S(1)}, u32[]{:S(2)}, u32[]{:S(2)}) %collective-permute-start.12) | collective-permute-done | bytes 163872 | tf_op jit(solution)/shard_map/ppermute | solution.py:110
  64.8 3.0 %collective-permute-start.13 = (bf16[64,640]{1,0:T(8,128)(2,1)S(1)}, bf16[64,640]{1,0:T(8,128)(2,1)S(1)}, u32[]{:S(2)}, u32[]{:S(2)}) collective-permute-start(bf16[64,640]{1,0:T(8,128)(2,1)S(1)} %slice.16), channel_id=1, source_target_pairs={{0,1},{1,0},{2,3},{3,2},{4,5},{5,4},{6,7},{7,6},{8,9},{9,8},{10,11... | collective-permute-start | bytes 245768 | tf_op jit(solution)/shard_map/ppermute | solution.py:113
  67.8 0.9 %collective-permute-done.13.refs_1_ = bf16[64,640]{1,0:T(8,128)(2,1)S(1)} collective-permute-done((bf16[64,640]{1,0:T(8,128)(2,1)S(1)}, bf16[64,640]{1,0:T(8,128)(2,1)S(1)}, u32[]{:S(2)}, u32[]{:S(2)}) %collective-permute-start.13) | collective-permute-done | bytes 81952 | tf_op jit(solution)/shard_map/ppermute | solution.py:113
  68.7 1.2 %shard_map.42.refs_6_ = bf16[64,5120]{1,0:T(8,128)(2,1)} custom-call(s32[2]{0:T(128)S(1)} %pad_add_fusion.at_ref, bf16[128,640]{1,0:T(8,128)(2,1)S(1)} %collective-permute-done.12.refs_0_, bf16[64,640]{1,0:T(8,128)(2,1)S(1)} %collective-permute-done.13.refs_1_), custom_call_target="tpu_custom_call" | custom-call | tf_op jit(solution)/shard_map/pallas_call | solution.py:176
  71.6 0.7 collective-permute-done.16.refs_3_
  72.5 1.4 %shard_map.44 = bf16[64,5120]{1,0:T(8,128)(2,1)} custom-call(s32[2]{0:T(128)S(1)} %pad_add_fusion.at_ref, bf16[128,640]{1,0:T(8,128)(2,1)S(1)} %collective-permute-done.11.refs_0_, bf16[64,640]{1,0:T(8,128)(2,1)S(1)} %collective-permute-done.14.refs_1_, bf16[128,640]{1,0:T(8,128)(2,1)S(1)} %collective-permute-done.15.refs_2_, ...), custom_call_target="tpu_custom_call", output_to_operand_aliasing={{}: (7, {})} | custom-call | tf_op jit(solution)/shard_map/pallas_call | solution.py:176
  (29 shorter events, 3.7 us)
Async XLA Ops:
  1.8 25.6 %collective-permute-start.1 = (bf16[192,640]{1,0:T(8,128)(2,1)S(1)}, bf16[192,640]{1,0:T(8,128)(2,1)S(1)}, u32[]{:S(2)}, u32[]{:S(2)}) collective-permute-start(bf16[192,640]{1,0:T(8,128)(2,1)S(1)} %get-tuple-element.36), channel_id=1, source_target_pairs={{0,4},{1,7},{2,6},{3,5},{4,0},{5,3},{6,2},{7,1},{8,12},{9,15},{10,... | collective-permute-start | bytes 737288 | tf_op jit(solution)/shard_map/ppermute | solution.py:110
  4.9 12.6 %collective-permute-start.2 = (bf16[128,640]{1,0:T(8,128)(2,1)S(1)}, bf16[128,640]{1,0:T(8,128)(2,1)S(1)}, u32[]{:S(2)}, u32[]{:S(2)}) collective-permute-start(bf16[128,640]{1,0:T(8,128)(2,1)S(1)} %get-tuple-element.37), channel_id=1, source_target_pairs={{0,15},{1,12},{2,13},{3,14},{4,11},{5,8},{6,9},{7,10},{8,7},{9,4},... | collective-permute-start | bytes 491528 | tf_op jit(solution)/shard_map/ppermute | solution.py:110
  7.4 19.9 %collective-permute-start = (bf16[128,640]{1,0:T(8,128)(2,1)S(1)}, bf16[128,640]{1,0:T(8,128)(2,1)S(1)}, u32[]{:S(2)}, u32[]{:S(2)}) collective-permute-start(bf16[128,640]{1,0:T(8,128)(2,1)S(1)} %get-tuple-element.35), channel_id=1, source_target_pairs={{0,12},{1,15},{2,14},{3,13},{4,8},{5,11},{6,10},{7,9},{8,4},{9,7},... | collective-permute-start | bytes 491528 | tf_op jit(solution)/shard_map/ppermute | solution.py:110
  10.9 1.7 %collective-permute-start.5 = (bf16[64,640]{1,0:T(8,128)(2,1)S(1)}, bf16[64,640]{1,0:T(8,128)(2,1)S(1)}, u32[]{:S(2)}, u32[]{:S(2)}) collective-permute-start(bf16[64,640]{1,0:T(8,128)(2,1)S(1)} %get-tuple-element.45), channel_id=1, source_target_pairs={{0,1},{1,0},{2,3},{3,2},{4,5},{5,4},{6,7},{7,6},{8,9},{9,8},{10,11... | collective-permute-start | bytes 245768 | tf_op jit(solution)/shard_map/ppermute | solution.py:113
  11.7 27.2 %collective-permute-start.3 = (bf16[192,640]{1,0:T(8,128)(2,1)S(1)}, bf16[192,640]{1,0:T(8,128)(2,1)S(1)}, u32[]{:S(2)}, u32[]{:S(2)}) collective-permute-start(bf16[192,640]{1,0:T(8,128)(2,1)S(1)} %get-tuple-element.41), channel_id=1, source_target_pairs={{0,8},{1,11},{2,10},{3,9},{4,12},{5,15},{6,14},{7,13},{8,0},{9,3},... | collective-permute-start | bytes 737288 | tf_op jit(solution)/shard_map/ppermute | solution.py:110
  12.6 26.3 %collective-permute-start.4 = (bf16[192,640]{1,0:T(8,128)(2,1)S(1)}, bf16[192,640]{1,0:T(8,128)(2,1)S(1)}, u32[]{:S(2)}, u32[]{:S(2)}) collective-permute-start(bf16[192,640]{1,0:T(8,128)(2,1)S(1)} %get-tuple-element.42), channel_id=1, source_target_pairs={{0,7},{1,4},{2,5},{3,6},{4,3},{5,0},{6,1},{7,2},{8,15},{9,12},{10,... | collective-permute-start | bytes 737288 | tf_op jit(solution)/shard_map/ppermute | solution.py:110
  17.5 26.3 %collective-permute-start.7 = (bf16[192,640]{1,0:T(8,128)(2,1)S(1)}, bf16[192,640]{1,0:T(8,128)(2,1)S(1)}, u32[]{:S(2)}, u32[]{:S(2)}) collective-permute-start(bf16[192,640]{1,0:T(8,128)(2,1)S(1)} %get-tuple-element.47), channel_id=1, source_target_pairs={{0,11},{1,8},{2,9},{3,10},{4,15},{5,12},{6,13},{7,14},{8,3},{9,0},... | collective-permute-start | bytes 737288 | tf_op jit(solution)/shard_map/ppermute | solution.py:110
  27.4 16.4 %collective-permute-start.8 = (bf16[192,640]{1,0:T(8,128)(2,1)S(1)}, bf16[192,640]{1,0:T(8,128)(2,1)S(1)}, u32[]{:S(2)}, u32[]{:S(2)}) collective-permute-start(bf16[192,640]{1,0:T(8,128)(2,1)S(1)} %get-tuple-element.48), channel_id=1, source_target_pairs={{0,3},{1,0},{2,1},{3,2},{4,7},{5,4},{6,5},{7,6},{8,11},{9,8},{10,9... | collective-permute-start | bytes 737288 | tf_op jit(solution)/shard_map/ppermute | solution.py:110
  27.4 16.4 %collective-permute-start.6 = (bf16[192,640]{1,0:T(8,128)(2,1)S(1)}, bf16[192,640]{1,0:T(8,128)(2,1)S(1)}, u32[]{:S(2)}, u32[]{:S(2)}) collective-permute-start(bf16[192,640]{1,0:T(8,128)(2,1)S(1)} %get-tuple-element.46), channel_id=1, source_target_pairs={{0,0},{1,3},{2,2},{3,1},{4,4},{5,7},{6,6},{7,5},{8,8},{9,11},{10,1... | collective-permute-start | bytes 737288 | tf_op jit(solution)/shard_map/ppermute | solution.py:110
  43.9 3.6 %collective-permute-start.9 = (bf16[2,512,640]{2,1,0:T(8,128)(2,1)S(1)}, bf16[2,512,640]{2,1,0:T(8,128)(2,1)S(1)}, u32[]{:S(2)}, u32[]{:S(2)}) collective-permute-start(bf16[2,512,640]{2,1,0:T(8,128)(2,1)S(1)} %shard_map.39.own), channel_id=1, source_target_pairs={{0,1},{1,0},{2,3},{3,2},{4,5},{5,4},{6,7},{7,6},{8,9},{9,8},{10,11... | collective-permute-start | bytes 3932168 | tf_op jit(solution)/shard_map/ppermute | solution.py:113
  44.1 9.0 %collective-permute-start.10 = (bf16[128,640]{1,0:T(8,128)(2,1)S(1)}, bf16[128,640]{1,0:T(8,128)(2,1)S(1)}, u32[]{:S(2)}, u32[]{:S(2)}) collective-permute-start(bf16[128,640]{1,0:T(8,128)(2,1)S(1)} %constant_dynamic-update-slice_fusion), channel_id=1, source_target_pairs={{0,12},{1,15},{2,14},{3,13},{4,8},{5,11},{6,10},{7,9},{8,4},{9,7},... | collective-permute-start | bytes 491528 | tf_op jit(solution)/shard_map/ppermute | solution.py:110
  48.6 15.5 %collective-permute-start.12 = (bf16[128,640]{1,0:T(8,128)(2,1)S(1)}, bf16[128,640]{1,0:T(8,128)(2,1)S(1)}, u32[]{:S(2)}, u32[]{:S(2)}) collective-permute-start(bf16[128,640]{1,0:T(8,128)(2,1)S(1)} %shard_map.40), channel_id=1, source_target_pairs={{0,8},{1,11},{2,10},{3,9},{4,12},{5,15},{6,14},{7,13},{8,0},{9,3},... | collective-permute-start | bytes 491528 | tf_op jit(solution)/shard_map/ppermute | solution.py:110
  54.2 15.7 %collective-permute-start.11 = (bf16[128,640]{1,0:T(8,128)(2,1)S(1)}, bf16[128,640]{1,0:T(8,128)(2,1)S(1)}, u32[]{:S(2)}, u32[]{:S(2)}) collective-permute-start(bf16[128,640]{1,0:T(8,128)(2,1)S(1)} %shard_map.41), channel_id=1, source_target_pairs={{0,12},{1,15},{2,14},{3,13},{4,8},{5,11},{6,10},{7,9},{8,4},{9,7},... | collective-permute-start | bytes 491528 | tf_op jit(solution)/shard_map/ppermute | solution.py:110
  64.2 6.7 %collective-permute-start.15 = (bf16[128,640]{1,0:T(8,128)(2,1)S(1)}, bf16[128,640]{1,0:T(8,128)(2,1)S(1)}, u32[]{:S(2)}, u32[]{:S(2)}) collective-permute-start(bf16[128,640]{1,0:T(8,128)(2,1)S(1)} %get-tuple-element.56), channel_id=1, source_target_pairs={{0,4},{1,7},{2,6},{3,5},{4,0},{5,3},{6,2},{7,1},{8,12},{9,15},{10,... | collective-permute-start | bytes 491528 | tf_op jit(solution)/shard_map/ppermute | solution.py:110
  64.2 6.8 %collective-permute-start.17 = (bf16[128,640]{1,0:T(8,128)(2,1)S(1)}, bf16[128,640]{1,0:T(8,128)(2,1)S(1)}, u32[]{:S(2)}, u32[]{:S(2)}) collective-permute-start(bf16[128,640]{1,0:T(8,128)(2,1)S(1)} %get-tuple-element.58), channel_id=1, source_target_pairs={{0,0},{1,3},{2,2},{3,1},{4,4},{5,7},{6,6},{7,5},{8,8},{9,11},{10,1... | collective-permute-start | bytes 491528 | tf_op jit(solution)/shard_map/ppermute | solution.py:110
  64.8 3.9 %collective-permute-start.13 = (bf16[64,640]{1,0:T(8,128)(2,1)S(1)}, bf16[64,640]{1,0:T(8,128)(2,1)S(1)}, u32[]{:S(2)}, u32[]{:S(2)}) collective-permute-start(bf16[64,640]{1,0:T(8,128)(2,1)S(1)} %slice.16), channel_id=1, source_target_pairs={{0,1},{1,0},{2,3},{3,2},{4,5},{5,4},{6,7},{7,6},{8,9},{9,8},{10,11... | collective-permute-start | bytes 245768 | tf_op jit(solution)/shard_map/ppermute | solution.py:113
  70.0 1.5 %collective-permute-start.14 = (bf16[64,640]{1,0:T(8,128)(2,1)S(1)}, bf16[64,640]{1,0:T(8,128)(2,1)S(1)}, u32[]{:S(2)}, u32[]{:S(2)}) collective-permute-start(bf16[64,640]{1,0:T(8,128)(2,1)S(1)} %slice.13), channel_id=1, source_target_pairs={{0,1},{1,0},{2,3},{3,2},{4,5},{5,4},{6,7},{7,6},{8,9},{9,8},{10,11... | collective-permute-start | bytes 245768 | tf_op jit(solution)/shard_map/ppermute | solution.py:113
  70.9 1.3 %collective-permute-start.16 = (bf16[64,640]{1,0:T(8,128)(2,1)S(1)}, bf16[64,640]{1,0:T(8,128)(2,1)S(1)}, u32[]{:S(2)}, u32[]{:S(2)}) collective-permute-start(bf16[64,640]{1,0:T(8,128)(2,1)S(1)} %slice.17), channel_id=1, source_target_pairs={{0,1},{1,0},{2,3},{3,2},{4,5},{5,4},{6,7},{7,6},{8,9},{9,8},{10,11... | collective-permute-start | bytes 245768 | tf_op jit(solution)/shard_map/ppermute | solution.py:113
  71.0 1.5 %collective-permute-start.18 = (bf16[64,640]{1,0:T(8,128)(2,1)S(1)}, bf16[64,640]{1,0:T(8,128)(2,1)S(1)}, u32[]{:S(2)}, u32[]{:S(2)}) collective-permute-start(bf16[64,640]{1,0:T(8,128)(2,1)S(1)} %slice.18), channel_id=1, source_target_pairs={{0,1},{1,0},{2,3},{3,2},{4,5},{5,4},{6,7},{7,6},{8,9},{9,8},{10,11... | collective-permute-start | bytes 245768 | tf_op jit(solution)/shard_map/ppermute | solution.py:113

commit v4 on v1

--- a/solution.py
+++ b/solution.py
@@ -36,9 +36,9 @@
     return jnp.concatenate([v, jnp.ones_like(v)], axis=1)
 
 
-FIRST = (6, 2, 7)
-REST = (4, 3, 1, 5, 0)
-LAST = (6, 7)
+FIRST = (4, 2, 5)
+REST = (6, 3, 1, 7, 0)
+LAST = (4, 5)
 NEAR = (2, 3, 1)
 
 
@@ -146,15 +146,16 @@
         outs = call(body, 2 + len(ks), [shape(rows, gw)] * len(ks))(own, other, *pieces)
         return dict(zip(ks, outs))
 
-    outs = attend((4, 5))
-    outs |= attend(NEAR + (0,), (outs[4],))
+    outs = attend((6, 7))
+    outs |= attend(NEAR + (0,), (outs[6],))
     outs |= attend(LAST, (outs[0],))
+
     def send(k, *after):
         return across(lax.optimization_barrier((outs[k], *after))[0], k)
 
-    back = {k: across(outs[k], k) for k in NEAR + (0,)}
-    back |= {k: send(k, outs[0]) for k in (4, 5)}
-    back |= {7: send(7, back[2]), 6: send(6, back[3])}
+    back = {k: across(outs[k], k) for k in (0, 6, 7) + LAST}
+    back[1] = send(1, outs[LAST[0]])
+    back |= {k: send(k, outs[LAST[0]], back[before]) for k, before in ((3, 7), (2, 6))}
 
     def unpack(order, so_far=()):
         return pl.pallas_call(
@@ -168,7 +169,7 @@
             cost_estimate=FREE,
         )(chip, *[back[k] for k in order], *so_far)
 
-    result = unpack((4, 5) + LAST, (unpack((0,) + NEAR),))
+    result = unpack(LAST + (3, 2), (unpack((0, 6, 7, 1)),))
     return result.reshape(layers, tok_rows, width)
 
 

time: 68.8 us -> 72 us (1.047)
  waiting for transfers between devices: 19 us -> 28.9 us
  starting transfers between devices: 40.8 us -> 34.1 us
    ppermute x16, waiting for transfers between devices: 19 us -> 28.9 us  [across(): lax.ppermute(piece, 'chip', [(i, i ^ k) for i in range(chips)])]
    ppermute x16, starting transfers between devices: 40.7 us -> 34.1 us  [across(): lax.ppermute(piece, 'chip', [(i, i ^ k) for i in range(chips)])]
  transfers between devices with their start and end apart: 17 -> 17, of which waited for: 5 -> 8; matrix products, arithmetic and copies ran while one was open for 0% -> 0% of each run, Pallas kernels for 10% -> 9%
where the time goes in v4:
time: 72 us; the launch traced here: 71.8 us
  starting transfers between devices  34.1 us (47%)
  waiting for transfers between devices  28.9 us (40%)
  Pallas kernels  8.66 us (12%)
    ppermute x16, starting transfers between devices, across(): lax.ppermute(piece, 'chip', [(i, i ^ k) for i in range(chips)])  34.1 us
    ppermute x16, waiting for transfers between devices, across(): lax.ppermute(piece, 'chip', [(i, i ^ k) for i in range(chips)])  28.9 us
    pallas_call x3, Pallas kernels, attend(): call(body, 2 + len(ks), [shape(rows, gw)] * len(ks))(own, other, *pieces)  4.33 us
    pallas_call x2, Pallas kernels, pack(): pl.pallas_call(functools.partial(pack_body, rows, gw, layout), in_specs=[...  2.73 us
    pallas_call x2, Pallas kernels, unpack(): pl.pallas_call(functools.partial(unpack_body, gw, order), in_specs=[SMEM]...  1.5 us
  transfers between devices with their start and end apart: 17, of which 8 were waited for; matrix products, arithmetic and copies ran while one was open for 0% of the time, Pallas kernels for 9%

profile of v4, /device:TPU:0, one launch (start us, length us, event | category | flops | bytes accessed | tf_op | source)
XLA Modules:
  0.0 71.8 jit_solution(12411096607752523091)
XLA Ops:
  0.0 1.2 %shard_map.37 = (bf16[128,640]{1,0:T(8,128)(2,1)S(1)}, bf16[192,640]{1,0:T(8,128)(2,1)S(1)}, bf16[128,640]{1,0:T(8,128)(2,1)S(1)}) custom-call(s32[1]{0:T(128)} %bitcast.chip_ref, bf16[64,5120]{1,0:T(8,128)(2,1)} %refs_0_.2, bf16[64,5120]{1,0:T(8,128)(2,1)} %refs_1_.2, bf16[64,5120]{1,0:T(8,128)(2,1)} %bitcast.3), custom_call_target="tpu_custom_call" | custom-call | tf_op jit(solution)/shard_map/pallas_call | solution.py:121
  1.2 5.1 %collective-permute-start.2 = (bf16[128,640]{1,0:T(8,128)(2,1)S(1)}, bf16[128,640]{1,0:T(8,128)(2,1)S(1)}, u32[]{:S(2)}, u32[]{:S(2)}) collective-permute-start(bf16[128,640]{1,0:T(8,128)(2,1)S(1)} %get-tuple-element.37), channel_id=1, source_target_pairs={{0,10},{2,8},{4,14},{6,12},{8,2},{10,0},{12,6},{14,4},{1,11},{3,9}... | collective-permute-start | bytes 491528 | tf_op jit(solution)/shard_map/ppermute | solution.py:100
  6.6 1.6 %collective-permute-start.1 = (bf16[192,640]{1,0:T(8,128)(2,1)S(1)}, bf16[192,640]{1,0:T(8,128)(2,1)S(1)}, u32[]{:S(2)}, u32[]{:S(2)}) collective-permute-start(bf16[192,640]{1,0:T(8,128)(2,1)S(1)} %get-tuple-element.36), channel_id=1, source_target_pairs={{0,4},{2,6},{4,0},{6,2},{8,12},{10,14},{12,8},{14,10},{1,5},{3,7},... | collective-permute-start | bytes 737288 | tf_op jit(solution)/shard_map/ppermute | solution.py:100
  8.2 1.5 %shard_map.38 = (bf16[192,640]{1,0:T(8,128)(2,1)S(1)}, bf16[192,640]{1,0:T(8,128)(2,1)S(1)}, bf16[192,640]{1,0:T(8,128)(2,1)S(1)}, bf16[192,640]{1,0:T(8,128)(2,...) custom-call(s32[1]{0:T(128)} %bitcast.chip_ref, ...), custom_call_target="tpu_custom_call" | custom-call | tf_op jit(solution)/shard_map/pallas_call | solution.py:121
  9.7 2.5 %collective-permute-start.3 = (bf16[192,640]{1,0:T(8,128)(2,1)S(1)}, bf16[192,640]{1,0:T(8,128)(2,1)S(1)}, u32[]{:S(2)}, u32[]{:S(2)}) collective-permute-start(bf16[192,640]{1,0:T(8,128)(2,1)S(1)} %get-tuple-element.41), channel_id=1, source_target_pairs={{0,12},{2,14},{4,8},{6,10},{8,4},{10,6},{12,0},{14,2},{1,13},{3,15... | collective-permute-start | bytes 737288 | tf_op jit(solution)/shard_map/ppermute | solution.py:100
  12.9 5.5 %collective-permute-done.2.refs_2_ = bf16[128,640]{1,0:T(8,128)(2,1)S(1)} collective-permute-done((bf16[128,640]{1,0:T(8,128)(2,1)S(1)}, bf16[128,640]{1,0:T(8,128)(2,1)S(1)}, u32[]{:S(2)}, u32[]{:S(2)}) %collective-permute-start.2) | collective-permute-done | bytes 163872 | tf_op jit(solution)/shard_map/ppermute | solution.py:100
  18.4 1.8 %collective-permute-start.5 = (bf16[192,640]{1,0:T(8,128)(2,1)S(1)}, bf16[192,640]{1,0:T(8,128)(2,1)S(1)}, u32[]{:S(2)}, u32[]{:S(2)}) collective-permute-start(bf16[192,640]{1,0:T(8,128)(2,1)S(1)} %get-tuple-element.43), channel_id=1, source_target_pairs={{0,2},{2,0},{4,6},{6,4},{8,10},{10,8},{12,14},{14,12},{1,3},{3,1},... | collective-permute-start | bytes 737288 | tf_op jit(solution)/shard_map/ppermute | solution.py:100
  20.2 7.3 %collective-permute-done.refs_0_ = bf16[128,640]{1,0:T(8,128)(2,1)S(1)} collective-permute-done((bf16[128,640]{1,0:T(8,128)(2,1)S(1)}, bf16[128,640]{1,0:T(8,128)(2,1)S(1)}, u32[]{:S(2)}, u32[]{:S(2)}) %collective-permute-start) | collective-permute-done | bytes 163872 | tf_op jit(solution)/shard_map/ppermute | solution.py:100
  27.5 2.4 %collective-permute-start.6 = (bf16[192,640]{1,0:T(8,128)(2,1)S(1)}, bf16[192,640]{1,0:T(8,128)(2,1)S(1)}, u32[]{:S(2)}, u32[]{:S(2)}) collective-permute-start(bf16[192,640]{1,0:T(8,128)(2,1)S(1)} %get-tuple-element.44), channel_id=1, source_target_pairs={{0,14},{2,12},{4,10},{6,8},{8,6},{10,4},{12,2},{14,0},{1,15},{3,13... | collective-permute-start | bytes 737288 | tf_op jit(solution)/shard_map/ppermute | solution.py:100
  29.9 0.8 %collective-permute-done.4.refs_4_.refs_1_ = bf16[192,640]{1,0:T(8,128)(2,1)S(1)} collective-permute-done((bf16[192,640]{1,0:T(8,128)(2,1)S(1)}, bf16[192,640]{1,0:T(8,128)(2,1)S(1)}, u32[]{:S(2)}, u32[]{:S(2)}) %collective-permute-start.4) | collective-permute-done | bytes 245792 | tf_op jit(solution)/shard_map/ppermute | solution.py:100
  30.7 5.7 %collective-permute-done.6.refs_6_.refs_1_ = bf16[192,640]{1,0:T(8,128)(2,1)S(1)} collective-permute-done((bf16[192,640]{1,0:T(8,128)(2,1)S(1)}, bf16[192,640]{1,0:T(8,128)(2,1)S(1)}, u32[]{:S(2)}, u32[]{:S(2)}) %collective-permute-start.6) | collective-permute-done | bytes 245792 | tf_op jit(solution)/shard_map/ppermute | solution.py:100
  36.6 8.4 %collective-permute-start.8 = (bf16[64,640]{1,0:T(8,128)(2,1)S(1)}, bf16[64,640]{1,0:T(8,128)(2,1)S(1)}, u32[]{:S(2)}, u32[]{:S(2)}) collective-permute-start(bf16[64,640]{1,0:T(8,128)(2,1)S(1)} %get-tuple-element.46), channel_id=1, source_target_pairs={{0,8},{2,10},{4,12},{6,14},{8,0},{10,2},{12,4},{14,6},{1,9},{3,11}... | collective-permute-start | bytes 245768 | tf_op jit(solution)/shard_map/ppermute | solution.py:100
  44.9 1.0 %collective-permute-start.9 = (bf16[64,640]{1,0:T(8,128)(2,1)S(1)}, bf16[64,640]{1,0:T(8,128)(2,1)S(1)}, u32[]{:S(2)}, u32[]{:S(2)}) collective-permute-start(bf16[64,640]{1,0:T(8,128)(2,1)S(1)} %get-tuple-element.47), channel_id=1, source_target_pairs={{0,10},{2,8},{4,14},{6,12},{8,2},{10,0},{12,6},{14,4},{1,11},{3,9}... | collective-permute-start | bytes 245768 | tf_op jit(solution)/shard_map/ppermute | solution.py:100
  46.0 1.2 %shard_map.40 = (bf16[64,640]{1,0:T(8,128)(2,1)S(1)}, bf16[64,640]{1,0:T(8,128)(2,1)S(1)}) custom-call(bf16[2,512,640]{2,1,0:T(8,128)(2,1)S(1)} %shard_map.39.own, bf16[2,512,640]{2,1,0:T(8,128)(2,1)S(1)} %collective-permute-done.7.other, bf16[192,640]{1,0:T(8,128)(2,1)S(1)} %collective-permute-done.3.refs_3_.refs_0_, ...), custom_call_target="tpu_custom_call" | custom-call | tf_op jit(solution)/shard_map/pallas_call | solution.py:146
  47.6 3.3 %collective-permute-start.14 = (bf16[64,640]{1,0:T(8,128)(2,1)S(1)}, bf16[64,640]{1,0:T(8,128)(2,1)S(1)}, u32[]{:S(2)}, u32[]{:S(2)}) collective-permute-start(bf16[64,640]{1,0:T(8,128)(2,1)S(1)} %get-tuple-element.48), channel_id=1, source_target_pairs={{0,12},{2,14},{4,8},{6,10},{8,4},{10,6},{12,0},{14,2},{1,13},{3,15... | collective-permute-start | bytes 245768 | tf_op jit(solution)/shard_map/ppermute | solution.py:100
  51.0 2.0 %shard_map.41 = (bf16[64,640]{1,0:T(8,128)(2,1)S(1)}, bf16[64,640]{1,0:T(8,128)(2,1)S(1)}, bf16[64,640]{1,0:T(8,128)(2,1)S(1)}, bf16[64,640]{1,0:T(8,128)(2,1)S(1)}) custom-call(bf16[2,512,640]{2,1,0:T(8,128)(2,1)S(1)} %shard_map.39.own, bf16[2,512,640]{2,1,0:T(8,128)(2,1)S(1)} %collective-permute-done.7.other, ...), custom_call_target="tpu_custom_call" | custom-call | tf_op jit(solution)/shard_map/pallas_call | solution.py:146
  53.0 4.9 %collective-permute-done.9.refs_1_ = bf16[64,640]{1,0:T(8,128)(2,1)S(1)} collective-permute-done((bf16[64,640]{1,0:T(8,128)(2,1)S(1)}, bf16[64,640]{1,0:T(8,128)(2,1)S(1)}, u32[]{:S(2)}, u32[]{:S(2)}) %collective-permute-start.9) | collective-permute-done | bytes 81952 | tf_op jit(solution)/shard_map/ppermute | solution.py:100
  57.9 1.2 %shard_map.42 = (bf16[64,640]{1,0:T(8,128)(2,1)S(1)}, bf16[64,640]{1,0:T(8,128)(2,1)S(1)}) custom-call(bf16[2,512,640]{2,1,0:T(8,128)(2,1)S(1)} %shard_map.39.own, bf16[2,512,640]{2,1,0:T(8,128)(2,1)S(1)} %collective-permute-done.7.other, bf16[64,640]{1,0:T(8,128)(2,1)S(1)} %collective-permute-done.8.refs_0_, bf16[64,640]{1,0:T(8,128)(2,1)S(1)} %collective-permute-done.9.refs_1_), custom_call_target="tpu_custom_call" | custom-call | tf_op jit(solution)/shard_map/pallas_call | solution.py:146
  59.8 3.7 %collective-permute-start.11 = (bf16[64,640]{1,0:T(8,128)(2,1)S(1)}, bf16[64,640]{1,0:T(8,128)(2,1)S(1)}, u32[]{:S(2)}, u32[]{:S(2)}) collective-permute-start(bf16[64,640]{1,0:T(8,128)(2,1)S(1)} %get-tuple-element.57), channel_id=1, source_target_pairs={{0,10},{2,8},{4,14},{6,12},{8,2},{10,0},{12,6},{14,4},{1,11},{3,9}... | collective-permute-start | bytes 245768 | tf_op jit(solution)/shard_map/ppermute | solution.py:100
  63.5 2.0 %collective-permute-start.15 = (bf16[64,640]{1,0:T(8,128)(2,1)S(1)}, bf16[64,640]{1,0:T(8,128)(2,1)S(1)}, u32[]{:S(2)}, u32[]{:S(2)}) collective-permute-start(bf16[64,640]{1,0:T(8,128)(2,1)S(1)} %get-tuple-element.62), channel_id=1, source_target_pairs={{0,4},{2,6},{4,0},{6,2},{8,12},{10,14},{12,8},{14,10},{1,5},{3,7},... | collective-permute-start | bytes 245768 | tf_op jit(solution)/shard_map/ppermute | solution.py:100
  65.6 0.8 %shard_map.43.refs_4_ = bf16[64,5120]{1,0:T(8,128)(2,1)} custom-call(s32[1]{0:T(128)} %bitcast.chip_ref, bf16[64,640]{1,0:T(8,128)(2,1)S(1)} %get-tuple-element.53.refs_0_, bf16[64,640]{1,0:T(8,128)(2,1)S(1)} %collective-permute-done.14.refs_1_, bf16[64,640]{1,0:T(8,128)(2,1)S(1)} %collective-permute-done.12.refs_2_, ...), custom_call_target="tpu_custom_call" | custom-call | tf_op jit(solution)/shard_map/pallas_call | solution.py:161
  66.3 2.3 %collective-permute-done.11.refs_1_ = bf16[64,640]{1,0:T(8,128)(2,1)S(1)} collective-permute-done((bf16[64,640]{1,0:T(8,128)(2,1)S(1)}, bf16[64,640]{1,0:T(8,128)(2,1)S(1)}, u32[]{:S(2)}, u32[]{:S(2)}) %collective-permute-start.11) | collective-permute-done | bytes 81952 | tf_op jit(solution)/shard_map/ppermute | solution.py:100
  68.6 1.5 %collective-permute-done.13.refs_2_ = bf16[64,640]{1,0:T(8,128)(2,1)S(1)} collective-permute-done((bf16[64,640]{1,0:T(8,128)(2,1)S(1)}, bf16[64,640]{1,0:T(8,128)(2,1)S(1)}, u32[]{:S(2)}, u32[]{:S(2)}) %collective-permute-start.13) | collective-permute-done | bytes 81952 | tf_op jit(solution)/shard_map/ppermute | solution.py:100
  70.1 0.9 %collective-permute-done.15.refs_3_ = bf16[64,640]{1,0:T(8,128)(2,1)S(1)} collective-permute-done((bf16[64,640]{1,0:T(8,128)(2,1)S(1)}, bf16[64,640]{1,0:T(8,128)(2,1)S(1)}, u32[]{:S(2)}, u32[]{:S(2)}) %collective-permute-start.15) | collective-permute-done | bytes 81952 | tf_op jit(solution)/shard_map/ppermute | solution.py:100
  (18 shorter events, 3.1 us)
Async XLA Ops:
  1.2 17.2 %collective-permute-start.2 = (bf16[128,640]{1,0:T(8,128)(2,1)S(1)}, bf16[128,640]{1,0:T(8,128)(2,1)S(1)}, u32[]{:S(2)}, u32[]{:S(2)}) collective-permute-start(bf16[128,640]{1,0:T(8,128)(2,1)S(1)} %get-tuple-element.37), channel_id=1, source_target_pairs={{0,10},{2,8},{4,14},{6,12},{8,2},{10,0},{12,6},{14,4},{1,11},{3,9}... | collective-permute-start | bytes 491528 | tf_op jit(solution)/shard_map/ppermute | solution.py:100
  6.3 21.2 %collective-permute-start = (bf16[128,640]{1,0:T(8,128)(2,1)S(1)}, bf16[128,640]{1,0:T(8,128)(2,1)S(1)}, u32[]{:S(2)}, u32[]{:S(2)}) collective-permute-start(bf16[128,640]{1,0:T(8,128)(2,1)S(1)} %get-tuple-element.35), channel_id=1, source_target_pairs={{0,8},{2,10},{4,12},{6,14},{8,0},{10,2},{12,4},{14,6},{1,9},{3,11}... | collective-permute-start | bytes 491528 | tf_op jit(solution)/shard_map/ppermute | solution.py:100
  6.6 23.3 %collective-permute-start.1 = (bf16[192,640]{1,0:T(8,128)(2,1)S(1)}, bf16[192,640]{1,0:T(8,128)(2,1)S(1)}, u32[]{:S(2)}, u32[]{:S(2)}) collective-permute-start(bf16[192,640]{1,0:T(8,128)(2,1)S(1)} %get-tuple-element.36), channel_id=1, source_target_pairs={{0,4},{2,6},{4,0},{6,2},{8,12},{10,14},{12,8},{14,10},{1,5},{3,7},... | collective-permute-start | bytes 737288 | tf_op jit(solution)/shard_map/ppermute | solution.py:100
  9.7 20.2 %collective-permute-start.3 = (bf16[192,640]{1,0:T(8,128)(2,1)S(1)}, bf16[192,640]{1,0:T(8,128)(2,1)S(1)}, u32[]{:S(2)}, u32[]{:S(2)}) collective-permute-start(bf16[192,640]{1,0:T(8,128)(2,1)S(1)} %get-tuple-element.41), channel_id=1, source_target_pairs={{0,12},{2,14},{4,8},{6,10},{8,4},{10,6},{12,0},{14,2},{1,13},{3,15... | collective-permute-start | bytes 737288 | tf_op jit(solution)/shard_map/ppermute | solution.py:100
  12.3 18.4 %collective-permute-start.4 = (bf16[192,640]{1,0:T(8,128)(2,1)S(1)}, bf16[192,640]{1,0:T(8,128)(2,1)S(1)}, u32[]{:S(2)}, u32[]{:S(2)}) collective-permute-start(bf16[192,640]{1,0:T(8,128)(2,1)S(1)} %get-tuple-element.42), channel_id=1, source_target_pairs={{0,6},{2,4},{4,2},{6,0},{8,14},{10,12},{12,10},{14,8},{1,7},{3,5},... | collective-permute-start | bytes 737288 | tf_op jit(solution)/shard_map/ppermute | solution.py:100
  18.4 12.3 %collective-permute-start.5 = (bf16[192,640]{1,0:T(8,128)(2,1)S(1)}, bf16[192,640]{1,0:T(8,128)(2,1)S(1)}, u32[]{:S(2)}, u32[]{:S(2)}) collective-permute-start(bf16[192,640]{1,0:T(8,128)(2,1)S(1)} %get-tuple-element.43), channel_id=1, source_target_pairs={{0,2},{2,0},{4,6},{6,4},{8,10},{10,8},{12,14},{14,12},{1,3},{3,1},... | collective-permute-start | bytes 737288 | tf_op jit(solution)/shard_map/ppermute | solution.py:100
  27.5 8.9 %collective-permute-start.6 = (bf16[192,640]{1,0:T(8,128)(2,1)S(1)}, bf16[192,640]{1,0:T(8,128)(2,1)S(1)}, u32[]{:S(2)}, u32[]{:S(2)}) collective-permute-start(bf16[192,640]{1,0:T(8,128)(2,1)S(1)} %get-tuple-element.44), channel_id=1, source_target_pairs={{0,14},{2,12},{4,10},{6,8},{8,6},{10,4},{12,2},{14,0},{1,15},{3,13... | collective-permute-start | bytes 737288 | tf_op jit(solution)/shard_map/ppermute | solution.py:100
  36.5 9.5 %collective-permute-start.7 = (bf16[2,512,640]{2,1,0:T(8,128)(2,1)S(1)}, bf16[2,512,640]{2,1,0:T(8,128)(2,1)S(1)}, u32[]{:S(2)}, u32[]{:S(2)}) collective-permute-start(bf16[2,512,640]{2,1,0:T(8,128)(2,1)S(1)} %shard_map.39.own), channel_id=1, source_target_pairs={{0,1},{1,0},{2,3},{3,2},{4,5},{5,4},{6,7},{7,6},{8,9},{9,8},{10,11... | collective-permute-start | bytes 3932168 | tf_op jit(solution)/shard_map/ppermute | solution.py:139
  36.6 16.4 %collective-permute-start.8 = (bf16[64,640]{1,0:T(8,128)(2,1)S(1)}, bf16[64,640]{1,0:T(8,128)(2,1)S(1)}, u32[]{:S(2)}, u32[]{:S(2)}) collective-permute-start(bf16[64,640]{1,0:T(8,128)(2,1)S(1)} %get-tuple-element.46), channel_id=1, source_target_pairs={{0,8},{2,10},{4,12},{6,14},{8,0},{10,2},{12,4},{14,6},{1,9},{3,11}... | collective-permute-start | bytes 245768 | tf_op jit(solution)/shard_map/ppermute | solution.py:100
  44.9 12.9 %collective-permute-start.9 = (bf16[64,640]{1,0:T(8,128)(2,1)S(1)}, bf16[64,640]{1,0:T(8,128)(2,1)S(1)}, u32[]{:S(2)}, u32[]{:S(2)}) collective-permute-start(bf16[64,640]{1,0:T(8,128)(2,1)S(1)} %get-tuple-element.47), channel_id=1, source_target_pairs={{0,10},{2,8},{4,14},{6,12},{8,2},{10,0},{12,6},{14,4},{1,11},{3,9}... | collective-permute-start | bytes 245768 | tf_op jit(solution)/shard_map/ppermute | solution.py:100
  47.1 16.4 %collective-permute-start.12 = (bf16[64,640]{1,0:T(8,128)(2,1)S(1)}, bf16[64,640]{1,0:T(8,128)(2,1)S(1)}, u32[]{:S(2)}, u32[]{:S(2)}) collective-permute-start(bf16[64,640]{1,0:T(8,128)(2,1)S(1)} %get-tuple-element.59), channel_id=1, source_target_pairs={{0,14},{2,12},{4,10},{6,8},{8,6},{10,4},{12,2},{14,0},{1,15},{3,13... | collective-permute-start | bytes 245768 | tf_op jit(solution)/shard_map/ppermute | solution.py:100
  47.6 15.9 %collective-permute-start.14 = (bf16[64,640]{1,0:T(8,128)(2,1)S(1)}, bf16[64,640]{1,0:T(8,128)(2,1)S(1)}, u32[]{:S(2)}, u32[]{:S(2)}) collective-permute-start(bf16[64,640]{1,0:T(8,128)(2,1)S(1)} %get-tuple-element.48), channel_id=1, source_target_pairs={{0,12},{2,14},{4,8},{6,10},{8,4},{10,6},{12,0},{14,2},{1,13},{3,15... | collective-permute-start | bytes 245768 | tf_op jit(solution)/shard_map/ppermute | solution.py:100
  59.0 9.6 %collective-permute-start.10 = (bf16[64,640]{1,0:T(8,128)(2,1)S(1)}, bf16[64,640]{1,0:T(8,128)(2,1)S(1)}, u32[]{:S(2)}, u32[]{:S(2)}) collective-permute-start(bf16[64,640]{1,0:T(8,128)(2,1)S(1)} %get-tuple-element.56), channel_id=1, source_target_pairs={{0,8},{2,10},{4,12},{6,14},{8,0},{10,2},{12,4},{14,6},{1,9},{3,11}... | collective-permute-start | bytes 245768 | tf_op jit(solution)/shard_map/ppermute | solution.py:100
  59.1 6.4 %collective-permute-start.16 = (bf16[64,640]{1,0:T(8,128)(2,1)S(1)}, bf16[64,640]{1,0:T(8,128)(2,1)S(1)}, u32[]{:S(2)}, u32[]{:S(2)}) collective-permute-start(bf16[64,640]{1,0:T(8,128)(2,1)S(1)} %get-tuple-element.64), channel_id=1, source_target_pairs={{0,2},{2,0},{4,6},{6,4},{8,10},{10,8},{12,14},{14,12},{1,3},{3,1},... | collective-permute-start | bytes 245768 | tf_op jit(solution)/shard_map/ppermute | solution.py:100
  59.8 8.8 %collective-permute-start.11 = (bf16[64,640]{1,0:T(8,128)(2,1)S(1)}, bf16[64,640]{1,0:T(8,128)(2,1)S(1)}, u32[]{:S(2)}, u32[]{:S(2)}) collective-permute-start(bf16[64,640]{1,0:T(8,128)(2,1)S(1)} %get-tuple-element.57), channel_id=1, source_target_pairs={{0,10},{2,8},{4,14},{6,12},{8,2},{10,0},{12,6},{14,4},{1,11},{3,9}... | collective-permute-start | bytes 245768 | tf_op jit(solution)/shard_map/ppermute | solution.py:100
  63.5 6.7 %collective-permute-start.13 = (bf16[64,640]{1,0:T(8,128)(2,1)S(1)}, bf16[64,640]{1,0:T(8,128)(2,1)S(1)}, u32[]{:S(2)}, u32[]{:S(2)}) collective-permute-start(bf16[64,640]{1,0:T(8,128)(2,1)S(1)} %get-tuple-element.60), channel_id=1, source_target_pairs={{0,6},{2,4},{4,2},{6,0},{8,14},{10,12},{12,10},{14,8},{1,7},{3,5},... | collective-permute-start | bytes 245768 | tf_op jit(solution)/shard_map/ppermute | solution.py:100
  63.5 7.6 %collective-permute-start.15 = (bf16[64,640]{1,0:T(8,128)(2,1)S(1)}, bf16[64,640]{1,0:T(8,128)(2,1)S(1)}, u32[]{:S(2)}, u32[]{:S(2)}) collective-permute-start(bf16[64,640]{1,0:T(8,128)(2,1)S(1)} %get-tuple-element.62), channel_id=1, source_target_pairs={{0,4},{2,6},{4,0},{6,2},{8,12},{10,14},{12,8},{14,10},{1,5},{3,7},... | collective-permute-start | bytes 245768 | tf_op jit(solution)/shard_map/ppermute | solution.py:100

commit v5 on v3

--- a/solution.py
+++ b/solution.py
@@ -38,23 +38,23 @@
 
 LAST = 3
 JOINED_BY = (0, 0)
-UNPACK = (2,), (LAST, 1, 0)
 FIRST = ((3, 0), (1, 0), (3, 1))
 REST = ((2, 0), (1, 1), (0, 0), (2, 1), (0, 1))
 
 
-def columns(at_ref, dz, cross, gw):
-    group = at_ref[0] ^ (2 * dz + (at_ref[1] ^ cross))
+def columns(at, dz, cross, gw):
+    group = at[0][0] ^ (2 * dz + (at[1][0] ^ cross))
     return pl.ds(pl.multiple_of(group * gw, HEAD_DIM), gw)
 
 
-def pack_body(rows, gw, layout, at_ref, *refs):
+def pack_body(rows, gw, layout, chip_ref, core_ref, *refs):
+    at = chip_ref, core_ref
     arrays, out_refs, sems = refs[:3], refs[3:-1], refs[-1]
     copies = []
     for out_ref, (piece, parts) in zip(out_refs, layout):
-        col = columns(at_ref, *piece, gw)
-        for at, n in enumerate(parts):
-            to = out_ref.at[at * rows : (at + 1) * rows]
+        col = columns(at, *piece, gw)
+        for first, n in enumerate(parts):
+            to = out_ref.at[first * rows : (first + 1) * rows]
             copies.append(pltpu.make_async_copy(arrays[n].at[:, col], to, sems.at[len(copies)]))
     for copy in copies:
         copy.start()
@@ -69,12 +69,13 @@
             out_ref[which, n * rows : (n + 1) * rows] = piece[which * rows : (which + 1) * rows]
 
 
-def unpack_body(gw, order, at_ref, *refs):
+def unpack_body(gw, order, chip_ref, core_ref, *refs):
+    at = chip_ref, core_ref
     pieces, out_ref, sems = refs[: len(order)], refs[-2], refs[-1]
     rows = out_ref.shape[0]
     copies = []
     for n, piece in enumerate(order):
-        to = out_ref.at[:, columns(at_ref, *piece, gw)]
+        to = out_ref.at[:, columns(at, *piece, gw)]
         copies.append(pltpu.make_async_copy(pieces[n].at[:rows], to, sems.at[n]))
     for copy in copies:
         copy.start()
@@ -101,7 +102,7 @@
     layers, tok_rows, _ = queries.shape
     rows_q = layers * tok_rows
     assert rows_q == rows
-    at = jnp.stack([lax.axis_index("chip"), lax.axis_index("core")]).astype(jnp.int32)
+    at = [lax.axis_index(name).reshape(1).astype(jnp.int32) for name in ("chip", "core")]
 
     def across(array, dz, cross):
         senders = [(chip, core) for chip in range(chips) for core in range(2)]
@@ -132,16 +133,16 @@
     sources = [pltpu.with_memory_space_constraint(a, pltpu.HBM) for a in sources]
 
     def pack(layout, *others):
-        arrays = lax.optimization_barrier((*sources, *others))[:3]
+        arrays = lax.optimization_barrier((*sources, *others))[:3] if others else sources
         return pl.pallas_call(
             functools.partial(pack_body, rows, gw, layout),
-            in_specs=[SMEM, HBM, HBM, HBM],
+            in_specs=[SMEM, SMEM, HBM, HBM, HBM],
             out_specs=[VMEM] * len(layout),
             out_shape=[shape(len(parts) * rows, gw) for _, parts in layout],
             scratch_shapes=[pltpu.SemaphoreType.DMA((sum(len(parts) for _, parts in layout),))],
             compiler_params=PARAMS,
             cost_estimate=FREE,
-        )(at, *arrays)
+        )(*at, *arrays)
 
     layout = [(p, (0, 1) if p[0] == LAST else (0, 1, 2)) for p in FIRST + REST]
     layout += [((LAST, cross), (2,)) for cross in range(2)]
@@ -164,29 +165,28 @@
         return dict(zip(dzs, outs))
 
     outs = attend((2,))
-    outs |= attend((LAST,), outs[2])
-    outs |= attend((1, 0), outs[LAST])
-    back = {dz: across(outs[dz], dz, 0) for dz in (2, LAST)}
-    back |= {dz: across(after(outs[dz], back[2]), dz, 0) for dz in (1, 0)}
-    handed = {dz: swap(back[dz][rows:]) for dz in (2, 1, 0)}
+    outs |= attend((1, 0), outs[2])
+    outs |= attend((LAST,), outs[0])
+    back = {(dz, 0): across(outs[dz], dz, 0) for dz in (2, 1, 0, LAST)}
+    back[2, 1] = swap(after(back[2, 0], outs[LAST])[rows:])
+    back |= {(dz, 1): swap(after(back[dz, 0], back[2, 1], back[LAST, 0])[rows:]) for dz in (1, 0)}
+    back[LAST, 1] = swap(back[LAST, 0][rows:])
 
     def unpack(dzs, *so_far):
         order = [(dz, cross) for dz in dzs for cross in range(2)]
-        pieces = [handed[dz] if cross else back[dz] for dz, cross in order]
+        pieces = [back[piece] for piece in order]
         return pl.pallas_call(
             functools.partial(unpack_body, gw, order),
-            in_specs=[SMEM] + [VMEM] * len(order) + [HBM] * len(so_far),
+            in_specs=[SMEM, SMEM] + [VMEM] * len(order) + [HBM] * len(so_far),
             out_specs=HBM,
             out_shape=shape(rows_q, width),
             scratch_shapes=[pltpu.SemaphoreType.DMA((len(order),))],
-            input_output_aliases={1 + len(order): 0} if so_far else {},
+            input_output_aliases={2 + len(order): 0} if so_far else {},
             compiler_params=PARAMS,
             cost_estimate=FREE,
-        )(at, *pieces, *so_far)
-
-    result = unpack(UNPACK[0])
-    handed[LAST] = swap(after(back[LAST], result)[rows:])
-    result = unpack(UNPACK[1], result)
+        )(*at, *pieces, *so_far)
+
+    result = unpack((LAST, 1, 0), unpack((2,)))
     return result.reshape(layers, tok_rows, width)
 
 

time: 74.1 us -> 70 us (0.945)
  Pallas kernels: 10.8 us -> 8.66 us
  starting transfers between devices: 33.3 us -> 31.8 us
    ppermute x6, starting transfers between devices: 5.02 us -> 2.2 us  [swap(): return lax.ppermute(array, 'core', [(0, 1), (1, 0)])]
    ppermute x13, starting transfers between devices: 28.2 us -> 29.6 us  [across(): return lax.ppermute(array, ('chip', 'core'), pairs)]
    pallas_call x2, Pallas kernels: 3.82 us -> 2.73 us  [pack(): pl.pallas_call(functools.partial(pack_body, rows, gw, layout), in_specs=[...]
    pallas_call x2, Pallas kernels: 2.59 us -> 1.5 us  [unpack(): pl.pallas_call(functools.partial(unpack_body, gw, order), in_specs=[SMEM,...]
    ppermute x6, waiting for transfers between devices: 1.97 us -> 1.16 us  [swap(): return lax.ppermute(array, 'core', [(0, 1), (1, 0)])]
  transfers between devices with their start and end apart: 19 -> 19, of which waited for: 10 -> 10; matrix products, arithmetic and copies ran while one was open for 0% -> 0% of each run, Pallas kernels for 10% -> 9%
where the time goes in v5:
time: 70 us; the launch traced here: 69.8 us
  starting transfers between devices  31.8 us (45%)
  waiting for transfers between devices  29.1 us (42%)
  Pallas kernels  8.66 us (12%)
    ppermute x13, starting transfers between devices, across(): return lax.ppermute(array, ('chip', 'core'), pairs)  29.6 us
    ppermute x13, waiting for transfers between devices, across(): return lax.ppermute(array, ('chip', 'core'), pairs)  27.9 us
    pallas_call x3, Pallas kernels, attend(): call(body, 2 + count, [shape(2 * rows, gw)] * len(dzs))(own, other, *pieces)  4.33 us
    pallas_call x2, Pallas kernels, pack(): pl.pallas_call(functools.partial(pack_body, rows, gw, layout), in_specs=[...  2.73 us
    ppermute x6, starting transfers between devices, swap(): return lax.ppermute(array, 'core', [(0, 1), (1, 0)])  2.2 us
    pallas_call x2, Pallas kernels, unpack(): pl.pallas_call(functools.partial(unpack_body, gw, order), in_specs=[SMEM,...  1.5 us
  transfers between devices with their start and end apart: 19, of which 10 were waited for; matrix products, arithmetic and copies ran while one was open for 0% of the time, Pallas kernels for 9%

profile of v5, /device:TPU:0, one launch (start us, length us, event | category | flops | bytes accessed | tf_op | source)
XLA Modules:
  0.0 69.8 jit_solution(14484690134259949736)
XLA Ops:
  0.0 1.2 %shard_map.37 = (bf16[128,640]{1,0:T(8,128)(2,1)S(1)}, bf16[192,640]{1,0:T(8,128)(2,1)S(1)}, bf16[128,640]{1,0:T(8,128)(2,1)S(1)}) custom-call(s32[1]{0:T(128)} %bitcast.chip_ref, s32[1]{0:T(128)} %bitcast.1.core_ref, bf16[64,5120]{1,0:T(8,128)(2,1)} %refs_0_.2, bf16[64,5120]{1,0:T(8,128)(2,1)} %refs_1_.2, bf16[64,5120]{1,0:T(8,128)(2,1)} %bitcast.4), custom_call_target="tpu_custom_call" | custom-call | tf_op jit(solution)/shard_map/pallas_call | solution.py:137
  1.2 3.1 %collective-permute-start.1 = (bf16[192,640]{1,0:T(8,128)(2,1)S(1)}, bf16[192,640]{1,0:T(8,128)(2,1)S(1)}, u32[]{:S(2)}, u32[]{:S(2)}) collective-permute-start(bf16[192,640]{1,0:T(8,128)(2,1)S(1)} %get-tuple-element.30), channel_id=1, source_target_pairs={{0,4},{1,7},{2,6},{3,5},{4,0},{5,3},{6,2},{7,1},{8,12},{9,15},{10,... | collective-permute-start | bytes 737288 | tf_op jit(solution)/shard_map/ppermute | solution.py:111
  4.3 2.5 %collective-permute-start.2 = (bf16[128,640]{1,0:T(8,128)(2,1)S(1)}, bf16[128,640]{1,0:T(8,128)(2,1)S(1)}, u32[]{:S(2)}, u32[]{:S(2)}) collective-permute-start(bf16[128,640]{1,0:T(8,128)(2,1)S(1)} %get-tuple-element.31), channel_id=1, source_target_pairs={{0,15},{1,12},{2,13},{3,14},{4,11},{5,8},{6,9},{7,10},{8,7},{9,4},... | collective-permute-start | bytes 491528 | tf_op jit(solution)/shard_map/ppermute | solution.py:111
  6.8 1.3 %collective-permute-start = (bf16[128,640]{1,0:T(8,128)(2,1)S(1)}, bf16[128,640]{1,0:T(8,128)(2,1)S(1)}, u32[]{:S(2)}, u32[]{:S(2)}) collective-permute-start(bf16[128,640]{1,0:T(8,128)(2,1)S(1)} %get-tuple-element.29), channel_id=1, source_target_pairs={{0,12},{1,15},{2,14},{3,13},{4,8},{5,11},{6,10},{7,9},{8,4},{9,7},... | collective-permute-start | bytes 491528 | tf_op jit(solution)/shard_map/ppermute | solution.py:111
  8.2 1.5 %shard_map.38 = (bf16[192,640]{1,0:T(8,128)(2,1)S(1)}, bf16[192,640]{1,0:T(8,128)(2,1)S(1)}, bf16[192,640]{1,0:T(8,128)(2,1)S(1)}, bf16[192,640]{1,0:T(8,128)(2,...) custom-call(s32[1]{0:T(128)} %bitcast.chip_ref, ...), custom_call_target="tpu_custom_call" | custom-call | tf_op jit(solution)/shard_map/pallas_call | solution.py:137
  9.7 0.8 %collective-permute-start.5 = (bf16[64,640]{1,0:T(8,128)(2,1)S(1)}, bf16[64,640]{1,0:T(8,128)(2,1)S(1)}, u32[]{:S(2)}, u32[]{:S(2)}) collective-permute-start(bf16[64,640]{1,0:T(8,128)(2,1)S(1)} %get-tuple-element.39), channel_id=1, source_target_pairs={{0,1},{1,0},{2,3},{3,2},{4,5},{5,4},{6,7},{7,6},{8,9},{9,8},{10,11... | collective-permute-start | bytes 245768 | tf_op jit(solution)/shard_map/ppermute | solution.py:114
  10.5 0.8 %collective-permute-start.3 = (bf16[192,640]{1,0:T(8,128)(2,1)S(1)}, bf16[192,640]{1,0:T(8,128)(2,1)S(1)}, u32[]{:S(2)}, u32[]{:S(2)}) collective-permute-start(bf16[192,640]{1,0:T(8,128)(2,1)S(1)} %get-tuple-element.35), channel_id=1, source_target_pairs={{0,8},{1,11},{2,10},{3,9},{4,12},{5,15},{6,14},{7,13},{8,0},{9,3},... | collective-permute-start | bytes 737288 | tf_op jit(solution)/shard_map/ppermute | solution.py:111
  11.4 2.5 %collective-permute-start.4 = (bf16[192,640]{1,0:T(8,128)(2,1)S(1)}, bf16[192,640]{1,0:T(8,128)(2,1)S(1)}, u32[]{:S(2)}, u32[]{:S(2)}) collective-permute-start(bf16[192,640]{1,0:T(8,128)(2,1)S(1)} %get-tuple-element.36), channel_id=1, source_target_pairs={{0,7},{1,4},{2,5},{3,6},{4,3},{5,0},{6,1},{7,2},{8,15},{9,12},{10,... | collective-permute-start | bytes 737288 | tf_op jit(solution)/shard_map/ppermute | solution.py:111
  13.9 3.0 %collective-permute-done.2.refs_2_ = bf16[128,640]{1,0:T(8,128)(2,1)S(1)} collective-permute-done((bf16[128,640]{1,0:T(8,128)(2,1)S(1)}, bf16[128,640]{1,0:T(8,128)(2,1)S(1)}, u32[]{:S(2)}, u32[]{:S(2)}) %collective-permute-start.2) | collective-permute-done | bytes 163872 | tf_op jit(solution)/shard_map/ppermute | solution.py:111
  16.9 9.8 %collective-permute-start.7 = (bf16[192,640]{1,0:T(8,128)(2,1)S(1)}, bf16[192,640]{1,0:T(8,128)(2,1)S(1)}, u32[]{:S(2)}, u32[]{:S(2)}) collective-permute-start(bf16[192,640]{1,0:T(8,128)(2,1)S(1)} %get-tuple-element.41), channel_id=1, source_target_pairs={{0,11},{1,8},{2,9},{3,10},{4,15},{5,12},{6,13},{7,14},{8,3},{9,0},... | collective-permute-start | bytes 737288 | tf_op jit(solution)/shard_map/ppermute | solution.py:111
  27.4 10.8 %collective-permute-done.3.refs_3_.refs_0_ = bf16[192,640]{1,0:T(8,128)(2,1)S(1)} collective-permute-done((bf16[192,640]{1,0:T(8,128)(2,1)S(1)}, bf16[192,640]{1,0:T(8,128)(2,1)S(1)}, u32[]{:S(2)}, u32[]{:S(2)}) %collective-permute-start.3) | collective-permute-done | bytes 245792 | tf_op jit(solution)/shard_map/ppermute | solution.py:111
  38.3 4.9 %collective-permute-done.7.refs_6_.refs_1_ = bf16[192,640]{1,0:T(8,128)(2,1)S(1)} collective-permute-done((bf16[192,640]{1,0:T(8,128)(2,1)S(1)}, bf16[192,640]{1,0:T(8,128)(2,1)S(1)}, u32[]{:S(2)}, u32[]{:S(2)}) %collective-permute-start.7) | collective-permute-done | bytes 245792 | tf_op jit(solution)/shard_map/ppermute | solution.py:111
  43.5 3.3 %collective-permute-start.10 = (bf16[128,640]{1,0:T(8,128)(2,1)S(1)}, bf16[128,640]{1,0:T(8,128)(2,1)S(1)}, u32[]{:S(2)}, u32[]{:S(2)}) collective-permute-start(bf16[128,640]{1,0:T(8,128)(2,1)S(1)} %constant_dynamic-update-slice_fusion), channel_id=1, source_target_pairs={{0,12},{1,15},{2,14},{3,13},{4,8},{5,11},{6,10},{7,9},{8,4},{9,7},... | collective-permute-start | bytes 491528 | tf_op jit(solution)/shard_map/ppermute | solution.py:111
  46.8 1.2 %shard_map.40 = bf16[128,640]{1,0:T(8,128)(2,1)S(1)} custom-call(bf16[2,512,640]{2,1,0:T(8,128)(2,1)S(1)} %shard_map.39.own, bf16[2,512,640]{2,1,0:T(8,128)(2,1)S(1)} %collective-permute-done.9.other, bf16[192,640]{1,0:T(8,128)(2,1)S(1)} %collective-permute-done.3.refs_3_.refs_0_, bf16[192,640]{1,0:T(8,128)(2,1)S(1)} %collective-permute-done.7.refs_6_.refs_1_), custom_call_target="tpu_custom_call" | custom-call | tf_op jit(solution)/shard_map/pallas_call | solution.py:164
  48.1 2.0 %shard_map.41 = (bf16[128,640]{1,0:T(8,128)(2,1)S(1)}, bf16[128,640]{1,0:T(8,128)(2,1)S(1)}) custom-call(bf16[2,512,640]{2,1,0:T(8,128)(2,1)S(1)} %shard_map.39.own, bf16[2,512,640]{2,1,0:T(8,128)(2,1)S(1)} %collective-permute-done.9.other, bf16[192,640]{1,0:T(8,128)(2,1)S(1)} %collective-permute-done.1.refs_1_.refs_0_, ...), custom_call_target="tpu_custom_call" | custom-call | tf_op jit(solution)/shard_map/pallas_call | solution.py:164
  50.1 2.4 %collective-permute-done.10.refs_0_ = bf16[128,640]{1,0:T(8,128)(2,1)S(1)} collective-permute-done((bf16[128,640]{1,0:T(8,128)(2,1)S(1)}, bf16[128,640]{1,0:T(8,128)(2,1)S(1)}, u32[]{:S(2)}, u32[]{:S(2)}) %collective-permute-start.10) | collective-permute-done | bytes 163872 | tf_op jit(solution)/shard_map/ppermute | solution.py:111
  52.5 1.2 %shard_map.42 = bf16[128,640]{1,0:T(8,128)(2,1)S(1)} custom-call(bf16[2,512,640]{2,1,0:T(8,128)(2,1)S(1)} %shard_map.39.own, bf16[2,512,640]{2,1,0:T(8,128)(2,1)S(1)} %collective-permute-done.9.other, bf16[128,640]{1,0:T(8,128)(2,1)S(1)} %collective-permute-done.10.refs_0_), custom_call_target="tpu_custom_call" | custom-call | tf_op jit(solution)/shard_map/pallas_call | solution.py:164
  53.6 3.4 %collective-permute-start.11 = (bf16[128,640]{1,0:T(8,128)(2,1)S(1)}, bf16[128,640]{1,0:T(8,128)(2,1)S(1)}, u32[]{:S(2)}, u32[]{:S(2)}) collective-permute-start(bf16[128,640]{1,0:T(8,128)(2,1)S(1)} %shard_map.42), channel_id=1, source_target_pairs={{0,12},{1,15},{2,14},{3,13},{4,8},{5,11},{6,10},{7,9},{8,4},{9,7},... | collective-permute-start | bytes 491528 | tf_op jit(solution)/shard_map/ppermute | solution.py:111
  57.7 1.4 %collective-permute-start.13 = (bf16[128,640]{1,0:T(8,128)(2,1)S(1)}, bf16[128,640]{1,0:T(8,128)(2,1)S(1)}, u32[]{:S(2)}, u32[]{:S(2)}) collective-permute-start(bf16[128,640]{1,0:T(8,128)(2,1)S(1)} %get-tuple-element.49), channel_id=1, source_target_pairs={{0,4},{1,7},{2,6},{3,5},{4,0},{5,3},{6,2},{7,1},{8,12},{9,15},{10,... | collective-permute-start | bytes 491528 | tf_op jit(solution)/shard_map/ppermute | solution.py:111
  59.1 4.6 %collective-permute-done.14.refs_0_ = bf16[128,640]{1,0:T(8,128)(2,1)S(1)} collective-permute-done((bf16[128,640]{1,0:T(8,128)(2,1)S(1)}, bf16[128,640]{1,0:T(8,128)(2,1)S(1)}, u32[]{:S(2)}, u32[]{:S(2)}) %collective-permute-start.14) | collective-permute-done | bytes 163872 | tf_op jit(solution)/shard_map/ppermute | solution.py:111
  64.3 0.7 collective-permute-done.15.refs_1_
  65.0 2.3 %collective-permute-done.13.refs_2_ = bf16[128,640]{1,0:T(8,128)(2,1)S(1)} collective-permute-done((bf16[128,640]{1,0:T(8,128)(2,1)S(1)}, bf16[128,640]{1,0:T(8,128)(2,1)S(1)}, u32[]{:S(2)}, u32[]{:S(2)}) %collective-permute-start.13) | collective-permute-done | bytes 163872 | tf_op jit(solution)/shard_map/ppermute | solution.py:111
  67.9 0.7 shard_map.43.refs_6_
  68.9 0.8 %shard_map.44 = bf16[64,5120]{1,0:T(8,128)(2,1)} custom-call(s32[1]{0:T(128)} %bitcast.chip_ref, s32[1]{0:T(128)} %bitcast.1.core_ref, bf16[128,640]{1,0:T(8,128)(2,1)S(1)} %collective-permute-done.11.refs_0_, bf16[64,640]{1,0:T(8,128)(2,1)S(1)} %collective-permute-done.12.refs_1_, ...), custom_call_target="tpu_custom_call", output_to_operand_aliasing={{}: (8, {})} | custom-call | tf_op jit(solution)/shard_map/pallas_call | solution.py:178
  (28 shorter events, 3.5 us)
Async XLA Ops:
  1.2 25.6 %collective-permute-start.1 = (bf16[192,640]{1,0:T(8,128)(2,1)S(1)}, bf16[192,640]{1,0:T(8,128)(2,1)S(1)}, u32[]{:S(2)}, u32[]{:S(2)}) collective-permute-start(bf16[192,640]{1,0:T(8,128)(2,1)S(1)} %get-tuple-element.30), channel_id=1, source_target_pairs={{0,4},{1,7},{2,6},{3,5},{4,0},{5,3},{6,2},{7,1},{8,12},{9,15},{10,... | collective-permute-start | bytes 737288 | tf_op jit(solution)/shard_map/ppermute | solution.py:111
  4.3 12.6 %collective-permute-start.2 = (bf16[128,640]{1,0:T(8,128)(2,1)S(1)}, bf16[128,640]{1,0:T(8,128)(2,1)S(1)}, u32[]{:S(2)}, u32[]{:S(2)}) collective-permute-start(bf16[128,640]{1,0:T(8,128)(2,1)S(1)} %get-tuple-element.31), channel_id=1, source_target_pairs={{0,15},{1,12},{2,13},{3,14},{4,11},{5,8},{6,9},{7,10},{8,7},{9,4},... | collective-permute-start | bytes 491528 | tf_op jit(solution)/shard_map/ppermute | solution.py:111
  6.8 19.9 %collective-permute-start = (bf16[128,640]{1,0:T(8,128)(2,1)S(1)}, bf16[128,640]{1,0:T(8,128)(2,1)S(1)}, u32[]{:S(2)}, u32[]{:S(2)}) collective-permute-start(bf16[128,640]{1,0:T(8,128)(2,1)S(1)} %get-tuple-element.29), channel_id=1, source_target_pairs={{0,12},{1,15},{2,14},{3,13},{4,8},{5,11},{6,10},{7,9},{8,4},{9,7},... | collective-permute-start | bytes 491528 | tf_op jit(solution)/shard_map/ppermute | solution.py:111
  9.7 1.7 %collective-permute-start.5 = (bf16[64,640]{1,0:T(8,128)(2,1)S(1)}, bf16[64,640]{1,0:T(8,128)(2,1)S(1)}, u32[]{:S(2)}, u32[]{:S(2)}) collective-permute-start(bf16[64,640]{1,0:T(8,128)(2,1)S(1)} %get-tuple-element.39), channel_id=1, source_target_pairs={{0,1},{1,0},{2,3},{3,2},{4,5},{5,4},{6,7},{7,6},{8,9},{9,8},{10,11... | collective-permute-start | bytes 245768 | tf_op jit(solution)/shard_map/ppermute | solution.py:114
  10.5 27.7 %collective-permute-start.3 = (bf16[192,640]{1,0:T(8,128)(2,1)S(1)}, bf16[192,640]{1,0:T(8,128)(2,1)S(1)}, u32[]{:S(2)}, u32[]{:S(2)}) collective-permute-start(bf16[192,640]{1,0:T(8,128)(2,1)S(1)} %get-tuple-element.35), channel_id=1, source_target_pairs={{0,8},{1,11},{2,10},{3,9},{4,12},{5,15},{6,14},{7,13},{8,0},{9,3},... | collective-permute-start | bytes 737288 | tf_op jit(solution)/shard_map/ppermute | solution.py:111
  11.4 26.8 %collective-permute-start.4 = (bf16[192,640]{1,0:T(8,128)(2,1)S(1)}, bf16[192,640]{1,0:T(8,128)(2,1)S(1)}, u32[]{:S(2)}, u32[]{:S(2)}) collective-permute-start(bf16[192,640]{1,0:T(8,128)(2,1)S(1)} %get-tuple-element.36), channel_id=1, source_target_pairs={{0,7},{1,4},{2,5},{3,6},{4,3},{5,0},{6,1},{7,2},{8,15},{9,12},{10,... | collective-permute-start | bytes 737288 | tf_op jit(solution)/shard_map/ppermute | solution.py:111
  16.9 26.3 %collective-permute-start.7 = (bf16[192,640]{1,0:T(8,128)(2,1)S(1)}, bf16[192,640]{1,0:T(8,128)(2,1)S(1)}, u32[]{:S(2)}, u32[]{:S(2)}) collective-permute-start(bf16[192,640]{1,0:T(8,128)(2,1)S(1)} %get-tuple-element.41), channel_id=1, source_target_pairs={{0,11},{1,8},{2,9},{3,10},{4,15},{5,12},{6,13},{7,14},{8,3},{9,0},... | collective-permute-start | bytes 737288 | tf_op jit(solution)/shard_map/ppermute | solution.py:111
  26.8 16.4 %collective-permute-start.8 = (bf16[192,640]{1,0:T(8,128)(2,1)S(1)}, bf16[192,640]{1,0:T(8,128)(2,1)S(1)}, u32[]{:S(2)}, u32[]{:S(2)}) collective-permute-start(bf16[192,640]{1,0:T(8,128)(2,1)S(1)} %get-tuple-element.42), channel_id=1, source_target_pairs={{0,3},{1,0},{2,1},{3,2},{4,7},{5,4},{6,5},{7,6},{8,11},{9,8},{10,9... | collective-permute-start | bytes 737288 | tf_op jit(solution)/shard_map/ppermute | solution.py:111
  26.8 16.4 %collective-permute-start.6 = (bf16[192,640]{1,0:T(8,128)(2,1)S(1)}, bf16[192,640]{1,0:T(8,128)(2,1)S(1)}, u32[]{:S(2)}, u32[]{:S(2)}) collective-permute-start(bf16[192,640]{1,0:T(8,128)(2,1)S(1)} %get-tuple-element.40), channel_id=1, source_target_pairs={{0,0},{1,3},{2,2},{3,1},{4,4},{5,7},{6,6},{7,5},{8,8},{9,11},{10,1... | collective-permute-start | bytes 737288 | tf_op jit(solution)/shard_map/ppermute | solution.py:111
  43.3 3.6 %collective-permute-start.9 = (bf16[2,512,640]{2,1,0:T(8,128)(2,1)S(1)}, bf16[2,512,640]{2,1,0:T(8,128)(2,1)S(1)}, u32[]{:S(2)}, u32[]{:S(2)}) collective-permute-start(bf16[2,512,640]{2,1,0:T(8,128)(2,1)S(1)} %shard_map.39.own), channel_id=1, source_target_pairs={{0,1},{1,0},{2,3},{3,2},{4,5},{5,4},{6,7},{7,6},{8,9},{9,8},{10,11... | collective-permute-start | bytes 3932168 | tf_op jit(solution)/shard_map/ppermute | solution.py:114
  43.5 9.0 %collective-permute-start.10 = (bf16[128,640]{1,0:T(8,128)(2,1)S(1)}, bf16[128,640]{1,0:T(8,128)(2,1)S(1)}, u32[]{:S(2)}, u32[]{:S(2)}) collective-permute-start(bf16[128,640]{1,0:T(8,128)(2,1)S(1)} %constant_dynamic-update-slice_fusion), channel_id=1, source_target_pairs={{0,12},{1,15},{2,14},{3,13},{4,8},{5,11},{6,10},{7,9},{8,4},{9,7},... | collective-permute-start | bytes 491528 | tf_op jit(solution)/shard_map/ppermute | solution.py:111
  48.0 15.6 %collective-permute-start.14 = (bf16[128,640]{1,0:T(8,128)(2,1)S(1)}, bf16[128,640]{1,0:T(8,128)(2,1)S(1)}, u32[]{:S(2)}, u32[]{:S(2)}) collective-permute-start(bf16[128,640]{1,0:T(8,128)(2,1)S(1)} %shard_map.40), channel_id=1, source_target_pairs={{0,8},{1,11},{2,10},{3,9},{4,12},{5,15},{6,14},{7,13},{8,0},{9,3},... | collective-permute-start | bytes 491528 | tf_op jit(solution)/shard_map/ppermute | solution.py:111
  53.6 10.1 %collective-permute-start.11 = (bf16[128,640]{1,0:T(8,128)(2,1)S(1)}, bf16[128,640]{1,0:T(8,128)(2,1)S(1)}, u32[]{:S(2)}, u32[]{:S(2)}) collective-permute-start(bf16[128,640]{1,0:T(8,128)(2,1)S(1)} %shard_map.42), channel_id=1, source_target_pairs={{0,12},{1,15},{2,14},{3,13},{4,8},{5,11},{6,10},{7,9},{8,4},{9,7},... | collective-permute-start | bytes 491528 | tf_op jit(solution)/shard_map/ppermute | solution.py:111
  57.0 7.3 %collective-permute-start.17 = (bf16[128,640]{1,0:T(8,128)(2,1)S(1)}, bf16[128,640]{1,0:T(8,128)(2,1)S(1)}, u32[]{:S(2)}, u32[]{:S(2)}) collective-permute-start(bf16[128,640]{1,0:T(8,128)(2,1)S(1)} %get-tuple-element.47), channel_id=1, source_target_pairs={{0,0},{1,3},{2,2},{3,1},{4,4},{5,7},{6,6},{7,5},{8,8},{9,11},{10,1... | collective-permute-start | bytes 491528 | tf_op jit(solution)/shard_map/ppermute | solution.py:111
  57.7 9.6 %collective-permute-start.13 = (bf16[128,640]{1,0:T(8,128)(2,1)S(1)}, bf16[128,640]{1,0:T(8,128)(2,1)S(1)}, u32[]{:S(2)}, u32[]{:S(2)}) collective-permute-start(bf16[128,640]{1,0:T(8,128)(2,1)S(1)} %get-tuple-element.49), channel_id=1, source_target_pairs={{0,4},{1,7},{2,6},{3,5},{4,0},{5,3},{6,2},{7,1},{8,12},{9,15},{10,... | collective-permute-start | bytes 491528 | tf_op jit(solution)/shard_map/ppermute | solution.py:111
  63.6 1.3 %collective-permute-start.15 = (bf16[64,640]{1,0:T(8,128)(2,1)S(1)}, bf16[64,640]{1,0:T(8,128)(2,1)S(1)}, u32[]{:S(2)}, u32[]{:S(2)}) collective-permute-start(bf16[64,640]{1,0:T(8,128)(2,1)S(1)} %slice.13), channel_id=1, source_target_pairs={{0,1},{1,0},{2,3},{3,2},{4,5},{5,4},{6,7},{7,6},{8,9},{9,8},{10,11... | collective-permute-start | bytes 245768 | tf_op jit(solution)/shard_map/ppermute | solution.py:114
  63.7 4.8 %collective-permute-start.12 = (bf16[64,640]{1,0:T(8,128)(2,1)S(1)}, bf16[64,640]{1,0:T(8,128)(2,1)S(1)}, u32[]{:S(2)}, u32[]{:S(2)}) collective-permute-start(bf16[64,640]{1,0:T(8,128)(2,1)S(1)} %slice.16), channel_id=1, source_target_pairs={{0,1},{1,0},{2,3},{3,2},{4,5},{5,4},{6,7},{7,6},{8,9},{9,8},{10,11... | collective-permute-start | bytes 245768 | tf_op jit(solution)/shard_map/ppermute | solution.py:114
  67.3 1.3 %collective-permute-start.18 = (bf16[64,640]{1,0:T(8,128)(2,1)S(1)}, bf16[64,640]{1,0:T(8,128)(2,1)S(1)}, u32[]{:S(2)}, u32[]{:S(2)}) collective-permute-start(bf16[64,640]{1,0:T(8,128)(2,1)S(1)} %slice.15), channel_id=1, source_target_pairs={{0,1},{1,0},{2,3},{3,2},{4,5},{5,4},{6,7},{7,6},{8,9},{9,8},{10,11... | collective-permute-start | bytes 245768 | tf_op jit(solution)/shard_map/ppermute | solution.py:114
  67.7 1.3 %collective-permute-start.16 = (bf16[64,640]{1,0:T(8,128)(2,1)S(1)}, bf16[64,640]{1,0:T(8,128)(2,1)S(1)}, u32[]{:S(2)}, u32[]{:S(2)}) collective-permute-start(bf16[64,640]{1,0:T(8,128)(2,1)S(1)} %slice.14), channel_id=1, source_target_pairs={{0,1},{1,0},{2,3},{3,2},{4,5},{5,4},{6,7},{7,6},{8,9},{9,8},{10,11... | collective-permute-start | bytes 245768 | tf_op jit(solution)/shard_map/ppermute | solution.py:114

commit v6 on v0

--- a/solution.py
+++ b/solution.py
@@ -36,8 +36,8 @@
     return jnp.concatenate([v, jnp.ones_like(v)], axis=1)
 
 
-FIRST = (6, 2, 7)
-REST = (4, 3, 1, 5, 0)
+FIRST = (6, 7)
+REST = (2, 4, 3, 1, 5, 0)
 LAST = (6, 7)
 NEAR = (2, 3, 1)
 
@@ -132,27 +132,30 @@
     layout += [(k, (2,)) for k in LAST]
     packed = pack(layout[: len(FIRST)])
     packed += pack(layout[len(FIRST) :], packed[:1])
-    got = [across(piece, k) for piece, (k, _) in zip(packed, layout)]
-    late = dict(zip(LAST, got[chips:]))
-    got = {k: piece for piece, (k, _) in zip(got[:chips], layout)}
+    got = {k: across(piece, k) for piece, (k, _) in zip(packed[:chips], layout)}
     own = call(functools.partial(merge_body, rows), chips, shape(2, chips * rows, gw))(*got.values())
     other = lax.ppermute(own, "core", [(0, 1), (1, 0)])
 
-    def attend(ks, after=()):
-        pieces = [late.get(k, got[k]) for k in ks]
-        if after:
-            pieces = lax.optimization_barrier((*pieces, *after))[: len(pieces)]
+    def after(array, *others):
+        return lax.optimization_barrier((array, *others))[0]
+
+    def attend(pieces, *others):
+        ks, arrays = tuple(pieces), tuple(pieces.values())
+        if others:
+            arrays = lax.optimization_barrier((*arrays, *others))[: len(ks)]
         body = functools.partial(attend_body, len(ks), rows)
-        outs = call(body, 2 + len(ks), [shape(rows, gw)] * len(ks))(own, other, *pieces)
+        outs = call(body, 2 + len(ks), [shape(rows, gw)] * len(ks))(own, other, *arrays)
         return dict(zip(ks, outs))
 
-    outs = attend((4, 5))
-    outs |= attend(NEAR + (0,), (outs[4],))
-    outs |= attend(LAST, (outs[0],))
-    back = {k: across(outs[k], k) for k in (4, 5) + LAST + (0,)}
-    back[2] = across(lax.optimization_barrier((outs[2], outs[LAST[0]]))[0], 2)
-    for k, before in ((3, 5), (1, 4)):
-        back[k] = across(lax.optimization_barrier((outs[k], outs[LAST[0]], back[before]))[0], k)
+    late = {LAST[0]: across(packed[chips], LAST[0])}
+    outs = attend({k: got[k] for k in (4, 5)})
+    late[LAST[1]] = across(after(packed[chips + 1], outs[4]), LAST[1])
+    outs |= attend({k: got[k] for k in NEAR + (0,)}, outs[4])
+    outs |= attend(late, outs[0])
+    back = {k: across(outs[k], k) for k in (0, 4, 5) + LAST}
+    back[1] = across(outs[1], 1)
+    for k, before in ((2, 5), (3, 4)):
+        back[k] = across(after(outs[k], outs[LAST[0]], back[before]), k)
 
     def unpack(order, so_far=()):
         return pl.pallas_call(
@@ -166,7 +169,7 @@
             cost_estimate=FREE,
         )(chip, *[back[k] for k in order], *so_far)
 
-    result = unpack(LAST + (3, 1), (unpack((0, 4, 5, 2)),))
+    result = unpack(LAST + (3, 2), (unpack((0, 4, 5, 1)),))
     return result.reshape(layers, tok_rows, width)
 
 

time: 68.2 us -> 70.1 us (1.028)
  starting transfers between devices: 39.2 us -> 42.1 us
  waiting for transfers between devices: 20.1 us -> 19 us
    ppermute x16, starting transfers between devices: 39.2 us -> 42.1 us  [across(): lax.ppermute(piece, 'chip', [(i, i ^ k) for i in range(chips)])]
    ppermute x16, waiting for transfers between devices: 20 us -> 18.6 us  [across(): lax.ppermute(piece, 'chip', [(i, i ^ k) for i in range(chips)])]
where the time goes in v6:
time: 70.1 us; the launch traced here: 69.9 us
  starting transfers between devices  42.1 us (60%)
  waiting for transfers between devices  19 us (27%)
  Pallas kernels  8.62 us (12%)
    ppermute x16, starting transfers between devices, across(): lax.ppermute(piece, 'chip', [(i, i ^ k) for i in range(chips)])  42.1 us
    ppermute x16, waiting for transfers between devices, across(): lax.ppermute(piece, 'chip', [(i, i ^ k) for i in range(chips)])  18.6 us
    pallas_call x3, Pallas kernels, attend(): call(body, 2 + len(ks), [shape(rows, gw)] * len(ks))(own, other, *arrays)  4.33 us
    pallas_call x2, Pallas kernels, pack(): pl.pallas_call(functools.partial(pack_body, rows, gw, layout), in_specs=[...  2.68 us
    pallas_call x2, Pallas kernels, unpack(): pl.pallas_call(functools.partial(unpack_body, gw, order), in_specs=[SMEM]...  1.5 us
  transfers between devices with their start and end apart: 17, of which 8 were waited for; matrix products, arithmetic and copies ran while one was open for 0% of the time, Pallas kernels for 10%

profile of v6, /device:TPU:0, one launch (start us, length us, event | category | flops | bytes accessed | tf_op | source)
XLA Modules:
  0.0 69.9 jit_solution(11406073355472666182)
XLA Ops:
  0.0 1.0 %shard_map.37 = (bf16[128,640]{1,0:T(8,128)(2,1)S(1)}, bf16[128,640]{1,0:T(8,128)(2,1)S(1)}) custom-call(s32[1]{0:T(128)} %bitcast.chip_ref, bf16[64,5120]{1,0:T(8,128)(2,1)} %refs_0_.2, bf16[64,5120]{1,0:T(8,128)(2,1)} %refs_1_.2, bf16[64,5120]{1,0:T(8,128)(2,1)} %bitcast.3), custom_call_target="tpu_custom_call" | custom-call | tf_op jit(solution)/shard_map/pallas_call | solution.py:121
  1.0 6.1 %collective-permute-start.1 = (bf16[128,640]{1,0:T(8,128)(2,1)S(1)}, bf16[128,640]{1,0:T(8,128)(2,1)S(1)}, u32[]{:S(2)}, u32[]{:S(2)}) collective-permute-start(bf16[128,640]{1,0:T(8,128)(2,1)S(1)} %get-tuple-element.36), channel_id=1, source_target_pairs={{0,14},{2,12},{4,10},{6,8},{8,6},{10,4},{12,2},{14,0},{1,15},{3,13... | collective-permute-start | bytes 491528 | tf_op jit(solution)/shard_map/ppermute | solution.py:100
  7.3 1.6 %shard_map.38 = (bf16[192,640]{1,0:T(8,128)(2,1)S(1)}, bf16[192,640]{1,0:T(8,128)(2,1)S(1)}, bf16[192,640]{1,0:T(8,128)(2,1)S(1)}, bf16[192,640]{1,0:T(8,128)(2,...) custom-call(s32[1]{0:T(128)} %bitcast.chip_ref, ...), custom_call_target="tpu_custom_call" | custom-call | tf_op jit(solution)/shard_map/pallas_call | solution.py:121
  9.1 4.2 %collective-permute-start.3 = (bf16[192,640]{1,0:T(8,128)(2,1)S(1)}, bf16[192,640]{1,0:T(8,128)(2,1)S(1)}, u32[]{:S(2)}, u32[]{:S(2)}) collective-permute-start(bf16[192,640]{1,0:T(8,128)(2,1)S(1)} %get-tuple-element.41), channel_id=1, source_target_pairs={{0,8},{2,10},{4,12},{6,14},{8,0},{10,2},{12,4},{14,6},{1,9},{3,11}... | collective-permute-start | bytes 737288 | tf_op jit(solution)/shard_map/ppermute | solution.py:100
  13.2 1.5 %collective-permute-start.5 = (bf16[192,640]{1,0:T(8,128)(2,1)S(1)}, bf16[192,640]{1,0:T(8,128)(2,1)S(1)}, u32[]{:S(2)}, u32[]{:S(2)}) collective-permute-start(bf16[192,640]{1,0:T(8,128)(2,1)S(1)} %get-tuple-element.43), channel_id=1, source_target_pairs={{0,2},{2,0},{4,6},{6,4},{8,10},{10,8},{12,14},{14,12},{1,3},{3,1},... | collective-permute-start | bytes 737288 | tf_op jit(solution)/shard_map/ppermute | solution.py:100
  14.8 1.3 %collective-permute-done.refs_0_ = bf16[128,640]{1,0:T(8,128)(2,1)S(1)} collective-permute-done((bf16[128,640]{1,0:T(8,128)(2,1)S(1)}, bf16[128,640]{1,0:T(8,128)(2,1)S(1)}, u32[]{:S(2)}, u32[]{:S(2)}) %collective-permute-start) | collective-permute-done | bytes 163872 | tf_op jit(solution)/shard_map/ppermute | solution.py:100
  16.1 12.6 %collective-permute-start.6 = (bf16[192,640]{1,0:T(8,128)(2,1)S(1)}, bf16[192,640]{1,0:T(8,128)(2,1)S(1)}, u32[]{:S(2)}, u32[]{:S(2)}) collective-permute-start(bf16[192,640]{1,0:T(8,128)(2,1)S(1)} %get-tuple-element.44), channel_id=1, source_target_pairs={{0,10},{2,8},{4,14},{6,12},{8,2},{10,0},{12,6},{14,4},{1,11},{3,9}... | collective-permute-start | bytes 737288 | tf_op jit(solution)/shard_map/ppermute | solution.py:100
  28.7 9.0 %collective-permute-done.3.refs_3_.refs_0_ = bf16[192,640]{1,0:T(8,128)(2,1)S(1)} collective-permute-done((bf16[192,640]{1,0:T(8,128)(2,1)S(1)}, bf16[192,640]{1,0:T(8,128)(2,1)S(1)}, u32[]{:S(2)}, u32[]{:S(2)}) %collective-permute-start.3) | collective-permute-done | bytes 245792 | tf_op jit(solution)/shard_map/ppermute | solution.py:100
  37.7 4.3 %collective-permute-done.6.refs_6_.refs_1_ = bf16[192,640]{1,0:T(8,128)(2,1)S(1)} collective-permute-done((bf16[192,640]{1,0:T(8,128)(2,1)S(1)}, bf16[192,640]{1,0:T(8,128)(2,1)S(1)}, u32[]{:S(2)}, u32[]{:S(2)}) %collective-permute-start.6) | collective-permute-done | bytes 245792 | tf_op jit(solution)/shard_map/ppermute | solution.py:100
  42.2 2.6 %collective-permute-start.8 = (bf16[64,640]{1,0:T(8,128)(2,1)S(1)}, bf16[64,640]{1,0:T(8,128)(2,1)S(1)}, u32[]{:S(2)}, u32[]{:S(2)}) collective-permute-start(bf16[64,640]{1,0:T(8,128)(2,1)S(1)} %get-tuple-element.46), channel_id=1, source_target_pairs={{0,12},{2,14},{4,8},{6,10},{8,4},{10,6},{12,0},{14,2},{1,13},{3,15... | collective-permute-start | bytes 245768 | tf_op jit(solution)/shard_map/ppermute | solution.py:100
  45.2 1.2 %shard_map.40 = (bf16[64,640]{1,0:T(8,128)(2,1)S(1)}, bf16[64,640]{1,0:T(8,128)(2,1)S(1)}) custom-call(bf16[2,512,640]{2,1,0:T(8,128)(2,1)S(1)} %shard_map.39.own, bf16[2,512,640]{2,1,0:T(8,128)(2,1)S(1)} %collective-permute-done.7.other, bf16[192,640]{1,0:T(8,128)(2,1)S(1)} %collective-permute-done.3.refs_3_.refs_0_, ...), custom_call_target="tpu_custom_call" | custom-call | tf_op jit(solution)/shard_map/pallas_call | solution.py:147
  46.4 3.5 %collective-permute-start.9 = (bf16[64,640]{1,0:T(8,128)(2,1)S(1)}, bf16[64,640]{1,0:T(8,128)(2,1)S(1)}, u32[]{:S(2)}, u32[]{:S(2)}) collective-permute-start(bf16[64,640]{1,0:T(8,128)(2,1)S(1)} %get-tuple-element.49), channel_id=1, source_target_pairs={{0,14},{2,12},{4,10},{6,8},{8,6},{10,4},{12,2},{14,0},{1,15},{3,13... | collective-permute-start | bytes 245768 | tf_op jit(solution)/shard_map/ppermute | solution.py:100
  49.9 2.9 %collective-permute-start.12 = (bf16[64,640]{1,0:T(8,128)(2,1)S(1)}, bf16[64,640]{1,0:T(8,128)(2,1)S(1)}, u32[]{:S(2)}, u32[]{:S(2)}) collective-permute-start(bf16[64,640]{1,0:T(8,128)(2,1)S(1)} %get-tuple-element.48), channel_id=1, source_target_pairs={{0,8},{2,10},{4,12},{6,14},{8,0},{10,2},{12,4},{14,6},{1,9},{3,11}... | collective-permute-start | bytes 245768 | tf_op jit(solution)/shard_map/ppermute | solution.py:100
  52.8 2.0 %shard_map.41 = (bf16[64,640]{1,0:T(8,128)(2,1)S(1)}, bf16[64,640]{1,0:T(8,128)(2,1)S(1)}, bf16[64,640]{1,0:T(8,128)(2,1)S(1)}, bf16[64,640]{1,0:T(8,128)(2,1)S(1)}) custom-call(bf16[2,512,640]{2,1,0:T(8,128)(2,1)S(1)} %shard_map.39.own, bf16[2,512,640]{2,1,0:T(8,128)(2,1)S(1)} %collective-permute-done.7.other, ...), custom_call_target="tpu_custom_call" | custom-call | tf_op jit(solution)/shard_map/pallas_call | solution.py:147
  54.8 1.6 %collective-permute-start.16 = (bf16[64,640]{1,0:T(8,128)(2,1)S(1)}, bf16[64,640]{1,0:T(8,128)(2,1)S(1)}, u32[]{:S(2)}, u32[]{:S(2)}) collective-permute-start(bf16[64,640]{1,0:T(8,128)(2,1)S(1)} %get-tuple-element.64), channel_id=1, source_target_pairs={{0,2},{2,0},{4,6},{6,4},{8,10},{10,8},{12,14},{14,12},{1,3},{3,1},... | collective-permute-start | bytes 245768 | tf_op jit(solution)/shard_map/ppermute | solution.py:100
  56.4 1.2 %shard_map.42 = (bf16[64,640]{1,0:T(8,128)(2,1)S(1)}, bf16[64,640]{1,0:T(8,128)(2,1)S(1)}) custom-call(bf16[2,512,640]{2,1,0:T(8,128)(2,1)S(1)} %shard_map.39.own, bf16[2,512,640]{2,1,0:T(8,128)(2,1)S(1)} %collective-permute-done.7.other, bf16[64,640]{1,0:T(8,128)(2,1)S(1)} %collective-permute-done.8.refs_0_, bf16[64,640]{1,0:T(8,128)(2,1)S(1)} %collective-permute-done.9.refs_1_), custom_call_target="tpu_custom_call" | custom-call | tf_op jit(solution)/shard_map/pallas_call | solution.py:147
  57.6 1.7 %collective-permute-start.11 = (bf16[64,640]{1,0:T(8,128)(2,1)S(1)}, bf16[64,640]{1,0:T(8,128)(2,1)S(1)}, u32[]{:S(2)}, u32[]{:S(2)}) collective-permute-start(bf16[64,640]{1,0:T(8,128)(2,1)S(1)} %get-tuple-element.58), channel_id=1, source_target_pairs={{0,14},{2,12},{4,10},{6,8},{8,6},{10,4},{12,2},{14,0},{1,15},{3,13... | collective-permute-start | bytes 245768 | tf_op jit(solution)/shard_map/ppermute | solution.py:100
  59.3 2.1 %collective-permute-start.10 = (bf16[64,640]{1,0:T(8,128)(2,1)S(1)}, bf16[64,640]{1,0:T(8,128)(2,1)S(1)}, u32[]{:S(2)}, u32[]{:S(2)}) collective-permute-start(bf16[64,640]{1,0:T(8,128)(2,1)S(1)} %get-tuple-element.57), channel_id=1, source_target_pairs={{0,12},{2,14},{4,8},{6,10},{8,4},{10,6},{12,0},{14,2},{1,13},{3,15... | collective-permute-start | bytes 245768 | tf_op jit(solution)/shard_map/ppermute | solution.py:100
  61.4 3.0 %collective-permute-start.13 = (bf16[64,640]{1,0:T(8,128)(2,1)S(1)}, bf16[64,640]{1,0:T(8,128)(2,1)S(1)}, u32[]{:S(2)}, u32[]{:S(2)}) collective-permute-start(bf16[64,640]{1,0:T(8,128)(2,1)S(1)} %get-tuple-element.60), channel_id=1, source_target_pairs={{0,6},{2,4},{4,2},{6,0},{8,14},{10,12},{12,10},{14,8},{1,7},{3,5},... | collective-permute-start | bytes 245768 | tf_op jit(solution)/shard_map/ppermute | solution.py:100
  64.4 0.8 %shard_map.43.refs_4_ = bf16[64,5120]{1,0:T(8,128)(2,1)} custom-call(s32[1]{0:T(128)} %bitcast.chip_ref, bf16[64,640]{1,0:T(8,128)(2,1)S(1)} %get-tuple-element.54.refs_0_, bf16[64,640]{1,0:T(8,128)(2,1)S(1)} %collective-permute-done.12.refs_1_, bf16[64,640]{1,0:T(8,128)(2,1)S(1)} %collective-permute-done.14.refs_2_, ...), custom_call_target="tpu_custom_call" | custom-call | tf_op jit(solution)/shard_map/pallas_call | solution.py:161
  65.2 0.5 collective-permute-done.11.refs_1_
  66.0 1.3 %collective-permute-done.15.refs_3_ = bf16[64,640]{1,0:T(8,128)(2,1)S(1)} collective-permute-done((bf16[64,640]{1,0:T(8,128)(2,1)S(1)}, bf16[64,640]{1,0:T(8,128)(2,1)S(1)}, u32[]{:S(2)}, u32[]{:S(2)}) %collective-permute-start.15) | collective-permute-done | bytes 81952 | tf_op jit(solution)/shard_map/ppermute | solution.py:100
  67.3 1.8 %collective-permute-done.13.refs_2_ = bf16[64,640]{1,0:T(8,128)(2,1)S(1)} collective-permute-done((bf16[64,640]{1,0:T(8,128)(2,1)S(1)}, bf16[64,640]{1,0:T(8,128)(2,1)S(1)}, u32[]{:S(2)}, u32[]{:S(2)}) %collective-permute-start.13) | collective-permute-done | bytes 81952 | tf_op jit(solution)/shard_map/ppermute | solution.py:100
  69.1 0.8 %shard_map.44 = bf16[64,5120]{1,0:T(8,128)(2,1)} custom-call(s32[1]{0:T(128)} %bitcast.chip_ref, bf16[64,640]{1,0:T(8,128)(2,1)S(1)} %collective-permute-done.10.refs_0_, bf16[64,640]{1,0:T(8,128)(2,1)S(1)} %collective-permute-done.11.refs_1_, bf16[64,640]{1,0:T(8,128)(2,1)S(1)} %collective-permute-done.13.refs_2_, ...), custom_call_target="tpu_custom_call", output_to_operand_aliasing={{}: (5, {})} | custom-call | tf_op jit(solution)/shard_map/pallas_call | solution.py:161
  (18 shorter events, 1.3 us)
Async XLA Ops:
  1.0 12.2 %collective-permute-start.1 = (bf16[128,640]{1,0:T(8,128)(2,1)S(1)}, bf16[128,640]{1,0:T(8,128)(2,1)S(1)}, u32[]{:S(2)}, u32[]{:S(2)}) collective-permute-start(bf16[128,640]{1,0:T(8,128)(2,1)S(1)} %get-tuple-element.36), channel_id=1, source_target_pairs={{0,14},{2,12},{4,10},{6,8},{8,6},{10,4},{12,2},{14,0},{1,15},{3,13... | collective-permute-start | bytes 491528 | tf_op jit(solution)/shard_map/ppermute | solution.py:100
  7.1 8.9 %collective-permute-start = (bf16[128,640]{1,0:T(8,128)(2,1)S(1)}, bf16[128,640]{1,0:T(8,128)(2,1)S(1)}, u32[]{:S(2)}, u32[]{:S(2)}) collective-permute-start(bf16[128,640]{1,0:T(8,128)(2,1)S(1)} %get-tuple-element.35), channel_id=1, source_target_pairs={{0,12},{2,14},{4,8},{6,10},{8,4},{10,6},{12,0},{14,2},{1,13},{3,15... | collective-permute-start | bytes 491528 | tf_op jit(solution)/shard_map/ppermute | solution.py:100
  9.0 19.7 %collective-permute-start.2 = (bf16[192,640]{1,0:T(8,128)(2,1)S(1)}, bf16[192,640]{1,0:T(8,128)(2,1)S(1)}, u32[]{:S(2)}, u32[]{:S(2)}) collective-permute-start(bf16[192,640]{1,0:T(8,128)(2,1)S(1)} %get-tuple-element.40), channel_id=1, source_target_pairs={{0,4},{2,6},{4,0},{6,2},{8,12},{10,14},{12,8},{14,10},{1,5},{3,7},... | collective-permute-start | bytes 737288 | tf_op jit(solution)/shard_map/ppermute | solution.py:100
  9.1 28.6 %collective-permute-start.3 = (bf16[192,640]{1,0:T(8,128)(2,1)S(1)}, bf16[192,640]{1,0:T(8,128)(2,1)S(1)}, u32[]{:S(2)}, u32[]{:S(2)}) collective-permute-start(bf16[192,640]{1,0:T(8,128)(2,1)S(1)} %get-tuple-element.41), channel_id=1, source_target_pairs={{0,8},{2,10},{4,12},{6,14},{8,0},{10,2},{12,4},{14,6},{1,9},{3,11}... | collective-permute-start | bytes 737288 | tf_op jit(solution)/shard_map/ppermute | solution.py:100
  13.2 24.5 %collective-permute-start.4 = (bf16[192,640]{1,0:T(8,128)(2,1)S(1)}, bf16[192,640]{1,0:T(8,128)(2,1)S(1)}, u32[]{:S(2)}, u32[]{:S(2)}) collective-permute-start(bf16[192,640]{1,0:T(8,128)(2,1)S(1)} %get-tuple-element.42), channel_id=1, source_target_pairs={{0,6},{2,4},{4,2},{6,0},{8,14},{10,12},{12,10},{14,8},{1,7},{3,5},... | collective-permute-start | bytes 737288 | tf_op jit(solution)/shard_map/ppermute | solution.py:100
  13.2 24.5 %collective-permute-start.5 = (bf16[192,640]{1,0:T(8,128)(2,1)S(1)}, bf16[192,640]{1,0:T(8,128)(2,1)S(1)}, u32[]{:S(2)}, u32[]{:S(2)}) collective-permute-start(bf16[192,640]{1,0:T(8,128)(2,1)S(1)} %get-tuple-element.43), channel_id=1, source_target_pairs={{0,2},{2,0},{4,6},{6,4},{8,10},{10,8},{12,14},{14,12},{1,3},{3,1},... | collective-permute-start | bytes 737288 | tf_op jit(solution)/shard_map/ppermute | solution.py:100
  16.1 25.9 %collective-permute-start.6 = (bf16[192,640]{1,0:T(8,128)(2,1)S(1)}, bf16[192,640]{1,0:T(8,128)(2,1)S(1)}, u32[]{:S(2)}, u32[]{:S(2)}) collective-permute-start(bf16[192,640]{1,0:T(8,128)(2,1)S(1)} %get-tuple-element.44), channel_id=1, source_target_pairs={{0,10},{2,8},{4,14},{6,12},{8,2},{10,0},{12,6},{14,4},{1,11},{3,9}... | collective-permute-start | bytes 737288 | tf_op jit(solution)/shard_map/ppermute | solution.py:100
  42.1 3.1 %collective-permute-start.7 = (bf16[2,512,640]{2,1,0:T(8,128)(2,1)S(1)}, bf16[2,512,640]{2,1,0:T(8,128)(2,1)S(1)}, u32[]{:S(2)}, u32[]{:S(2)}) collective-permute-start(bf16[2,512,640]{2,1,0:T(8,128)(2,1)S(1)} %shard_map.39.own), channel_id=1, source_target_pairs={{0,1},{1,0},{2,3},{3,2},{4,5},{5,4},{6,7},{7,6},{8,9},{9,8},{10,11... | collective-permute-start | bytes 3932168 | tf_op jit(solution)/shard_map/ppermute | solution.py:137
  42.2 14.2 %collective-permute-start.8 = (bf16[64,640]{1,0:T(8,128)(2,1)S(1)}, bf16[64,640]{1,0:T(8,128)(2,1)S(1)}, u32[]{:S(2)}, u32[]{:S(2)}) collective-permute-start(bf16[64,640]{1,0:T(8,128)(2,1)S(1)} %get-tuple-element.46), channel_id=1, source_target_pairs={{0,12},{2,14},{4,8},{6,10},{8,4},{10,6},{12,0},{14,2},{1,13},{3,15... | collective-permute-start | bytes 245768 | tf_op jit(solution)/shard_map/ppermute | solution.py:100
  46.4 10.0 %collective-permute-start.9 = (bf16[64,640]{1,0:T(8,128)(2,1)S(1)}, bf16[64,640]{1,0:T(8,128)(2,1)S(1)}, u32[]{:S(2)}, u32[]{:S(2)}) collective-permute-start(bf16[64,640]{1,0:T(8,128)(2,1)S(1)} %get-tuple-element.49), channel_id=1, source_target_pairs={{0,14},{2,12},{4,10},{6,8},{8,6},{10,4},{12,2},{14,0},{1,15},{3,13... | collective-permute-start | bytes 245768 | tf_op jit(solution)/shard_map/ppermute | solution.py:100
  49.9 11.5 %collective-permute-start.14 = (bf16[64,640]{1,0:T(8,128)(2,1)S(1)}, bf16[64,640]{1,0:T(8,128)(2,1)S(1)}, u32[]{:S(2)}, u32[]{:S(2)}) collective-permute-start(bf16[64,640]{1,0:T(8,128)(2,1)S(1)} %get-tuple-element.62), channel_id=1, source_target_pairs={{0,10},{2,8},{4,14},{6,12},{8,2},{10,0},{12,6},{14,4},{1,11},{3,9}... | collective-permute-start | bytes 245768 | tf_op jit(solution)/shard_map/ppermute | solution.py:100
  49.9 11.5 %collective-permute-start.12 = (bf16[64,640]{1,0:T(8,128)(2,1)S(1)}, bf16[64,640]{1,0:T(8,128)(2,1)S(1)}, u32[]{:S(2)}, u32[]{:S(2)}) collective-permute-start(bf16[64,640]{1,0:T(8,128)(2,1)S(1)} %get-tuple-element.48), channel_id=1, source_target_pairs={{0,8},{2,10},{4,12},{6,14},{8,0},{10,2},{12,4},{14,6},{1,9},{3,11}... | collective-permute-start | bytes 245768 | tf_op jit(solution)/shard_map/ppermute | solution.py:100
  54.8 9.6 %collective-permute-start.16 = (bf16[64,640]{1,0:T(8,128)(2,1)S(1)}, bf16[64,640]{1,0:T(8,128)(2,1)S(1)}, u32[]{:S(2)}, u32[]{:S(2)}) collective-permute-start(bf16[64,640]{1,0:T(8,128)(2,1)S(1)} %get-tuple-element.64), channel_id=1, source_target_pairs={{0,2},{2,0},{4,6},{6,4},{8,10},{10,8},{12,14},{14,12},{1,3},{3,1},... | collective-permute-start | bytes 245768 | tf_op jit(solution)/shard_map/ppermute | solution.py:100
  57.6 8.1 %collective-permute-start.11 = (bf16[64,640]{1,0:T(8,128)(2,1)S(1)}, bf16[64,640]{1,0:T(8,128)(2,1)S(1)}, u32[]{:S(2)}, u32[]{:S(2)}) collective-permute-start(bf16[64,640]{1,0:T(8,128)(2,1)S(1)} %get-tuple-element.58), channel_id=1, source_target_pairs={{0,14},{2,12},{4,10},{6,8},{8,6},{10,4},{12,2},{14,0},{1,15},{3,13... | collective-permute-start | bytes 245768 | tf_op jit(solution)/shard_map/ppermute | solution.py:100
  59.3 6.7 %collective-permute-start.10 = (bf16[64,640]{1,0:T(8,128)(2,1)S(1)}, bf16[64,640]{1,0:T(8,128)(2,1)S(1)}, u32[]{:S(2)}, u32[]{:S(2)}) collective-permute-start(bf16[64,640]{1,0:T(8,128)(2,1)S(1)} %get-tuple-element.57), channel_id=1, source_target_pairs={{0,12},{2,14},{4,8},{6,10},{8,4},{10,6},{12,0},{14,2},{1,13},{3,15... | collective-permute-start | bytes 245768 | tf_op jit(solution)/shard_map/ppermute | solution.py:100
  61.4 5.9 %collective-permute-start.15 = (bf16[64,640]{1,0:T(8,128)(2,1)S(1)}, bf16[64,640]{1,0:T(8,128)(2,1)S(1)}, u32[]{:S(2)}, u32[]{:S(2)}) collective-permute-start(bf16[64,640]{1,0:T(8,128)(2,1)S(1)} %get-tuple-element.63), channel_id=1, source_target_pairs={{0,4},{2,6},{4,0},{6,2},{8,12},{10,14},{12,8},{14,10},{1,5},{3,7},... | collective-permute-start | bytes 245768 | tf_op jit(solution)/shard_map/ppermute | solution.py:100
  61.4 7.7 %collective-permute-start.13 = (bf16[64,640]{1,0:T(8,128)(2,1)S(1)}, bf16[64,640]{1,0:T(8,128)(2,1)S(1)}, u32[]{:S(2)}, u32[]{:S(2)}) collective-permute-start(bf16[64,640]{1,0:T(8,128)(2,1)S(1)} %get-tuple-element.60), channel_id=1, source_target_pairs={{0,6},{2,4},{4,2},{6,0},{8,14},{10,12},{12,10},{14,8},{1,7},{3,5},... | collective-permute-start | bytes 245768 | tf_op jit(solution)/shard_map/ppermute | solution.py:100

commit v7 on v5

--- a/solution.py
+++ b/solution.py
@@ -165,12 +165,12 @@
         return dict(zip(dzs, outs))
 
     outs = attend((2,))
-    outs |= attend((1, 0), outs[2])
+    outs |= attend((0, 1), outs[2])
     outs |= attend((LAST,), outs[0])
-    back = {(dz, 0): across(outs[dz], dz, 0) for dz in (2, 1, 0, LAST)}
+    back = {(dz, 0): across(outs[dz], dz, 0) for dz in (2, 0, 1, LAST)}
     back[2, 1] = swap(after(back[2, 0], outs[LAST])[rows:])
-    back |= {(dz, 1): swap(after(back[dz, 0], back[2, 1], back[LAST, 0])[rows:]) for dz in (1, 0)}
-    back[LAST, 1] = swap(back[LAST, 0][rows:])
+    back |= {(dz, 1): swap(after(back[dz, 0], back[2, 1])[rows:]) for dz in (0, 1)}
+    back[LAST, 1] = swap(after(back[LAST, 0], back[2, 1])[rows:])
 
     def unpack(dzs, *so_far):
         order = [(dz, cross) for dz in dzs for cross in range(2)]
@@ -186,7 +186,7 @@
             cost_estimate=FREE,
         )(*at, *pieces, *so_far)
 
-    result = unpack((LAST, 1, 0), unpack((2,)))
+    result = unpack((LAST, 0, 1, 2))
     return result.reshape(layers, tok_rows, width)
 
 

time: 70 us -> 68.5 us (0.979)
  waiting for transfers between devices: 29.1 us -> 27.4 us
    ppermute x13, waiting for transfers between devices: 27.9 us -> 26.4 us  [across(): return lax.ppermute(array, ('chip', 'core'), pairs)]
    pallas_call x2 -> x1, Pallas kernels: 1.5 us -> 0.89 us  [unpack(): pl.pallas_call(functools.partial(unpack_body, gw, order), in_specs=[SMEM,...]
  transfers between devices with their start and end apart: 19 -> 19, of which waited for: 10 -> 9; matrix products, arithmetic and copies ran while one was open for 0% -> 0% of each run, Pallas kernels for 9% -> 9%
where the time goes in v7:
time: 68.5 us; the launch traced here: 67.7 us
  starting transfers between devices  32 us (47%)
  waiting for transfers between devices  27.4 us (40%)
  Pallas kernels  8.06 us (12%)
    ppermute x13, starting transfers between devices, across(): return lax.ppermute(array, ('chip', 'core'), pairs)  29.9 us
    ppermute x13, waiting for transfers between devices, across(): return lax.ppermute(array, ('chip', 'core'), pairs)  26.4 us
    pallas_call x3, Pallas kernels, attend(): call(body, 2 + count, [shape(2 * rows, gw)] * len(dzs))(own, other, *pieces)  4.33 us
    pallas_call x2, Pallas kernels, pack(): pl.pallas_call(functools.partial(pack_body, rows, gw, layout), in_specs=[...  2.73 us
    ppermute x6, starting transfers between devices, swap(): return lax.ppermute(array, 'core', [(0, 1), (1, 0)])  2.09 us
  transfers between devices with their start and end apart: 19, of which 9 were waited for; matrix products, arithmetic and copies ran while one was open for 0% of the time, Pallas kernels for 9%

profile of v7, /device:TPU:0, one launch (start us, length us, event | category | flops | bytes accessed | tf_op | source)
XLA Modules:
  0.0 67.7 jit_solution(8279724044251377412)
XLA Ops:
  0.0 1.2 %shard_map.37 = (bf16[128,640]{1,0:T(8,128)(2,1)S(1)}, bf16[192,640]{1,0:T(8,128)(2,1)S(1)}, bf16[128,640]{1,0:T(8,128)(2,1)S(1)}) custom-call(s32[1]{0:T(128)} %bitcast.chip_ref, s32[1]{0:T(128)} %bitcast.1.core_ref, bf16[64,5120]{1,0:T(8,128)(2,1)} %refs_0_.2, bf16[64,5120]{1,0:T(8,128)(2,1)} %refs_1_.2, bf16[64,5120]{1,0:T(8,128)(2,1)} %bitcast.4), custom_call_target="tpu_custom_call" | custom-call | tf_op jit(solution)/shard_map/pallas_call | solution.py:137
  1.2 3.1 %collective-permute-start.1 = (bf16[192,640]{1,0:T(8,128)(2,1)S(1)}, bf16[192,640]{1,0:T(8,128)(2,1)S(1)}, u32[]{:S(2)}, u32[]{:S(2)}) collective-permute-start(bf16[192,640]{1,0:T(8,128)(2,1)S(1)} %get-tuple-element.31), channel_id=1, source_target_pairs={{0,4},{1,7},{2,6},{3,5},{4,0},{5,3},{6,2},{7,1},{8,12},{9,15},{10,... | collective-permute-start | bytes 737288 | tf_op jit(solution)/shard_map/ppermute | solution.py:111
  4.3 2.5 %collective-permute-start.2 = (bf16[128,640]{1,0:T(8,128)(2,1)S(1)}, bf16[128,640]{1,0:T(8,128)(2,1)S(1)}, u32[]{:S(2)}, u32[]{:S(2)}) collective-permute-start(bf16[128,640]{1,0:T(8,128)(2,1)S(1)} %get-tuple-element.32), channel_id=1, source_target_pairs={{0,15},{1,12},{2,13},{3,14},{4,11},{5,8},{6,9},{7,10},{8,7},{9,4},... | collective-permute-start | bytes 491528 | tf_op jit(solution)/shard_map/ppermute | solution.py:111
  6.8 1.3 %collective-permute-start = (bf16[128,640]{1,0:T(8,128)(2,1)S(1)}, bf16[128,640]{1,0:T(8,128)(2,1)S(1)}, u32[]{:S(2)}, u32[]{:S(2)}) collective-permute-start(bf16[128,640]{1,0:T(8,128)(2,1)S(1)} %get-tuple-element.30), channel_id=1, source_target_pairs={{0,12},{1,15},{2,14},{3,13},{4,8},{5,11},{6,10},{7,9},{8,4},{9,7},... | collective-permute-start | bytes 491528 | tf_op jit(solution)/shard_map/ppermute | solution.py:111
  8.2 1.5 %shard_map.38 = (bf16[192,640]{1,0:T(8,128)(2,1)S(1)}, bf16[192,640]{1,0:T(8,128)(2,1)S(1)}, bf16[192,640]{1,0:T(8,128)(2,1)S(1)}, bf16[192,640]{1,0:T(8,128)(2,...) custom-call(s32[1]{0:T(128)} %bitcast.chip_ref, ...), custom_call_target="tpu_custom_call" | custom-call | tf_op jit(solution)/shard_map/pallas_call | solution.py:137
  9.7 0.8 %collective-permute-start.5 = (bf16[64,640]{1,0:T(8,128)(2,1)S(1)}, bf16[64,640]{1,0:T(8,128)(2,1)S(1)}, u32[]{:S(2)}, u32[]{:S(2)}) collective-permute-start(bf16[64,640]{1,0:T(8,128)(2,1)S(1)} %get-tuple-element.40), channel_id=1, source_target_pairs={{0,1},{1,0},{2,3},{3,2},{4,5},{5,4},{6,7},{7,6},{8,9},{9,8},{10,11... | collective-permute-start | bytes 245768 | tf_op jit(solution)/shard_map/ppermute | solution.py:114
  10.5 0.8 %collective-permute-start.3 = (bf16[192,640]{1,0:T(8,128)(2,1)S(1)}, bf16[192,640]{1,0:T(8,128)(2,1)S(1)}, u32[]{:S(2)}, u32[]{:S(2)}) collective-permute-start(bf16[192,640]{1,0:T(8,128)(2,1)S(1)} %get-tuple-element.36), channel_id=1, source_target_pairs={{0,8},{1,11},{2,10},{3,9},{4,12},{5,15},{6,14},{7,13},{8,0},{9,3},... | collective-permute-start | bytes 737288 | tf_op jit(solution)/shard_map/ppermute | solution.py:111
  11.4 2.5 %collective-permute-start.4 = (bf16[192,640]{1,0:T(8,128)(2,1)S(1)}, bf16[192,640]{1,0:T(8,128)(2,1)S(1)}, u32[]{:S(2)}, u32[]{:S(2)}) collective-permute-start(bf16[192,640]{1,0:T(8,128)(2,1)S(1)} %get-tuple-element.37), channel_id=1, source_target_pairs={{0,7},{1,4},{2,5},{3,6},{4,3},{5,0},{6,1},{7,2},{8,15},{9,12},{10,... | collective-permute-start | bytes 737288 | tf_op jit(solution)/shard_map/ppermute | solution.py:111
  13.9 3.0 %collective-permute-done.2.refs_2_ = bf16[128,640]{1,0:T(8,128)(2,1)S(1)} collective-permute-done((bf16[128,640]{1,0:T(8,128)(2,1)S(1)}, bf16[128,640]{1,0:T(8,128)(2,1)S(1)}, u32[]{:S(2)}, u32[]{:S(2)}) %collective-permute-start.2) | collective-permute-done | bytes 163872 | tf_op jit(solution)/shard_map/ppermute | solution.py:111
  16.9 9.8 %collective-permute-start.7 = (bf16[192,640]{1,0:T(8,128)(2,1)S(1)}, bf16[192,640]{1,0:T(8,128)(2,1)S(1)}, u32[]{:S(2)}, u32[]{:S(2)}) collective-permute-start(bf16[192,640]{1,0:T(8,128)(2,1)S(1)} %get-tuple-element.42), channel_id=1, source_target_pairs={{0,11},{1,8},{2,9},{3,10},{4,15},{5,12},{6,13},{7,14},{8,3},{9,0},... | collective-permute-start | bytes 737288 | tf_op jit(solution)/shard_map/ppermute | solution.py:111
  26.8 0.7 collective-permute-start.6
  27.4 10.8 %collective-permute-done.3.refs_3_.refs_0_ = bf16[192,640]{1,0:T(8,128)(2,1)S(1)} collective-permute-done((bf16[192,640]{1,0:T(8,128)(2,1)S(1)}, bf16[192,640]{1,0:T(8,128)(2,1)S(1)}, u32[]{:S(2)}, u32[]{:S(2)}) %collective-permute-start.3) | collective-permute-done | bytes 245792 | tf_op jit(solution)/shard_map/ppermute | solution.py:111
  38.3 4.9 %collective-permute-done.7.refs_6_.refs_1_ = bf16[192,640]{1,0:T(8,128)(2,1)S(1)} collective-permute-done((bf16[192,640]{1,0:T(8,128)(2,1)S(1)}, bf16[192,640]{1,0:T(8,128)(2,1)S(1)}, u32[]{:S(2)}, u32[]{:S(2)}) %collective-permute-start.7) | collective-permute-done | bytes 245792 | tf_op jit(solution)/shard_map/ppermute | solution.py:111
  43.5 3.3 %collective-permute-start.10 = (bf16[128,640]{1,0:T(8,128)(2,1)S(1)}, bf16[128,640]{1,0:T(8,128)(2,1)S(1)}, u32[]{:S(2)}, u32[]{:S(2)}) collective-permute-start(bf16[128,640]{1,0:T(8,128)(2,1)S(1)} %constant_dynamic-update-slice_fusion), channel_id=1, source_target_pairs={{0,12},{1,15},{2,14},{3,13},{4,8},{5,11},{6,10},{7,9},{8,4},{9,7},... | collective-permute-start | bytes 491528 | tf_op jit(solution)/shard_map/ppermute | solution.py:111
  46.8 1.2 %shard_map.40 = bf16[128,640]{1,0:T(8,128)(2,1)S(1)} custom-call(bf16[2,512,640]{2,1,0:T(8,128)(2,1)S(1)} %shard_map.39.own, bf16[2,512,640]{2,1,0:T(8,128)(2,1)S(1)} %collective-permute-done.9.other, bf16[192,640]{1,0:T(8,128)(2,1)S(1)} %collective-permute-done.3.refs_3_.refs_0_, bf16[192,640]{1,0:T(8,128)(2,1)S(1)} %collective-permute-done.7.refs_6_.refs_1_), custom_call_target="tpu_custom_call" | custom-call | tf_op jit(solution)/shard_map/pallas_call | solution.py:164
  48.1 2.0 %shard_map.41 = (bf16[128,640]{1,0:T(8,128)(2,1)S(1)}, bf16[128,640]{1,0:T(8,128)(2,1)S(1)}) custom-call(bf16[2,512,640]{2,1,0:T(8,128)(2,1)S(1)} %shard_map.39.own, bf16[2,512,640]{2,1,0:T(8,128)(2,1)S(1)} %collective-permute-done.9.other, bf16[192,640]{1,0:T(8,128)(2,1)S(1)} %collective-permute-done.6.refs_5_.refs_0_, ...), custom_call_target="tpu_custom_call" | custom-call | tf_op jit(solution)/shard_map/pallas_call | solution.py:164
  50.1 3.3 %collective-permute-start.17 = (bf16[128,640]{1,0:T(8,128)(2,1)S(1)}, bf16[128,640]{1,0:T(8,128)(2,1)S(1)}, u32[]{:S(2)}, u32[]{:S(2)}) collective-permute-start(bf16[128,640]{1,0:T(8,128)(2,1)S(1)} %get-tuple-element.53), channel_id=1, source_target_pairs={{0,4},{1,7},{2,6},{3,5},{4,0},{5,3},{6,2},{7,1},{8,12},{9,15},{10,... | collective-permute-start | bytes 491528 | tf_op jit(solution)/shard_map/ppermute | solution.py:111
  53.4 0.7 collective-permute-start.15
  54.0 1.2 %shard_map.42 = bf16[128,640]{1,0:T(8,128)(2,1)S(1)} custom-call(bf16[2,512,640]{2,1,0:T(8,128)(2,1)S(1)} %shard_map.39.own, bf16[2,512,640]{2,1,0:T(8,128)(2,1)S(1)} %collective-permute-done.9.other, bf16[128,640]{1,0:T(8,128)(2,1)S(1)} %collective-permute-done.10.refs_0_), custom_call_target="tpu_custom_call" | custom-call | tf_op jit(solution)/shard_map/pallas_call | solution.py:164
  55.2 1.8 %collective-permute-start.11 = (bf16[128,640]{1,0:T(8,128)(2,1)S(1)}, bf16[128,640]{1,0:T(8,128)(2,1)S(1)}, u32[]{:S(2)}, u32[]{:S(2)}) collective-permute-start(bf16[128,640]{1,0:T(8,128)(2,1)S(1)} %shard_map.42), channel_id=1, source_target_pairs={{0,12},{1,15},{2,14},{3,13},{4,8},{5,11},{6,10},{7,9},{8,4},{9,7},... | collective-permute-start | bytes 491528 | tf_op jit(solution)/shard_map/ppermute | solution.py:111
  57.0 3.1 %collective-permute-done.12.refs_6_ = bf16[128,640]{1,0:T(8,128)(2,1)S(1)} collective-permute-done((bf16[128,640]{1,0:T(8,128)(2,1)S(1)}, bf16[128,640]{1,0:T(8,128)(2,1)S(1)}, u32[]{:S(2)}, u32[]{:S(2)}) %collective-permute-start.12) | collective-permute-done | bytes 163872 | tf_op jit(solution)/shard_map/ppermute | solution.py:111
  60.2 4.6 %collective-permute-done.17.refs_4_ = bf16[128,640]{1,0:T(8,128)(2,1)S(1)} collective-permute-done((bf16[128,640]{1,0:T(8,128)(2,1)S(1)}, bf16[128,640]{1,0:T(8,128)(2,1)S(1)}, u32[]{:S(2)}, u32[]{:S(2)}) %collective-permute-start.17) | collective-permute-done | bytes 163872 | tf_op jit(solution)/shard_map/ppermute | solution.py:111
  64.8 0.5 collective-permute-start.18
  66.8 0.9 %shard_map.43 = bf16[64,5120]{1,0:T(8,128)(2,1)} custom-call(s32[1]{0:T(128)} %bitcast.chip_ref, s32[1]{0:T(128)} %bitcast.1.core_ref, bf16[128,640]{1,0:T(8,128)(2,1)S(1)} %collective-permute-done.11.refs_0_, bf16[64,640]{1,0:T(8,128)(2,1)S(1)} %collective-permute-done.14.refs_1_, bf16[128,640]{1,0:T(8,128)(2,1)S(1)} %collective-permute-done.15.refs_2_, ...), custom_call_target="tpu_custom_call" | custom-call | tf_op jit(solution)/shard_map/pallas_call | solution.py:178
  (27 shorter events, 2.1 us)
Async XLA Ops:
  1.2 25.6 %collective-permute-start.1 = (bf16[192,640]{1,0:T(8,128)(2,1)S(1)}, bf16[192,640]{1,0:T(8,128)(2,1)S(1)}, u32[]{:S(2)}, u32[]{:S(2)}) collective-permute-start(bf16[192,640]{1,0:T(8,128)(2,1)S(1)} %get-tuple-element.31), channel_id=1, source_target_pairs={{0,4},{1,7},{2,6},{3,5},{4,0},{5,3},{6,2},{7,1},{8,12},{9,15},{10,... | collective-permute-start | bytes 737288 | tf_op jit(solution)/shard_map/ppermute | solution.py:111
  4.3 12.6 %collective-permute-start.2 = (bf16[128,640]{1,0:T(8,128)(2,1)S(1)}, bf16[128,640]{1,0:T(8,128)(2,1)S(1)}, u32[]{:S(2)}, u32[]{:S(2)}) collective-permute-start(bf16[128,640]{1,0:T(8,128)(2,1)S(1)} %get-tuple-element.32), channel_id=1, source_target_pairs={{0,15},{1,12},{2,13},{3,14},{4,11},{5,8},{6,9},{7,10},{8,7},{9,4},... | collective-permute-start | bytes 491528 | tf_op jit(solution)/shard_map/ppermute | solution.py:111
  6.8 19.9 %collective-permute-start = (bf16[128,640]{1,0:T(8,128)(2,1)S(1)}, bf16[128,640]{1,0:T(8,128)(2,1)S(1)}, u32[]{:S(2)}, u32[]{:S(2)}) collective-permute-start(bf16[128,640]{1,0:T(8,128)(2,1)S(1)} %get-tuple-element.30), channel_id=1, source_target_pairs={{0,12},{1,15},{2,14},{3,13},{4,8},{5,11},{6,10},{7,9},{8,4},{9,7},... | collective-permute-start | bytes 491528 | tf_op jit(solution)/shard_map/ppermute | solution.py:111
  9.7 1.7 %collective-permute-start.5 = (bf16[64,640]{1,0:T(8,128)(2,1)S(1)}, bf16[64,640]{1,0:T(8,128)(2,1)S(1)}, u32[]{:S(2)}, u32[]{:S(2)}) collective-permute-start(bf16[64,640]{1,0:T(8,128)(2,1)S(1)} %get-tuple-element.40), channel_id=1, source_target_pairs={{0,1},{1,0},{2,3},{3,2},{4,5},{5,4},{6,7},{7,6},{8,9},{9,8},{10,11... | collective-permute-start | bytes 245768 | tf_op jit(solution)/shard_map/ppermute | solution.py:114
  10.5 27.7 %collective-permute-start.3 = (bf16[192,640]{1,0:T(8,128)(2,1)S(1)}, bf16[192,640]{1,0:T(8,128)(2,1)S(1)}, u32[]{:S(2)}, u32[]{:S(2)}) collective-permute-start(bf16[192,640]{1,0:T(8,128)(2,1)S(1)} %get-tuple-element.36), channel_id=1, source_target_pairs={{0,8},{1,11},{2,10},{3,9},{4,12},{5,15},{6,14},{7,13},{8,0},{9,3},... | collective-permute-start | bytes 737288 | tf_op jit(solution)/shard_map/ppermute | solution.py:111
  11.4 26.8 %collective-permute-start.4 = (bf16[192,640]{1,0:T(8,128)(2,1)S(1)}, bf16[192,640]{1,0:T(8,128)(2,1)S(1)}, u32[]{:S(2)}, u32[]{:S(2)}) collective-permute-start(bf16[192,640]{1,0:T(8,128)(2,1)S(1)} %get-tuple-element.37), channel_id=1, source_target_pairs={{0,7},{1,4},{2,5},{3,6},{4,3},{5,0},{6,1},{7,2},{8,15},{9,12},{10,... | collective-permute-start | bytes 737288 | tf_op jit(solution)/shard_map/ppermute | solution.py:111
  16.9 26.3 %collective-permute-start.7 = (bf16[192,640]{1,0:T(8,128)(2,1)S(1)}, bf16[192,640]{1,0:T(8,128)(2,1)S(1)}, u32[]{:S(2)}, u32[]{:S(2)}) collective-permute-start(bf16[192,640]{1,0:T(8,128)(2,1)S(1)} %get-tuple-element.42), channel_id=1, source_target_pairs={{0,11},{1,8},{2,9},{3,10},{4,15},{5,12},{6,13},{7,14},{8,3},{9,0},... | collective-permute-start | bytes 737288 | tf_op jit(solution)/shard_map/ppermute | solution.py:111
  26.8 16.4 %collective-permute-start.8 = (bf16[192,640]{1,0:T(8,128)(2,1)S(1)}, bf16[192,640]{1,0:T(8,128)(2,1)S(1)}, u32[]{:S(2)}, u32[]{:S(2)}) collective-permute-start(bf16[192,640]{1,0:T(8,128)(2,1)S(1)} %get-tuple-element.43), channel_id=1, source_target_pairs={{0,3},{1,0},{2,1},{3,2},{4,7},{5,4},{6,5},{7,6},{8,11},{9,8},{10,9... | collective-permute-start | bytes 737288 | tf_op jit(solution)/shard_map/ppermute | solution.py:111
  26.8 16.4 %collective-permute-start.6 = (bf16[192,640]{1,0:T(8,128)(2,1)S(1)}, bf16[192,640]{1,0:T(8,128)(2,1)S(1)}, u32[]{:S(2)}, u32[]{:S(2)}) collective-permute-start(bf16[192,640]{1,0:T(8,128)(2,1)S(1)} %get-tuple-element.41), channel_id=1, source_target_pairs={{0,0},{1,3},{2,2},{3,1},{4,4},{5,7},{6,6},{7,5},{8,8},{9,11},{10,1... | collective-permute-start | bytes 737288 | tf_op jit(solution)/shard_map/ppermute | solution.py:111
  43.3 3.6 %collective-permute-start.9 = (bf16[2,512,640]{2,1,0:T(8,128)(2,1)S(1)}, bf16[2,512,640]{2,1,0:T(8,128)(2,1)S(1)}, u32[]{:S(2)}, u32[]{:S(2)}) collective-permute-start(bf16[2,512,640]{2,1,0:T(8,128)(2,1)S(1)} %shard_map.39.own), channel_id=1, source_target_pairs={{0,1},{1,0},{2,3},{3,2},{4,5},{5,4},{6,7},{7,6},{8,9},{9,8},{10,11... | collective-permute-start | bytes 3932168 | tf_op jit(solution)/shard_map/ppermute | solution.py:114
  43.5 10.5 %collective-permute-start.10 = (bf16[128,640]{1,0:T(8,128)(2,1)S(1)}, bf16[128,640]{1,0:T(8,128)(2,1)S(1)}, u32[]{:S(2)}, u32[]{:S(2)}) collective-permute-start(bf16[128,640]{1,0:T(8,128)(2,1)S(1)} %constant_dynamic-update-slice_fusion), channel_id=1, source_target_pairs={{0,12},{1,15},{2,14},{3,13},{4,8},{5,11},{6,10},{7,9},{8,4},{9,7},... | collective-permute-start | bytes 491528 | tf_op jit(solution)/shard_map/ppermute | solution.py:111
  48.0 12.1 %collective-permute-start.12 = (bf16[128,640]{1,0:T(8,128)(2,1)S(1)}, bf16[128,640]{1,0:T(8,128)(2,1)S(1)}, u32[]{:S(2)}, u32[]{:S(2)}) collective-permute-start(bf16[128,640]{1,0:T(8,128)(2,1)S(1)} %shard_map.40), channel_id=1, source_target_pairs={{0,8},{1,11},{2,10},{3,9},{4,12},{5,15},{6,14},{7,13},{8,0},{9,3},... | collective-permute-start | bytes 491528 | tf_op jit(solution)/shard_map/ppermute | solution.py:111
  50.1 14.7 %collective-permute-start.17 = (bf16[128,640]{1,0:T(8,128)(2,1)S(1)}, bf16[128,640]{1,0:T(8,128)(2,1)S(1)}, u32[]{:S(2)}, u32[]{:S(2)}) collective-permute-start(bf16[128,640]{1,0:T(8,128)(2,1)S(1)} %get-tuple-element.53), channel_id=1, source_target_pairs={{0,4},{1,7},{2,6},{3,5},{4,0},{5,3},{6,2},{7,1},{8,12},{9,15},{10,... | collective-permute-start | bytes 491528 | tf_op jit(solution)/shard_map/ppermute | solution.py:111
  53.4 11.4 %collective-permute-start.15 = (bf16[128,640]{1,0:T(8,128)(2,1)S(1)}, bf16[128,640]{1,0:T(8,128)(2,1)S(1)}, u32[]{:S(2)}, u32[]{:S(2)}) collective-permute-start(bf16[128,640]{1,0:T(8,128)(2,1)S(1)} %get-tuple-element.48), channel_id=1, source_target_pairs={{0,0},{1,3},{2,2},{3,1},{4,4},{5,7},{6,6},{7,5},{8,8},{9,11},{10,1... | collective-permute-start | bytes 491528 | tf_op jit(solution)/shard_map/ppermute | solution.py:111
  55.2 9.6 %collective-permute-start.11 = (bf16[128,640]{1,0:T(8,128)(2,1)S(1)}, bf16[128,640]{1,0:T(8,128)(2,1)S(1)}, u32[]{:S(2)}, u32[]{:S(2)}) collective-permute-start(bf16[128,640]{1,0:T(8,128)(2,1)S(1)} %shard_map.42), channel_id=1, source_target_pairs={{0,12},{1,15},{2,14},{3,13},{4,8},{5,11},{6,10},{7,9},{8,4},{9,7},... | collective-permute-start | bytes 491528 | tf_op jit(solution)/shard_map/ppermute | solution.py:111
  60.1 4.7 %collective-permute-start.13 = (bf16[64,640]{1,0:T(8,128)(2,1)S(1)}, bf16[64,640]{1,0:T(8,128)(2,1)S(1)}, u32[]{:S(2)}, u32[]{:S(2)}) collective-permute-start(bf16[64,640]{1,0:T(8,128)(2,1)S(1)} %slice.12), channel_id=1, source_target_pairs={{0,1},{1,0},{2,3},{3,2},{4,5},{5,4},{6,7},{7,6},{8,9},{9,8},{10,11... | collective-permute-start | bytes 245768 | tf_op jit(solution)/shard_map/ppermute | solution.py:114
  64.8 1.4 %collective-permute-start.18 = (bf16[64,640]{1,0:T(8,128)(2,1)S(1)}, bf16[64,640]{1,0:T(8,128)(2,1)S(1)}, u32[]{:S(2)}, u32[]{:S(2)}) collective-permute-start(bf16[64,640]{1,0:T(8,128)(2,1)S(1)} %slice.15), channel_id=1, source_target_pairs={{0,1},{1,0},{2,3},{3,2},{4,5},{5,4},{6,7},{7,6},{8,9},{9,8},{10,11... | collective-permute-start | bytes 245768 | tf_op jit(solution)/shard_map/ppermute | solution.py:114
  65.4 1.3 %collective-permute-start.16 = (bf16[64,640]{1,0:T(8,128)(2,1)S(1)}, bf16[64,640]{1,0:T(8,128)(2,1)S(1)}, u32[]{:S(2)}, u32[]{:S(2)}) collective-permute-start(bf16[64,640]{1,0:T(8,128)(2,1)S(1)} %slice.14), channel_id=1, source_target_pairs={{0,1},{1,0},{2,3},{3,2},{4,5},{5,4},{6,7},{7,6},{8,9},{9,8},{10,11... | collective-permute-start | bytes 245768 | tf_op jit(solution)/shard_map/ppermute | solution.py:114
  65.4 1.4 %collective-permute-start.14 = (bf16[64,640]{1,0:T(8,128)(2,1)S(1)}, bf16[64,640]{1,0:T(8,128)(2,1)S(1)}, u32[]{:S(2)}, u32[]{:S(2)}) collective-permute-start(bf16[64,640]{1,0:T(8,128)(2,1)S(1)} %slice.13), channel_id=1, source_target_pairs={{0,1},{1,0},{2,3},{3,2},{4,5},{5,4},{6,7},{7,6},{8,9},{9,8},{10,11... | collective-permute-start | bytes 245768 | tf_op jit(solution)/shard_map/ppermute | solution.py:114

commit v8 on v7

--- a/solution.py
+++ b/solution.py
@@ -104,9 +104,9 @@
     assert rows_q == rows
     at = [lax.axis_index(name).reshape(1).astype(jnp.int32) for name in ("chip", "core")]
 
-    def across(array, dz, cross):
+    def across(array, dz, cross, back=False):
         senders = [(chip, core) for chip in range(chips) for core in range(2)]
-        to = [(chip ^ (2 * dz + (core ^ cross)), core ^ cross) for chip, core in senders]
+        to = [(chip ^ (2 * dz + (core if back else core ^ cross)), core ^ cross) for chip, core in senders]
         pairs = [(2 * a + b, 2 * c + d) for (a, b), (c, d) in zip(senders, to)]
         return lax.ppermute(array, ("chip", "core"), pairs)
 
@@ -167,10 +167,10 @@
     outs = attend((2,))
     outs |= attend((0, 1), outs[2])
     outs |= attend((LAST,), outs[0])
-    back = {(dz, 0): across(outs[dz], dz, 0) for dz in (2, 0, 1, LAST)}
-    back[2, 1] = swap(after(back[2, 0], outs[LAST])[rows:])
-    back |= {(dz, 1): swap(after(back[dz, 0], back[2, 1])[rows:]) for dz in (0, 1)}
-    back[LAST, 1] = swap(after(back[LAST, 0], back[2, 1])[rows:])
+    back = {(dz, 0): across(outs[dz], dz, 0) for dz in (2, 0, 1)}
+    for cross in (1, 0):
+        back[LAST, cross] = across(outs[LAST][cross * rows : (cross + 1) * rows], LAST, cross, True)
+    back |= {(dz, 1): swap(back[dz, 0][rows:]) for dz in (0, 1, 2)}
 
     def unpack(dzs, *so_far):
         order = [(dz, cross) for dz in dzs for cross in range(2)]

time: 68.5 us -> 70.6 us (1.031)
  starting transfers between devices: 32 us -> 39.7 us
  waiting for transfers between devices: 27.4 us -> 22.4 us
    ppermute x13 -> x14, waiting for transfers between devices: 26.4 us -> 21.4 us  [across(): return lax.ppermute(array, ('chip', 'core'), pairs)]
    ppermute x13 -> x14, starting transfers between devices: 29.9 us -> 34.1 us  [across(): return lax.ppermute(array, ('chip', 'core'), pairs)]
    ppermute x6 -> x5, starting transfers between devices: 2.09 us -> 5.64 us  [swap(): return lax.ppermute(array, 'core', [(0, 1), (1, 0)])]
  transfers between devices with their start and end apart: 19 -> 19, of which waited for: 9 -> 9; matrix products, arithmetic and copies ran while one was open for 0% -> 0% of each run, Pallas kernels for 9% -> 8%
where the time goes in v8:
time: 70.6 us; the launch traced here: 70.4 us
  starting transfers between devices  39.7 us (56%)
  waiting for transfers between devices  22.4 us (32%)
  Pallas kernels  8.05 us (11%)
    ppermute x14, starting transfers between devices, across(): return lax.ppermute(array, ('chip', 'core'), pairs)  34.1 us
    ppermute x14, waiting for transfers between devices, across(): return lax.ppermute(array, ('chip', 'core'), pairs)  21.4 us
    ppermute x5, starting transfers between devices, swap(): return lax.ppermute(array, 'core', [(0, 1), (1, 0)])  5.64 us
    pallas_call x3, Pallas kernels, attend(): call(body, 2 + count, [shape(2 * rows, gw)] * len(dzs))(own, other, *pieces)  4.33 us
    pallas_call x2, Pallas kernels, pack(): pl.pallas_call(functools.partial(pack_body, rows, gw, layout), in_specs=[...  2.73 us
  transfers between devices with their start and end apart: 19, of which 9 were waited for; matrix products, arithmetic and copies ran while one was open for 0% of the time, Pallas kernels for 8%

profile of v8, /device:TPU:0, one launch (start us, length us, event | category | flops | bytes accessed | tf_op | source)
XLA Modules:
  0.0 70.4 jit_solution(676584180881181574)
XLA Ops:
  0.0 1.2 %shard_map.37 = (bf16[128,640]{1,0:T(8,128)(2,1)S(1)}, bf16[192,640]{1,0:T(8,128)(2,1)S(1)}, bf16[128,640]{1,0:T(8,128)(2,1)S(1)}) custom-call(s32[1]{0:T(128)} %bitcast.chip_ref, s32[1]{0:T(128)} %bitcast.1.core_ref, bf16[64,5120]{1,0:T(8,128)(2,1)} %refs_0_.2, bf16[64,5120]{1,0:T(8,128)(2,1)} %refs_1_.2, bf16[64,5120]{1,0:T(8,128)(2,1)} %bitcast.4), custom_call_target="tpu_custom_call" | custom-call | tf_op jit(solution)/shard_map/pallas_call | solution.py:137
  1.2 3.1 %collective-permute-start.1 = (bf16[192,640]{1,0:T(8,128)(2,1)S(1)}, bf16[192,640]{1,0:T(8,128)(2,1)S(1)}, u32[]{:S(2)}, u32[]{:S(2)}) collective-permute-start(bf16[192,640]{1,0:T(8,128)(2,1)S(1)} %get-tuple-element.27), channel_id=1, source_target_pairs={{0,4},{1,7},{2,6},{3,5},{4,0},{5,3},{6,2},{7,1},{8,12},{9,15},{10,... | collective-permute-start | bytes 737288 | tf_op jit(solution)/shard_map/ppermute | solution.py:111
  4.3 2.5 %collective-permute-start.2 = (bf16[128,640]{1,0:T(8,128)(2,1)S(1)}, bf16[128,640]{1,0:T(8,128)(2,1)S(1)}, u32[]{:S(2)}, u32[]{:S(2)}) collective-permute-start(bf16[128,640]{1,0:T(8,128)(2,1)S(1)} %get-tuple-element.28), channel_id=1, source_target_pairs={{0,15},{1,12},{2,13},{3,14},{4,11},{5,8},{6,9},{7,10},{8,7},{9,4},... | collective-permute-start | bytes 491528 | tf_op jit(solution)/shard_map/ppermute | solution.py:111
  6.8 1.3 %collective-permute-start = (bf16[128,640]{1,0:T(8,128)(2,1)S(1)}, bf16[128,640]{1,0:T(8,128)(2,1)S(1)}, u32[]{:S(2)}, u32[]{:S(2)}) collective-permute-start(bf16[128,640]{1,0:T(8,128)(2,1)S(1)} %get-tuple-element.26), channel_id=1, source_target_pairs={{0,12},{1,15},{2,14},{3,13},{4,8},{5,11},{6,10},{7,9},{8,4},{9,7},... | collective-permute-start | bytes 491528 | tf_op jit(solution)/shard_map/ppermute | solution.py:111
  8.2 1.5 %shard_map.38 = (bf16[192,640]{1,0:T(8,128)(2,1)S(1)}, bf16[192,640]{1,0:T(8,128)(2,1)S(1)}, bf16[192,640]{1,0:T(8,128)(2,1)S(1)}, bf16[192,640]{1,0:T(8,128)(2,...) custom-call(s32[1]{0:T(128)} %bitcast.chip_ref, ...), custom_call_target="tpu_custom_call" | custom-call | tf_op jit(solution)/shard_map/pallas_call | solution.py:137
  9.7 0.8 %collective-permute-start.5 = (bf16[64,640]{1,0:T(8,128)(2,1)S(1)}, bf16[64,640]{1,0:T(8,128)(2,1)S(1)}, u32[]{:S(2)}, u32[]{:S(2)}) collective-permute-start(bf16[64,640]{1,0:T(8,128)(2,1)S(1)} %get-tuple-element.36), channel_id=1, source_target_pairs={{0,1},{1,0},{2,3},{3,2},{4,5},{5,4},{6,7},{7,6},{8,9},{9,8},{10,11... | collective-permute-start | bytes 245768 | tf_op jit(solution)/shard_map/ppermute | solution.py:114
  10.5 0.8 %collective-permute-start.3 = (bf16[192,640]{1,0:T(8,128)(2,1)S(1)}, bf16[192,640]{1,0:T(8,128)(2,1)S(1)}, u32[]{:S(2)}, u32[]{:S(2)}) collective-permute-start(bf16[192,640]{1,0:T(8,128)(2,1)S(1)} %get-tuple-element.32), channel_id=1, source_target_pairs={{0,8},{1,11},{2,10},{3,9},{4,12},{5,15},{6,14},{7,13},{8,0},{9,3},... | collective-permute-start | bytes 737288 | tf_op jit(solution)/shard_map/ppermute | solution.py:111
  11.4 2.5 %collective-permute-start.4 = (bf16[192,640]{1,0:T(8,128)(2,1)S(1)}, bf16[192,640]{1,0:T(8,128)(2,1)S(1)}, u32[]{:S(2)}, u32[]{:S(2)}) collective-permute-start(bf16[192,640]{1,0:T(8,128)(2,1)S(1)} %get-tuple-element.33), channel_id=1, source_target_pairs={{0,7},{1,4},{2,5},{3,6},{4,3},{5,0},{6,1},{7,2},{8,15},{9,12},{10,... | collective-permute-start | bytes 737288 | tf_op jit(solution)/shard_map/ppermute | solution.py:111
  13.9 3.0 %collective-permute-done.2.refs_2_ = bf16[128,640]{1,0:T(8,128)(2,1)S(1)} collective-permute-done((bf16[128,640]{1,0:T(8,128)(2,1)S(1)}, bf16[128,640]{1,0:T(8,128)(2,1)S(1)}, u32[]{:S(2)}, u32[]{:S(2)}) %collective-permute-start.2) | collective-permute-done | bytes 163872 | tf_op jit(solution)/shard_map/ppermute | solution.py:111
  16.9 9.8 %collective-permute-start.7 = (bf16[192,640]{1,0:T(8,128)(2,1)S(1)}, bf16[192,640]{1,0:T(8,128)(2,1)S(1)}, u32[]{:S(2)}, u32[]{:S(2)}) collective-permute-start(bf16[192,640]{1,0:T(8,128)(2,1)S(1)} %get-tuple-element.38), channel_id=1, source_target_pairs={{0,11},{1,8},{2,9},{3,10},{4,15},{5,12},{6,13},{7,14},{8,3},{9,0},... | collective-permute-start | bytes 737288 | tf_op jit(solution)/shard_map/ppermute | solution.py:111
  26.8 0.7 collective-permute-start.6
  27.4 10.8 %collective-permute-done.3.refs_3_.refs_0_ = bf16[192,640]{1,0:T(8,128)(2,1)S(1)} collective-permute-done((bf16[192,640]{1,0:T(8,128)(2,1)S(1)}, bf16[192,640]{1,0:T(8,128)(2,1)S(1)}, u32[]{:S(2)}, u32[]{:S(2)}) %collective-permute-start.3) | collective-permute-done | bytes 245792 | tf_op jit(solution)/shard_map/ppermute | solution.py:111
  38.3 4.9 %collective-permute-done.7.refs_6_.refs_1_ = bf16[192,640]{1,0:T(8,128)(2,1)S(1)} collective-permute-done((bf16[192,640]{1,0:T(8,128)(2,1)S(1)}, bf16[192,640]{1,0:T(8,128)(2,1)S(1)}, u32[]{:S(2)}, u32[]{:S(2)}) %collective-permute-start.7) | collective-permute-done | bytes 245792 | tf_op jit(solution)/shard_map/ppermute | solution.py:111
  43.5 3.3 %collective-permute-start.10 = (bf16[128,640]{1,0:T(8,128)(2,1)S(1)}, bf16[128,640]{1,0:T(8,128)(2,1)S(1)}, u32[]{:S(2)}, u32[]{:S(2)}) collective-permute-start(bf16[128,640]{1,0:T(8,128)(2,1)S(1)} %constant_dynamic-update-slice_fusion), channel_id=1, source_target_pairs={{0,12},{1,15},{2,14},{3,13},{4,8},{5,11},{6,10},{7,9},{8,4},{9,7},... | collective-permute-start | bytes 491528 | tf_op jit(solution)/shard_map/ppermute | solution.py:111
  46.8 1.2 %shard_map.40 = bf16[128,640]{1,0:T(8,128)(2,1)S(1)} custom-call(bf16[2,512,640]{2,1,0:T(8,128)(2,1)S(1)} %shard_map.39.own, bf16[2,512,640]{2,1,0:T(8,128)(2,1)S(1)} %collective-permute-done.9.other, bf16[192,640]{1,0:T(8,128)(2,1)S(1)} %collective-permute-done.3.refs_3_.refs_0_, bf16[192,640]{1,0:T(8,128)(2,1)S(1)} %collective-permute-done.7.refs_6_.refs_1_), custom_call_target="tpu_custom_call" | custom-call | tf_op jit(solution)/shard_map/pallas_call | solution.py:164
  48.1 2.0 %shard_map.41 = (bf16[128,640]{1,0:T(8,128)(2,1)S(1)}, bf16[128,640]{1,0:T(8,128)(2,1)S(1)}) custom-call(bf16[2,512,640]{2,1,0:T(8,128)(2,1)S(1)} %shard_map.39.own, bf16[2,512,640]{2,1,0:T(8,128)(2,1)S(1)} %collective-permute-done.9.other, bf16[192,640]{1,0:T(8,128)(2,1)S(1)} %collective-permute-done.6.refs_5_.refs_0_, ...), custom_call_target="tpu_custom_call" | custom-call | tf_op jit(solution)/shard_map/pallas_call | solution.py:164
  50.1 0.7 collective-permute-start.13
  50.8 1.7 %collective-permute-done.10.refs_0_ = bf16[128,640]{1,0:T(8,128)(2,1)S(1)} collective-permute-done((bf16[128,640]{1,0:T(8,128)(2,1)S(1)}, bf16[128,640]{1,0:T(8,128)(2,1)S(1)}, u32[]{:S(2)}, u32[]{:S(2)}) %collective-permute-start.10) | collective-permute-done | bytes 163872 | tf_op jit(solution)/shard_map/ppermute | solution.py:111
  52.5 4.6 %collective-permute-start.15 = (bf16[128,640]{1,0:T(8,128)(2,1)S(1)}, bf16[128,640]{1,0:T(8,128)(2,1)S(1)}, u32[]{:S(2)}, u32[]{:S(2)}) collective-permute-start(bf16[128,640]{1,0:T(8,128)(2,1)S(1)} %get-tuple-element.46), channel_id=1, source_target_pairs={{0,4},{1,7},{2,6},{3,5},{4,0},{5,3},{6,2},{7,1},{8,12},{9,15},{10,... | collective-permute-start | bytes 491528 | tf_op jit(solution)/shard_map/ppermute | solution.py:111
  57.1 1.2 %shard_map.42 = bf16[128,640]{1,0:T(8,128)(2,1)S(1)} custom-call(bf16[2,512,640]{2,1,0:T(8,128)(2,1)S(1)} %shard_map.39.own, bf16[2,512,640]{2,1,0:T(8,128)(2,1)S(1)} %collective-permute-done.9.other, bf16[128,640]{1,0:T(8,128)(2,1)S(1)} %collective-permute-done.10.refs_0_), custom_call_target="tpu_custom_call" | custom-call | tf_op jit(solution)/shard_map/pallas_call | solution.py:164
  58.6 4.2 %collective-permute-start.11 = (bf16[64,640]{1,0:T(8,128)(2,1)S(1)}, bf16[64,640]{1,0:T(8,128)(2,1)S(1)}, u32[]{:S(2)}, u32[]{:S(2)}) collective-permute-start(bf16[64,640]{1,0:T(8,128)(2,1)S(1)} %get-tuple-element.48), channel_id=1, source_target_pairs={{0,12},{1,15},{2,14},{3,13},{4,8},{5,11},{6,10},{7,9},{8,4},{9,7},... | collective-permute-start | bytes 245768 | tf_op jit(solution)/shard_map/ppermute | solution.py:111
  62.9 1.0 %collective-permute-done.15.refs_4_ = bf16[128,640]{1,0:T(8,128)(2,1)S(1)} collective-permute-done((bf16[128,640]{1,0:T(8,128)(2,1)S(1)}, bf16[128,640]{1,0:T(8,128)(2,1)S(1)}, u32[]{:S(2)}, u32[]{:S(2)}) %collective-permute-start.15) | collective-permute-done | bytes 163872 | tf_op jit(solution)/shard_map/ppermute | solution.py:111
  63.9 4.0 %collective-permute-start.16 = (bf16[64,640]{1,0:T(8,128)(2,1)S(1)}, bf16[64,640]{1,0:T(8,128)(2,1)S(1)}, u32[]{:S(2)}, u32[]{:S(2)}) collective-permute-start(bf16[64,640]{1,0:T(8,128)(2,1)S(1)} %slice.23), channel_id=1, source_target_pairs={{0,1},{1,0},{2,3},{3,2},{4,5},{5,4},{6,7},{7,6},{8,9},{9,8},{10,11... | collective-permute-start | bytes 245768 | tf_op jit(solution)/shard_map/ppermute | solution.py:114
  69.5 0.9 %shard_map.43 = bf16[64,5120]{1,0:T(8,128)(2,1)} custom-call(s32[1]{0:T(128)} %bitcast.chip_ref, s32[1]{0:T(128)} %bitcast.1.core_ref, bf16[64,640]{1,0:T(8,128)(2,1)S(1)} %collective-permute-done.11.refs_0_, bf16[64,640]{1,0:T(8,128)(2,1)S(1)} %collective-permute-done.12.refs_1_, bf16[128,640]{1,0:T(8,128)(2,1)S(1)} %collective-permute-done.13.refs_2_, ...), custom_call_target="tpu_custom_call" | custom-call | tf_op jit(solution)/shard_map/pallas_call | solution.py:178
  (27 shorter events, 2.5 us)
Async XLA Ops:
  1.2 25.6 %collective-permute-start.1 = (bf16[192,640]{1,0:T(8,128)(2,1)S(1)}, bf16[192,640]{1,0:T(8,128)(2,1)S(1)}, u32[]{:S(2)}, u32[]{:S(2)}) collective-permute-start(bf16[192,640]{1,0:T(8,128)(2,1)S(1)} %get-tuple-element.27), channel_id=1, source_target_pairs={{0,4},{1,7},{2,6},{3,5},{4,0},{5,3},{6,2},{7,1},{8,12},{9,15},{10,... | collective-permute-start | bytes 737288 | tf_op jit(solution)/shard_map/ppermute | solution.py:111
  4.3 12.6 %collective-permute-start.2 = (bf16[128,640]{1,0:T(8,128)(2,1)S(1)}, bf16[128,640]{1,0:T(8,128)(2,1)S(1)}, u32[]{:S(2)}, u32[]{:S(2)}) collective-permute-start(bf16[128,640]{1,0:T(8,128)(2,1)S(1)} %get-tuple-element.28), channel_id=1, source_target_pairs={{0,15},{1,12},{2,13},{3,14},{4,11},{5,8},{6,9},{7,10},{8,7},{9,4},... | collective-permute-start | bytes 491528 | tf_op jit(solution)/shard_map/ppermute | solution.py:111
  6.8 19.9 %collective-permute-start = (bf16[128,640]{1,0:T(8,128)(2,1)S(1)}, bf16[128,640]{1,0:T(8,128)(2,1)S(1)}, u32[]{:S(2)}, u32[]{:S(2)}) collective-permute-start(bf16[128,640]{1,0:T(8,128)(2,1)S(1)} %get-tuple-element.26), channel_id=1, source_target_pairs={{0,12},{1,15},{2,14},{3,13},{4,8},{5,11},{6,10},{7,9},{8,4},{9,7},... | collective-permute-start | bytes 491528 | tf_op jit(solution)/shard_map/ppermute | solution.py:111
  9.7 1.7 %collective-permute-start.5 = (bf16[64,640]{1,0:T(8,128)(2,1)S(1)}, bf16[64,640]{1,0:T(8,128)(2,1)S(1)}, u32[]{:S(2)}, u32[]{:S(2)}) collective-permute-start(bf16[64,640]{1,0:T(8,128)(2,1)S(1)} %get-tuple-element.36), channel_id=1, source_target_pairs={{0,1},{1,0},{2,3},{3,2},{4,5},{5,4},{6,7},{7,6},{8,9},{9,8},{10,11... | collective-permute-start | bytes 245768 | tf_op jit(solution)/shard_map/ppermute | solution.py:114
  10.5 27.7 %collective-permute-start.3 = (bf16[192,640]{1,0:T(8,128)(2,1)S(1)}, bf16[192,640]{1,0:T(8,128)(2,1)S(1)}, u32[]{:S(2)}, u32[]{:S(2)}) collective-permute-start(bf16[192,640]{1,0:T(8,128)(2,1)S(1)} %get-tuple-element.32), channel_id=1, source_target_pairs={{0,8},{1,11},{2,10},{3,9},{4,12},{5,15},{6,14},{7,13},{8,0},{9,3},... | collective-permute-start | bytes 737288 | tf_op jit(solution)/shard_map/ppermute | solution.py:111
  11.4 26.8 %collective-permute-start.4 = (bf16[192,640]{1,0:T(8,128)(2,1)S(1)}, bf16[192,640]{1,0:T(8,128)(2,1)S(1)}, u32[]{:S(2)}, u32[]{:S(2)}) collective-permute-start(bf16[192,640]{1,0:T(8,128)(2,1)S(1)} %get-tuple-element.33), channel_id=1, source_target_pairs={{0,7},{1,4},{2,5},{3,6},{4,3},{5,0},{6,1},{7,2},{8,15},{9,12},{10,... | collective-permute-start | bytes 737288 | tf_op jit(solution)/shard_map/ppermute | solution.py:111
  16.9 26.3 %collective-permute-start.7 = (bf16[192,640]{1,0:T(8,128)(2,1)S(1)}, bf16[192,640]{1,0:T(8,128)(2,1)S(1)}, u32[]{:S(2)}, u32[]{:S(2)}) collective-permute-start(bf16[192,640]{1,0:T(8,128)(2,1)S(1)} %get-tuple-element.38), channel_id=1, source_target_pairs={{0,11},{1,8},{2,9},{3,10},{4,15},{5,12},{6,13},{7,14},{8,3},{9,0},... | collective-permute-start | bytes 737288 | tf_op jit(solution)/shard_map/ppermute | solution.py:111
  26.8 16.4 %collective-permute-start.8 = (bf16[192,640]{1,0:T(8,128)(2,1)S(1)}, bf16[192,640]{1,0:T(8,128)(2,1)S(1)}, u32[]{:S(2)}, u32[]{:S(2)}) collective-permute-start(bf16[192,640]{1,0:T(8,128)(2,1)S(1)} %get-tuple-element.39), channel_id=1, source_target_pairs={{0,3},{1,0},{2,1},{3,2},{4,7},{5,4},{6,5},{7,6},{8,11},{9,8},{10,9... | collective-permute-start | bytes 737288 | tf_op jit(solution)/shard_map/ppermute | solution.py:111
  26.8 16.4 %collective-permute-start.6 = (bf16[192,640]{1,0:T(8,128)(2,1)S(1)}, bf16[192,640]{1,0:T(8,128)(2,1)S(1)}, u32[]{:S(2)}, u32[]{:S(2)}) collective-permute-start(bf16[192,640]{1,0:T(8,128)(2,1)S(1)} %get-tuple-element.37), channel_id=1, source_target_pairs={{0,0},{1,3},{2,2},{3,1},{4,4},{5,7},{6,6},{7,5},{8,8},{9,11},{10,1... | collective-permute-start | bytes 737288 | tf_op jit(solution)/shard_map/ppermute | solution.py:111
  43.3 3.6 %collective-permute-start.9 = (bf16[2,512,640]{2,1,0:T(8,128)(2,1)S(1)}, bf16[2,512,640]{2,1,0:T(8,128)(2,1)S(1)}, u32[]{:S(2)}, u32[]{:S(2)}) collective-permute-start(bf16[2,512,640]{2,1,0:T(8,128)(2,1)S(1)} %shard_map.39.own), channel_id=1, source_target_pairs={{0,1},{1,0},{2,3},{3,2},{4,5},{5,4},{6,7},{7,6},{8,9},{9,8},{10,11... | collective-permute-start | bytes 3932168 | tf_op jit(solution)/shard_map/ppermute | solution.py:114
  43.5 9.0 %collective-permute-start.10 = (bf16[128,640]{1,0:T(8,128)(2,1)S(1)}, bf16[128,640]{1,0:T(8,128)(2,1)S(1)}, u32[]{:S(2)}, u32[]{:S(2)}) collective-permute-start(bf16[128,640]{1,0:T(8,128)(2,1)S(1)} %constant_dynamic-update-slice_fusion), channel_id=1, source_target_pairs={{0,12},{1,15},{2,14},{3,13},{4,8},{5,11},{6,10},{7,9},{8,4},{9,7},... | collective-permute-start | bytes 491528 | tf_op jit(solution)/shard_map/ppermute | solution.py:111
  48.0 20.0 %collective-permute-start.17 = (bf16[128,640]{1,0:T(8,128)(2,1)S(1)}, bf16[128,640]{1,0:T(8,128)(2,1)S(1)}, u32[]{:S(2)}, u32[]{:S(2)}) collective-permute-start(bf16[128,640]{1,0:T(8,128)(2,1)S(1)} %shard_map.40), channel_id=1, source_target_pairs={{0,8},{1,11},{2,10},{3,9},{4,12},{5,15},{6,14},{7,13},{8,0},{9,3},... | collective-permute-start | bytes 491528 | tf_op jit(solution)/shard_map/ppermute | solution.py:111
  50.1 17.8 %collective-permute-start.13 = (bf16[128,640]{1,0:T(8,128)(2,1)S(1)}, bf16[128,640]{1,0:T(8,128)(2,1)S(1)}, u32[]{:S(2)}, u32[]{:S(2)}) collective-permute-start(bf16[128,640]{1,0:T(8,128)(2,1)S(1)} %get-tuple-element.44), channel_id=1, source_target_pairs={{0,0},{1,3},{2,2},{3,1},{4,4},{5,7},{6,6},{7,5},{8,8},{9,11},{10,1... | collective-permute-start | bytes 491528 | tf_op jit(solution)/shard_map/ppermute | solution.py:111
  52.5 11.4 %collective-permute-start.15 = (bf16[128,640]{1,0:T(8,128)(2,1)S(1)}, bf16[128,640]{1,0:T(8,128)(2,1)S(1)}, u32[]{:S(2)}, u32[]{:S(2)}) collective-permute-start(bf16[128,640]{1,0:T(8,128)(2,1)S(1)} %get-tuple-element.46), channel_id=1, source_target_pairs={{0,4},{1,7},{2,6},{3,5},{4,0},{5,3},{6,2},{7,1},{8,12},{9,15},{10,... | collective-permute-start | bytes 491528 | tf_op jit(solution)/shard_map/ppermute | solution.py:111
  58.3 10.3 %collective-permute-start.12 = (bf16[64,640]{1,0:T(8,128)(2,1)S(1)}, bf16[64,640]{1,0:T(8,128)(2,1)S(1)}, u32[]{:S(2)}, u32[]{:S(2)}) collective-permute-start(bf16[64,640]{1,0:T(8,128)(2,1)S(1)} %get-tuple-element.47), channel_id=1, source_target_pairs={{0,13},{1,14},{2,15},{3,12},{4,9},{5,10},{6,11},{7,8},{8,5},{9,6},... | collective-permute-start | bytes 245768 | tf_op jit(solution)/shard_map/ppermute | solution.py:111
  58.6 9.9 %collective-permute-start.11 = (bf16[64,640]{1,0:T(8,128)(2,1)S(1)}, bf16[64,640]{1,0:T(8,128)(2,1)S(1)}, u32[]{:S(2)}, u32[]{:S(2)}) collective-permute-start(bf16[64,640]{1,0:T(8,128)(2,1)S(1)} %get-tuple-element.48), channel_id=1, source_target_pairs={{0,12},{1,15},{2,14},{3,13},{4,8},{5,11},{6,10},{7,9},{8,4},{9,7},... | collective-permute-start | bytes 245768 | tf_op jit(solution)/shard_map/ppermute | solution.py:111
  63.9 4.9 %collective-permute-start.16 = (bf16[64,640]{1,0:T(8,128)(2,1)S(1)}, bf16[64,640]{1,0:T(8,128)(2,1)S(1)}, u32[]{:S(2)}, u32[]{:S(2)}) collective-permute-start(bf16[64,640]{1,0:T(8,128)(2,1)S(1)} %slice.23), channel_id=1, source_target_pairs={{0,1},{1,0},{2,3},{3,2},{4,5},{5,4},{6,7},{7,6},{8,9},{9,8},{10,11... | collective-permute-start | bytes 245768 | tf_op jit(solution)/shard_map/ppermute | solution.py:114
  67.9 1.3 %collective-permute-start.14 = (bf16[64,640]{1,0:T(8,128)(2,1)S(1)}, bf16[64,640]{1,0:T(8,128)(2,1)S(1)}, u32[]{:S(2)}, u32[]{:S(2)}) collective-permute-start(bf16[64,640]{1,0:T(8,128)(2,1)S(1)} %slice.22), channel_id=1, source_target_pairs={{0,1},{1,0},{2,3},{3,2},{4,5},{5,4},{6,7},{7,6},{8,9},{9,8},{10,11... | collective-permute-start | bytes 245768 | tf_op jit(solution)/shard_map/ppermute | solution.py:114
  68.0 1.5 %collective-permute-start.18 = (bf16[64,640]{1,0:T(8,128)(2,1)S(1)}, bf16[64,640]{1,0:T(8,128)(2,1)S(1)}, u32[]{:S(2)}, u32[]{:S(2)}) collective-permute-start(bf16[64,640]{1,0:T(8,128)(2,1)S(1)} %slice.24), channel_id=1, source_target_pairs={{0,1},{1,0},{2,3},{3,2},{4,5},{5,4},{6,7},{7,6},{8,9},{9,8},{10,11... | collective-permute-start | bytes 245768 | tf_op jit(solution)/shard_map/ppermute | solution.py:114

commit v9 on v8

--- a/solution.py
+++ b/solution.py
@@ -165,12 +165,12 @@
         return dict(zip(dzs, outs))
 
     outs = attend((2,))
-    outs |= attend((0, 1), outs[2])
-    outs |= attend((LAST,), outs[0])
-    back = {(dz, 0): across(outs[dz], dz, 0) for dz in (2, 0, 1)}
+    outs |= attend((1, 0), outs[2])
+    back = {(dz, 0): across(outs[dz], dz, 0) for dz in (2, 1, 0)}
+    outs |= attend((LAST,), back[0, 0])
     for cross in (1, 0):
         back[LAST, cross] = across(outs[LAST][cross * rows : (cross + 1) * rows], LAST, cross, True)
-    back |= {(dz, 1): swap(back[dz, 0][rows:]) for dz in (0, 1, 2)}
+    back |= {(dz, 1): swap(back[dz, 0][rows:]) for dz in (1, 0, 2)}
 
     def unpack(dzs, *so_far):
         order = [(dz, cross) for dz in dzs for cross in range(2)]
@@ -186,7 +186,7 @@
             cost_estimate=FREE,
         )(*at, *pieces, *so_far)
 
-    result = unpack((LAST, 0, 1, 2))
+    result = unpack((LAST, 1, 0, 2))
     return result.reshape(layers, tok_rows, width)
 
 

time: 70.6 us -> 69.6 us (0.986)
  starting transfers between devices: 39.7 us -> 36.6 us
  waiting for transfers between devices: 22.4 us -> 24.6 us
    ppermute x14, waiting for transfers between devices: 21.4 us -> 24.4 us  [across(): return lax.ppermute(array, ('chip', 'core'), pairs)]
    ppermute x5, starting transfers between devices: 5.64 us -> 3.92 us  [swap(): return lax.ppermute(array, 'core', [(0, 1), (1, 0)])]
    ppermute x14, starting transfers between devices: 34.1 us -> 32.7 us  [across(): return lax.ppermute(array, ('chip', 'core'), pairs)]
    ppermute x5, waiting for transfers between devices: 1.04 us -> 0.13 us  [swap(): return lax.ppermute(array, 'core', [(0, 1), (1, 0)])]
  transfers between devices with their start and end apart: 19 -> 19, of which waited for: 9 -> 6; matrix products, arithmetic and copies ran while one was open for 0% -> 0% of each run, Pallas kernels for 8% -> 8%
where the time goes in v9:
time: 69.6 us; the launch traced here: 69.4 us
  starting transfers between devices  36.6 us (53%)
  waiting for transfers between devices  24.6 us (35%)
  Pallas kernels  8.06 us (12%)
    ppermute x14, starting transfers between devices, across(): return lax.ppermute(array, ('chip', 'core'), pairs)  32.7 us
    ppermute x14, waiting for transfers between devices, across(): return lax.ppermute(array, ('chip', 'core'), pairs)  24.4 us
    pallas_call x3, Pallas kernels, attend(): call(body, 2 + count, [shape(2 * rows, gw)] * len(dzs))(own, other, *pieces)  4.33 us
    ppermute x5, starting transfers between devices, swap(): return lax.ppermute(array, 'core', [(0, 1), (1, 0)])  3.92 us
    pallas_call x2, Pallas kernels, pack(): pl.pallas_call(functools.partial(pack_body, rows, gw, layout), in_specs=[...  2.73 us
  transfers between devices with their start and end apart: 19, of which 6 were waited for; matrix products, arithmetic and copies ran while one was open for 0% of the time, Pallas kernels for 8%

profile of v9, /device:TPU:0, one launch (start us, length us, event | category | flops | bytes accessed | tf_op | source)
XLA Modules:
  0.0 69.4 jit_solution(4200151293489415977)
XLA Ops:
  0.0 1.2 %shard_map.37 = (bf16[128,640]{1,0:T(8,128)(2,1)S(1)}, bf16[192,640]{1,0:T(8,128)(2,1)S(1)}, bf16[128,640]{1,0:T(8,128)(2,1)S(1)}) custom-call(s32[1]{0:T(128)} %bitcast.chip_ref, s32[1]{0:T(128)} %bitcast.1.core_ref, bf16[64,5120]{1,0:T(8,128)(2,1)} %refs_0_.2, bf16[64,5120]{1,0:T(8,128)(2,1)} %refs_1_.2, bf16[64,5120]{1,0:T(8,128)(2,1)} %bitcast.4), custom_call_target="tpu_custom_call" | custom-call | tf_op jit(solution)/shard_map/pallas_call | solution.py:137
  1.2 3.1 %collective-permute-start.1 = (bf16[192,640]{1,0:T(8,128)(2,1)S(1)}, bf16[192,640]{1,0:T(8,128)(2,1)S(1)}, u32[]{:S(2)}, u32[]{:S(2)}) collective-permute-start(bf16[192,640]{1,0:T(8,128)(2,1)S(1)} %get-tuple-element.27), channel_id=1, source_target_pairs={{0,4},{1,7},{2,6},{3,5},{4,0},{5,3},{6,2},{7,1},{8,12},{9,15},{10,... | collective-permute-start | bytes 737288 | tf_op jit(solution)/shard_map/ppermute | solution.py:111
  4.3 2.5 %collective-permute-start.2 = (bf16[128,640]{1,0:T(8,128)(2,1)S(1)}, bf16[128,640]{1,0:T(8,128)(2,1)S(1)}, u32[]{:S(2)}, u32[]{:S(2)}) collective-permute-start(bf16[128,640]{1,0:T(8,128)(2,1)S(1)} %get-tuple-element.28), channel_id=1, source_target_pairs={{0,15},{1,12},{2,13},{3,14},{4,11},{5,8},{6,9},{7,10},{8,7},{9,4},... | collective-permute-start | bytes 491528 | tf_op jit(solution)/shard_map/ppermute | solution.py:111
  6.8 1.3 %collective-permute-start = (bf16[128,640]{1,0:T(8,128)(2,1)S(1)}, bf16[128,640]{1,0:T(8,128)(2,1)S(1)}, u32[]{:S(2)}, u32[]{:S(2)}) collective-permute-start(bf16[128,640]{1,0:T(8,128)(2,1)S(1)} %get-tuple-element.26), channel_id=1, source_target_pairs={{0,12},{1,15},{2,14},{3,13},{4,8},{5,11},{6,10},{7,9},{8,4},{9,7},... | collective-permute-start | bytes 491528 | tf_op jit(solution)/shard_map/ppermute | solution.py:111
  8.2 1.5 %shard_map.38 = (bf16[192,640]{1,0:T(8,128)(2,1)S(1)}, bf16[192,640]{1,0:T(8,128)(2,1)S(1)}, bf16[192,640]{1,0:T(8,128)(2,1)S(1)}, bf16[192,640]{1,0:T(8,128)(2,...) custom-call(s32[1]{0:T(128)} %bitcast.chip_ref, ...), custom_call_target="tpu_custom_call" | custom-call | tf_op jit(solution)/shard_map/pallas_call | solution.py:137
  9.7 0.8 %collective-permute-start.5 = (bf16[64,640]{1,0:T(8,128)(2,1)S(1)}, bf16[64,640]{1,0:T(8,128)(2,1)S(1)}, u32[]{:S(2)}, u32[]{:S(2)}) collective-permute-start(bf16[64,640]{1,0:T(8,128)(2,1)S(1)} %get-tuple-element.36), channel_id=1, source_target_pairs={{0,1},{1,0},{2,3},{3,2},{4,5},{5,4},{6,7},{7,6},{8,9},{9,8},{10,11... | collective-permute-start | bytes 245768 | tf_op jit(solution)/shard_map/ppermute | solution.py:114
  10.5 0.8 %collective-permute-start.3 = (bf16[192,640]{1,0:T(8,128)(2,1)S(1)}, bf16[192,640]{1,0:T(8,128)(2,1)S(1)}, u32[]{:S(2)}, u32[]{:S(2)}) collective-permute-start(bf16[192,640]{1,0:T(8,128)(2,1)S(1)} %get-tuple-element.32), channel_id=1, source_target_pairs={{0,8},{1,11},{2,10},{3,9},{4,12},{5,15},{6,14},{7,13},{8,0},{9,3},... | collective-permute-start | bytes 737288 | tf_op jit(solution)/shard_map/ppermute | solution.py:111
  11.4 2.5 %collective-permute-start.4 = (bf16[192,640]{1,0:T(8,128)(2,1)S(1)}, bf16[192,640]{1,0:T(8,128)(2,1)S(1)}, u32[]{:S(2)}, u32[]{:S(2)}) collective-permute-start(bf16[192,640]{1,0:T(8,128)(2,1)S(1)} %get-tuple-element.33), channel_id=1, source_target_pairs={{0,7},{1,4},{2,5},{3,6},{4,3},{5,0},{6,1},{7,2},{8,15},{9,12},{10,... | collective-permute-start | bytes 737288 | tf_op jit(solution)/shard_map/ppermute | solution.py:111
  13.9 3.0 %collective-permute-done.2.refs_2_ = bf16[128,640]{1,0:T(8,128)(2,1)S(1)} collective-permute-done((bf16[128,640]{1,0:T(8,128)(2,1)S(1)}, bf16[128,640]{1,0:T(8,128)(2,1)S(1)}, u32[]{:S(2)}, u32[]{:S(2)}) %collective-permute-start.2) | collective-permute-done | bytes 163872 | tf_op jit(solution)/shard_map/ppermute | solution.py:111
  16.9 9.8 %collective-permute-start.7 = (bf16[192,640]{1,0:T(8,128)(2,1)S(1)}, bf16[192,640]{1,0:T(8,128)(2,1)S(1)}, u32[]{:S(2)}, u32[]{:S(2)}) collective-permute-start(bf16[192,640]{1,0:T(8,128)(2,1)S(1)} %get-tuple-element.38), channel_id=1, source_target_pairs={{0,11},{1,8},{2,9},{3,10},{4,15},{5,12},{6,13},{7,14},{8,3},{9,0},... | collective-permute-start | bytes 737288 | tf_op jit(solution)/shard_map/ppermute | solution.py:111
  26.8 0.7 collective-permute-start.6
  27.4 10.8 %collective-permute-done.3.refs_3_.refs_0_ = bf16[192,640]{1,0:T(8,128)(2,1)S(1)} collective-permute-done((bf16[192,640]{1,0:T(8,128)(2,1)S(1)}, bf16[192,640]{1,0:T(8,128)(2,1)S(1)}, u32[]{:S(2)}, u32[]{:S(2)}) %collective-permute-start.3) | collective-permute-done | bytes 245792 | tf_op jit(solution)/shard_map/ppermute | solution.py:111
  38.3 4.9 %collective-permute-done.7.refs_6_.refs_1_ = bf16[192,640]{1,0:T(8,128)(2,1)S(1)} collective-permute-done((bf16[192,640]{1,0:T(8,128)(2,1)S(1)}, bf16[192,640]{1,0:T(8,128)(2,1)S(1)}, u32[]{:S(2)}, u32[]{:S(2)}) %collective-permute-start.7) | collective-permute-done | bytes 245792 | tf_op jit(solution)/shard_map/ppermute | solution.py:111
  43.5 3.3 %collective-permute-start.10 = (bf16[128,640]{1,0:T(8,128)(2,1)S(1)}, bf16[128,640]{1,0:T(8,128)(2,1)S(1)}, u32[]{:S(2)}, u32[]{:S(2)}) collective-permute-start(bf16[128,640]{1,0:T(8,128)(2,1)S(1)} %constant_dynamic-update-slice_fusion), channel_id=1, source_target_pairs={{0,12},{1,15},{2,14},{3,13},{4,8},{5,11},{6,10},{7,9},{8,4},{9,7},... | collective-permute-start | bytes 491528 | tf_op jit(solution)/shard_map/ppermute | solution.py:111
  46.8 1.2 %shard_map.40 = bf16[128,640]{1,0:T(8,128)(2,1)S(1)} custom-call(bf16[2,512,640]{2,1,0:T(8,128)(2,1)S(1)} %shard_map.39.own, bf16[2,512,640]{2,1,0:T(8,128)(2,1)S(1)} %collective-permute-done.9.other, bf16[192,640]{1,0:T(8,128)(2,1)S(1)} %collective-permute-done.3.refs_3_.refs_0_, bf16[192,640]{1,0:T(8,128)(2,1)S(1)} %collective-permute-done.7.refs_6_.refs_1_), custom_call_target="tpu_custom_call" | custom-call | tf_op jit(solution)/shard_map/pallas_call | solution.py:164
  48.0 2.0 %shard_map.41 = (bf16[128,640]{1,0:T(8,128)(2,1)S(1)}, bf16[128,640]{1,0:T(8,128)(2,1)S(1)}) custom-call(bf16[2,512,640]{2,1,0:T(8,128)(2,1)S(1)} %shard_map.39.own, bf16[2,512,640]{2,1,0:T(8,128)(2,1)S(1)} %collective-permute-done.9.other, bf16[192,640]{1,0:T(8,128)(2,1)S(1)} %collective-permute-done.1.refs_1_.refs_0_, ...), custom_call_target="tpu_custom_call" | custom-call | tf_op jit(solution)/shard_map/pallas_call | solution.py:164
  50.0 0.7 collective-permute-start.11
  50.8 3.2 %collective-permute-start.14 = (bf16[128,640]{1,0:T(8,128)(2,1)S(1)}, bf16[128,640]{1,0:T(8,128)(2,1)S(1)}, u32[]{:S(2)}, u32[]{:S(2)}) collective-permute-start(bf16[128,640]{1,0:T(8,128)(2,1)S(1)} %get-tuple-element.46), channel_id=1, source_target_pairs={{0,4},{1,7},{2,6},{3,5},{4,0},{5,3},{6,2},{7,1},{8,12},{9,15},{10,... | collective-permute-start | bytes 491528 | tf_op jit(solution)/shard_map/ppermute | solution.py:111
  54.0 2.3 %collective-permute-start.16 = (bf16[64,640]{1,0:T(8,128)(2,1)S(1)}, bf16[64,640]{1,0:T(8,128)(2,1)S(1)}, u32[]{:S(2)}, u32[]{:S(2)}) collective-permute-start(bf16[64,640]{1,0:T(8,128)(2,1)S(1)} %slice.23), channel_id=1, source_target_pairs={{0,1},{1,0},{2,3},{3,2},{4,5},{5,4},{6,7},{7,6},{8,9},{9,8},{10,11... | collective-permute-start | bytes 245768 | tf_op jit(solution)/shard_map/ppermute | solution.py:114
  56.3 1.2 %shard_map.42 = bf16[128,640]{1,0:T(8,128)(2,1)S(1)} custom-call(bf16[2,512,640]{2,1,0:T(8,128)(2,1)S(1)} %shard_map.39.own, bf16[2,512,640]{2,1,0:T(8,128)(2,1)S(1)} %collective-permute-done.9.other, bf16[128,640]{1,0:T(8,128)(2,1)S(1)} %collective-permute-done.10.refs_0_), custom_call_target="tpu_custom_call" | custom-call | tf_op jit(solution)/shard_map/pallas_call | solution.py:164
  57.5 4.2 %collective-permute-start.13 = (bf16[64,640]{1,0:T(8,128)(2,1)S(1)}, bf16[64,640]{1,0:T(8,128)(2,1)S(1)}, u32[]{:S(2)}, u32[]{:S(2)}) collective-permute-start(bf16[64,640]{1,0:T(8,128)(2,1)S(1)} %get-tuple-element.47), channel_id=1, source_target_pairs={{0,13},{1,14},{2,15},{3,12},{4,9},{5,10},{6,11},{7,8},{8,5},{9,6},... | collective-permute-start | bytes 245768 | tf_op jit(solution)/shard_map/ppermute | solution.py:111
  62.8 2.1 %collective-permute-done.13.refs_1_ = bf16[64,640]{1,0:T(8,128)(2,1)S(1)} collective-permute-done((bf16[64,640]{1,0:T(8,128)(2,1)S(1)}, bf16[64,640]{1,0:T(8,128)(2,1)S(1)}, u32[]{:S(2)}, u32[]{:S(2)}) %collective-permute-start.13) | collective-permute-done | bytes 81952 | tf_op jit(solution)/shard_map/ppermute | solution.py:111
  64.8 3.7 %collective-permute-done.12.refs_0_ = bf16[64,640]{1,0:T(8,128)(2,1)S(1)} collective-permute-done((bf16[64,640]{1,0:T(8,128)(2,1)S(1)}, bf16[64,640]{1,0:T(8,128)(2,1)S(1)}, u32[]{:S(2)}, u32[]{:S(2)}) %collective-permute-start.12) | collective-permute-done | bytes 81952 | tf_op jit(solution)/shard_map/ppermute | solution.py:111
  68.5 0.9 %shard_map.43 = bf16[64,5120]{1,0:T(8,128)(2,1)} custom-call(s32[1]{0:T(128)} %bitcast.chip_ref, s32[1]{0:T(128)} %bitcast.1.core_ref, bf16[64,640]{1,0:T(8,128)(2,1)S(1)} %collective-permute-done.12.refs_0_, bf16[64,640]{1,0:T(8,128)(2,1)S(1)} %collective-permute-done.13.refs_1_, bf16[128,640]{1,0:T(8,128)(2,1)S(1)} %collective-permute-done.14.refs_2_, ...), custom_call_target="tpu_custom_call" | custom-call | tf_op jit(solution)/shard_map/pallas_call | solution.py:178
  (27 shorter events, 1.7 us)
Async XLA Ops:
  1.2 25.6 %collective-permute-start.1 = (bf16[192,640]{1,0:T(8,128)(2,1)S(1)}, bf16[192,640]{1,0:T(8,128)(2,1)S(1)}, u32[]{:S(2)}, u32[]{:S(2)}) collective-permute-start(bf16[192,640]{1,0:T(8,128)(2,1)S(1)} %get-tuple-element.27), channel_id=1, source_target_pairs={{0,4},{1,7},{2,6},{3,5},{4,0},{5,3},{6,2},{7,1},{8,12},{9,15},{10,... | collective-permute-start | bytes 737288 | tf_op jit(solution)/shard_map/ppermute | solution.py:111
  4.3 12.6 %collective-permute-start.2 = (bf16[128,640]{1,0:T(8,128)(2,1)S(1)}, bf16[128,640]{1,0:T(8,128)(2,1)S(1)}, u32[]{:S(2)}, u32[]{:S(2)}) collective-permute-start(bf16[128,640]{1,0:T(8,128)(2,1)S(1)} %get-tuple-element.28), channel_id=1, source_target_pairs={{0,15},{1,12},{2,13},{3,14},{4,11},{5,8},{6,9},{7,10},{8,7},{9,4},... | collective-permute-start | bytes 491528 | tf_op jit(solution)/shard_map/ppermute | solution.py:111
  6.8 19.9 %collective-permute-start = (bf16[128,640]{1,0:T(8,128)(2,1)S(1)}, bf16[128,640]{1,0:T(8,128)(2,1)S(1)}, u32[]{:S(2)}, u32[]{:S(2)}) collective-permute-start(bf16[128,640]{1,0:T(8,128)(2,1)S(1)} %get-tuple-element.26), channel_id=1, source_target_pairs={{0,12},{1,15},{2,14},{3,13},{4,8},{5,11},{6,10},{7,9},{8,4},{9,7},... | collective-permute-start | bytes 491528 | tf_op jit(solution)/shard_map/ppermute | solution.py:111
  9.7 1.7 %collective-permute-start.5 = (bf16[64,640]{1,0:T(8,128)(2,1)S(1)}, bf16[64,640]{1,0:T(8,128)(2,1)S(1)}, u32[]{:S(2)}, u32[]{:S(2)}) collective-permute-start(bf16[64,640]{1,0:T(8,128)(2,1)S(1)} %get-tuple-element.36), channel_id=1, source_target_pairs={{0,1},{1,0},{2,3},{3,2},{4,5},{5,4},{6,7},{7,6},{8,9},{9,8},{10,11... | collective-permute-start | bytes 245768 | tf_op jit(solution)/shard_map/ppermute | solution.py:114
  10.5 27.7 %collective-permute-start.3 = (bf16[192,640]{1,0:T(8,128)(2,1)S(1)}, bf16[192,640]{1,0:T(8,128)(2,1)S(1)}, u32[]{:S(2)}, u32[]{:S(2)}) collective-permute-start(bf16[192,640]{1,0:T(8,128)(2,1)S(1)} %get-tuple-element.32), channel_id=1, source_target_pairs={{0,8},{1,11},{2,10},{3,9},{4,12},{5,15},{6,14},{7,13},{8,0},{9,3},... | collective-permute-start | bytes 737288 | tf_op jit(solution)/shard_map/ppermute | solution.py:111
  11.4 26.8 %collective-permute-start.4 = (bf16[192,640]{1,0:T(8,128)(2,1)S(1)}, bf16[192,640]{1,0:T(8,128)(2,1)S(1)}, u32[]{:S(2)}, u32[]{:S(2)}) collective-permute-start(bf16[192,640]{1,0:T(8,128)(2,1)S(1)} %get-tuple-element.33), channel_id=1, source_target_pairs={{0,7},{1,4},{2,5},{3,6},{4,3},{5,0},{6,1},{7,2},{8,15},{9,12},{10,... | collective-permute-start | bytes 737288 | tf_op jit(solution)/shard_map/ppermute | solution.py:111
  16.9 26.3 %collective-permute-start.7 = (bf16[192,640]{1,0:T(8,128)(2,1)S(1)}, bf16[192,640]{1,0:T(8,128)(2,1)S(1)}, u32[]{:S(2)}, u32[]{:S(2)}) collective-permute-start(bf16[192,640]{1,0:T(8,128)(2,1)S(1)} %get-tuple-element.38), channel_id=1, source_target_pairs={{0,11},{1,8},{2,9},{3,10},{4,15},{5,12},{6,13},{7,14},{8,3},{9,0},... | collective-permute-start | bytes 737288 | tf_op jit(solution)/shard_map/ppermute | solution.py:111
  26.8 16.4 %collective-permute-start.8 = (bf16[192,640]{1,0:T(8,128)(2,1)S(1)}, bf16[192,640]{1,0:T(8,128)(2,1)S(1)}, u32[]{:S(2)}, u32[]{:S(2)}) collective-permute-start(bf16[192,640]{1,0:T(8,128)(2,1)S(1)} %get-tuple-element.39), channel_id=1, source_target_pairs={{0,3},{1,0},{2,1},{3,2},{4,7},{5,4},{6,5},{7,6},{8,11},{9,8},{10,9... | collective-permute-start | bytes 737288 | tf_op jit(solution)/shard_map/ppermute | solution.py:111
  26.8 16.4 %collective-permute-start.6 = (bf16[192,640]{1,0:T(8,128)(2,1)S(1)}, bf16[192,640]{1,0:T(8,128)(2,1)S(1)}, u32[]{:S(2)}, u32[]{:S(2)}) collective-permute-start(bf16[192,640]{1,0:T(8,128)(2,1)S(1)} %get-tuple-element.37), channel_id=1, source_target_pairs={{0,0},{1,3},{2,2},{3,1},{4,4},{5,7},{6,6},{7,5},{8,8},{9,11},{10,1... | collective-permute-start | bytes 737288 | tf_op jit(solution)/shard_map/ppermute | solution.py:111
  43.3 3.6 %collective-permute-start.9 = (bf16[2,512,640]{2,1,0:T(8,128)(2,1)S(1)}, bf16[2,512,640]{2,1,0:T(8,128)(2,1)S(1)}, u32[]{:S(2)}, u32[]{:S(2)}) collective-permute-start(bf16[2,512,640]{2,1,0:T(8,128)(2,1)S(1)} %shard_map.39.own), channel_id=1, source_target_pairs={{0,1},{1,0},{2,3},{3,2},{4,5},{5,4},{6,7},{7,6},{8,9},{9,8},{10,11... | collective-permute-start | bytes 3932168 | tf_op jit(solution)/shard_map/ppermute | solution.py:114
  43.5 10.5 %collective-permute-start.10 = (bf16[128,640]{1,0:T(8,128)(2,1)S(1)}, bf16[128,640]{1,0:T(8,128)(2,1)S(1)}, u32[]{:S(2)}, u32[]{:S(2)}) collective-permute-start(bf16[128,640]{1,0:T(8,128)(2,1)S(1)} %constant_dynamic-update-slice_fusion), channel_id=1, source_target_pairs={{0,12},{1,15},{2,14},{3,13},{4,8},{5,11},{6,10},{7,9},{8,4},{9,7},... | collective-permute-start | bytes 491528 | tf_op jit(solution)/shard_map/ppermute | solution.py:111
  50.0 4.0 %collective-permute-start.11 = (bf16[128,640]{1,0:T(8,128)(2,1)S(1)}, bf16[128,640]{1,0:T(8,128)(2,1)S(1)}, u32[]{:S(2)}, u32[]{:S(2)}) collective-permute-start(bf16[128,640]{1,0:T(8,128)(2,1)S(1)} %get-tuple-element.44), channel_id=1, source_target_pairs={{0,0},{1,3},{2,2},{3,1},{4,4},{5,7},{6,6},{7,5},{8,8},{9,11},{10,1... | collective-permute-start | bytes 491528 | tf_op jit(solution)/shard_map/ppermute | solution.py:111
  50.7 11.6 %collective-permute-start.17 = (bf16[128,640]{1,0:T(8,128)(2,1)S(1)}, bf16[128,640]{1,0:T(8,128)(2,1)S(1)}, u32[]{:S(2)}, u32[]{:S(2)}) collective-permute-start(bf16[128,640]{1,0:T(8,128)(2,1)S(1)} %shard_map.40), channel_id=1, source_target_pairs={{0,8},{1,11},{2,10},{3,9},{4,12},{5,15},{6,14},{7,13},{8,0},{9,3},... | collective-permute-start | bytes 491528 | tf_op jit(solution)/shard_map/ppermute | solution.py:111
  50.8 11.3 %collective-permute-start.14 = (bf16[128,640]{1,0:T(8,128)(2,1)S(1)}, bf16[128,640]{1,0:T(8,128)(2,1)S(1)}, u32[]{:S(2)}, u32[]{:S(2)}) collective-permute-start(bf16[128,640]{1,0:T(8,128)(2,1)S(1)} %get-tuple-element.46), channel_id=1, source_target_pairs={{0,4},{1,7},{2,6},{3,5},{4,0},{5,3},{6,2},{7,1},{8,12},{9,15},{10,... | collective-permute-start | bytes 491528 | tf_op jit(solution)/shard_map/ppermute | solution.py:111
  54.0 8.8 %collective-permute-start.16 = (bf16[64,640]{1,0:T(8,128)(2,1)S(1)}, bf16[64,640]{1,0:T(8,128)(2,1)S(1)}, u32[]{:S(2)}, u32[]{:S(2)}) collective-permute-start(bf16[64,640]{1,0:T(8,128)(2,1)S(1)} %slice.23), channel_id=1, source_target_pairs={{0,1},{1,0},{2,3},{3,2},{4,5},{5,4},{6,7},{7,6},{8,9},{9,8},{10,11... | collective-permute-start | bytes 245768 | tf_op jit(solution)/shard_map/ppermute | solution.py:114
  57.5 7.4 %collective-permute-start.13 = (bf16[64,640]{1,0:T(8,128)(2,1)S(1)}, bf16[64,640]{1,0:T(8,128)(2,1)S(1)}, u32[]{:S(2)}, u32[]{:S(2)}) collective-permute-start(bf16[64,640]{1,0:T(8,128)(2,1)S(1)} %get-tuple-element.47), channel_id=1, source_target_pairs={{0,13},{1,14},{2,15},{3,12},{4,9},{5,10},{6,11},{7,8},{8,5},{9,6},... | collective-permute-start | bytes 245768 | tf_op jit(solution)/shard_map/ppermute | solution.py:111
  61.6 6.9 %collective-permute-start.12 = (bf16[64,640]{1,0:T(8,128)(2,1)S(1)}, bf16[64,640]{1,0:T(8,128)(2,1)S(1)}, u32[]{:S(2)}, u32[]{:S(2)}) collective-permute-start(bf16[64,640]{1,0:T(8,128)(2,1)S(1)} %get-tuple-element.48), channel_id=1, source_target_pairs={{0,12},{1,15},{2,14},{3,13},{4,8},{5,11},{6,10},{7,9},{8,4},{9,7},... | collective-permute-start | bytes 245768 | tf_op jit(solution)/shard_map/ppermute | solution.py:111
  62.1 6.4 %collective-permute-start.15 = (bf16[64,640]{1,0:T(8,128)(2,1)S(1)}, bf16[64,640]{1,0:T(8,128)(2,1)S(1)}, u32[]{:S(2)}, u32[]{:S(2)}) collective-permute-start(bf16[64,640]{1,0:T(8,128)(2,1)S(1)} %slice.22), channel_id=1, source_target_pairs={{0,1},{1,0},{2,3},{3,2},{4,5},{5,4},{6,7},{7,6},{8,9},{9,8},{10,11... | collective-permute-start | bytes 245768 | tf_op jit(solution)/shard_map/ppermute | solution.py:114
  62.3 6.2 %collective-permute-start.18 = (bf16[64,640]{1,0:T(8,128)(2,1)S(1)}, bf16[64,640]{1,0:T(8,128)(2,1)S(1)}, u32[]{:S(2)}, u32[]{:S(2)}) collective-permute-start(bf16[64,640]{1,0:T(8,128)(2,1)S(1)} %slice.24), channel_id=1, source_target_pairs={{0,1},{1,0},{2,3},{3,2},{4,5},{5,4},{6,7},{7,6},{8,9},{9,8},{10,11... | collective-permute-start | bytes 245768 | tf_op jit(solution)/shard_map/ppermute | solution.py:114

commit v10 on v9

--- a/solution.py
+++ b/solution.py
@@ -170,7 +170,8 @@
     outs |= attend((LAST,), back[0, 0])
     for cross in (1, 0):
         back[LAST, cross] = across(outs[LAST][cross * rows : (cross + 1) * rows], LAST, cross, True)
-    back |= {(dz, 1): swap(back[dz, 0][rows:]) for dz in (1, 0, 2)}
+    back |= {(dz, 1): swap(after(back[dz, 0], back[2, 0])[rows:]) for dz in (1, 0)}
+    back[2, 1] = swap(back[2, 0][rows:])
 
     def unpack(dzs, *so_far):
         order = [(dz, cross) for dz in dzs for cross in range(2)]

time: 69.6 us -> 69 us (level)
  waiting for transfers between devices: 24.6 us -> 21.5 us
  starting transfers between devices: 36.6 us -> 39.1 us
    ppermute x14, waiting for transfers between devices: 24.4 us -> 21.4 us  [across(): return lax.ppermute(array, ('chip', 'core'), pairs)]
    ppermute x14, starting transfers between devices: 32.7 us -> 34.4 us  [across(): return lax.ppermute(array, ('chip', 'core'), pairs)]
    ppermute x5, starting transfers between devices: 3.92 us -> 4.63 us  [swap(): return lax.ppermute(array, 'core', [(0, 1), (1, 0)])]
  transfers between devices with their start and end apart: 19 -> 19, of which waited for: 6 -> 6; matrix products, arithmetic and copies ran while one was open for 0% -> 0% of each run, Pallas kernels for 8% -> 9%
where the time goes in v10:
time: 69 us; the launch traced here: 68.8 us
  starting transfers between devices  39.1 us (57%)
  waiting for transfers between devices  21.5 us (31%)
  Pallas kernels  8.07 us (12%)
    ppermute x14, starting transfers between devices, across(): return lax.ppermute(array, ('chip', 'core'), pairs)  34.4 us
    ppermute x14, waiting for transfers between devices, across(): return lax.ppermute(array, ('chip', 'core'), pairs)  21.4 us
    ppermute x5, starting transfers between devices, swap(): return lax.ppermute(array, 'core', [(0, 1), (1, 0)])  4.63 us
    pallas_call x3, Pallas kernels, attend(): call(body, 2 + count, [shape(2 * rows, gw)] * len(dzs))(own, other, *pieces)  4.33 us
    pallas_call x2, Pallas kernels, pack(): pl.pallas_call(functools.partial(pack_body, rows, gw, layout), in_specs=[...  2.73 us
  transfers between devices with their start and end apart: 19, of which 6 were waited for; matrix products, arithmetic and copies ran while one was open for 0% of the time, Pallas kernels for 9%

profile of v10, /device:TPU:0, one launch (start us, length us, event | category | flops | bytes accessed | tf_op | source)
XLA Modules:
  0.0 68.8 jit_solution(8972641886434940631)
XLA Ops:
  0.0 1.2 %shard_map.37 = (bf16[128,640]{1,0:T(8,128)(2,1)S(1)}, bf16[192,640]{1,0:T(8,128)(2,1)S(1)}, bf16[128,640]{1,0:T(8,128)(2,1)S(1)}) custom-call(s32[1]{0:T(128)} %bitcast.chip_ref, s32[1]{0:T(128)} %bitcast.1.core_ref, bf16[64,5120]{1,0:T(8,128)(2,1)} %refs_0_.2, bf16[64,5120]{1,0:T(8,128)(2,1)} %refs_1_.2, bf16[64,5120]{1,0:T(8,128)(2,1)} %bitcast.4), custom_call_target="tpu_custom_call" | custom-call | tf_op jit(solution)/shard_map/pallas_call | solution.py:137
  1.2 3.1 %collective-permute-start.1 = (bf16[192,640]{1,0:T(8,128)(2,1)S(1)}, bf16[192,640]{1,0:T(8,128)(2,1)S(1)}, u32[]{:S(2)}, u32[]{:S(2)}) collective-permute-start(bf16[192,640]{1,0:T(8,128)(2,1)S(1)} %get-tuple-element.29), channel_id=1, source_target_pairs={{0,4},{1,7},{2,6},{3,5},{4,0},{5,3},{6,2},{7,1},{8,12},{9,15},{10,... | collective-permute-start | bytes 737288 | tf_op jit(solution)/shard_map/ppermute | solution.py:111
  4.3 2.5 %collective-permute-start.2 = (bf16[128,640]{1,0:T(8,128)(2,1)S(1)}, bf16[128,640]{1,0:T(8,128)(2,1)S(1)}, u32[]{:S(2)}, u32[]{:S(2)}) collective-permute-start(bf16[128,640]{1,0:T(8,128)(2,1)S(1)} %get-tuple-element.30), channel_id=1, source_target_pairs={{0,15},{1,12},{2,13},{3,14},{4,11},{5,8},{6,9},{7,10},{8,7},{9,4},... | collective-permute-start | bytes 491528 | tf_op jit(solution)/shard_map/ppermute | solution.py:111
  6.8 1.3 %collective-permute-start = (bf16[128,640]{1,0:T(8,128)(2,1)S(1)}, bf16[128,640]{1,0:T(8,128)(2,1)S(1)}, u32[]{:S(2)}, u32[]{:S(2)}) collective-permute-start(bf16[128,640]{1,0:T(8,128)(2,1)S(1)} %get-tuple-element.28), channel_id=1, source_target_pairs={{0,12},{1,15},{2,14},{3,13},{4,8},{5,11},{6,10},{7,9},{8,4},{9,7},... | collective-permute-start | bytes 491528 | tf_op jit(solution)/shard_map/ppermute | solution.py:111
  8.2 1.5 %shard_map.38 = (bf16[192,640]{1,0:T(8,128)(2,1)S(1)}, bf16[192,640]{1,0:T(8,128)(2,1)S(1)}, bf16[192,640]{1,0:T(8,128)(2,1)S(1)}, bf16[192,640]{1,0:T(8,128)(2,...) custom-call(s32[1]{0:T(128)} %bitcast.chip_ref, ...), custom_call_target="tpu_custom_call" | custom-call | tf_op jit(solution)/shard_map/pallas_call | solution.py:137
  9.7 0.8 %collective-permute-start.5 = (bf16[64,640]{1,0:T(8,128)(2,1)S(1)}, bf16[64,640]{1,0:T(8,128)(2,1)S(1)}, u32[]{:S(2)}, u32[]{:S(2)}) collective-permute-start(bf16[64,640]{1,0:T(8,128)(2,1)S(1)} %get-tuple-element.38), channel_id=1, source_target_pairs={{0,1},{1,0},{2,3},{3,2},{4,5},{5,4},{6,7},{7,6},{8,9},{9,8},{10,11... | collective-permute-start | bytes 245768 | tf_op jit(solution)/shard_map/ppermute | solution.py:114
  10.5 0.8 %collective-permute-start.3 = (bf16[192,640]{1,0:T(8,128)(2,1)S(1)}, bf16[192,640]{1,0:T(8,128)(2,1)S(1)}, u32[]{:S(2)}, u32[]{:S(2)}) collective-permute-start(bf16[192,640]{1,0:T(8,128)(2,1)S(1)} %get-tuple-element.34), channel_id=1, source_target_pairs={{0,8},{1,11},{2,10},{3,9},{4,12},{5,15},{6,14},{7,13},{8,0},{9,3},... | collective-permute-start | bytes 737288 | tf_op jit(solution)/shard_map/ppermute | solution.py:111
  11.4 2.5 %collective-permute-start.4 = (bf16[192,640]{1,0:T(8,128)(2,1)S(1)}, bf16[192,640]{1,0:T(8,128)(2,1)S(1)}, u32[]{:S(2)}, u32[]{:S(2)}) collective-permute-start(bf16[192,640]{1,0:T(8,128)(2,1)S(1)} %get-tuple-element.35), channel_id=1, source_target_pairs={{0,7},{1,4},{2,5},{3,6},{4,3},{5,0},{6,1},{7,2},{8,15},{9,12},{10,... | collective-permute-start | bytes 737288 | tf_op jit(solution)/shard_map/ppermute | solution.py:111
  13.9 3.0 %collective-permute-done.2.refs_2_ = bf16[128,640]{1,0:T(8,128)(2,1)S(1)} collective-permute-done((bf16[128,640]{1,0:T(8,128)(2,1)S(1)}, bf16[128,640]{1,0:T(8,128)(2,1)S(1)}, u32[]{:S(2)}, u32[]{:S(2)}) %collective-permute-start.2) | collective-permute-done | bytes 163872 | tf_op jit(solution)/shard_map/ppermute | solution.py:111
  16.9 9.8 %collective-permute-start.7 = (bf16[192,640]{1,0:T(8,128)(2,1)S(1)}, bf16[192,640]{1,0:T(8,128)(2,1)S(1)}, u32[]{:S(2)}, u32[]{:S(2)}) collective-permute-start(bf16[192,640]{1,0:T(8,128)(2,1)S(1)} %get-tuple-element.40), channel_id=1, source_target_pairs={{0,11},{1,8},{2,9},{3,10},{4,15},{5,12},{6,13},{7,14},{8,3},{9,0},... | collective-permute-start | bytes 737288 | tf_op jit(solution)/shard_map/ppermute | solution.py:111
  26.8 0.7 collective-permute-start.6
  27.4 10.8 %collective-permute-done.3.refs_3_.refs_0_ = bf16[192,640]{1,0:T(8,128)(2,1)S(1)} collective-permute-done((bf16[192,640]{1,0:T(8,128)(2,1)S(1)}, bf16[192,640]{1,0:T(8,128)(2,1)S(1)}, u32[]{:S(2)}, u32[]{:S(2)}) %collective-permute-start.3) | collective-permute-done | bytes 245792 | tf_op jit(solution)/shard_map/ppermute | solution.py:111
  38.3 4.9 %collective-permute-done.7.refs_6_.refs_1_ = bf16[192,640]{1,0:T(8,128)(2,1)S(1)} collective-permute-done((bf16[192,640]{1,0:T(8,128)(2,1)S(1)}, bf16[192,640]{1,0:T(8,128)(2,1)S(1)}, u32[]{:S(2)}, u32[]{:S(2)}) %collective-permute-start.7) | collective-permute-done | bytes 245792 | tf_op jit(solution)/shard_map/ppermute | solution.py:111
  43.5 3.3 %collective-permute-start.10 = (bf16[128,640]{1,0:T(8,128)(2,1)S(1)}, bf16[128,640]{1,0:T(8,128)(2,1)S(1)}, u32[]{:S(2)}, u32[]{:S(2)}) collective-permute-start(bf16[128,640]{1,0:T(8,128)(2,1)S(1)} %constant_dynamic-update-slice_fusion), channel_id=1, source_target_pairs={{0,12},{1,15},{2,14},{3,13},{4,8},{5,11},{6,10},{7,9},{8,4},{9,7},... | collective-permute-start | bytes 491528 | tf_op jit(solution)/shard_map/ppermute | solution.py:111
  46.8 1.2 %shard_map.40 = bf16[128,640]{1,0:T(8,128)(2,1)S(1)} custom-call(bf16[2,512,640]{2,1,0:T(8,128)(2,1)S(1)} %shard_map.39.own, bf16[2,512,640]{2,1,0:T(8,128)(2,1)S(1)} %collective-permute-done.9.other, bf16[192,640]{1,0:T(8,128)(2,1)S(1)} %collective-permute-done.3.refs_3_.refs_0_, bf16[192,640]{1,0:T(8,128)(2,1)S(1)} %collective-permute-done.7.refs_6_.refs_1_), custom_call_target="tpu_custom_call" | custom-call | tf_op jit(solution)/shard_map/pallas_call | solution.py:164
  48.0 2.0 %shard_map.41 = (bf16[128,640]{1,0:T(8,128)(2,1)S(1)}, bf16[128,640]{1,0:T(8,128)(2,1)S(1)}) custom-call(bf16[2,512,640]{2,1,0:T(8,128)(2,1)S(1)} %shard_map.39.own, bf16[2,512,640]{2,1,0:T(8,128)(2,1)S(1)} %collective-permute-done.9.other, bf16[192,640]{1,0:T(8,128)(2,1)S(1)} %collective-permute-done.1.refs_1_.refs_0_, ...), custom_call_target="tpu_custom_call" | custom-call | tf_op jit(solution)/shard_map/pallas_call | solution.py:164
  50.0 0.7 collective-permute-start.11
  50.8 3.2 %collective-permute-start.14 = (bf16[128,640]{1,0:T(8,128)(2,1)S(1)}, bf16[128,640]{1,0:T(8,128)(2,1)S(1)}, u32[]{:S(2)}, u32[]{:S(2)}) collective-permute-start(bf16[128,640]{1,0:T(8,128)(2,1)S(1)} %get-tuple-element.48), channel_id=1, source_target_pairs={{0,4},{1,7},{2,6},{3,5},{4,0},{5,3},{6,2},{7,1},{8,12},{9,15},{10,... | collective-permute-start | bytes 491528 | tf_op jit(solution)/shard_map/ppermute | solution.py:111
  54.0 1.2 %shard_map.42 = bf16[128,640]{1,0:T(8,128)(2,1)S(1)} custom-call(bf16[2,512,640]{2,1,0:T(8,128)(2,1)S(1)} %shard_map.39.own, bf16[2,512,640]{2,1,0:T(8,128)(2,1)S(1)} %collective-permute-done.9.other, bf16[128,640]{1,0:T(8,128)(2,1)S(1)} %collective-permute-done.10.refs_0_), custom_call_target="tpu_custom_call" | custom-call | tf_op jit(solution)/shard_map/pallas_call | solution.py:164
  55.2 6.4 %collective-permute-start.13 = (bf16[64,640]{1,0:T(8,128)(2,1)S(1)}, bf16[64,640]{1,0:T(8,128)(2,1)S(1)}, u32[]{:S(2)}, u32[]{:S(2)}) collective-permute-start(bf16[64,640]{1,0:T(8,128)(2,1)S(1)} %get-tuple-element.51), channel_id=1, source_target_pairs={{0,13},{1,14},{2,15},{3,12},{4,9},{5,10},{6,11},{7,8},{8,5},{9,6},... | collective-permute-start | bytes 245768 | tf_op jit(solution)/shard_map/ppermute | solution.py:111
  62.0 3.1 %collective-permute-start.18 = (bf16[64,640]{1,0:T(8,128)(2,1)S(1)}, bf16[64,640]{1,0:T(8,128)(2,1)S(1)}, u32[]{:S(2)}, u32[]{:S(2)}) collective-permute-start(bf16[64,640]{1,0:T(8,128)(2,1)S(1)} %slice.22), channel_id=1, source_target_pairs={{0,1},{1,0},{2,3},{3,2},{4,5},{5,4},{6,7},{7,6},{8,9},{9,8},{10,11... | collective-permute-start | bytes 245768 | tf_op jit(solution)/shard_map/ppermute | solution.py:114
  65.2 0.4 collective-permute-start.16
  65.7 2.2 %collective-permute-done.12.refs_0_ = bf16[64,640]{1,0:T(8,128)(2,1)S(1)} collective-permute-done((bf16[64,640]{1,0:T(8,128)(2,1)S(1)}, bf16[64,640]{1,0:T(8,128)(2,1)S(1)}, u32[]{:S(2)}, u32[]{:S(2)}) %collective-permute-start.12) | collective-permute-done | bytes 81952 | tf_op jit(solution)/shard_map/ppermute | solution.py:111
  67.9 0.9 %shard_map.43 = bf16[64,5120]{1,0:T(8,128)(2,1)} custom-call(s32[1]{0:T(128)} %bitcast.chip_ref, s32[1]{0:T(128)} %bitcast.1.core_ref, bf16[64,640]{1,0:T(8,128)(2,1)S(1)} %collective-permute-done.12.refs_0_, bf16[64,640]{1,0:T(8,128)(2,1)S(1)} %collective-permute-done.13.refs_1_, bf16[128,640]{1,0:T(8,128)(2,1)S(1)} %collective-permute-done.14.refs_2_, ...), custom_call_target="tpu_custom_call" | custom-call | tf_op jit(solution)/shard_map/pallas_call | solution.py:179
  (27 shorter events, 1.1 us)
Async XLA Ops:
  1.2 25.6 %collective-permute-start.1 = (bf16[192,640]{1,0:T(8,128)(2,1)S(1)}, bf16[192,640]{1,0:T(8,128)(2,1)S(1)}, u32[]{:S(2)}, u32[]{:S(2)}) collective-permute-start(bf16[192,640]{1,0:T(8,128)(2,1)S(1)} %get-tuple-element.29), channel_id=1, source_target_pairs={{0,4},{1,7},{2,6},{3,5},{4,0},{5,3},{6,2},{7,1},{8,12},{9,15},{10,... | collective-permute-start | bytes 737288 | tf_op jit(solution)/shard_map/ppermute | solution.py:111
  4.3 12.6 %collective-permute-start.2 = (bf16[128,640]{1,0:T(8,128)(2,1)S(1)}, bf16[128,640]{1,0:T(8,128)(2,1)S(1)}, u32[]{:S(2)}, u32[]{:S(2)}) collective-permute-start(bf16[128,640]{1,0:T(8,128)(2,1)S(1)} %get-tuple-element.30), channel_id=1, source_target_pairs={{0,15},{1,12},{2,13},{3,14},{4,11},{5,8},{6,9},{7,10},{8,7},{9,4},... | collective-permute-start | bytes 491528 | tf_op jit(solution)/shard_map/ppermute | solution.py:111
  6.8 19.9 %collective-permute-start = (bf16[128,640]{1,0:T(8,128)(2,1)S(1)}, bf16[128,640]{1,0:T(8,128)(2,1)S(1)}, u32[]{:S(2)}, u32[]{:S(2)}) collective-permute-start(bf16[128,640]{1,0:T(8,128)(2,1)S(1)} %get-tuple-element.28), channel_id=1, source_target_pairs={{0,12},{1,15},{2,14},{3,13},{4,8},{5,11},{6,10},{7,9},{8,4},{9,7},... | collective-permute-start | bytes 491528 | tf_op jit(solution)/shard_map/ppermute | solution.py:111
  9.7 1.7 %collective-permute-start.5 = (bf16[64,640]{1,0:T(8,128)(2,1)S(1)}, bf16[64,640]{1,0:T(8,128)(2,1)S(1)}, u32[]{:S(2)}, u32[]{:S(2)}) collective-permute-start(bf16[64,640]{1,0:T(8,128)(2,1)S(1)} %get-tuple-element.38), channel_id=1, source_target_pairs={{0,1},{1,0},{2,3},{3,2},{4,5},{5,4},{6,7},{7,6},{8,9},{9,8},{10,11... | collective-permute-start | bytes 245768 | tf_op jit(solution)/shard_map/ppermute | solution.py:114
  10.5 27.7 %collective-permute-start.3 = (bf16[192,640]{1,0:T(8,128)(2,1)S(1)}, bf16[192,640]{1,0:T(8,128)(2,1)S(1)}, u32[]{:S(2)}, u32[]{:S(2)}) collective-permute-start(bf16[192,640]{1,0:T(8,128)(2,1)S(1)} %get-tuple-element.34), channel_id=1, source_target_pairs={{0,8},{1,11},{2,10},{3,9},{4,12},{5,15},{6,14},{7,13},{8,0},{9,3},... | collective-permute-start | bytes 737288 | tf_op jit(solution)/shard_map/ppermute | solution.py:111
  11.4 26.8 %collective-permute-start.4 = (bf16[192,640]{1,0:T(8,128)(2,1)S(1)}, bf16[192,640]{1,0:T(8,128)(2,1)S(1)}, u32[]{:S(2)}, u32[]{:S(2)}) collective-permute-start(bf16[192,640]{1,0:T(8,128)(2,1)S(1)} %get-tuple-element.35), channel_id=1, source_target_pairs={{0,7},{1,4},{2,5},{3,6},{4,3},{5,0},{6,1},{7,2},{8,15},{9,12},{10,... | collective-permute-start | bytes 737288 | tf_op jit(solution)/shard_map/ppermute | solution.py:111
  16.9 26.3 %collective-permute-start.7 = (bf16[192,640]{1,0:T(8,128)(2,1)S(1)}, bf16[192,640]{1,0:T(8,128)(2,1)S(1)}, u32[]{:S(2)}, u32[]{:S(2)}) collective-permute-start(bf16[192,640]{1,0:T(8,128)(2,1)S(1)} %get-tuple-element.40), channel_id=1, source_target_pairs={{0,11},{1,8},{2,9},{3,10},{4,15},{5,12},{6,13},{7,14},{8,3},{9,0},... | collective-permute-start | bytes 737288 | tf_op jit(solution)/shard_map/ppermute | solution.py:111
  26.8 16.4 %collective-permute-start.8 = (bf16[192,640]{1,0:T(8,128)(2,1)S(1)}, bf16[192,640]{1,0:T(8,128)(2,1)S(1)}, u32[]{:S(2)}, u32[]{:S(2)}) collective-permute-start(bf16[192,640]{1,0:T(8,128)(2,1)S(1)} %get-tuple-element.41), channel_id=1, source_target_pairs={{0,3},{1,0},{2,1},{3,2},{4,7},{5,4},{6,5},{7,6},{8,11},{9,8},{10,9... | collective-permute-start | bytes 737288 | tf_op jit(solution)/shard_map/ppermute | solution.py:111
  26.8 16.4 %collective-permute-start.6 = (bf16[192,640]{1,0:T(8,128)(2,1)S(1)}, bf16[192,640]{1,0:T(8,128)(2,1)S(1)}, u32[]{:S(2)}, u32[]{:S(2)}) collective-permute-start(bf16[192,640]{1,0:T(8,128)(2,1)S(1)} %get-tuple-element.39), channel_id=1, source_target_pairs={{0,0},{1,3},{2,2},{3,1},{4,4},{5,7},{6,6},{7,5},{8,8},{9,11},{10,1... | collective-permute-start | bytes 737288 | tf_op jit(solution)/shard_map/ppermute | solution.py:111
  43.3 3.6 %collective-permute-start.9 = (bf16[2,512,640]{2,1,0:T(8,128)(2,1)S(1)}, bf16[2,512,640]{2,1,0:T(8,128)(2,1)S(1)}, u32[]{:S(2)}, u32[]{:S(2)}) collective-permute-start(bf16[2,512,640]{2,1,0:T(8,128)(2,1)S(1)} %shard_map.39.own), channel_id=1, source_target_pairs={{0,1},{1,0},{2,3},{3,2},{4,5},{5,4},{6,7},{7,6},{8,9},{9,8},{10,11... | collective-permute-start | bytes 3932168 | tf_op jit(solution)/shard_map/ppermute | solution.py:114
  43.5 10.5 %collective-permute-start.10 = (bf16[128,640]{1,0:T(8,128)(2,1)S(1)}, bf16[128,640]{1,0:T(8,128)(2,1)S(1)}, u32[]{:S(2)}, u32[]{:S(2)}) collective-permute-start(bf16[128,640]{1,0:T(8,128)(2,1)S(1)} %constant_dynamic-update-slice_fusion), channel_id=1, source_target_pairs={{0,12},{1,15},{2,14},{3,13},{4,8},{5,11},{6,10},{7,9},{8,4},{9,7},... | collective-permute-start | bytes 491528 | tf_op jit(solution)/shard_map/ppermute | solution.py:111
  50.0 4.0 %collective-permute-start.11 = (bf16[128,640]{1,0:T(8,128)(2,1)S(1)}, bf16[128,640]{1,0:T(8,128)(2,1)S(1)}, u32[]{:S(2)}, u32[]{:S(2)}) collective-permute-start(bf16[128,640]{1,0:T(8,128)(2,1)S(1)} %get-tuple-element.46), channel_id=1, source_target_pairs={{0,0},{1,3},{2,2},{3,1},{4,4},{5,7},{6,6},{7,5},{8,8},{9,11},{10,1... | collective-permute-start | bytes 491528 | tf_op jit(solution)/shard_map/ppermute | solution.py:111
  50.7 11.3 %collective-permute-start.15 = (bf16[128,640]{1,0:T(8,128)(2,1)S(1)}, bf16[128,640]{1,0:T(8,128)(2,1)S(1)}, u32[]{:S(2)}, u32[]{:S(2)}) collective-permute-start(bf16[128,640]{1,0:T(8,128)(2,1)S(1)} %shard_map.40), channel_id=1, source_target_pairs={{0,8},{1,11},{2,10},{3,9},{4,12},{5,15},{6,14},{7,13},{8,0},{9,3},... | collective-permute-start | bytes 491528 | tf_op jit(solution)/shard_map/ppermute | solution.py:111
  50.8 11.2 %collective-permute-start.14 = (bf16[128,640]{1,0:T(8,128)(2,1)S(1)}, bf16[128,640]{1,0:T(8,128)(2,1)S(1)}, u32[]{:S(2)}, u32[]{:S(2)}) collective-permute-start(bf16[128,640]{1,0:T(8,128)(2,1)S(1)} %get-tuple-element.48), channel_id=1, source_target_pairs={{0,4},{1,7},{2,6},{3,5},{4,0},{5,3},{6,2},{7,1},{8,12},{9,15},{10,... | collective-permute-start | bytes 491528 | tf_op jit(solution)/shard_map/ppermute | solution.py:111
  55.2 10.5 %collective-permute-start.13 = (bf16[64,640]{1,0:T(8,128)(2,1)S(1)}, bf16[64,640]{1,0:T(8,128)(2,1)S(1)}, u32[]{:S(2)}, u32[]{:S(2)}) collective-permute-start(bf16[64,640]{1,0:T(8,128)(2,1)S(1)} %get-tuple-element.51), channel_id=1, source_target_pairs={{0,13},{1,14},{2,15},{3,12},{4,9},{5,10},{6,11},{7,8},{8,5},{9,6},... | collective-permute-start | bytes 245768 | tf_op jit(solution)/shard_map/ppermute | solution.py:111
  61.5 6.3 %collective-permute-start.12 = (bf16[64,640]{1,0:T(8,128)(2,1)S(1)}, bf16[64,640]{1,0:T(8,128)(2,1)S(1)}, u32[]{:S(2)}, u32[]{:S(2)}) collective-permute-start(bf16[64,640]{1,0:T(8,128)(2,1)S(1)} %get-tuple-element.52), channel_id=1, source_target_pairs={{0,12},{1,15},{2,14},{3,13},{4,8},{5,11},{6,10},{7,9},{8,4},{9,7},... | collective-permute-start | bytes 245768 | tf_op jit(solution)/shard_map/ppermute | solution.py:111
  62.0 5.9 %collective-permute-start.18 = (bf16[64,640]{1,0:T(8,128)(2,1)S(1)}, bf16[64,640]{1,0:T(8,128)(2,1)S(1)}, u32[]{:S(2)}, u32[]{:S(2)}) collective-permute-start(bf16[64,640]{1,0:T(8,128)(2,1)S(1)} %slice.22), channel_id=1, source_target_pairs={{0,1},{1,0},{2,3},{3,2},{4,5},{5,4},{6,7},{7,6},{8,9},{9,8},{10,11... | collective-permute-start | bytes 245768 | tf_op jit(solution)/shard_map/ppermute | solution.py:114
  65.1 2.7 %collective-permute-start.17 = (bf16[64,640]{1,0:T(8,128)(2,1)S(1)}, bf16[64,640]{1,0:T(8,128)(2,1)S(1)}, u32[]{:S(2)}, u32[]{:S(2)}) collective-permute-start(bf16[64,640]{1,0:T(8,128)(2,1)S(1)} %slice.18), channel_id=1, source_target_pairs={{0,1},{1,0},{2,3},{3,2},{4,5},{5,4},{6,7},{7,6},{8,9},{9,8},{10,11... | collective-permute-start | bytes 245768 | tf_op jit(solution)/shard_map/ppermute | solution.py:114
  65.2 2.7 %collective-permute-start.16 = (bf16[64,640]{1,0:T(8,128)(2,1)S(1)}, bf16[64,640]{1,0:T(8,128)(2,1)S(1)}, u32[]{:S(2)}, u32[]{:S(2)}) collective-permute-start(bf16[64,640]{1,0:T(8,128)(2,1)S(1)} %slice.17), channel_id=1, source_target_pairs={{0,1},{1,0},{2,3},{3,2},{4,5},{5,4},{6,7},{7,6},{8,9},{9,8},{10,11... | collective-permute-start | bytes 245768 | tf_op jit(solution)/shard_map/ppermute | solution.py:114

commit v11 on v10

--- a/solution.py
+++ b/solution.py
@@ -168,8 +168,7 @@
     outs |= attend((1, 0), outs[2])
     back = {(dz, 0): across(outs[dz], dz, 0) for dz in (2, 1, 0)}
     outs |= attend((LAST,), back[0, 0])
-    for cross in (1, 0):
-        back[LAST, cross] = across(outs[LAST][cross * rows : (cross + 1) * rows], LAST, cross, True)
+    back[LAST, 0] = across(outs[LAST], LAST, 0)
     back |= {(dz, 1): swap(after(back[dz, 0], back[2, 0])[rows:]) for dz in (1, 0)}
     back[2, 1] = swap(back[2, 0][rows:])
 
@@ -187,7 +186,9 @@
             cost_estimate=FREE,
         )(*at, *pieces, *so_far)
 
-    result = unpack((LAST, 1, 0, 2))
+    result = unpack((1, 0, 2))
+    back[LAST, 1] = swap(after(back[LAST, 0], result)[rows:])
+    result = unpack((LAST,), result)
     return result.reshape(layers, tok_rows, width)
 
 

time: 69 us -> 70.6 us (1.023)
  waiting for transfers between devices: 21.5 us -> 27.3 us
  starting transfers between devices: 39.1 us -> 34.2 us
    ppermute x14 -> x13, starting transfers between devices: 34.4 us -> 29.3 us  [across(): return lax.ppermute(array, ('chip', 'core'), pairs)]
    ppermute x14 -> x13, waiting for transfers between devices: 21.4 us -> 25.4 us  [across(): return lax.ppermute(array, ('chip', 'core'), pairs)]
    ppermute x5 -> x6, waiting for transfers between devices: 0.13 us -> 1.97 us  [swap(): return lax.ppermute(array, 'core', [(0, 1), (1, 0)])]
    pallas_call x1 -> x2, Pallas kernels: 0.9 us -> 1.5 us  [unpack(): pl.pallas_call(functools.partial(unpack_body, gw, order), in_specs=[SMEM,...]
    ppermute x5 -> x6, starting transfers between devices: 4.63 us -> 4.86 us  [swap(): return lax.ppermute(array, 'core', [(0, 1), (1, 0)])]
  transfers between devices with their start and end apart: 19 -> 19, of which waited for: 6 -> 9; matrix products, arithmetic and copies ran while one was open for 0% -> 0% of each run, Pallas kernels for 9% -> 10%
where the time goes in v11:
time: 70.6 us; the launch traced here: 70.3 us
  starting transfers between devices  34.2 us (48%)
  waiting for transfers between devices  27.3 us (39%)
  Pallas kernels  8.66 us (12%)
    ppermute x13, starting transfers between devices, across(): return lax.ppermute(array, ('chip', 'core'), pairs)  29.3 us
    ppermute x13, waiting for transfers between devices, across(): return lax.ppermute(array, ('chip', 'core'), pairs)  25.4 us
    ppermute x6, starting transfers between devices, swap(): return lax.ppermute(array, 'core', [(0, 1), (1, 0)])  4.86 us
    pallas_call x3, Pallas kernels, attend(): call(body, 2 + count, [shape(2 * rows, gw)] * len(dzs))(own, other, *pieces)  4.33 us
    pallas_call x2, Pallas kernels, pack(): pl.pallas_call(functools.partial(pack_body, rows, gw, layout), in_specs=[...  2.73 us
    ppermute x6, waiting for transfers between devices, swap(): return lax.ppermute(array, 'core', [(0, 1), (1, 0)])  1.97 us
    pallas_call x2, Pallas kernels, unpack(): pl.pallas_call(functools.partial(unpack_body, gw, order), in_specs=[SMEM,...  1.5 us
  transfers between devices with their start and end apart: 19, of which 9 were waited for; matrix products, arithmetic and copies ran while one was open for 0% of the time, Pallas kernels for 10%

profile of v11, /device:TPU:0, one launch (start us, length us, event | category | flops | bytes accessed | tf_op | source)
XLA Modules:
  0.0 70.3 jit_solution(5013561356108874465)
XLA Ops:
  0.0 1.2 %shard_map.37 = (bf16[128,640]{1,0:T(8,128)(2,1)S(1)}, bf16[192,640]{1,0:T(8,128)(2,1)S(1)}, bf16[128,640]{1,0:T(8,128)(2,1)S(1)}) custom-call(s32[1]{0:T(128)} %bitcast.chip_ref, s32[1]{0:T(128)} %bitcast.1.core_ref, bf16[64,5120]{1,0:T(8,128)(2,1)} %refs_0_.2, bf16[64,5120]{1,0:T(8,128)(2,1)} %refs_1_.2, bf16[64,5120]{1,0:T(8,128)(2,1)} %bitcast.4), custom_call_target="tpu_custom_call" | custom-call | tf_op jit(solution)/shard_map/pallas_call | solution.py:137
  1.2 3.1 %collective-permute-start.1 = (bf16[192,640]{1,0:T(8,128)(2,1)S(1)}, bf16[192,640]{1,0:T(8,128)(2,1)S(1)}, u32[]{:S(2)}, u32[]{:S(2)}) collective-permute-start(bf16[192,640]{1,0:T(8,128)(2,1)S(1)} %get-tuple-element.30), channel_id=1, source_target_pairs={{0,4},{1,7},{2,6},{3,5},{4,0},{5,3},{6,2},{7,1},{8,12},{9,15},{10,... | collective-permute-start | bytes 737288 | tf_op jit(solution)/shard_map/ppermute | solution.py:111
  4.3 2.5 %collective-permute-start.2 = (bf16[128,640]{1,0:T(8,128)(2,1)S(1)}, bf16[128,640]{1,0:T(8,128)(2,1)S(1)}, u32[]{:S(2)}, u32[]{:S(2)}) collective-permute-start(bf16[128,640]{1,0:T(8,128)(2,1)S(1)} %get-tuple-element.31), channel_id=1, source_target_pairs={{0,15},{1,12},{2,13},{3,14},{4,11},{5,8},{6,9},{7,10},{8,7},{9,4},... | collective-permute-start | bytes 491528 | tf_op jit(solution)/shard_map/ppermute | solution.py:111
  6.8 1.3 %collective-permute-start = (bf16[128,640]{1,0:T(8,128)(2,1)S(1)}, bf16[128,640]{1,0:T(8,128)(2,1)S(1)}, u32[]{:S(2)}, u32[]{:S(2)}) collective-permute-start(bf16[128,640]{1,0:T(8,128)(2,1)S(1)} %get-tuple-element.29), channel_id=1, source_target_pairs={{0,12},{1,15},{2,14},{3,13},{4,8},{5,11},{6,10},{7,9},{8,4},{9,7},... | collective-permute-start | bytes 491528 | tf_op jit(solution)/shard_map/ppermute | solution.py:111
  8.2 1.5 %shard_map.38 = (bf16[192,640]{1,0:T(8,128)(2,1)S(1)}, bf16[192,640]{1,0:T(8,128)(2,1)S(1)}, bf16[192,640]{1,0:T(8,128)(2,1)S(1)}, bf16[192,640]{1,0:T(8,128)(2,...) custom-call(s32[1]{0:T(128)} %bitcast.chip_ref, ...), custom_call_target="tpu_custom_call" | custom-call | tf_op jit(solution)/shard_map/pallas_call | solution.py:137
  9.7 0.8 %collective-permute-start.5 = (bf16[64,640]{1,0:T(8,128)(2,1)S(1)}, bf16[64,640]{1,0:T(8,128)(2,1)S(1)}, u32[]{:S(2)}, u32[]{:S(2)}) collective-permute-start(bf16[64,640]{1,0:T(8,128)(2,1)S(1)} %get-tuple-element.39), channel_id=1, source_target_pairs={{0,1},{1,0},{2,3},{3,2},{4,5},{5,4},{6,7},{7,6},{8,9},{9,8},{10,11... | collective-permute-start | bytes 245768 | tf_op jit(solution)/shard_map/ppermute | solution.py:114
  10.5 0.8 %collective-permute-start.3 = (bf16[192,640]{1,0:T(8,128)(2,1)S(1)}, bf16[192,640]{1,0:T(8,128)(2,1)S(1)}, u32[]{:S(2)}, u32[]{:S(2)}) collective-permute-start(bf16[192,640]{1,0:T(8,128)(2,1)S(1)} %get-tuple-element.35), channel_id=1, source_target_pairs={{0,8},{1,11},{2,10},{3,9},{4,12},{5,15},{6,14},{7,13},{8,0},{9,3},... | collective-permute-start | bytes 737288 | tf_op jit(solution)/shard_map/ppermute | solution.py:111
  11.4 2.5 %collective-permute-start.4 = (bf16[192,640]{1,0:T(8,128)(2,1)S(1)}, bf16[192,640]{1,0:T(8,128)(2,1)S(1)}, u32[]{:S(2)}, u32[]{:S(2)}) collective-permute-start(bf16[192,640]{1,0:T(8,128)(2,1)S(1)} %get-tuple-element.36), channel_id=1, source_target_pairs={{0,7},{1,4},{2,5},{3,6},{4,3},{5,0},{6,1},{7,2},{8,15},{9,12},{10,... | collective-permute-start | bytes 737288 | tf_op jit(solution)/shard_map/ppermute | solution.py:111
  13.9 3.0 %collective-permute-done.2.refs_2_ = bf16[128,640]{1,0:T(8,128)(2,1)S(1)} collective-permute-done((bf16[128,640]{1,0:T(8,128)(2,1)S(1)}, bf16[128,640]{1,0:T(8,128)(2,1)S(1)}, u32[]{:S(2)}, u32[]{:S(2)}) %collective-permute-start.2) | collective-permute-done | bytes 163872 | tf_op jit(solution)/shard_map/ppermute | solution.py:111
  16.9 9.8 %collective-permute-start.7 = (bf16[192,640]{1,0:T(8,128)(2,1)S(1)}, bf16[192,640]{1,0:T(8,128)(2,1)S(1)}, u32[]{:S(2)}, u32[]{:S(2)}) collective-permute-start(bf16[192,640]{1,0:T(8,128)(2,1)S(1)} %get-tuple-element.41), channel_id=1, source_target_pairs={{0,11},{1,8},{2,9},{3,10},{4,15},{5,12},{6,13},{7,14},{8,3},{9,0},... | collective-permute-start | bytes 737288 | tf_op jit(solution)/shard_map/ppermute | solution.py:111
  26.8 0.7 collective-permute-start.6
  27.4 10.8 %collective-permute-done.3.refs_3_.refs_0_ = bf16[192,640]{1,0:T(8,128)(2,1)S(1)} collective-permute-done((bf16[192,640]{1,0:T(8,128)(2,1)S(1)}, bf16[192,640]{1,0:T(8,128)(2,1)S(1)}, u32[]{:S(2)}, u32[]{:S(2)}) %collective-permute-start.3) | collective-permute-done | bytes 245792 | tf_op jit(solution)/shard_map/ppermute | solution.py:111
  38.3 4.9 %collective-permute-done.7.refs_6_.refs_1_ = bf16[192,640]{1,0:T(8,128)(2,1)S(1)} collective-permute-done((bf16[192,640]{1,0:T(8,128)(2,1)S(1)}, bf16[192,640]{1,0:T(8,128)(2,1)S(1)}, u32[]{:S(2)}, u32[]{:S(2)}) %collective-permute-start.7) | collective-permute-done | bytes 245792 | tf_op jit(solution)/shard_map/ppermute | solution.py:111
  43.5 3.3 %collective-permute-start.10 = (bf16[128,640]{1,0:T(8,128)(2,1)S(1)}, bf16[128,640]{1,0:T(8,128)(2,1)S(1)}, u32[]{:S(2)}, u32[]{:S(2)}) collective-permute-start(bf16[128,640]{1,0:T(8,128)(2,1)S(1)} %constant_dynamic-update-slice_fusion), channel_id=1, source_target_pairs={{0,12},{1,15},{2,14},{3,13},{4,8},{5,11},{6,10},{7,9},{8,4},{9,7},... | collective-permute-start | bytes 491528 | tf_op jit(solution)/shard_map/ppermute | solution.py:111
  46.8 1.2 %shard_map.40 = bf16[128,640]{1,0:T(8,128)(2,1)S(1)} custom-call(bf16[2,512,640]{2,1,0:T(8,128)(2,1)S(1)} %shard_map.39.own, bf16[2,512,640]{2,1,0:T(8,128)(2,1)S(1)} %collective-permute-done.9.other, bf16[192,640]{1,0:T(8,128)(2,1)S(1)} %collective-permute-done.3.refs_3_.refs_0_, bf16[192,640]{1,0:T(8,128)(2,1)S(1)} %collective-permute-done.7.refs_6_.refs_1_), custom_call_target="tpu_custom_call" | custom-call | tf_op jit(solution)/shard_map/pallas_call | solution.py:164
  48.0 2.0 %shard_map.41 = (bf16[128,640]{1,0:T(8,128)(2,1)S(1)}, bf16[128,640]{1,0:T(8,128)(2,1)S(1)}) custom-call(bf16[2,512,640]{2,1,0:T(8,128)(2,1)S(1)} %shard_map.39.own, bf16[2,512,640]{2,1,0:T(8,128)(2,1)S(1)} %collective-permute-done.9.other, bf16[192,640]{1,0:T(8,128)(2,1)S(1)} %collective-permute-done.1.refs_1_.refs_0_, ...), custom_call_target="tpu_custom_call" | custom-call | tf_op jit(solution)/shard_map/pallas_call | solution.py:164
  50.8 3.2 %collective-permute-start.13 = (bf16[128,640]{1,0:T(8,128)(2,1)S(1)}, bf16[128,640]{1,0:T(8,128)(2,1)S(1)}, u32[]{:S(2)}, u32[]{:S(2)}) collective-permute-start(bf16[128,640]{1,0:T(8,128)(2,1)S(1)} %get-tuple-element.49), channel_id=1, source_target_pairs={{0,4},{1,7},{2,6},{3,5},{4,0},{5,3},{6,2},{7,1},{8,12},{9,15},{10,... | collective-permute-start | bytes 491528 | tf_op jit(solution)/shard_map/ppermute | solution.py:111
  54.0 1.2 %shard_map.42 = bf16[128,640]{1,0:T(8,128)(2,1)S(1)} custom-call(bf16[2,512,640]{2,1,0:T(8,128)(2,1)S(1)} %shard_map.39.own, bf16[2,512,640]{2,1,0:T(8,128)(2,1)S(1)} %collective-permute-done.9.other, bf16[128,640]{1,0:T(8,128)(2,1)S(1)} %collective-permute-done.10.refs_0_), custom_call_target="tpu_custom_call" | custom-call | tf_op jit(solution)/shard_map/pallas_call | solution.py:164
  55.2 1.2 %collective-permute-start.12 = (bf16[128,640]{1,0:T(8,128)(2,1)S(1)}, bf16[128,640]{1,0:T(8,128)(2,1)S(1)}, u32[]{:S(2)}, u32[]{:S(2)}) collective-permute-start(bf16[128,640]{1,0:T(8,128)(2,1)S(1)} %shard_map.42), channel_id=1, source_target_pairs={{0,12},{1,15},{2,14},{3,13},{4,8},{5,11},{6,10},{7,9},{8,4},{9,7},... | collective-permute-start | bytes 491528 | tf_op jit(solution)/shard_map/ppermute | solution.py:111
  56.4 6.7 %collective-permute-done.14.refs_4_ = bf16[128,640]{1,0:T(8,128)(2,1)S(1)} collective-permute-done((bf16[128,640]{1,0:T(8,128)(2,1)S(1)}, bf16[128,640]{1,0:T(8,128)(2,1)S(1)}, u32[]{:S(2)}, u32[]{:S(2)}) %collective-permute-start.14) | collective-permute-done | bytes 163872 | tf_op jit(solution)/shard_map/ppermute | solution.py:111
  63.1 2.9 %collective-permute-start.17 = (bf16[64,640]{1,0:T(8,128)(2,1)S(1)}, bf16[64,640]{1,0:T(8,128)(2,1)S(1)}, u32[]{:S(2)}, u32[]{:S(2)}) collective-permute-start(bf16[64,640]{1,0:T(8,128)(2,1)S(1)} %slice.16), channel_id=1, source_target_pairs={{0,1},{1,0},{2,3},{3,2},{4,5},{5,4},{6,7},{7,6},{8,9},{9,8},{10,11... | collective-permute-start | bytes 245768 | tf_op jit(solution)/shard_map/ppermute | solution.py:114
  67.5 0.8 %shard_map.43.refs_2_ = bf16[64,5120]{1,0:T(8,128)(2,1)} custom-call(s32[1]{0:T(128)} %bitcast.chip_ref, s32[1]{0:T(128)} %bitcast.1.core_ref, bf16[128,640]{1,0:T(8,128)(2,1)S(1)} %collective-permute-done.13.refs_0_, bf16[64,640]{1,0:T(8,128)(2,1)S(1)} %collective-permute-done.15.refs_1_, bf16[128,640]{1,0:T(8,128)(2,1)S(1)} %collective-permute-done.11.refs_2_, ...), custom_call_target="tpu_custom_call" | custom-call | tf_op jit(solution)/shard_map/pallas_call | solution.py:178
  68.7 0.9 %collective-permute-done.18.refs_1_ = bf16[64,640]{1,0:T(8,128)(2,1)S(1)} collective-permute-done((bf16[64,640]{1,0:T(8,128)(2,1)S(1)}, bf16[64,640]{1,0:T(8,128)(2,1)S(1)}, u32[]{:S(2)}, u32[]{:S(2)}) %collective-permute-start.18) | collective-permute-done | bytes 81952 | tf_op jit(solution)/shard_map/ppermute | solution.py:114
  69.7 0.7 shard_map.44
  (28 shorter events, 3.1 us)
Async XLA Ops:
  1.2 25.6 %collective-permute-start.1 = (bf16[192,640]{1,0:T(8,128)(2,1)S(1)}, bf16[192,640]{1,0:T(8,128)(2,1)S(1)}, u32[]{:S(2)}, u32[]{:S(2)}) collective-permute-start(bf16[192,640]{1,0:T(8,128)(2,1)S(1)} %get-tuple-element.30), channel_id=1, source_target_pairs={{0,4},{1,7},{2,6},{3,5},{4,0},{5,3},{6,2},{7,1},{8,12},{9,15},{10,... | collective-permute-start | bytes 737288 | tf_op jit(solution)/shard_map/ppermute | solution.py:111
  4.3 12.6 %collective-permute-start.2 = (bf16[128,640]{1,0:T(8,128)(2,1)S(1)}, bf16[128,640]{1,0:T(8,128)(2,1)S(1)}, u32[]{:S(2)}, u32[]{:S(2)}) collective-permute-start(bf16[128,640]{1,0:T(8,128)(2,1)S(1)} %get-tuple-element.31), channel_id=1, source_target_pairs={{0,15},{1,12},{2,13},{3,14},{4,11},{5,8},{6,9},{7,10},{8,7},{9,4},... | collective-permute-start | bytes 491528 | tf_op jit(solution)/shard_map/ppermute | solution.py:111
  6.8 19.9 %collective-permute-start = (bf16[128,640]{1,0:T(8,128)(2,1)S(1)}, bf16[128,640]{1,0:T(8,128)(2,1)S(1)}, u32[]{:S(2)}, u32[]{:S(2)}) collective-permute-start(bf16[128,640]{1,0:T(8,128)(2,1)S(1)} %get-tuple-element.29), channel_id=1, source_target_pairs={{0,12},{1,15},{2,14},{3,13},{4,8},{5,11},{6,10},{7,9},{8,4},{9,7},... | collective-permute-start | bytes 491528 | tf_op jit(solution)/shard_map/ppermute | solution.py:111
  9.7 1.7 %collective-permute-start.5 = (bf16[64,640]{1,0:T(8,128)(2,1)S(1)}, bf16[64,640]{1,0:T(8,128)(2,1)S(1)}, u32[]{:S(2)}, u32[]{:S(2)}) collective-permute-start(bf16[64,640]{1,0:T(8,128)(2,1)S(1)} %get-tuple-element.39), channel_id=1, source_target_pairs={{0,1},{1,0},{2,3},{3,2},{4,5},{5,4},{6,7},{7,6},{8,9},{9,8},{10,11... | collective-permute-start | bytes 245768 | tf_op jit(solution)/shard_map/ppermute | solution.py:114
  10.5 27.7 %collective-permute-start.3 = (bf16[192,640]{1,0:T(8,128)(2,1)S(1)}, bf16[192,640]{1,0:T(8,128)(2,1)S(1)}, u32[]{:S(2)}, u32[]{:S(2)}) collective-permute-start(bf16[192,640]{1,0:T(8,128)(2,1)S(1)} %get-tuple-element.35), channel_id=1, source_target_pairs={{0,8},{1,11},{2,10},{3,9},{4,12},{5,15},{6,14},{7,13},{8,0},{9,3},... | collective-permute-start | bytes 737288 | tf_op jit(solution)/shard_map/ppermute | solution.py:111
  11.4 26.8 %collective-permute-start.4 = (bf16[192,640]{1,0:T(8,128)(2,1)S(1)}, bf16[192,640]{1,0:T(8,128)(2,1)S(1)}, u32[]{:S(2)}, u32[]{:S(2)}) collective-permute-start(bf16[192,640]{1,0:T(8,128)(2,1)S(1)} %get-tuple-element.36), channel_id=1, source_target_pairs={{0,7},{1,4},{2,5},{3,6},{4,3},{5,0},{6,1},{7,2},{8,15},{9,12},{10,... | collective-permute-start | bytes 737288 | tf_op jit(solution)/shard_map/ppermute | solution.py:111
  16.9 26.3 %collective-permute-start.7 = (bf16[192,640]{1,0:T(8,128)(2,1)S(1)}, bf16[192,640]{1,0:T(8,128)(2,1)S(1)}, u32[]{:S(2)}, u32[]{:S(2)}) collective-permute-start(bf16[192,640]{1,0:T(8,128)(2,1)S(1)} %get-tuple-element.41), channel_id=1, source_target_pairs={{0,11},{1,8},{2,9},{3,10},{4,15},{5,12},{6,13},{7,14},{8,3},{9,0},... | collective-permute-start | bytes 737288 | tf_op jit(solution)/shard_map/ppermute | solution.py:111
  26.8 16.4 %collective-permute-start.8 = (bf16[192,640]{1,0:T(8,128)(2,1)S(1)}, bf16[192,640]{1,0:T(8,128)(2,1)S(1)}, u32[]{:S(2)}, u32[]{:S(2)}) collective-permute-start(bf16[192,640]{1,0:T(8,128)(2,1)S(1)} %get-tuple-element.42), channel_id=1, source_target_pairs={{0,3},{1,0},{2,1},{3,2},{4,7},{5,4},{6,5},{7,6},{8,11},{9,8},{10,9... | collective-permute-start | bytes 737288 | tf_op jit(solution)/shard_map/ppermute | solution.py:111
  26.8 16.4 %collective-permute-start.6 = (bf16[192,640]{1,0:T(8,128)(2,1)S(1)}, bf16[192,640]{1,0:T(8,128)(2,1)S(1)}, u32[]{:S(2)}, u32[]{:S(2)}) collective-permute-start(bf16[192,640]{1,0:T(8,128)(2,1)S(1)} %get-tuple-element.40), channel_id=1, source_target_pairs={{0,0},{1,3},{2,2},{3,1},{4,4},{5,7},{6,6},{7,5},{8,8},{9,11},{10,1... | collective-permute-start | bytes 737288 | tf_op jit(solution)/shard_map/ppermute | solution.py:111
  43.3 3.6 %collective-permute-start.9 = (bf16[2,512,640]{2,1,0:T(8,128)(2,1)S(1)}, bf16[2,512,640]{2,1,0:T(8,128)(2,1)S(1)}, u32[]{:S(2)}, u32[]{:S(2)}) collective-permute-start(bf16[2,512,640]{2,1,0:T(8,128)(2,1)S(1)} %shard_map.39.own), channel_id=1, source_target_pairs={{0,1},{1,0},{2,3},{3,2},{4,5},{5,4},{6,7},{7,6},{8,9},{9,8},{10,11... | collective-permute-start | bytes 3932168 | tf_op jit(solution)/shard_map/ppermute | solution.py:114
  43.5 10.5 %collective-permute-start.10 = (bf16[128,640]{1,0:T(8,128)(2,1)S(1)}, bf16[128,640]{1,0:T(8,128)(2,1)S(1)}, u32[]{:S(2)}, u32[]{:S(2)}) collective-permute-start(bf16[128,640]{1,0:T(8,128)(2,1)S(1)} %constant_dynamic-update-slice_fusion), channel_id=1, source_target_pairs={{0,12},{1,15},{2,14},{3,13},{4,8},{5,11},{6,10},{7,9},{8,4},{9,7},... | collective-permute-start | bytes 491528 | tf_op jit(solution)/shard_map/ppermute | solution.py:111
  50.0 4.0 %collective-permute-start.11 = (bf16[128,640]{1,0:T(8,128)(2,1)S(1)}, bf16[128,640]{1,0:T(8,128)(2,1)S(1)}, u32[]{:S(2)}, u32[]{:S(2)}) collective-permute-start(bf16[128,640]{1,0:T(8,128)(2,1)S(1)} %get-tuple-element.47), channel_id=1, source_target_pairs={{0,0},{1,3},{2,2},{3,1},{4,4},{5,7},{6,6},{7,5},{8,8},{9,11},{10,1... | collective-permute-start | bytes 491528 | tf_op jit(solution)/shard_map/ppermute | solution.py:111
  50.7 12.4 %collective-permute-start.14 = (bf16[128,640]{1,0:T(8,128)(2,1)S(1)}, bf16[128,640]{1,0:T(8,128)(2,1)S(1)}, u32[]{:S(2)}, u32[]{:S(2)}) collective-permute-start(bf16[128,640]{1,0:T(8,128)(2,1)S(1)} %shard_map.40), channel_id=1, source_target_pairs={{0,8},{1,11},{2,10},{3,9},{4,12},{5,15},{6,14},{7,13},{8,0},{9,3},... | collective-permute-start | bytes 491528 | tf_op jit(solution)/shard_map/ppermute | solution.py:111
  50.8 12.3 %collective-permute-start.13 = (bf16[128,640]{1,0:T(8,128)(2,1)S(1)}, bf16[128,640]{1,0:T(8,128)(2,1)S(1)}, u32[]{:S(2)}, u32[]{:S(2)}) collective-permute-start(bf16[128,640]{1,0:T(8,128)(2,1)S(1)} %get-tuple-element.49), channel_id=1, source_target_pairs={{0,4},{1,7},{2,6},{3,5},{4,0},{5,3},{6,2},{7,1},{8,12},{9,15},{10,... | collective-permute-start | bytes 491528 | tf_op jit(solution)/shard_map/ppermute | solution.py:111
  55.2 13.1 %collective-permute-start.12 = (bf16[128,640]{1,0:T(8,128)(2,1)S(1)}, bf16[128,640]{1,0:T(8,128)(2,1)S(1)}, u32[]{:S(2)}, u32[]{:S(2)}) collective-permute-start(bf16[128,640]{1,0:T(8,128)(2,1)S(1)} %shard_map.42), channel_id=1, source_target_pairs={{0,12},{1,15},{2,14},{3,13},{4,8},{5,11},{6,10},{7,9},{8,4},{9,7},... | collective-permute-start | bytes 491528 | tf_op jit(solution)/shard_map/ppermute | solution.py:111
  63.1 3.9 %collective-permute-start.17 = (bf16[64,640]{1,0:T(8,128)(2,1)S(1)}, bf16[64,640]{1,0:T(8,128)(2,1)S(1)}, u32[]{:S(2)}, u32[]{:S(2)}) collective-permute-start(bf16[64,640]{1,0:T(8,128)(2,1)S(1)} %slice.16), channel_id=1, source_target_pairs={{0,1},{1,0},{2,3},{3,2},{4,5},{5,4},{6,7},{7,6},{8,9},{9,8},{10,11... | collective-permute-start | bytes 245768 | tf_op jit(solution)/shard_map/ppermute | solution.py:114
  66.0 1.3 %collective-permute-start.16 = (bf16[64,640]{1,0:T(8,128)(2,1)S(1)}, bf16[64,640]{1,0:T(8,128)(2,1)S(1)}, u32[]{:S(2)}, u32[]{:S(2)}) collective-permute-start(bf16[64,640]{1,0:T(8,128)(2,1)S(1)} %slice.13), channel_id=1, source_target_pairs={{0,1},{1,0},{2,3},{3,2},{4,5},{5,4},{6,7},{7,6},{8,9},{9,8},{10,11... | collective-permute-start | bytes 245768 | tf_op jit(solution)/shard_map/ppermute | solution.py:114
  66.1 1.4 %collective-permute-start.15 = (bf16[64,640]{1,0:T(8,128)(2,1)S(1)}, bf16[64,640]{1,0:T(8,128)(2,1)S(1)}, u32[]{:S(2)}, u32[]{:S(2)}) collective-permute-start(bf16[64,640]{1,0:T(8,128)(2,1)S(1)} %slice.12), channel_id=1, source_target_pairs={{0,1},{1,0},{2,3},{3,2},{4,5},{5,4},{6,7},{7,6},{8,9},{9,8},{10,11... | collective-permute-start | bytes 245768 | tf_op jit(solution)/shard_map/ppermute | solution.py:114
  68.3 1.3 %collective-permute-start.18 = (bf16[64,640]{1,0:T(8,128)(2,1)S(1)}, bf16[64,640]{1,0:T(8,128)(2,1)S(1)}, u32[]{:S(2)}, u32[]{:S(2)}) collective-permute-start(bf16[64,640]{1,0:T(8,128)(2,1)S(1)} %slice.15), channel_id=1, source_target_pairs={{0,1},{1,0},{2,3},{3,2},{4,5},{5,4},{6,7},{7,6},{8,9},{9,8},{10,11... | collective-permute-start | bytes 245768 | tf_op jit(solution)/shard_map/ppermute | solution.py:114

commit v12 on v0

--- a/solution.py
+++ b/solution.py
@@ -149,10 +149,12 @@
     outs = attend((4, 5))
     outs |= attend(NEAR + (0,), (outs[4],))
     outs |= attend(LAST, (outs[0],))
-    back = {k: across(outs[k], k) for k in (4, 5) + LAST + (0,)}
-    back[2] = across(lax.optimization_barrier((outs[2], outs[LAST[0]]))[0], 2)
-    for k, before in ((3, 5), (1, 4)):
-        back[k] = across(lax.optimization_barrier((outs[k], outs[LAST[0]], back[before]))[0], k)
+    back = {k: across(outs[k], k) for k in (4, 5, 1) + LAST + (0,)}
+    def after(array, *others):
+        return lax.optimization_barrier((array, *others))[0]
+
+    back[2] = across(after(outs[2], outs[LAST[0]]), 2)
+    back[3] = across(after(outs[3], outs[LAST[0]], back[5]), 3)
 
     def unpack(order, so_far=()):
         return pl.pallas_call(
@@ -166,7 +168,7 @@
             cost_estimate=FREE,
         )(chip, *[back[k] for k in order], *so_far)
 
-    result = unpack(LAST + (3, 1), (unpack((0, 4, 5, 2)),))
+    result = unpack(LAST + (3, 2), (unpack((0, 4, 5, 1)),))
     return result.reshape(layers, tok_rows, width)
 
 

time: 68.2 us -> 67.9 us (level)
  waiting for transfers between devices: 20.1 us -> 19 us
  starting transfers between devices: 39.2 us -> 40 us
    ppermute x16, waiting for transfers between devices: 20 us -> 19 us  [across(): lax.ppermute(piece, 'chip', [(i, i ^ k) for i in range(chips)])]
    ppermute x16, starting transfers between devices: 39.2 us -> 39.9 us  [across(): lax.ppermute(piece, 'chip', [(i, i ^ k) for i in range(chips)])]
  transfers between devices with their start and end apart: 17 -> 17, of which waited for: 8 -> 6; matrix products, arithmetic and copies ran while one was open for 0% -> 0% of each run, Pallas kernels for 10% -> 10%
where the time goes in v12:
time: 67.9 us; the launch traced here: 67.7 us
  starting transfers between devices  40 us (59%)
  waiting for transfers between devices  19 us (28%)
  Pallas kernels  8.67 us (13%)
    ppermute x16, starting transfers between devices, across(): lax.ppermute(piece, 'chip', [(i, i ^ k) for i in range(chips)])  39.9 us
    ppermute x16, waiting for transfers between devices, across(): lax.ppermute(piece, 'chip', [(i, i ^ k) for i in range(chips)])  19 us
    pallas_call x3, Pallas kernels, attend(): call(body, 2 + len(ks), [shape(rows, gw)] * len(ks))(own, other, *pieces)  4.34 us
    pallas_call x2, Pallas kernels, pack(): pl.pallas_call(functools.partial(pack_body, rows, gw, layout), in_specs=[...  2.73 us
    pallas_call x2, Pallas kernels, unpack(): pl.pallas_call(functools.partial(unpack_body, gw, order), in_specs=[SMEM]...  1.5 us
  transfers between devices with their start and end apart: 17, of which 6 were waited for; matrix products, arithmetic and copies ran while one was open for 0% of the time, Pallas kernels for 10%

profile of v12, /device:TPU:0, one launch (start us, length us, event | category | flops | bytes accessed | tf_op | source)
XLA Modules:
  0.0 67.7 jit_solution(7391975380307697668)
XLA Ops:
  0.0 1.2 %shard_map.37 = (bf16[128,640]{1,0:T(8,128)(2,1)S(1)}, bf16[192,640]{1,0:T(8,128)(2,1)S(1)}, bf16[128,640]{1,0:T(8,128)(2,1)S(1)}) custom-call(s32[1]{0:T(128)} %bitcast.chip_ref, bf16[64,5120]{1,0:T(8,128)(2,1)} %refs_0_.2, bf16[64,5120]{1,0:T(8,128)(2,1)} %refs_1_.2, bf16[64,5120]{1,0:T(8,128)(2,1)} %bitcast.3), custom_call_target="tpu_custom_call" | custom-call | tf_op jit(solution)/shard_map/pallas_call | solution.py:121
  1.2 6.1 %collective-permute-start.2 = (bf16[128,640]{1,0:T(8,128)(2,1)S(1)}, bf16[128,640]{1,0:T(8,128)(2,1)S(1)}, u32[]{:S(2)}, u32[]{:S(2)}) collective-permute-start(bf16[128,640]{1,0:T(8,128)(2,1)S(1)} %get-tuple-element.36), channel_id=1, source_target_pairs={{0,14},{2,12},{4,10},{6,8},{8,6},{10,4},{12,2},{14,0},{1,15},{3,13... | collective-permute-start | bytes 491528 | tf_op jit(solution)/shard_map/ppermute | solution.py:100
  7.5 1.5 %shard_map.38 = (bf16[192,640]{1,0:T(8,128)(2,1)S(1)}, bf16[192,640]{1,0:T(8,128)(2,1)S(1)}, bf16[192,640]{1,0:T(8,128)(2,1)S(1)}, bf16[192,640]{1,0:T(8,128)(2,...) custom-call(s32[1]{0:T(128)} %bitcast.chip_ref, ...), custom_call_target="tpu_custom_call" | custom-call | tf_op jit(solution)/shard_map/pallas_call | solution.py:121
  9.0 4.2 %collective-permute-start.3 = (bf16[192,640]{1,0:T(8,128)(2,1)S(1)}, bf16[192,640]{1,0:T(8,128)(2,1)S(1)}, u32[]{:S(2)}, u32[]{:S(2)}) collective-permute-start(bf16[192,640]{1,0:T(8,128)(2,1)S(1)} %get-tuple-element.40), channel_id=1, source_target_pairs={{0,8},{2,10},{4,12},{6,14},{8,0},{10,2},{12,4},{14,6},{1,9},{3,11}... | collective-permute-start | bytes 737288 | tf_op jit(solution)/shard_map/ppermute | solution.py:100
  13.3 1.5 %collective-permute-start.5 = (bf16[192,640]{1,0:T(8,128)(2,1)S(1)}, bf16[192,640]{1,0:T(8,128)(2,1)S(1)}, u32[]{:S(2)}, u32[]{:S(2)}) collective-permute-start(bf16[192,640]{1,0:T(8,128)(2,1)S(1)} %get-tuple-element.42), channel_id=1, source_target_pairs={{0,2},{2,0},{4,6},{6,4},{8,10},{10,8},{12,14},{14,12},{1,3},{3,1},... | collective-permute-start | bytes 737288 | tf_op jit(solution)/shard_map/ppermute | solution.py:100
  14.7 1.4 %collective-permute-done.refs_0_ = bf16[128,640]{1,0:T(8,128)(2,1)S(1)} collective-permute-done((bf16[128,640]{1,0:T(8,128)(2,1)S(1)}, bf16[128,640]{1,0:T(8,128)(2,1)S(1)}, u32[]{:S(2)}, u32[]{:S(2)}) %collective-permute-start) | collective-permute-done | bytes 163872 | tf_op jit(solution)/shard_map/ppermute | solution.py:100
  16.2 12.6 %collective-permute-start.6 = (bf16[192,640]{1,0:T(8,128)(2,1)S(1)}, bf16[192,640]{1,0:T(8,128)(2,1)S(1)}, u32[]{:S(2)}, u32[]{:S(2)}) collective-permute-start(bf16[192,640]{1,0:T(8,128)(2,1)S(1)} %get-tuple-element.43), channel_id=1, source_target_pairs={{0,10},{2,8},{4,14},{6,12},{8,2},{10,0},{12,6},{14,4},{1,11},{3,9}... | collective-permute-start | bytes 737288 | tf_op jit(solution)/shard_map/ppermute | solution.py:100
  28.8 9.0 %collective-permute-done.3.refs_3_.refs_0_ = bf16[192,640]{1,0:T(8,128)(2,1)S(1)} collective-permute-done((bf16[192,640]{1,0:T(8,128)(2,1)S(1)}, bf16[192,640]{1,0:T(8,128)(2,1)S(1)}, u32[]{:S(2)}, u32[]{:S(2)}) %collective-permute-start.3) | collective-permute-done | bytes 245792 | tf_op jit(solution)/shard_map/ppermute | solution.py:100
  37.9 4.3 %collective-permute-done.6.refs_6_.refs_1_ = bf16[192,640]{1,0:T(8,128)(2,1)S(1)} collective-permute-done((bf16[192,640]{1,0:T(8,128)(2,1)S(1)}, bf16[192,640]{1,0:T(8,128)(2,1)S(1)}, u32[]{:S(2)}, u32[]{:S(2)}) %collective-permute-start.6) | collective-permute-done | bytes 245792 | tf_op jit(solution)/shard_map/ppermute | solution.py:100
  42.3 2.6 %collective-permute-start.8 = (bf16[64,640]{1,0:T(8,128)(2,1)S(1)}, bf16[64,640]{1,0:T(8,128)(2,1)S(1)}, u32[]{:S(2)}, u32[]{:S(2)}) collective-permute-start(bf16[64,640]{1,0:T(8,128)(2,1)S(1)} %get-tuple-element.45), channel_id=1, source_target_pairs={{0,12},{2,14},{4,8},{6,10},{8,4},{10,6},{12,0},{14,2},{1,13},{3,15... | collective-permute-start | bytes 245768 | tf_op jit(solution)/shard_map/ppermute | solution.py:100
  44.9 2.3 %collective-permute-start.9 = (bf16[64,640]{1,0:T(8,128)(2,1)S(1)}, bf16[64,640]{1,0:T(8,128)(2,1)S(1)}, u32[]{:S(2)}, u32[]{:S(2)}) collective-permute-start(bf16[64,640]{1,0:T(8,128)(2,1)S(1)} %get-tuple-element.46), channel_id=1, source_target_pairs={{0,14},{2,12},{4,10},{6,8},{8,6},{10,4},{12,2},{14,0},{1,15},{3,13... | collective-permute-start | bytes 245768 | tf_op jit(solution)/shard_map/ppermute | solution.py:100
  47.2 1.2 %shard_map.40 = (bf16[64,640]{1,0:T(8,128)(2,1)S(1)}, bf16[64,640]{1,0:T(8,128)(2,1)S(1)}) custom-call(bf16[2,512,640]{2,1,0:T(8,128)(2,1)S(1)} %shard_map.39.own, bf16[2,512,640]{2,1,0:T(8,128)(2,1)S(1)} %collective-permute-done.7.other, bf16[192,640]{1,0:T(8,128)(2,1)S(1)} %collective-permute-done.3.refs_3_.refs_0_, ...), custom_call_target="tpu_custom_call" | custom-call | tf_op jit(solution)/shard_map/pallas_call | solution.py:146
  48.4 2.0 %shard_map.41 = (bf16[64,640]{1,0:T(8,128)(2,1)S(1)}, bf16[64,640]{1,0:T(8,128)(2,1)S(1)}, bf16[64,640]{1,0:T(8,128)(2,1)S(1)}, bf16[64,640]{1,0:T(8,128)(2,1)S(1)}) custom-call(bf16[2,512,640]{2,1,0:T(8,128)(2,1)S(1)} %shard_map.39.own, bf16[2,512,640]{2,1,0:T(8,128)(2,1)S(1)} %collective-permute-done.7.other, ...), custom_call_target="tpu_custom_call" | custom-call | tf_op jit(solution)/shard_map/pallas_call | solution.py:146
  50.4 0.6 collective-permute-start.16
  51.0 3.9 %collective-permute-start.15 = (bf16[64,640]{1,0:T(8,128)(2,1)S(1)}, bf16[64,640]{1,0:T(8,128)(2,1)S(1)}, u32[]{:S(2)}, u32[]{:S(2)}) collective-permute-start(bf16[64,640]{1,0:T(8,128)(2,1)S(1)} %get-tuple-element.47), channel_id=1, source_target_pairs={{0,8},{2,10},{4,12},{6,14},{8,0},{10,2},{12,4},{14,6},{1,9},{3,11}... | collective-permute-start | bytes 245768 | tf_op jit(solution)/shard_map/ppermute | solution.py:100
  54.9 1.2 %shard_map.42 = (bf16[64,640]{1,0:T(8,128)(2,1)S(1)}, bf16[64,640]{1,0:T(8,128)(2,1)S(1)}) custom-call(bf16[2,512,640]{2,1,0:T(8,128)(2,1)S(1)} %shard_map.39.own, bf16[2,512,640]{2,1,0:T(8,128)(2,1)S(1)} %collective-permute-done.7.other, bf16[64,640]{1,0:T(8,128)(2,1)S(1)} %collective-permute-done.8.refs_0_, bf16[64,640]{1,0:T(8,128)(2,1)S(1)} %collective-permute-done.9.refs_1_), custom_call_target="tpu_custom_call" | custom-call | tf_op jit(solution)/shard_map/pallas_call | solution.py:146
  56.1 2.6 %collective-permute-start.10 = (bf16[64,640]{1,0:T(8,128)(2,1)S(1)}, bf16[64,640]{1,0:T(8,128)(2,1)S(1)}, u32[]{:S(2)}, u32[]{:S(2)}) collective-permute-start(bf16[64,640]{1,0:T(8,128)(2,1)S(1)} %get-tuple-element.55), channel_id=1, source_target_pairs={{0,12},{2,14},{4,8},{6,10},{8,4},{10,6},{12,0},{14,2},{1,13},{3,15... | collective-permute-start | bytes 245768 | tf_op jit(solution)/shard_map/ppermute | solution.py:100
  58.7 1.2 %collective-permute-start.11 = (bf16[64,640]{1,0:T(8,128)(2,1)S(1)}, bf16[64,640]{1,0:T(8,128)(2,1)S(1)}, u32[]{:S(2)}, u32[]{:S(2)}) collective-permute-start(bf16[64,640]{1,0:T(8,128)(2,1)S(1)} %get-tuple-element.56), channel_id=1, source_target_pairs={{0,14},{2,12},{4,10},{6,8},{8,6},{10,4},{12,2},{14,0},{1,15},{3,13... | collective-permute-start | bytes 245768 | tf_op jit(solution)/shard_map/ppermute | solution.py:100
  59.9 2.1 %collective-permute-start.13 = (bf16[64,640]{1,0:T(8,128)(2,1)S(1)}, bf16[64,640]{1,0:T(8,128)(2,1)S(1)}, u32[]{:S(2)}, u32[]{:S(2)}) collective-permute-start(bf16[64,640]{1,0:T(8,128)(2,1)S(1)} %get-tuple-element.59), channel_id=1, source_target_pairs={{0,6},{2,4},{4,2},{6,0},{8,14},{10,12},{12,10},{14,8},{1,7},{3,5},... | collective-permute-start | bytes 245768 | tf_op jit(solution)/shard_map/ppermute | solution.py:100
  62.0 0.8 %shard_map.43.refs_4_ = bf16[64,5120]{1,0:T(8,128)(2,1)} custom-call(s32[1]{0:T(128)} %bitcast.chip_ref, bf16[64,640]{1,0:T(8,128)(2,1)S(1)} %get-tuple-element.52.refs_0_, bf16[64,640]{1,0:T(8,128)(2,1)S(1)} %collective-permute-done.15.refs_1_, bf16[64,640]{1,0:T(8,128)(2,1)S(1)} %collective-permute-done.12.refs_2_, ...), custom_call_target="tpu_custom_call" | custom-call | tf_op jit(solution)/shard_map/pallas_call | solution.py:160
  62.8 2.6 %collective-permute-done.14.refs_3_ = bf16[64,640]{1,0:T(8,128)(2,1)S(1)} collective-permute-done((bf16[64,640]{1,0:T(8,128)(2,1)S(1)}, bf16[64,640]{1,0:T(8,128)(2,1)S(1)}, u32[]{:S(2)}, u32[]{:S(2)}) %collective-permute-start.14) | collective-permute-done | bytes 81952 | tf_op jit(solution)/shard_map/ppermute | solution.py:100
  65.4 0.7 %collective-permute-done.11.refs_1_ = bf16[64,640]{1,0:T(8,128)(2,1)S(1)} collective-permute-done((bf16[64,640]{1,0:T(8,128)(2,1)S(1)}, bf16[64,640]{1,0:T(8,128)(2,1)S(1)}, u32[]{:S(2)}, u32[]{:S(2)}) %collective-permute-start.11) | collective-permute-done | bytes 81952 | tf_op jit(solution)/shard_map/ppermute | solution.py:100
  66.1 0.9 %collective-permute-done.13.refs_2_ = bf16[64,640]{1,0:T(8,128)(2,1)S(1)} collective-permute-done((bf16[64,640]{1,0:T(8,128)(2,1)S(1)}, bf16[64,640]{1,0:T(8,128)(2,1)S(1)}, u32[]{:S(2)}, u32[]{:S(2)}) %collective-permute-start.13) | collective-permute-done | bytes 81952 | tf_op jit(solution)/shard_map/ppermute | solution.py:100
  66.9 0.8 %shard_map.44 = bf16[64,5120]{1,0:T(8,128)(2,1)} custom-call(s32[1]{0:T(128)} %bitcast.chip_ref, bf16[64,640]{1,0:T(8,128)(2,1)S(1)} %collective-permute-done.10.refs_0_, bf16[64,640]{1,0:T(8,128)(2,1)S(1)} %collective-permute-done.11.refs_1_, bf16[64,640]{1,0:T(8,128)(2,1)S(1)} %collective-permute-done.13.refs_2_, ...), custom_call_target="tpu_custom_call", output_to_operand_aliasing={{}: (5, {})} | custom-call | tf_op jit(solution)/shard_map/pallas_call | solution.py:160
  (18 shorter events, 0.5 us)
Async XLA Ops:
  1.2 12.1 %collective-permute-start.2 = (bf16[128,640]{1,0:T(8,128)(2,1)S(1)}, bf16[128,640]{1,0:T(8,128)(2,1)S(1)}, u32[]{:S(2)}, u32[]{:S(2)}) collective-permute-start(bf16[128,640]{1,0:T(8,128)(2,1)S(1)} %get-tuple-element.36), channel_id=1, source_target_pairs={{0,14},{2,12},{4,10},{6,8},{8,6},{10,4},{12,2},{14,0},{1,15},{3,13... | collective-permute-start | bytes 491528 | tf_op jit(solution)/shard_map/ppermute | solution.py:100
  7.3 8.9 %collective-permute-start = (bf16[128,640]{1,0:T(8,128)(2,1)S(1)}, bf16[128,640]{1,0:T(8,128)(2,1)S(1)}, u32[]{:S(2)}, u32[]{:S(2)}) collective-permute-start(bf16[128,640]{1,0:T(8,128)(2,1)S(1)} %get-tuple-element.34), channel_id=1, source_target_pairs={{0,12},{2,14},{4,8},{6,10},{8,4},{10,6},{12,0},{14,2},{1,13},{3,15... | collective-permute-start | bytes 491528 | tf_op jit(solution)/shard_map/ppermute | solution.py:100
  7.5 21.3 %collective-permute-start.1 = (bf16[192,640]{1,0:T(8,128)(2,1)S(1)}, bf16[192,640]{1,0:T(8,128)(2,1)S(1)}, u32[]{:S(2)}, u32[]{:S(2)}) collective-permute-start(bf16[192,640]{1,0:T(8,128)(2,1)S(1)} %get-tuple-element.35), channel_id=1, source_target_pairs={{0,4},{2,6},{4,0},{6,2},{8,12},{10,14},{12,8},{14,10},{1,5},{3,7},... | collective-permute-start | bytes 737288 | tf_op jit(solution)/shard_map/ppermute | solution.py:100
  9.0 28.8 %collective-permute-start.3 = (bf16[192,640]{1,0:T(8,128)(2,1)S(1)}, bf16[192,640]{1,0:T(8,128)(2,1)S(1)}, u32[]{:S(2)}, u32[]{:S(2)}) collective-permute-start(bf16[192,640]{1,0:T(8,128)(2,1)S(1)} %get-tuple-element.40), channel_id=1, source_target_pairs={{0,8},{2,10},{4,12},{6,14},{8,0},{10,2},{12,4},{14,6},{1,9},{3,11}... | collective-permute-start | bytes 737288 | tf_op jit(solution)/shard_map/ppermute | solution.py:100
  13.3 24.6 %collective-permute-start.4 = (bf16[192,640]{1,0:T(8,128)(2,1)S(1)}, bf16[192,640]{1,0:T(8,128)(2,1)S(1)}, u32[]{:S(2)}, u32[]{:S(2)}) collective-permute-start(bf16[192,640]{1,0:T(8,128)(2,1)S(1)} %get-tuple-element.41), channel_id=1, source_target_pairs={{0,6},{2,4},{4,2},{6,0},{8,14},{10,12},{12,10},{14,8},{1,7},{3,5},... | collective-permute-start | bytes 737288 | tf_op jit(solution)/shard_map/ppermute | solution.py:100
  13.3 24.6 %collective-permute-start.5 = (bf16[192,640]{1,0:T(8,128)(2,1)S(1)}, bf16[192,640]{1,0:T(8,128)(2,1)S(1)}, u32[]{:S(2)}, u32[]{:S(2)}) collective-permute-start(bf16[192,640]{1,0:T(8,128)(2,1)S(1)} %get-tuple-element.42), channel_id=1, source_target_pairs={{0,2},{2,0},{4,6},{6,4},{8,10},{10,8},{12,14},{14,12},{1,3},{3,1},... | collective-permute-start | bytes 737288 | tf_op jit(solution)/shard_map/ppermute | solution.py:100
  16.2 26.0 %collective-permute-start.6 = (bf16[192,640]{1,0:T(8,128)(2,1)S(1)}, bf16[192,640]{1,0:T(8,128)(2,1)S(1)}, u32[]{:S(2)}, u32[]{:S(2)}) collective-permute-start(bf16[192,640]{1,0:T(8,128)(2,1)S(1)} %get-tuple-element.43), channel_id=1, source_target_pairs={{0,10},{2,8},{4,14},{6,12},{8,2},{10,0},{12,6},{14,4},{1,11},{3,9}... | collective-permute-start | bytes 737288 | tf_op jit(solution)/shard_map/ppermute | solution.py:100
  42.3 4.9 %collective-permute-start.7 = (bf16[2,512,640]{2,1,0:T(8,128)(2,1)S(1)}, bf16[2,512,640]{2,1,0:T(8,128)(2,1)S(1)}, u32[]{:S(2)}, u32[]{:S(2)}) collective-permute-start(bf16[2,512,640]{2,1,0:T(8,128)(2,1)S(1)} %shard_map.39.own), channel_id=1, source_target_pairs={{0,1},{1,0},{2,3},{3,2},{4,5},{5,4},{6,7},{7,6},{8,9},{9,8},{10,11... | collective-permute-start | bytes 3932168 | tf_op jit(solution)/shard_map/ppermute | solution.py:139
  42.3 12.5 %collective-permute-start.8 = (bf16[64,640]{1,0:T(8,128)(2,1)S(1)}, bf16[64,640]{1,0:T(8,128)(2,1)S(1)}, u32[]{:S(2)}, u32[]{:S(2)}) collective-permute-start(bf16[64,640]{1,0:T(8,128)(2,1)S(1)} %get-tuple-element.45), channel_id=1, source_target_pairs={{0,12},{2,14},{4,8},{6,10},{8,4},{10,6},{12,0},{14,2},{1,13},{3,15... | collective-permute-start | bytes 245768 | tf_op jit(solution)/shard_map/ppermute | solution.py:100
  44.9 10.0 %collective-permute-start.9 = (bf16[64,640]{1,0:T(8,128)(2,1)S(1)}, bf16[64,640]{1,0:T(8,128)(2,1)S(1)}, u32[]{:S(2)}, u32[]{:S(2)}) collective-permute-start(bf16[64,640]{1,0:T(8,128)(2,1)S(1)} %get-tuple-element.46), channel_id=1, source_target_pairs={{0,14},{2,12},{4,10},{6,8},{8,6},{10,4},{12,2},{14,0},{1,15},{3,13... | collective-permute-start | bytes 245768 | tf_op jit(solution)/shard_map/ppermute | solution.py:100
  48.4 10.3 %collective-permute-start.12 = (bf16[64,640]{1,0:T(8,128)(2,1)S(1)}, bf16[64,640]{1,0:T(8,128)(2,1)S(1)}, u32[]{:S(2)}, u32[]{:S(2)}) collective-permute-start(bf16[64,640]{1,0:T(8,128)(2,1)S(1)} %get-tuple-element.58), channel_id=1, source_target_pairs={{0,10},{2,8},{4,14},{6,12},{8,2},{10,0},{12,6},{14,4},{1,11},{3,9}... | collective-permute-start | bytes 245768 | tf_op jit(solution)/shard_map/ppermute | solution.py:100
  50.4 9.5 %collective-permute-start.16 = (bf16[64,640]{1,0:T(8,128)(2,1)S(1)}, bf16[64,640]{1,0:T(8,128)(2,1)S(1)}, u32[]{:S(2)}, u32[]{:S(2)}) collective-permute-start(bf16[64,640]{1,0:T(8,128)(2,1)S(1)} %get-tuple-element.62), channel_id=1, source_target_pairs={{0,2},{2,0},{4,6},{6,4},{8,10},{10,8},{12,14},{14,12},{1,3},{3,1},... | collective-permute-start | bytes 245768 | tf_op jit(solution)/shard_map/ppermute | solution.py:100
  51.0 11.0 %collective-permute-start.15 = (bf16[64,640]{1,0:T(8,128)(2,1)S(1)}, bf16[64,640]{1,0:T(8,128)(2,1)S(1)}, u32[]{:S(2)}, u32[]{:S(2)}) collective-permute-start(bf16[64,640]{1,0:T(8,128)(2,1)S(1)} %get-tuple-element.47), channel_id=1, source_target_pairs={{0,8},{2,10},{4,12},{6,14},{8,0},{10,2},{12,4},{14,6},{1,9},{3,11}... | collective-permute-start | bytes 245768 | tf_op jit(solution)/shard_map/ppermute | solution.py:100
  56.1 10.0 %collective-permute-start.10 = (bf16[64,640]{1,0:T(8,128)(2,1)S(1)}, bf16[64,640]{1,0:T(8,128)(2,1)S(1)}, u32[]{:S(2)}, u32[]{:S(2)}) collective-permute-start(bf16[64,640]{1,0:T(8,128)(2,1)S(1)} %get-tuple-element.55), channel_id=1, source_target_pairs={{0,12},{2,14},{4,8},{6,10},{8,4},{10,6},{12,0},{14,2},{1,13},{3,15... | collective-permute-start | bytes 245768 | tf_op jit(solution)/shard_map/ppermute | solution.py:100
  58.6 6.7 %collective-permute-start.14 = (bf16[64,640]{1,0:T(8,128)(2,1)S(1)}, bf16[64,640]{1,0:T(8,128)(2,1)S(1)}, u32[]{:S(2)}, u32[]{:S(2)}) collective-permute-start(bf16[64,640]{1,0:T(8,128)(2,1)S(1)} %get-tuple-element.61), channel_id=1, source_target_pairs={{0,4},{2,6},{4,0},{6,2},{8,12},{10,14},{12,8},{14,10},{1,5},{3,7},... | collective-permute-start | bytes 245768 | tf_op jit(solution)/shard_map/ppermute | solution.py:100
  58.7 7.4 %collective-permute-start.11 = (bf16[64,640]{1,0:T(8,128)(2,1)S(1)}, bf16[64,640]{1,0:T(8,128)(2,1)S(1)}, u32[]{:S(2)}, u32[]{:S(2)}) collective-permute-start(bf16[64,640]{1,0:T(8,128)(2,1)S(1)} %get-tuple-element.56), channel_id=1, source_target_pairs={{0,14},{2,12},{4,10},{6,8},{8,6},{10,4},{12,2},{14,0},{1,15},{3,13... | collective-permute-start | bytes 245768 | tf_op jit(solution)/shard_map/ppermute | solution.py:100
  59.9 7.0 %collective-permute-start.13 = (bf16[64,640]{1,0:T(8,128)(2,1)S(1)}, bf16[64,640]{1,0:T(8,128)(2,1)S(1)}, u32[]{:S(2)}, u32[]{:S(2)}) collective-permute-start(bf16[64,640]{1,0:T(8,128)(2,1)S(1)} %get-tuple-element.59), channel_id=1, source_target_pairs={{0,6},{2,4},{4,2},{6,0},{8,14},{10,12},{12,10},{14,8},{1,7},{3,5},... | collective-permute-start | bytes 245768 | tf_op jit(solution)/shard_map/ppermute | solution.py:100

commit v13 on v12

--- a/solution.py
+++ b/solution.py
@@ -37,7 +37,7 @@
 
 
 FIRST = (6, 2, 7)
-REST = (4, 3, 1, 5, 0)
+REST = (4, 5, 3, 1, 0)
 LAST = (6, 7)
 NEAR = (2, 3, 1)
 

time: 67.9 us -> 67.9 us (level)
  starting transfers between devices: 40 us -> 33.2 us
  waiting for transfers between devices: 19 us -> 25.7 us
    ppermute x16, starting transfers between devices: 39.9 us -> 33.1 us  [across(): lax.ppermute(piece, 'chip', [(i, i ^ k) for i in range(chips)])]
    ppermute x16, waiting for transfers between devices: 19 us -> 25.7 us  [across(): lax.ppermute(piece, 'chip', [(i, i ^ k) for i in range(chips)])]
where the time goes in v13:
time: 67.9 us; the launch traced here: 67.6 us
  starting transfers between devices  33.2 us (49%)
  waiting for transfers between devices  25.7 us (38%)
  Pallas kernels  8.67 us (13%)
    ppermute x16, starting transfers between devices, across(): lax.ppermute(piece, 'chip', [(i, i ^ k) for i in range(chips)])  33.1 us
    ppermute x16, waiting for transfers between devices, across(): lax.ppermute(piece, 'chip', [(i, i ^ k) for i in range(chips)])  25.7 us
    pallas_call x3, Pallas kernels, attend(): call(body, 2 + len(ks), [shape(rows, gw)] * len(ks))(own, other, *pieces)  4.34 us
    pallas_call x2, Pallas kernels, pack(): pl.pallas_call(functools.partial(pack_body, rows, gw, layout), in_specs=[...  2.73 us
    pallas_call x2, Pallas kernels, unpack(): pl.pallas_call(functools.partial(unpack_body, gw, order), in_specs=[SMEM]...  1.5 us
  transfers between devices with their start and end apart: 17, of which 6 were waited for; matrix products, arithmetic and copies ran while one was open for 0% of the time, Pallas kernels for 10%

profile of v13, /device:TPU:0, one launch (start us, length us, event | category | flops | bytes accessed | tf_op | source)
XLA Modules:
  0.0 67.6 jit_solution(3574996645336142866)
XLA Ops:
  0.0 1.2 %shard_map.37 = (bf16[128,640]{1,0:T(8,128)(2,1)S(1)}, bf16[192,640]{1,0:T(8,128)(2,1)S(1)}, bf16[128,640]{1,0:T(8,128)(2,1)S(1)}) custom-call(s32[1]{0:T(128)} %bitcast.chip_ref, bf16[64,5120]{1,0:T(8,128)(2,1)} %refs_0_.2, bf16[64,5120]{1,0:T(8,128)(2,1)} %refs_1_.2, bf16[64,5120]{1,0:T(8,128)(2,1)} %bitcast.3), custom_call_target="tpu_custom_call" | custom-call | tf_op jit(solution)/shard_map/pallas_call | solution.py:121
  1.2 6.1 %collective-permute-start.2 = (bf16[128,640]{1,0:T(8,128)(2,1)S(1)}, bf16[128,640]{1,0:T(8,128)(2,1)S(1)}, u32[]{:S(2)}, u32[]{:S(2)}) collective-permute-start(bf16[128,640]{1,0:T(8,128)(2,1)S(1)} %get-tuple-element.36), channel_id=1, source_target_pairs={{0,14},{2,12},{4,10},{6,8},{8,6},{10,4},{12,2},{14,0},{1,15},{3,13... | collective-permute-start | bytes 491528 | tf_op jit(solution)/shard_map/ppermute | solution.py:100
  7.3 0.2 collective-permute-start
  7.5 1.5 %shard_map.38 = (bf16[192,640]{1,0:T(8,128)(2,1)S(1)}, bf16[192,640]{1,0:T(8,128)(2,1)S(1)}, bf16[192,640]{1,0:T(8,128)(2,1)S(1)}, bf16[192,640]{1,0:T(8,128)(2,...) custom-call(s32[1]{0:T(128)} %bitcast.chip_ref, ...), custom_call_target="tpu_custom_call" | custom-call | tf_op jit(solution)/shard_map/pallas_call | solution.py:121
  9.0 4.2 %collective-permute-start.3 = (bf16[192,640]{1,0:T(8,128)(2,1)S(1)}, bf16[192,640]{1,0:T(8,128)(2,1)S(1)}, u32[]{:S(2)}, u32[]{:S(2)}) collective-permute-start(bf16[192,640]{1,0:T(8,128)(2,1)S(1)} %get-tuple-element.40), channel_id=1, source_target_pairs={{0,8},{2,10},{4,12},{6,14},{8,0},{10,2},{12,4},{14,6},{1,9},{3,11}... | collective-permute-start | bytes 737288 | tf_op jit(solution)/shard_map/ppermute | solution.py:100
  13.3 6.7 %collective-permute-start.5 = (bf16[192,640]{1,0:T(8,128)(2,1)S(1)}, bf16[192,640]{1,0:T(8,128)(2,1)S(1)}, u32[]{:S(2)}, u32[]{:S(2)}) collective-permute-start(bf16[192,640]{1,0:T(8,128)(2,1)S(1)} %get-tuple-element.42), channel_id=1, source_target_pairs={{0,6},{2,4},{4,2},{6,0},{8,14},{10,12},{12,10},{14,8},{1,7},{3,5},... | collective-permute-start | bytes 737288 | tf_op jit(solution)/shard_map/ppermute | solution.py:100
  20.0 0.6 collective-permute-start.6
  20.7 17.2 %collective-permute-done.3.refs_3_.refs_0_ = bf16[192,640]{1,0:T(8,128)(2,1)S(1)} collective-permute-done((bf16[192,640]{1,0:T(8,128)(2,1)S(1)}, bf16[192,640]{1,0:T(8,128)(2,1)S(1)}, u32[]{:S(2)}, u32[]{:S(2)}) %collective-permute-start.3) | collective-permute-done | bytes 245792 | tf_op jit(solution)/shard_map/ppermute | solution.py:100
  37.8 4.3 %collective-permute-done.4.refs_4_.refs_1_ = bf16[192,640]{1,0:T(8,128)(2,1)S(1)} collective-permute-done((bf16[192,640]{1,0:T(8,128)(2,1)S(1)}, bf16[192,640]{1,0:T(8,128)(2,1)S(1)}, u32[]{:S(2)}, u32[]{:S(2)}) %collective-permute-start.4) | collective-permute-done | bytes 245792 | tf_op jit(solution)/shard_map/ppermute | solution.py:100
  42.4 2.5 %collective-permute-start.8 = (bf16[64,640]{1,0:T(8,128)(2,1)S(1)}, bf16[64,640]{1,0:T(8,128)(2,1)S(1)}, u32[]{:S(2)}, u32[]{:S(2)}) collective-permute-start(bf16[64,640]{1,0:T(8,128)(2,1)S(1)} %get-tuple-element.45), channel_id=1, source_target_pairs={{0,12},{2,14},{4,8},{6,10},{8,4},{10,6},{12,0},{14,2},{1,13},{3,15... | collective-permute-start | bytes 245768 | tf_op jit(solution)/shard_map/ppermute | solution.py:100
  44.9 2.3 %collective-permute-start.9 = (bf16[64,640]{1,0:T(8,128)(2,1)S(1)}, bf16[64,640]{1,0:T(8,128)(2,1)S(1)}, u32[]{:S(2)}, u32[]{:S(2)}) collective-permute-start(bf16[64,640]{1,0:T(8,128)(2,1)S(1)} %get-tuple-element.46), channel_id=1, source_target_pairs={{0,14},{2,12},{4,10},{6,8},{8,6},{10,4},{12,2},{14,0},{1,15},{3,13... | collective-permute-start | bytes 245768 | tf_op jit(solution)/shard_map/ppermute | solution.py:100
  47.2 1.2 %shard_map.40 = (bf16[64,640]{1,0:T(8,128)(2,1)S(1)}, bf16[64,640]{1,0:T(8,128)(2,1)S(1)}) custom-call(bf16[2,512,640]{2,1,0:T(8,128)(2,1)S(1)} %shard_map.39.own, bf16[2,512,640]{2,1,0:T(8,128)(2,1)S(1)} %collective-permute-done.7.other, bf16[192,640]{1,0:T(8,128)(2,1)S(1)} %collective-permute-done.3.refs_3_.refs_0_, ...), custom_call_target="tpu_custom_call" | custom-call | tf_op jit(solution)/shard_map/pallas_call | solution.py:146
  48.5 2.0 %shard_map.41 = (bf16[64,640]{1,0:T(8,128)(2,1)S(1)}, bf16[64,640]{1,0:T(8,128)(2,1)S(1)}, bf16[64,640]{1,0:T(8,128)(2,1)S(1)}, bf16[64,640]{1,0:T(8,128)(2,1)S(1)}) custom-call(bf16[2,512,640]{2,1,0:T(8,128)(2,1)S(1)} %shard_map.39.own, bf16[2,512,640]{2,1,0:T(8,128)(2,1)S(1)} %collective-permute-done.7.other, ...), custom_call_target="tpu_custom_call" | custom-call | tf_op jit(solution)/shard_map/pallas_call | solution.py:146
  50.5 0.6 collective-permute-start.16
  51.0 3.9 %collective-permute-start.15 = (bf16[64,640]{1,0:T(8,128)(2,1)S(1)}, bf16[64,640]{1,0:T(8,128)(2,1)S(1)}, u32[]{:S(2)}, u32[]{:S(2)}) collective-permute-start(bf16[64,640]{1,0:T(8,128)(2,1)S(1)} %get-tuple-element.47), channel_id=1, source_target_pairs={{0,8},{2,10},{4,12},{6,14},{8,0},{10,2},{12,4},{14,6},{1,9},{3,11}... | collective-permute-start | bytes 245768 | tf_op jit(solution)/shard_map/ppermute | solution.py:100
  54.9 1.2 %shard_map.42 = (bf16[64,640]{1,0:T(8,128)(2,1)S(1)}, bf16[64,640]{1,0:T(8,128)(2,1)S(1)}) custom-call(bf16[2,512,640]{2,1,0:T(8,128)(2,1)S(1)} %shard_map.39.own, bf16[2,512,640]{2,1,0:T(8,128)(2,1)S(1)} %collective-permute-done.7.other, bf16[64,640]{1,0:T(8,128)(2,1)S(1)} %collective-permute-done.8.refs_0_, bf16[64,640]{1,0:T(8,128)(2,1)S(1)} %collective-permute-done.9.refs_1_), custom_call_target="tpu_custom_call" | custom-call | tf_op jit(solution)/shard_map/pallas_call | solution.py:146
  56.1 2.5 %collective-permute-start.10 = (bf16[64,640]{1,0:T(8,128)(2,1)S(1)}, bf16[64,640]{1,0:T(8,128)(2,1)S(1)}, u32[]{:S(2)}, u32[]{:S(2)}) collective-permute-start(bf16[64,640]{1,0:T(8,128)(2,1)S(1)} %get-tuple-element.55), channel_id=1, source_target_pairs={{0,12},{2,14},{4,8},{6,10},{8,4},{10,6},{12,0},{14,2},{1,13},{3,15... | collective-permute-start | bytes 245768 | tf_op jit(solution)/shard_map/ppermute | solution.py:100
  58.6 1.3 %collective-permute-start.11 = (bf16[64,640]{1,0:T(8,128)(2,1)S(1)}, bf16[64,640]{1,0:T(8,128)(2,1)S(1)}, u32[]{:S(2)}, u32[]{:S(2)}) collective-permute-start(bf16[64,640]{1,0:T(8,128)(2,1)S(1)} %get-tuple-element.56), channel_id=1, source_target_pairs={{0,14},{2,12},{4,10},{6,8},{8,6},{10,4},{12,2},{14,0},{1,15},{3,13... | collective-permute-start | bytes 245768 | tf_op jit(solution)/shard_map/ppermute | solution.py:100
  59.9 2.1 %collective-permute-start.13 = (bf16[64,640]{1,0:T(8,128)(2,1)S(1)}, bf16[64,640]{1,0:T(8,128)(2,1)S(1)}, u32[]{:S(2)}, u32[]{:S(2)}) collective-permute-start(bf16[64,640]{1,0:T(8,128)(2,1)S(1)} %get-tuple-element.59), channel_id=1, source_target_pairs={{0,6},{2,4},{4,2},{6,0},{8,14},{10,12},{12,10},{14,8},{1,7},{3,5},... | collective-permute-start | bytes 245768 | tf_op jit(solution)/shard_map/ppermute | solution.py:100
  62.0 0.8 %shard_map.43.refs_4_ = bf16[64,5120]{1,0:T(8,128)(2,1)} custom-call(s32[1]{0:T(128)} %bitcast.chip_ref, bf16[64,640]{1,0:T(8,128)(2,1)S(1)} %get-tuple-element.52.refs_0_, bf16[64,640]{1,0:T(8,128)(2,1)S(1)} %collective-permute-done.15.refs_1_, bf16[64,640]{1,0:T(8,128)(2,1)S(1)} %collective-permute-done.12.refs_2_, ...), custom_call_target="tpu_custom_call" | custom-call | tf_op jit(solution)/shard_map/pallas_call | solution.py:160
  62.8 2.6 %collective-permute-done.14.refs_3_ = bf16[64,640]{1,0:T(8,128)(2,1)S(1)} collective-permute-done((bf16[64,640]{1,0:T(8,128)(2,1)S(1)}, bf16[64,640]{1,0:T(8,128)(2,1)S(1)}, u32[]{:S(2)}, u32[]{:S(2)}) %collective-permute-start.14) | collective-permute-done | bytes 81952 | tf_op jit(solution)/shard_map/ppermute | solution.py:100
  65.3 0.7 %collective-permute-done.11.refs_1_ = bf16[64,640]{1,0:T(8,128)(2,1)S(1)} collective-permute-done((bf16[64,640]{1,0:T(8,128)(2,1)S(1)}, bf16[64,640]{1,0:T(8,128)(2,1)S(1)}, u32[]{:S(2)}, u32[]{:S(2)}) %collective-permute-start.11) | collective-permute-done | bytes 81952 | tf_op jit(solution)/shard_map/ppermute | solution.py:100
  66.0 0.9 %collective-permute-done.13.refs_2_ = bf16[64,640]{1,0:T(8,128)(2,1)S(1)} collective-permute-done((bf16[64,640]{1,0:T(8,128)(2,1)S(1)}, bf16[64,640]{1,0:T(8,128)(2,1)S(1)}, u32[]{:S(2)}, u32[]{:S(2)}) %collective-permute-start.13) | collective-permute-done | bytes 81952 | tf_op jit(solution)/shard_map/ppermute | solution.py:100
  66.9 0.8 %shard_map.44 = bf16[64,5120]{1,0:T(8,128)(2,1)} custom-call(s32[1]{0:T(128)} %bitcast.chip_ref, bf16[64,640]{1,0:T(8,128)(2,1)S(1)} %collective-permute-done.10.refs_0_, bf16[64,640]{1,0:T(8,128)(2,1)S(1)} %collective-permute-done.11.refs_1_, bf16[64,640]{1,0:T(8,128)(2,1)S(1)} %collective-permute-done.13.refs_2_, ...), custom_call_target="tpu_custom_call", output_to_operand_aliasing={{}: (5, {})} | custom-call | tf_op jit(solution)/shard_map/pallas_call | solution.py:160
  (18 shorter events, 0.4 us)
Async XLA Ops:
  1.2 12.1 %collective-permute-start.2 = (bf16[128,640]{1,0:T(8,128)(2,1)S(1)}, bf16[128,640]{1,0:T(8,128)(2,1)S(1)}, u32[]{:S(2)}, u32[]{:S(2)}) collective-permute-start(bf16[128,640]{1,0:T(8,128)(2,1)S(1)} %get-tuple-element.36), channel_id=1, source_target_pairs={{0,14},{2,12},{4,10},{6,8},{8,6},{10,4},{12,2},{14,0},{1,15},{3,13... | collective-permute-start | bytes 491528 | tf_op jit(solution)/shard_map/ppermute | solution.py:100
  7.3 12.7 %collective-permute-start = (bf16[128,640]{1,0:T(8,128)(2,1)S(1)}, bf16[128,640]{1,0:T(8,128)(2,1)S(1)}, u32[]{:S(2)}, u32[]{:S(2)}) collective-permute-start(bf16[128,640]{1,0:T(8,128)(2,1)S(1)} %get-tuple-element.34), channel_id=1, source_target_pairs={{0,12},{2,14},{4,8},{6,10},{8,4},{10,6},{12,0},{14,2},{1,13},{3,15... | collective-permute-start | bytes 491528 | tf_op jit(solution)/shard_map/ppermute | solution.py:100
  7.5 13.2 %collective-permute-start.1 = (bf16[192,640]{1,0:T(8,128)(2,1)S(1)}, bf16[192,640]{1,0:T(8,128)(2,1)S(1)}, u32[]{:S(2)}, u32[]{:S(2)}) collective-permute-start(bf16[192,640]{1,0:T(8,128)(2,1)S(1)} %get-tuple-element.35), channel_id=1, source_target_pairs={{0,4},{2,6},{4,0},{6,2},{8,12},{10,14},{12,8},{14,10},{1,5},{3,7},... | collective-permute-start | bytes 737288 | tf_op jit(solution)/shard_map/ppermute | solution.py:100
  9.0 28.8 %collective-permute-start.3 = (bf16[192,640]{1,0:T(8,128)(2,1)S(1)}, bf16[192,640]{1,0:T(8,128)(2,1)S(1)}, u32[]{:S(2)}, u32[]{:S(2)}) collective-permute-start(bf16[192,640]{1,0:T(8,128)(2,1)S(1)} %get-tuple-element.40), channel_id=1, source_target_pairs={{0,8},{2,10},{4,12},{6,14},{8,0},{10,2},{12,4},{14,6},{1,9},{3,11}... | collective-permute-start | bytes 737288 | tf_op jit(solution)/shard_map/ppermute | solution.py:100
  13.3 28.9 %collective-permute-start.4 = (bf16[192,640]{1,0:T(8,128)(2,1)S(1)}, bf16[192,640]{1,0:T(8,128)(2,1)S(1)}, u32[]{:S(2)}, u32[]{:S(2)}) collective-permute-start(bf16[192,640]{1,0:T(8,128)(2,1)S(1)} %get-tuple-element.41), channel_id=1, source_target_pairs={{0,10},{2,8},{4,14},{6,12},{8,2},{10,0},{12,6},{14,4},{1,11},{3,9}... | collective-permute-start | bytes 737288 | tf_op jit(solution)/shard_map/ppermute | solution.py:100
  13.3 28.9 %collective-permute-start.5 = (bf16[192,640]{1,0:T(8,128)(2,1)S(1)}, bf16[192,640]{1,0:T(8,128)(2,1)S(1)}, u32[]{:S(2)}, u32[]{:S(2)}) collective-permute-start(bf16[192,640]{1,0:T(8,128)(2,1)S(1)} %get-tuple-element.42), channel_id=1, source_target_pairs={{0,6},{2,4},{4,2},{6,0},{8,14},{10,12},{12,10},{14,8},{1,7},{3,5},... | collective-permute-start | bytes 737288 | tf_op jit(solution)/shard_map/ppermute | solution.py:100
  20.0 22.2 %collective-permute-start.6 = (bf16[192,640]{1,0:T(8,128)(2,1)S(1)}, bf16[192,640]{1,0:T(8,128)(2,1)S(1)}, u32[]{:S(2)}, u32[]{:S(2)}) collective-permute-start(bf16[192,640]{1,0:T(8,128)(2,1)S(1)} %get-tuple-element.43), channel_id=1, source_target_pairs={{0,2},{2,0},{4,6},{6,4},{8,10},{10,8},{12,14},{14,12},{1,3},{3,1},... | collective-permute-start | bytes 737288 | tf_op jit(solution)/shard_map/ppermute | solution.py:100
  42.3 4.9 %collective-permute-start.7 = (bf16[2,512,640]{2,1,0:T(8,128)(2,1)S(1)}, bf16[2,512,640]{2,1,0:T(8,128)(2,1)S(1)}, u32[]{:S(2)}, u32[]{:S(2)}) collective-permute-start(bf16[2,512,640]{2,1,0:T(8,128)(2,1)S(1)} %shard_map.39.own), channel_id=1, source_target_pairs={{0,1},{1,0},{2,3},{3,2},{4,5},{5,4},{6,7},{7,6},{8,9},{9,8},{10,11... | collective-permute-start | bytes 3932168 | tf_op jit(solution)/shard_map/ppermute | solution.py:139
  42.4 12.5 %collective-permute-start.8 = (bf16[64,640]{1,0:T(8,128)(2,1)S(1)}, bf16[64,640]{1,0:T(8,128)(2,1)S(1)}, u32[]{:S(2)}, u32[]{:S(2)}) collective-permute-start(bf16[64,640]{1,0:T(8,128)(2,1)S(1)} %get-tuple-element.45), channel_id=1, source_target_pairs={{0,12},{2,14},{4,8},{6,10},{8,4},{10,6},{12,0},{14,2},{1,13},{3,15... | collective-permute-start | bytes 245768 | tf_op jit(solution)/shard_map/ppermute | solution.py:100
  44.9 10.0 %collective-permute-start.9 = (bf16[64,640]{1,0:T(8,128)(2,1)S(1)}, bf16[64,640]{1,0:T(8,128)(2,1)S(1)}, u32[]{:S(2)}, u32[]{:S(2)}) collective-permute-start(bf16[64,640]{1,0:T(8,128)(2,1)S(1)} %get-tuple-element.46), channel_id=1, source_target_pairs={{0,14},{2,12},{4,10},{6,8},{8,6},{10,4},{12,2},{14,0},{1,15},{3,13... | collective-permute-start | bytes 245768 | tf_op jit(solution)/shard_map/ppermute | solution.py:100
  48.4 10.3 %collective-permute-start.12 = (bf16[64,640]{1,0:T(8,128)(2,1)S(1)}, bf16[64,640]{1,0:T(8,128)(2,1)S(1)}, u32[]{:S(2)}, u32[]{:S(2)}) collective-permute-start(bf16[64,640]{1,0:T(8,128)(2,1)S(1)} %get-tuple-element.58), channel_id=1, source_target_pairs={{0,10},{2,8},{4,14},{6,12},{8,2},{10,0},{12,6},{14,4},{1,11},{3,9}... | collective-permute-start | bytes 245768 | tf_op jit(solution)/shard_map/ppermute | solution.py:100
  50.5 9.5 %collective-permute-start.16 = (bf16[64,640]{1,0:T(8,128)(2,1)S(1)}, bf16[64,640]{1,0:T(8,128)(2,1)S(1)}, u32[]{:S(2)}, u32[]{:S(2)}) collective-permute-start(bf16[64,640]{1,0:T(8,128)(2,1)S(1)} %get-tuple-element.62), channel_id=1, source_target_pairs={{0,2},{2,0},{4,6},{6,4},{8,10},{10,8},{12,14},{14,12},{1,3},{3,1},... | collective-permute-start | bytes 245768 | tf_op jit(solution)/shard_map/ppermute | solution.py:100
  51.0 11.0 %collective-permute-start.15 = (bf16[64,640]{1,0:T(8,128)(2,1)S(1)}, bf16[64,640]{1,0:T(8,128)(2,1)S(1)}, u32[]{:S(2)}, u32[]{:S(2)}) collective-permute-start(bf16[64,640]{1,0:T(8,128)(2,1)S(1)} %get-tuple-element.47), channel_id=1, source_target_pairs={{0,8},{2,10},{4,12},{6,14},{8,0},{10,2},{12,4},{14,6},{1,9},{3,11}... | collective-permute-start | bytes 245768 | tf_op jit(solution)/shard_map/ppermute | solution.py:100
  56.1 9.9 %collective-permute-start.10 = (bf16[64,640]{1,0:T(8,128)(2,1)S(1)}, bf16[64,640]{1,0:T(8,128)(2,1)S(1)}, u32[]{:S(2)}, u32[]{:S(2)}) collective-permute-start(bf16[64,640]{1,0:T(8,128)(2,1)S(1)} %get-tuple-element.55), channel_id=1, source_target_pairs={{0,12},{2,14},{4,8},{6,10},{8,4},{10,6},{12,0},{14,2},{1,13},{3,15... | collective-permute-start | bytes 245768 | tf_op jit(solution)/shard_map/ppermute | solution.py:100
  58.6 6.7 %collective-permute-start.14 = (bf16[64,640]{1,0:T(8,128)(2,1)S(1)}, bf16[64,640]{1,0:T(8,128)(2,1)S(1)}, u32[]{:S(2)}, u32[]{:S(2)}) collective-permute-start(bf16[64,640]{1,0:T(8,128)(2,1)S(1)} %get-tuple-element.61), channel_id=1, source_target_pairs={{0,4},{2,6},{4,0},{6,2},{8,12},{10,14},{12,8},{14,10},{1,5},{3,7},... | collective-permute-start | bytes 245768 | tf_op jit(solution)/shard_map/ppermute | solution.py:100
  58.6 7.4 %collective-permute-start.11 = (bf16[64,640]{1,0:T(8,128)(2,1)S(1)}, bf16[64,640]{1,0:T(8,128)(2,1)S(1)}, u32[]{:S(2)}, u32[]{:S(2)}) collective-permute-start(bf16[64,640]{1,0:T(8,128)(2,1)S(1)} %get-tuple-element.56), channel_id=1, source_target_pairs={{0,14},{2,12},{4,10},{6,8},{8,6},{10,4},{12,2},{14,0},{1,15},{3,13... | collective-permute-start | bytes 245768 | tf_op jit(solution)/shard_map/ppermute | solution.py:100
  59.9 7.0 %collective-permute-start.13 = (bf16[64,640]{1,0:T(8,128)(2,1)S(1)}, bf16[64,640]{1,0:T(8,128)(2,1)S(1)}, u32[]{:S(2)}, u32[]{:S(2)}) collective-permute-start(bf16[64,640]{1,0:T(8,128)(2,1)S(1)} %get-tuple-element.59), channel_id=1, source_target_pairs={{0,6},{2,4},{4,2},{6,0},{8,14},{10,12},{12,10},{14,8},{1,7},{3,5},... | collective-permute-start | bytes 245768 | tf_op jit(solution)/shard_map/ppermute | solution.py:100

commit v14 on v13

--- a/solution.py
+++ b/solution.py
@@ -36,8 +36,8 @@
     return jnp.concatenate([v, jnp.ones_like(v)], axis=1)
 
 
-FIRST = (6, 2, 7)
-REST = (4, 5, 3, 1, 0)
+FIRST = (6, 7)
+REST = (2, 4, 5, 3, 1, 0)
 LAST = (6, 7)
 NEAR = (2, 3, 1)
 
@@ -168,7 +168,7 @@
             cost_estimate=FREE,
         )(chip, *[back[k] for k in order], *so_far)
 
-    result = unpack(LAST + (3, 2), (unpack((0, 4, 5, 1)),))
+    result = unpack(LAST + (3,), (unpack((0, 4, 5, 1, 2)),))
     return result.reshape(layers, tok_rows, width)
 
 

time: 67.9 us -> 69.5 us (1.024)
  waiting for transfers between devices: 25.7 us -> 27.6 us
    ppermute x16, waiting for transfers between devices: 25.7 us -> 27.6 us  [across(): lax.ppermute(piece, 'chip', [(i, i ^ k) for i in range(chips)])]
  transfers between devices with their start and end apart: 17 -> 17, of which waited for: 6 -> 7; matrix products, arithmetic and copies ran while one was open for 0% -> 0% of each run, Pallas kernels for 10% -> 10%
where the time goes in v14:
time: 69.5 us; the launch traced here: 69.3 us
  starting transfers between devices  33 us (47%)
  waiting for transfers between devices  27.6 us (40%)
  Pallas kernels  8.62 us (12%)
    ppermute x16, starting transfers between devices, across(): lax.ppermute(piece, 'chip', [(i, i ^ k) for i in range(chips)])  32.9 us
    ppermute x16, waiting for transfers between devices, across(): lax.ppermute(piece, 'chip', [(i, i ^ k) for i in range(chips)])  27.6 us
    pallas_call x3, Pallas kernels, attend(): call(body, 2 + len(ks), [shape(rows, gw)] * len(ks))(own, other, *pieces)  4.33 us
    pallas_call x2, Pallas kernels, pack(): pl.pallas_call(functools.partial(pack_body, rows, gw, layout), in_specs=[...  2.68 us
    pallas_call x2, Pallas kernels, unpack(): pl.pallas_call(functools.partial(unpack_body, gw, order), in_specs=[SMEM]...  1.5 us
  transfers between devices with their start and end apart: 17, of which 7 were waited for; matrix products, arithmetic and copies ran while one was open for 0% of the time, Pallas kernels for 10%

profile of v14, /device:TPU:0, one launch (start us, length us, event | category | flops | bytes accessed | tf_op | source)
XLA Modules:
  0.0 69.3 jit_solution(16913340306166635715)
XLA Ops:
  0.0 1.0 %shard_map.37 = (bf16[128,640]{1,0:T(8,128)(2,1)S(1)}, bf16[128,640]{1,0:T(8,128)(2,1)S(1)}) custom-call(s32[1]{0:T(128)} %bitcast.chip_ref, bf16[64,5120]{1,0:T(8,128)(2,1)} %refs_0_.2, bf16[64,5120]{1,0:T(8,128)(2,1)} %refs_1_.2, bf16[64,5120]{1,0:T(8,128)(2,1)} %bitcast.3), custom_call_target="tpu_custom_call" | custom-call | tf_op jit(solution)/shard_map/pallas_call | solution.py:121
  1.0 6.1 %collective-permute-start.1 = (bf16[128,640]{1,0:T(8,128)(2,1)S(1)}, bf16[128,640]{1,0:T(8,128)(2,1)S(1)}, u32[]{:S(2)}, u32[]{:S(2)}) collective-permute-start(bf16[128,640]{1,0:T(8,128)(2,1)S(1)} %get-tuple-element.35), channel_id=1, source_target_pairs={{0,14},{2,12},{4,10},{6,8},{8,6},{10,4},{12,2},{14,0},{1,15},{3,13... | collective-permute-start | bytes 491528 | tf_op jit(solution)/shard_map/ppermute | solution.py:100
  7.1 0.2 collective-permute-start
  7.3 1.6 %shard_map.38 = (bf16[192,640]{1,0:T(8,128)(2,1)S(1)}, bf16[192,640]{1,0:T(8,128)(2,1)S(1)}, bf16[192,640]{1,0:T(8,128)(2,1)S(1)}, bf16[192,640]{1,0:T(8,128)(2,...) custom-call(s32[1]{0:T(128)} %bitcast.chip_ref, ...), custom_call_target="tpu_custom_call" | custom-call | tf_op jit(solution)/shard_map/pallas_call | solution.py:121
  9.1 4.2 %collective-permute-start.3 = (bf16[192,640]{1,0:T(8,128)(2,1)S(1)}, bf16[192,640]{1,0:T(8,128)(2,1)S(1)}, u32[]{:S(2)}, u32[]{:S(2)}) collective-permute-start(bf16[192,640]{1,0:T(8,128)(2,1)S(1)} %get-tuple-element.40), channel_id=1, source_target_pairs={{0,8},{2,10},{4,12},{6,14},{8,0},{10,2},{12,4},{14,6},{1,9},{3,11}... | collective-permute-start | bytes 737288 | tf_op jit(solution)/shard_map/ppermute | solution.py:100
  13.2 6.6 %collective-permute-start.5 = (bf16[192,640]{1,0:T(8,128)(2,1)S(1)}, bf16[192,640]{1,0:T(8,128)(2,1)S(1)}, u32[]{:S(2)}, u32[]{:S(2)}) collective-permute-start(bf16[192,640]{1,0:T(8,128)(2,1)S(1)} %get-tuple-element.42), channel_id=1, source_target_pairs={{0,6},{2,4},{4,2},{6,0},{8,14},{10,12},{12,10},{14,8},{1,7},{3,5},... | collective-permute-start | bytes 737288 | tf_op jit(solution)/shard_map/ppermute | solution.py:100
  19.9 0.6 collective-permute-start.6
  20.5 17.2 %collective-permute-done.3.refs_3_.refs_0_ = bf16[192,640]{1,0:T(8,128)(2,1)S(1)} collective-permute-done((bf16[192,640]{1,0:T(8,128)(2,1)S(1)}, bf16[192,640]{1,0:T(8,128)(2,1)S(1)}, u32[]{:S(2)}, u32[]{:S(2)}) %collective-permute-start.3) | collective-permute-done | bytes 245792 | tf_op jit(solution)/shard_map/ppermute | solution.py:100
  37.7 4.3 %collective-permute-done.4.refs_4_.refs_1_ = bf16[192,640]{1,0:T(8,128)(2,1)S(1)} collective-permute-done((bf16[192,640]{1,0:T(8,128)(2,1)S(1)}, bf16[192,640]{1,0:T(8,128)(2,1)S(1)}, u32[]{:S(2)}, u32[]{:S(2)}) %collective-permute-start.4) | collective-permute-done | bytes 245792 | tf_op jit(solution)/shard_map/ppermute | solution.py:100
  42.2 2.5 %collective-permute-start.8 = (bf16[64,640]{1,0:T(8,128)(2,1)S(1)}, bf16[64,640]{1,0:T(8,128)(2,1)S(1)}, u32[]{:S(2)}, u32[]{:S(2)}) collective-permute-start(bf16[64,640]{1,0:T(8,128)(2,1)S(1)} %get-tuple-element.45), channel_id=1, source_target_pairs={{0,12},{2,14},{4,8},{6,10},{8,4},{10,6},{12,0},{14,2},{1,13},{3,15... | collective-permute-start | bytes 245768 | tf_op jit(solution)/shard_map/ppermute | solution.py:100
  44.7 2.3 %collective-permute-start.9 = (bf16[64,640]{1,0:T(8,128)(2,1)S(1)}, bf16[64,640]{1,0:T(8,128)(2,1)S(1)}, u32[]{:S(2)}, u32[]{:S(2)}) collective-permute-start(bf16[64,640]{1,0:T(8,128)(2,1)S(1)} %get-tuple-element.46), channel_id=1, source_target_pairs={{0,14},{2,12},{4,10},{6,8},{8,6},{10,4},{12,2},{14,0},{1,15},{3,13... | collective-permute-start | bytes 245768 | tf_op jit(solution)/shard_map/ppermute | solution.py:100
  47.1 1.2 %shard_map.40 = (bf16[64,640]{1,0:T(8,128)(2,1)S(1)}, bf16[64,640]{1,0:T(8,128)(2,1)S(1)}) custom-call(bf16[2,512,640]{2,1,0:T(8,128)(2,1)S(1)} %shard_map.39.own, bf16[2,512,640]{2,1,0:T(8,128)(2,1)S(1)} %collective-permute-done.7.other, bf16[192,640]{1,0:T(8,128)(2,1)S(1)} %collective-permute-done.3.refs_3_.refs_0_, ...), custom_call_target="tpu_custom_call" | custom-call | tf_op jit(solution)/shard_map/pallas_call | solution.py:146
  48.2 2.0 %shard_map.41 = (bf16[64,640]{1,0:T(8,128)(2,1)S(1)}, bf16[64,640]{1,0:T(8,128)(2,1)S(1)}, bf16[64,640]{1,0:T(8,128)(2,1)S(1)}, bf16[64,640]{1,0:T(8,128)(2,1)S(1)}) custom-call(bf16[2,512,640]{2,1,0:T(8,128)(2,1)S(1)} %shard_map.39.own, bf16[2,512,640]{2,1,0:T(8,128)(2,1)S(1)} %collective-permute-done.7.other, ...), custom_call_target="tpu_custom_call" | custom-call | tf_op jit(solution)/shard_map/pallas_call | solution.py:146
  50.2 1.7 %collective-permute-done.9.refs_1_ = bf16[64,640]{1,0:T(8,128)(2,1)S(1)} collective-permute-done((bf16[64,640]{1,0:T(8,128)(2,1)S(1)}, bf16[64,640]{1,0:T(8,128)(2,1)S(1)}, u32[]{:S(2)}, u32[]{:S(2)}) %collective-permute-start.9) | collective-permute-done | bytes 81952 | tf_op jit(solution)/shard_map/ppermute | solution.py:100
  52.0 1.2 %shard_map.42 = (bf16[64,640]{1,0:T(8,128)(2,1)S(1)}, bf16[64,640]{1,0:T(8,128)(2,1)S(1)}) custom-call(bf16[2,512,640]{2,1,0:T(8,128)(2,1)S(1)} %shard_map.39.own, bf16[2,512,640]{2,1,0:T(8,128)(2,1)S(1)} %collective-permute-done.7.other, bf16[64,640]{1,0:T(8,128)(2,1)S(1)} %collective-permute-done.8.refs_0_, bf16[64,640]{1,0:T(8,128)(2,1)S(1)} %collective-permute-done.9.refs_1_), custom_call_target="tpu_custom_call" | custom-call | tf_op jit(solution)/shard_map/pallas_call | solution.py:146
  53.1 2.9 %collective-permute-start.16 = (bf16[64,640]{1,0:T(8,128)(2,1)S(1)}, bf16[64,640]{1,0:T(8,128)(2,1)S(1)}, u32[]{:S(2)}, u32[]{:S(2)}) collective-permute-start(bf16[64,640]{1,0:T(8,128)(2,1)S(1)} %get-tuple-element.62), channel_id=1, source_target_pairs={{0,4},{2,6},{4,0},{6,2},{8,12},{10,14},{12,8},{14,10},{1,5},{3,7},... | collective-permute-start | bytes 245768 | tf_op jit(solution)/shard_map/ppermute | solution.py:100
  56.1 2.5 %collective-permute-start.10 = (bf16[64,640]{1,0:T(8,128)(2,1)S(1)}, bf16[64,640]{1,0:T(8,128)(2,1)S(1)}, u32[]{:S(2)}, u32[]{:S(2)}) collective-permute-start(bf16[64,640]{1,0:T(8,128)(2,1)S(1)} %get-tuple-element.55), channel_id=1, source_target_pairs={{0,12},{2,14},{4,8},{6,10},{8,4},{10,6},{12,0},{14,2},{1,13},{3,15... | collective-permute-start | bytes 245768 | tf_op jit(solution)/shard_map/ppermute | solution.py:100
  58.5 2.0 %collective-permute-start.11 = (bf16[64,640]{1,0:T(8,128)(2,1)S(1)}, bf16[64,640]{1,0:T(8,128)(2,1)S(1)}, u32[]{:S(2)}, u32[]{:S(2)}) collective-permute-start(bf16[64,640]{1,0:T(8,128)(2,1)S(1)} %get-tuple-element.56), channel_id=1, source_target_pairs={{0,14},{2,12},{4,10},{6,8},{8,6},{10,4},{12,2},{14,0},{1,15},{3,13... | collective-permute-start | bytes 245768 | tf_op jit(solution)/shard_map/ppermute | solution.py:100
  60.6 1.0 %collective-permute-start.15 = (bf16[64,640]{1,0:T(8,128)(2,1)S(1)}, bf16[64,640]{1,0:T(8,128)(2,1)S(1)}, u32[]{:S(2)}, u32[]{:S(2)}) collective-permute-start(bf16[64,640]{1,0:T(8,128)(2,1)S(1)} %get-tuple-element.60), channel_id=1, source_target_pairs={{0,2},{2,0},{4,6},{6,4},{8,10},{10,8},{12,14},{14,12},{1,3},{3,1},... | collective-permute-start | bytes 245768 | tf_op jit(solution)/shard_map/ppermute | solution.py:100
  61.6 1.9 %collective-permute-start.13 = (bf16[64,640]{1,0:T(8,128)(2,1)S(1)}, bf16[64,640]{1,0:T(8,128)(2,1)S(1)}, u32[]{:S(2)}, u32[]{:S(2)}) collective-permute-start(bf16[64,640]{1,0:T(8,128)(2,1)S(1)} %get-tuple-element.59), channel_id=1, source_target_pairs={{0,6},{2,4},{4,2},{6,0},{8,14},{10,12},{12,10},{14,8},{1,7},{3,5},... | collective-permute-start | bytes 245768 | tf_op jit(solution)/shard_map/ppermute | solution.py:100
  63.4 3.1 %collective-permute-done.15.refs_3_ = bf16[64,640]{1,0:T(8,128)(2,1)S(1)} collective-permute-done((bf16[64,640]{1,0:T(8,128)(2,1)S(1)}, bf16[64,640]{1,0:T(8,128)(2,1)S(1)}, u32[]{:S(2)}, u32[]{:S(2)}) %collective-permute-start.15) | collective-permute-done | bytes 81952 | tf_op jit(solution)/shard_map/ppermute | solution.py:100
  66.5 1.1 %collective-permute-done.14.refs_1_ = bf16[64,640]{1,0:T(8,128)(2,1)S(1)} collective-permute-done((bf16[64,640]{1,0:T(8,128)(2,1)S(1)}, bf16[64,640]{1,0:T(8,128)(2,1)S(1)}, u32[]{:S(2)}, u32[]{:S(2)}) %collective-permute-start.14) | collective-permute-done | bytes 81952 | tf_op jit(solution)/shard_map/ppermute | solution.py:100
  67.6 0.8 %shard_map.43.refs_3_ = bf16[64,5120]{1,0:T(8,128)(2,1)} custom-call(s32[1]{0:T(128)} %bitcast.chip_ref, bf16[64,640]{1,0:T(8,128)(2,1)S(1)} %get-tuple-element.52.refs_0_, bf16[64,640]{1,0:T(8,128)(2,1)S(1)} %collective-permute-done.14.refs_1_, bf16[64,640]{1,0:T(8,128)(2,1)S(1)} %collective-permute-done.12.refs_2_, ...), custom_call_target="tpu_custom_call" | custom-call | tf_op jit(solution)/shard_map/pallas_call | solution.py:160
  68.6 0.7 %shard_map.44 = bf16[64,5120]{1,0:T(8,128)(2,1)} custom-call(s32[1]{0:T(128)} %bitcast.chip_ref, bf16[64,640]{1,0:T(8,128)(2,1)S(1)} %collective-permute-done.10.refs_0_, bf16[64,640]{1,0:T(8,128)(2,1)S(1)} %collective-permute-done.11.refs_1_, bf16[64,640]{1,0:T(8,128)(2,1)S(1)} %collective-permute-done.13.refs_2_, ...), custom_call_target="tpu_custom_call", output_to_operand_aliasing={{}: (4, {})} | custom-call | tf_op jit(solution)/shard_map/pallas_call | solution.py:160
  (18 shorter events, 0.5 us)
Async XLA Ops:
  1.0 12.2 %collective-permute-start.1 = (bf16[128,640]{1,0:T(8,128)(2,1)S(1)}, bf16[128,640]{1,0:T(8,128)(2,1)S(1)}, u32[]{:S(2)}, u32[]{:S(2)}) collective-permute-start(bf16[128,640]{1,0:T(8,128)(2,1)S(1)} %get-tuple-element.35), channel_id=1, source_target_pairs={{0,14},{2,12},{4,10},{6,8},{8,6},{10,4},{12,2},{14,0},{1,15},{3,13... | collective-permute-start | bytes 491528 | tf_op jit(solution)/shard_map/ppermute | solution.py:100
  7.1 12.7 %collective-permute-start = (bf16[128,640]{1,0:T(8,128)(2,1)S(1)}, bf16[128,640]{1,0:T(8,128)(2,1)S(1)}, u32[]{:S(2)}, u32[]{:S(2)}) collective-permute-start(bf16[128,640]{1,0:T(8,128)(2,1)S(1)} %get-tuple-element.34), channel_id=1, source_target_pairs={{0,12},{2,14},{4,8},{6,10},{8,4},{10,6},{12,0},{14,2},{1,13},{3,15... | collective-permute-start | bytes 491528 | tf_op jit(solution)/shard_map/ppermute | solution.py:100
  9.0 11.6 %collective-permute-start.2 = (bf16[192,640]{1,0:T(8,128)(2,1)S(1)}, bf16[192,640]{1,0:T(8,128)(2,1)S(1)}, u32[]{:S(2)}, u32[]{:S(2)}) collective-permute-start(bf16[192,640]{1,0:T(8,128)(2,1)S(1)} %get-tuple-element.39), channel_id=1, source_target_pairs={{0,4},{2,6},{4,0},{6,2},{8,12},{10,14},{12,8},{14,10},{1,5},{3,7},... | collective-permute-start | bytes 737288 | tf_op jit(solution)/shard_map/ppermute | solution.py:100
  9.1 28.6 %collective-permute-start.3 = (bf16[192,640]{1,0:T(8,128)(2,1)S(1)}, bf16[192,640]{1,0:T(8,128)(2,1)S(1)}, u32[]{:S(2)}, u32[]{:S(2)}) collective-permute-start(bf16[192,640]{1,0:T(8,128)(2,1)S(1)} %get-tuple-element.40), channel_id=1, source_target_pairs={{0,8},{2,10},{4,12},{6,14},{8,0},{10,2},{12,4},{14,6},{1,9},{3,11}... | collective-permute-start | bytes 737288 | tf_op jit(solution)/shard_map/ppermute | solution.py:100
  13.2 28.8 %collective-permute-start.4 = (bf16[192,640]{1,0:T(8,128)(2,1)S(1)}, bf16[192,640]{1,0:T(8,128)(2,1)S(1)}, u32[]{:S(2)}, u32[]{:S(2)}) collective-permute-start(bf16[192,640]{1,0:T(8,128)(2,1)S(1)} %get-tuple-element.41), channel_id=1, source_target_pairs={{0,10},{2,8},{4,14},{6,12},{8,2},{10,0},{12,6},{14,4},{1,11},{3,9}... | collective-permute-start | bytes 737288 | tf_op jit(solution)/shard_map/ppermute | solution.py:100
  13.2 28.8 %collective-permute-start.5 = (bf16[192,640]{1,0:T(8,128)(2,1)S(1)}, bf16[192,640]{1,0:T(8,128)(2,1)S(1)}, u32[]{:S(2)}, u32[]{:S(2)}) collective-permute-start(bf16[192,640]{1,0:T(8,128)(2,1)S(1)} %get-tuple-element.42), channel_id=1, source_target_pairs={{0,6},{2,4},{4,2},{6,0},{8,14},{10,12},{12,10},{14,8},{1,7},{3,5},... | collective-permute-start | bytes 737288 | tf_op jit(solution)/shard_map/ppermute | solution.py:100
  19.9 22.2 %collective-permute-start.6 = (bf16[192,640]{1,0:T(8,128)(2,1)S(1)}, bf16[192,640]{1,0:T(8,128)(2,1)S(1)}, u32[]{:S(2)}, u32[]{:S(2)}) collective-permute-start(bf16[192,640]{1,0:T(8,128)(2,1)S(1)} %get-tuple-element.43), channel_id=1, source_target_pairs={{0,2},{2,0},{4,6},{6,4},{8,10},{10,8},{12,14},{14,12},{1,3},{3,1},... | collective-permute-start | bytes 737288 | tf_op jit(solution)/shard_map/ppermute | solution.py:100
  42.1 4.9 %collective-permute-start.7 = (bf16[2,512,640]{2,1,0:T(8,128)(2,1)S(1)}, bf16[2,512,640]{2,1,0:T(8,128)(2,1)S(1)}, u32[]{:S(2)}, u32[]{:S(2)}) collective-permute-start(bf16[2,512,640]{2,1,0:T(8,128)(2,1)S(1)} %shard_map.39.own), channel_id=1, source_target_pairs={{0,1},{1,0},{2,3},{3,2},{4,5},{5,4},{6,7},{7,6},{8,9},{9,8},{10,11... | collective-permute-start | bytes 3932168 | tf_op jit(solution)/shard_map/ppermute | solution.py:139
  42.2 8.0 %collective-permute-start.8 = (bf16[64,640]{1,0:T(8,128)(2,1)S(1)}, bf16[64,640]{1,0:T(8,128)(2,1)S(1)}, u32[]{:S(2)}, u32[]{:S(2)}) collective-permute-start(bf16[64,640]{1,0:T(8,128)(2,1)S(1)} %get-tuple-element.45), channel_id=1, source_target_pairs={{0,12},{2,14},{4,8},{6,10},{8,4},{10,6},{12,0},{14,2},{1,13},{3,15... | collective-permute-start | bytes 245768 | tf_op jit(solution)/shard_map/ppermute | solution.py:100
  44.7 7.2 %collective-permute-start.9 = (bf16[64,640]{1,0:T(8,128)(2,1)S(1)}, bf16[64,640]{1,0:T(8,128)(2,1)S(1)}, u32[]{:S(2)}, u32[]{:S(2)}) collective-permute-start(bf16[64,640]{1,0:T(8,128)(2,1)S(1)} %get-tuple-element.46), channel_id=1, source_target_pairs={{0,14},{2,12},{4,10},{6,8},{8,6},{10,4},{12,2},{14,0},{1,15},{3,13... | collective-permute-start | bytes 245768 | tf_op jit(solution)/shard_map/ppermute | solution.py:100
  52.0 8.6 %collective-permute-start.12 = (bf16[64,640]{1,0:T(8,128)(2,1)S(1)}, bf16[64,640]{1,0:T(8,128)(2,1)S(1)}, u32[]{:S(2)}, u32[]{:S(2)}) collective-permute-start(bf16[64,640]{1,0:T(8,128)(2,1)S(1)} %get-tuple-element.58), channel_id=1, source_target_pairs={{0,10},{2,8},{4,14},{6,12},{8,2},{10,0},{12,6},{14,4},{1,11},{3,9}... | collective-permute-start | bytes 245768 | tf_op jit(solution)/shard_map/ppermute | solution.py:100
  53.1 8.4 %collective-permute-start.16 = (bf16[64,640]{1,0:T(8,128)(2,1)S(1)}, bf16[64,640]{1,0:T(8,128)(2,1)S(1)}, u32[]{:S(2)}, u32[]{:S(2)}) collective-permute-start(bf16[64,640]{1,0:T(8,128)(2,1)S(1)} %get-tuple-element.62), channel_id=1, source_target_pairs={{0,4},{2,6},{4,0},{6,2},{8,12},{10,14},{12,8},{14,10},{1,5},{3,7},... | collective-permute-start | bytes 245768 | tf_op jit(solution)/shard_map/ppermute | solution.py:100
  56.1 12.3 %collective-permute-start.10 = (bf16[64,640]{1,0:T(8,128)(2,1)S(1)}, bf16[64,640]{1,0:T(8,128)(2,1)S(1)}, u32[]{:S(2)}, u32[]{:S(2)}) collective-permute-start(bf16[64,640]{1,0:T(8,128)(2,1)S(1)} %get-tuple-element.55), channel_id=1, source_target_pairs={{0,12},{2,14},{4,8},{6,10},{8,4},{10,6},{12,0},{14,2},{1,13},{3,15... | collective-permute-start | bytes 245768 | tf_op jit(solution)/shard_map/ppermute | solution.py:100
  58.5 9.1 %collective-permute-start.14 = (bf16[64,640]{1,0:T(8,128)(2,1)S(1)}, bf16[64,640]{1,0:T(8,128)(2,1)S(1)}, u32[]{:S(2)}, u32[]{:S(2)}) collective-permute-start(bf16[64,640]{1,0:T(8,128)(2,1)S(1)} %get-tuple-element.47), channel_id=1, source_target_pairs={{0,8},{2,10},{4,12},{6,14},{8,0},{10,2},{12,4},{14,6},{1,9},{3,11}... | collective-permute-start | bytes 245768 | tf_op jit(solution)/shard_map/ppermute | solution.py:100
  58.5 9.8 %collective-permute-start.11 = (bf16[64,640]{1,0:T(8,128)(2,1)S(1)}, bf16[64,640]{1,0:T(8,128)(2,1)S(1)}, u32[]{:S(2)}, u32[]{:S(2)}) collective-permute-start(bf16[64,640]{1,0:T(8,128)(2,1)S(1)} %get-tuple-element.56), channel_id=1, source_target_pairs={{0,14},{2,12},{4,10},{6,8},{8,6},{10,4},{12,2},{14,0},{1,15},{3,13... | collective-permute-start | bytes 245768 | tf_op jit(solution)/shard_map/ppermute | solution.py:100
  60.6 6.0 %collective-permute-start.15 = (bf16[64,640]{1,0:T(8,128)(2,1)S(1)}, bf16[64,640]{1,0:T(8,128)(2,1)S(1)}, u32[]{:S(2)}, u32[]{:S(2)}) collective-permute-start(bf16[64,640]{1,0:T(8,128)(2,1)S(1)} %get-tuple-element.60), channel_id=1, source_target_pairs={{0,2},{2,0},{4,6},{6,4},{8,10},{10,8},{12,14},{14,12},{1,3},{3,1},... | collective-permute-start | bytes 245768 | tf_op jit(solution)/shard_map/ppermute | solution.py:100
  61.6 7.1 %collective-permute-start.13 = (bf16[64,640]{1,0:T(8,128)(2,1)S(1)}, bf16[64,640]{1,0:T(8,128)(2,1)S(1)}, u32[]{:S(2)}, u32[]{:S(2)}) collective-permute-start(bf16[64,640]{1,0:T(8,128)(2,1)S(1)} %get-tuple-element.59), channel_id=1, source_target_pairs={{0,6},{2,4},{4,2},{6,0},{8,14},{10,12},{12,10},{14,8},{1,7},{3,5},... | collective-permute-start | bytes 245768 | tf_op jit(solution)/shard_map/ppermute | solution.py:100

commit v15 on v14

--- a/solution.py
+++ b/solution.py
@@ -168,7 +168,7 @@
             cost_estimate=FREE,
         )(chip, *[back[k] for k in order], *so_far)
 
-    result = unpack(LAST + (3,), (unpack((0, 4, 5, 1, 2)),))
+    result = unpack(LAST + (3, 2), (unpack((0, 4, 5, 1)),))
     return result.reshape(layers, tok_rows, width)
 
 

time: 69.5 us -> 67.7 us (0.974)
  waiting for transfers between devices: 27.6 us -> 25.7 us
    ppermute x16, waiting for transfers between devices: 27.6 us -> 25.7 us  [across(): lax.ppermute(piece, 'chip', [(i, i ^ k) for i in range(chips)])]
  transfers between devices with their start and end apart: 17 -> 17, of which waited for: 7 -> 6; matrix products, arithmetic and copies ran while one was open for 0% -> 0% of each run, Pallas kernels for 10% -> 10%
where the time goes in v15:
time: 67.7 us; the launch traced here: 67.5 us
  starting transfers between devices  33.1 us (49%)
  waiting for transfers between devices  25.7 us (38%)
  Pallas kernels  8.62 us (13%)
    ppermute x16, starting transfers between devices, across(): lax.ppermute(piece, 'chip', [(i, i ^ k) for i in range(chips)])  33 us
    ppermute x16, waiting for transfers between devices, across(): lax.ppermute(piece, 'chip', [(i, i ^ k) for i in range(chips)])  25.7 us
    pallas_call x3, Pallas kernels, attend(): call(body, 2 + len(ks), [shape(rows, gw)] * len(ks))(own, other, *pieces)  4.33 us
    pallas_call x2, Pallas kernels, pack(): pl.pallas_call(functools.partial(pack_body, rows, gw, layout), in_specs=[...  2.68 us
    pallas_call x2, Pallas kernels, unpack(): pl.pallas_call(functools.partial(unpack_body, gw, order), in_specs=[SMEM]...  1.5 us
  transfers between devices with their start and end apart: 17, of which 6 were waited for; matrix products, arithmetic and copies ran while one was open for 0% of the time, Pallas kernels for 10%

profile of v15, /device:TPU:0, one launch (start us, length us, event | category | flops | bytes accessed | tf_op | source)
XLA Modules:
  0.0 67.5 jit_solution(3068191820961382294)
XLA Ops:
  0.0 1.0 %shard_map.37 = (bf16[128,640]{1,0:T(8,128)(2,1)S(1)}, bf16[128,640]{1,0:T(8,128)(2,1)S(1)}) custom-call(s32[1]{0:T(128)} %bitcast.chip_ref, bf16[64,5120]{1,0:T(8,128)(2,1)} %refs_0_.2, bf16[64,5120]{1,0:T(8,128)(2,1)} %refs_1_.2, bf16[64,5120]{1,0:T(8,128)(2,1)} %bitcast.3), custom_call_target="tpu_custom_call" | custom-call | tf_op jit(solution)/shard_map/pallas_call | solution.py:121
  1.0 6.1 %collective-permute-start.1 = (bf16[128,640]{1,0:T(8,128)(2,1)S(1)}, bf16[128,640]{1,0:T(8,128)(2,1)S(1)}, u32[]{:S(2)}, u32[]{:S(2)}) collective-permute-start(bf16[128,640]{1,0:T(8,128)(2,1)S(1)} %get-tuple-element.35), channel_id=1, source_target_pairs={{0,14},{2,12},{4,10},{6,8},{8,6},{10,4},{12,2},{14,0},{1,15},{3,13... | collective-permute-start | bytes 491528 | tf_op jit(solution)/shard_map/ppermute | solution.py:100
  7.1 0.2 collective-permute-start
  7.3 1.6 %shard_map.38 = (bf16[192,640]{1,0:T(8,128)(2,1)S(1)}, bf16[192,640]{1,0:T(8,128)(2,1)S(1)}, bf16[192,640]{1,0:T(8,128)(2,1)S(1)}, bf16[192,640]{1,0:T(8,128)(2,...) custom-call(s32[1]{0:T(128)} %bitcast.chip_ref, ...), custom_call_target="tpu_custom_call" | custom-call | tf_op jit(solution)/shard_map/pallas_call | solution.py:121
  9.1 4.2 %collective-permute-start.3 = (bf16[192,640]{1,0:T(8,128)(2,1)S(1)}, bf16[192,640]{1,0:T(8,128)(2,1)S(1)}, u32[]{:S(2)}, u32[]{:S(2)}) collective-permute-start(bf16[192,640]{1,0:T(8,128)(2,1)S(1)} %get-tuple-element.40), channel_id=1, source_target_pairs={{0,8},{2,10},{4,12},{6,14},{8,0},{10,2},{12,4},{14,6},{1,9},{3,11}... | collective-permute-start | bytes 737288 | tf_op jit(solution)/shard_map/ppermute | solution.py:100
  13.2 6.6 %collective-permute-start.5 = (bf16[192,640]{1,0:T(8,128)(2,1)S(1)}, bf16[192,640]{1,0:T(8,128)(2,1)S(1)}, u32[]{:S(2)}, u32[]{:S(2)}) collective-permute-start(bf16[192,640]{1,0:T(8,128)(2,1)S(1)} %get-tuple-element.42), channel_id=1, source_target_pairs={{0,6},{2,4},{4,2},{6,0},{8,14},{10,12},{12,10},{14,8},{1,7},{3,5},... | collective-permute-start | bytes 737288 | tf_op jit(solution)/shard_map/ppermute | solution.py:100
  19.9 0.6 collective-permute-start.6
  20.5 17.2 %collective-permute-done.3.refs_3_.refs_0_ = bf16[192,640]{1,0:T(8,128)(2,1)S(1)} collective-permute-done((bf16[192,640]{1,0:T(8,128)(2,1)S(1)}, bf16[192,640]{1,0:T(8,128)(2,1)S(1)}, u32[]{:S(2)}, u32[]{:S(2)}) %collective-permute-start.3) | collective-permute-done | bytes 245792 | tf_op jit(solution)/shard_map/ppermute | solution.py:100
  37.7 4.3 %collective-permute-done.4.refs_4_.refs_1_ = bf16[192,640]{1,0:T(8,128)(2,1)S(1)} collective-permute-done((bf16[192,640]{1,0:T(8,128)(2,1)S(1)}, bf16[192,640]{1,0:T(8,128)(2,1)S(1)}, u32[]{:S(2)}, u32[]{:S(2)}) %collective-permute-start.4) | collective-permute-done | bytes 245792 | tf_op jit(solution)/shard_map/ppermute | solution.py:100
  42.2 2.5 %collective-permute-start.8 = (bf16[64,640]{1,0:T(8,128)(2,1)S(1)}, bf16[64,640]{1,0:T(8,128)(2,1)S(1)}, u32[]{:S(2)}, u32[]{:S(2)}) collective-permute-start(bf16[64,640]{1,0:T(8,128)(2,1)S(1)} %get-tuple-element.45), channel_id=1, source_target_pairs={{0,12},{2,14},{4,8},{6,10},{8,4},{10,6},{12,0},{14,2},{1,13},{3,15... | collective-permute-start | bytes 245768 | tf_op jit(solution)/shard_map/ppermute | solution.py:100
  44.7 2.3 %collective-permute-start.9 = (bf16[64,640]{1,0:T(8,128)(2,1)S(1)}, bf16[64,640]{1,0:T(8,128)(2,1)S(1)}, u32[]{:S(2)}, u32[]{:S(2)}) collective-permute-start(bf16[64,640]{1,0:T(8,128)(2,1)S(1)} %get-tuple-element.46), channel_id=1, source_target_pairs={{0,14},{2,12},{4,10},{6,8},{8,6},{10,4},{12,2},{14,0},{1,15},{3,13... | collective-permute-start | bytes 245768 | tf_op jit(solution)/shard_map/ppermute | solution.py:100
  47.1 1.2 %shard_map.40 = (bf16[64,640]{1,0:T(8,128)(2,1)S(1)}, bf16[64,640]{1,0:T(8,128)(2,1)S(1)}) custom-call(bf16[2,512,640]{2,1,0:T(8,128)(2,1)S(1)} %shard_map.39.own, bf16[2,512,640]{2,1,0:T(8,128)(2,1)S(1)} %collective-permute-done.7.other, bf16[192,640]{1,0:T(8,128)(2,1)S(1)} %collective-permute-done.3.refs_3_.refs_0_, ...), custom_call_target="tpu_custom_call" | custom-call | tf_op jit(solution)/shard_map/pallas_call | solution.py:146
  48.3 2.0 %shard_map.41 = (bf16[64,640]{1,0:T(8,128)(2,1)S(1)}, bf16[64,640]{1,0:T(8,128)(2,1)S(1)}, bf16[64,640]{1,0:T(8,128)(2,1)S(1)}, bf16[64,640]{1,0:T(8,128)(2,1)S(1)}) custom-call(bf16[2,512,640]{2,1,0:T(8,128)(2,1)S(1)} %shard_map.39.own, bf16[2,512,640]{2,1,0:T(8,128)(2,1)S(1)} %collective-permute-done.7.other, ...), custom_call_target="tpu_custom_call" | custom-call | tf_op jit(solution)/shard_map/pallas_call | solution.py:146
  50.3 0.6 collective-permute-start.16
  50.9 3.9 %collective-permute-start.15 = (bf16[64,640]{1,0:T(8,128)(2,1)S(1)}, bf16[64,640]{1,0:T(8,128)(2,1)S(1)}, u32[]{:S(2)}, u32[]{:S(2)}) collective-permute-start(bf16[64,640]{1,0:T(8,128)(2,1)S(1)} %get-tuple-element.47), channel_id=1, source_target_pairs={{0,8},{2,10},{4,12},{6,14},{8,0},{10,2},{12,4},{14,6},{1,9},{3,11}... | collective-permute-start | bytes 245768 | tf_op jit(solution)/shard_map/ppermute | solution.py:100
  54.8 1.2 %shard_map.42 = (bf16[64,640]{1,0:T(8,128)(2,1)S(1)}, bf16[64,640]{1,0:T(8,128)(2,1)S(1)}) custom-call(bf16[2,512,640]{2,1,0:T(8,128)(2,1)S(1)} %shard_map.39.own, bf16[2,512,640]{2,1,0:T(8,128)(2,1)S(1)} %collective-permute-done.7.other, bf16[64,640]{1,0:T(8,128)(2,1)S(1)} %collective-permute-done.8.refs_0_, bf16[64,640]{1,0:T(8,128)(2,1)S(1)} %collective-permute-done.9.refs_1_), custom_call_target="tpu_custom_call" | custom-call | tf_op jit(solution)/shard_map/pallas_call | solution.py:146
  55.9 2.5 %collective-permute-start.10 = (bf16[64,640]{1,0:T(8,128)(2,1)S(1)}, bf16[64,640]{1,0:T(8,128)(2,1)S(1)}, u32[]{:S(2)}, u32[]{:S(2)}) collective-permute-start(bf16[64,640]{1,0:T(8,128)(2,1)S(1)} %get-tuple-element.55), channel_id=1, source_target_pairs={{0,12},{2,14},{4,8},{6,10},{8,4},{10,6},{12,0},{14,2},{1,13},{3,15... | collective-permute-start | bytes 245768 | tf_op jit(solution)/shard_map/ppermute | solution.py:100
  58.5 1.3 %collective-permute-start.11 = (bf16[64,640]{1,0:T(8,128)(2,1)S(1)}, bf16[64,640]{1,0:T(8,128)(2,1)S(1)}, u32[]{:S(2)}, u32[]{:S(2)}) collective-permute-start(bf16[64,640]{1,0:T(8,128)(2,1)S(1)} %get-tuple-element.56), channel_id=1, source_target_pairs={{0,14},{2,12},{4,10},{6,8},{8,6},{10,4},{12,2},{14,0},{1,15},{3,13... | collective-permute-start | bytes 245768 | tf_op jit(solution)/shard_map/ppermute | solution.py:100
  59.8 2.1 %collective-permute-start.13 = (bf16[64,640]{1,0:T(8,128)(2,1)S(1)}, bf16[64,640]{1,0:T(8,128)(2,1)S(1)}, u32[]{:S(2)}, u32[]{:S(2)}) collective-permute-start(bf16[64,640]{1,0:T(8,128)(2,1)S(1)} %get-tuple-element.59), channel_id=1, source_target_pairs={{0,6},{2,4},{4,2},{6,0},{8,14},{10,12},{12,10},{14,8},{1,7},{3,5},... | collective-permute-start | bytes 245768 | tf_op jit(solution)/shard_map/ppermute | solution.py:100
  61.9 0.8 %shard_map.43.refs_4_ = bf16[64,5120]{1,0:T(8,128)(2,1)} custom-call(s32[1]{0:T(128)} %bitcast.chip_ref, bf16[64,640]{1,0:T(8,128)(2,1)S(1)} %get-tuple-element.52.refs_0_, bf16[64,640]{1,0:T(8,128)(2,1)S(1)} %collective-permute-done.15.refs_1_, bf16[64,640]{1,0:T(8,128)(2,1)S(1)} %collective-permute-done.12.refs_2_, ...), custom_call_target="tpu_custom_call" | custom-call | tf_op jit(solution)/shard_map/pallas_call | solution.py:160
  62.6 2.6 %collective-permute-done.14.refs_3_ = bf16[64,640]{1,0:T(8,128)(2,1)S(1)} collective-permute-done((bf16[64,640]{1,0:T(8,128)(2,1)S(1)}, bf16[64,640]{1,0:T(8,128)(2,1)S(1)}, u32[]{:S(2)}, u32[]{:S(2)}) %collective-permute-start.14) | collective-permute-done | bytes 81952 | tf_op jit(solution)/shard_map/ppermute | solution.py:100
  65.2 0.7 collective-permute-done.11.refs_1_
  65.9 0.9 %collective-permute-done.13.refs_2_ = bf16[64,640]{1,0:T(8,128)(2,1)S(1)} collective-permute-done((bf16[64,640]{1,0:T(8,128)(2,1)S(1)}, bf16[64,640]{1,0:T(8,128)(2,1)S(1)}, u32[]{:S(2)}, u32[]{:S(2)}) %collective-permute-start.13) | collective-permute-done | bytes 81952 | tf_op jit(solution)/shard_map/ppermute | solution.py:100
  66.7 0.8 %shard_map.44 = bf16[64,5120]{1,0:T(8,128)(2,1)} custom-call(s32[1]{0:T(128)} %bitcast.chip_ref, bf16[64,640]{1,0:T(8,128)(2,1)S(1)} %collective-permute-done.10.refs_0_, bf16[64,640]{1,0:T(8,128)(2,1)S(1)} %collective-permute-done.11.refs_1_, bf16[64,640]{1,0:T(8,128)(2,1)S(1)} %collective-permute-done.13.refs_2_, ...), custom_call_target="tpu_custom_call", output_to_operand_aliasing={{}: (5, {})} | custom-call | tf_op jit(solution)/shard_map/pallas_call | solution.py:160
  (18 shorter events, 0.4 us)
Async XLA Ops:
  1.0 12.2 %collective-permute-start.1 = (bf16[128,640]{1,0:T(8,128)(2,1)S(1)}, bf16[128,640]{1,0:T(8,128)(2,1)S(1)}, u32[]{:S(2)}, u32[]{:S(2)}) collective-permute-start(bf16[128,640]{1,0:T(8,128)(2,1)S(1)} %get-tuple-element.35), channel_id=1, source_target_pairs={{0,14},{2,12},{4,10},{6,8},{8,6},{10,4},{12,2},{14,0},{1,15},{3,13... | collective-permute-start | bytes 491528 | tf_op jit(solution)/shard_map/ppermute | solution.py:100
  7.1 12.7 %collective-permute-start = (bf16[128,640]{1,0:T(8,128)(2,1)S(1)}, bf16[128,640]{1,0:T(8,128)(2,1)S(1)}, u32[]{:S(2)}, u32[]{:S(2)}) collective-permute-start(bf16[128,640]{1,0:T(8,128)(2,1)S(1)} %get-tuple-element.34), channel_id=1, source_target_pairs={{0,12},{2,14},{4,8},{6,10},{8,4},{10,6},{12,0},{14,2},{1,13},{3,15... | collective-permute-start | bytes 491528 | tf_op jit(solution)/shard_map/ppermute | solution.py:100
  9.0 11.6 %collective-permute-start.2 = (bf16[192,640]{1,0:T(8,128)(2,1)S(1)}, bf16[192,640]{1,0:T(8,128)(2,1)S(1)}, u32[]{:S(2)}, u32[]{:S(2)}) collective-permute-start(bf16[192,640]{1,0:T(8,128)(2,1)S(1)} %get-tuple-element.39), channel_id=1, source_target_pairs={{0,4},{2,6},{4,0},{6,2},{8,12},{10,14},{12,8},{14,10},{1,5},{3,7},... | collective-permute-start | bytes 737288 | tf_op jit(solution)/shard_map/ppermute | solution.py:100
  9.1 28.6 %collective-permute-start.3 = (bf16[192,640]{1,0:T(8,128)(2,1)S(1)}, bf16[192,640]{1,0:T(8,128)(2,1)S(1)}, u32[]{:S(2)}, u32[]{:S(2)}) collective-permute-start(bf16[192,640]{1,0:T(8,128)(2,1)S(1)} %get-tuple-element.40), channel_id=1, source_target_pairs={{0,8},{2,10},{4,12},{6,14},{8,0},{10,2},{12,4},{14,6},{1,9},{3,11}... | collective-permute-start | bytes 737288 | tf_op jit(solution)/shard_map/ppermute | solution.py:100
  13.2 28.8 %collective-permute-start.4 = (bf16[192,640]{1,0:T(8,128)(2,1)S(1)}, bf16[192,640]{1,0:T(8,128)(2,1)S(1)}, u32[]{:S(2)}, u32[]{:S(2)}) collective-permute-start(bf16[192,640]{1,0:T(8,128)(2,1)S(1)} %get-tuple-element.41), channel_id=1, source_target_pairs={{0,10},{2,8},{4,14},{6,12},{8,2},{10,0},{12,6},{14,4},{1,11},{3,9}... | collective-permute-start | bytes 737288 | tf_op jit(solution)/shard_map/ppermute | solution.py:100
  13.2 28.8 %collective-permute-start.5 = (bf16[192,640]{1,0:T(8,128)(2,1)S(1)}, bf16[192,640]{1,0:T(8,128)(2,1)S(1)}, u32[]{:S(2)}, u32[]{:S(2)}) collective-permute-start(bf16[192,640]{1,0:T(8,128)(2,1)S(1)} %get-tuple-element.42), channel_id=1, source_target_pairs={{0,6},{2,4},{4,2},{6,0},{8,14},{10,12},{12,10},{14,8},{1,7},{3,5},... | collective-permute-start | bytes 737288 | tf_op jit(solution)/shard_map/ppermute | solution.py:100
  19.9 22.2 %collective-permute-start.6 = (bf16[192,640]{1,0:T(8,128)(2,1)S(1)}, bf16[192,640]{1,0:T(8,128)(2,1)S(1)}, u32[]{:S(2)}, u32[]{:S(2)}) collective-permute-start(bf16[192,640]{1,0:T(8,128)(2,1)S(1)} %get-tuple-element.43), channel_id=1, source_target_pairs={{0,2},{2,0},{4,6},{6,4},{8,10},{10,8},{12,14},{14,12},{1,3},{3,1},... | collective-permute-start | bytes 737288 | tf_op jit(solution)/shard_map/ppermute | solution.py:100
  42.1 4.9 %collective-permute-start.7 = (bf16[2,512,640]{2,1,0:T(8,128)(2,1)S(1)}, bf16[2,512,640]{2,1,0:T(8,128)(2,1)S(1)}, u32[]{:S(2)}, u32[]{:S(2)}) collective-permute-start(bf16[2,512,640]{2,1,0:T(8,128)(2,1)S(1)} %shard_map.39.own), channel_id=1, source_target_pairs={{0,1},{1,0},{2,3},{3,2},{4,5},{5,4},{6,7},{7,6},{8,9},{9,8},{10,11... | collective-permute-start | bytes 3932168 | tf_op jit(solution)/shard_map/ppermute | solution.py:139
  42.2 12.5 %collective-permute-start.8 = (bf16[64,640]{1,0:T(8,128)(2,1)S(1)}, bf16[64,640]{1,0:T(8,128)(2,1)S(1)}, u32[]{:S(2)}, u32[]{:S(2)}) collective-permute-start(bf16[64,640]{1,0:T(8,128)(2,1)S(1)} %get-tuple-element.45), channel_id=1, source_target_pairs={{0,12},{2,14},{4,8},{6,10},{8,4},{10,6},{12,0},{14,2},{1,13},{3,15... | collective-permute-start | bytes 245768 | tf_op jit(solution)/shard_map/ppermute | solution.py:100
  44.7 10.0 %collective-permute-start.9 = (bf16[64,640]{1,0:T(8,128)(2,1)S(1)}, bf16[64,640]{1,0:T(8,128)(2,1)S(1)}, u32[]{:S(2)}, u32[]{:S(2)}) collective-permute-start(bf16[64,640]{1,0:T(8,128)(2,1)S(1)} %get-tuple-element.46), channel_id=1, source_target_pairs={{0,14},{2,12},{4,10},{6,8},{8,6},{10,4},{12,2},{14,0},{1,15},{3,13... | collective-permute-start | bytes 245768 | tf_op jit(solution)/shard_map/ppermute | solution.py:100
  48.2 10.2 %collective-permute-start.12 = (bf16[64,640]{1,0:T(8,128)(2,1)S(1)}, bf16[64,640]{1,0:T(8,128)(2,1)S(1)}, u32[]{:S(2)}, u32[]{:S(2)}) collective-permute-start(bf16[64,640]{1,0:T(8,128)(2,1)S(1)} %get-tuple-element.58), channel_id=1, source_target_pairs={{0,10},{2,8},{4,14},{6,12},{8,2},{10,0},{12,6},{14,4},{1,11},{3,9}... | collective-permute-start | bytes 245768 | tf_op jit(solution)/shard_map/ppermute | solution.py:100
  50.3 9.5 %collective-permute-start.16 = (bf16[64,640]{1,0:T(8,128)(2,1)S(1)}, bf16[64,640]{1,0:T(8,128)(2,1)S(1)}, u32[]{:S(2)}, u32[]{:S(2)}) collective-permute-start(bf16[64,640]{1,0:T(8,128)(2,1)S(1)} %get-tuple-element.62), channel_id=1, source_target_pairs={{0,2},{2,0},{4,6},{6,4},{8,10},{10,8},{12,14},{14,12},{1,3},{3,1},... | collective-permute-start | bytes 245768 | tf_op jit(solution)/shard_map/ppermute | solution.py:100
  50.9 11.0 %collective-permute-start.15 = (bf16[64,640]{1,0:T(8,128)(2,1)S(1)}, bf16[64,640]{1,0:T(8,128)(2,1)S(1)}, u32[]{:S(2)}, u32[]{:S(2)}) collective-permute-start(bf16[64,640]{1,0:T(8,128)(2,1)S(1)} %get-tuple-element.47), channel_id=1, source_target_pairs={{0,8},{2,10},{4,12},{6,14},{8,0},{10,2},{12,4},{14,6},{1,9},{3,11}... | collective-permute-start | bytes 245768 | tf_op jit(solution)/shard_map/ppermute | solution.py:100
  55.9 9.9 %collective-permute-start.10 = (bf16[64,640]{1,0:T(8,128)(2,1)S(1)}, bf16[64,640]{1,0:T(8,128)(2,1)S(1)}, u32[]{:S(2)}, u32[]{:S(2)}) collective-permute-start(bf16[64,640]{1,0:T(8,128)(2,1)S(1)} %get-tuple-element.55), channel_id=1, source_target_pairs={{0,12},{2,14},{4,8},{6,10},{8,4},{10,6},{12,0},{14,2},{1,13},{3,15... | collective-permute-start | bytes 245768 | tf_op jit(solution)/shard_map/ppermute | solution.py:100
  58.5 6.7 %collective-permute-start.14 = (bf16[64,640]{1,0:T(8,128)(2,1)S(1)}, bf16[64,640]{1,0:T(8,128)(2,1)S(1)}, u32[]{:S(2)}, u32[]{:S(2)}) collective-permute-start(bf16[64,640]{1,0:T(8,128)(2,1)S(1)} %get-tuple-element.61), channel_id=1, source_target_pairs={{0,4},{2,6},{4,0},{6,2},{8,12},{10,14},{12,8},{14,10},{1,5},{3,7},... | collective-permute-start | bytes 245768 | tf_op jit(solution)/shard_map/ppermute | solution.py:100
  58.5 7.4 %collective-permute-start.11 = (bf16[64,640]{1,0:T(8,128)(2,1)S(1)}, bf16[64,640]{1,0:T(8,128)(2,1)S(1)}, u32[]{:S(2)}, u32[]{:S(2)}) collective-permute-start(bf16[64,640]{1,0:T(8,128)(2,1)S(1)} %get-tuple-element.56), channel_id=1, source_target_pairs={{0,14},{2,12},{4,10},{6,8},{8,6},{10,4},{12,2},{14,0},{1,15},{3,13... | collective-permute-start | bytes 245768 | tf_op jit(solution)/shard_map/ppermute | solution.py:100
  59.8 7.0 %collective-permute-start.13 = (bf16[64,640]{1,0:T(8,128)(2,1)S(1)}, bf16[64,640]{1,0:T(8,128)(2,1)S(1)}, u32[]{:S(2)}, u32[]{:S(2)}) collective-permute-start(bf16[64,640]{1,0:T(8,128)(2,1)S(1)} %get-tuple-element.59), channel_id=1, source_target_pairs={{0,6},{2,4},{4,2},{6,0},{8,14},{10,12},{12,10},{14,8},{1,7},{3,5},... | collective-permute-start | bytes 245768 | tf_op jit(solution)/shard_map/ppermute | solution.py:100

commit v16 on v15

--- a/solution.py
+++ b/solution.py
@@ -37,7 +37,7 @@
 
 
 FIRST = (6, 7)
-REST = (2, 4, 5, 3, 1, 0)
+REST = (4, 5, 2, 3, 1, 0)
 LAST = (6, 7)
 NEAR = (2, 3, 1)
 

time: 67.7 us -> 70.6 us (1.043)
  starting transfers between devices: 33.1 us -> 42.2 us
  waiting for transfers between devices: 25.7 us -> 19.5 us
    ppermute x16, starting transfers between devices: 33 us -> 42.2 us  [across(): lax.ppermute(piece, 'chip', [(i, i ^ k) for i in range(chips)])]
    ppermute x16, waiting for transfers between devices: 25.7 us -> 19.5 us  [across(): lax.ppermute(piece, 'chip', [(i, i ^ k) for i in range(chips)])]
  transfers between devices with their start and end apart: 17 -> 17, of which waited for: 6 -> 7; matrix products, arithmetic and copies ran while one was open for 0% -> 0% of each run, Pallas kernels for 10% -> 10%
where the time goes in v16:
time: 70.6 us; the launch traced here: 70.4 us
  starting transfers between devices  42.2 us (60%)
  waiting for transfers between devices  19.5 us (28%)
  Pallas kernels  8.62 us (12%)
    ppermute x16, starting transfers between devices, across(): lax.ppermute(piece, 'chip', [(i, i ^ k) for i in range(chips)])  42.2 us
    ppermute x16, waiting for transfers between devices, across(): lax.ppermute(piece, 'chip', [(i, i ^ k) for i in range(chips)])  19.5 us
    pallas_call x3, Pallas kernels, attend(): call(body, 2 + len(ks), [shape(rows, gw)] * len(ks))(own, other, *pieces)  4.33 us
    pallas_call x2, Pallas kernels, pack(): pl.pallas_call(functools.partial(pack_body, rows, gw, layout), in_specs=[...  2.68 us
    pallas_call x2, Pallas kernels, unpack(): pl.pallas_call(functools.partial(unpack_body, gw, order), in_specs=[SMEM]...  1.5 us
  transfers between devices with their start and end apart: 17, of which 7 were waited for; matrix products, arithmetic and copies ran while one was open for 0% of the time, Pallas kernels for 10%

profile of v16, /device:TPU:0, one launch (start us, length us, event | category | flops | bytes accessed | tf_op | source)
XLA Modules:
  0.0 70.4 jit_solution(18407415496645944891)
XLA Ops:
  0.0 1.0 %shard_map.37 = (bf16[128,640]{1,0:T(8,128)(2,1)S(1)}, bf16[128,640]{1,0:T(8,128)(2,1)S(1)}) custom-call(s32[1]{0:T(128)} %bitcast.chip_ref, bf16[64,5120]{1,0:T(8,128)(2,1)} %refs_0_.2, bf16[64,5120]{1,0:T(8,128)(2,1)} %refs_1_.2, bf16[64,5120]{1,0:T(8,128)(2,1)} %bitcast.3), custom_call_target="tpu_custom_call" | custom-call | tf_op jit(solution)/shard_map/pallas_call | solution.py:121
  1.0 6.1 %collective-permute-start.1 = (bf16[128,640]{1,0:T(8,128)(2,1)S(1)}, bf16[128,640]{1,0:T(8,128)(2,1)S(1)}, u32[]{:S(2)}, u32[]{:S(2)}) collective-permute-start(bf16[128,640]{1,0:T(8,128)(2,1)S(1)} %get-tuple-element.35), channel_id=1, source_target_pairs={{0,14},{2,12},{4,10},{6,8},{8,6},{10,4},{12,2},{14,0},{1,15},{3,13... | collective-permute-start | bytes 491528 | tf_op jit(solution)/shard_map/ppermute | solution.py:100
  7.3 1.6 %shard_map.38 = (bf16[192,640]{1,0:T(8,128)(2,1)S(1)}, bf16[192,640]{1,0:T(8,128)(2,1)S(1)}, bf16[192,640]{1,0:T(8,128)(2,1)S(1)}, bf16[192,640]{1,0:T(8,128)(2,...) custom-call(s32[1]{0:T(128)} %bitcast.chip_ref, ...), custom_call_target="tpu_custom_call" | custom-call | tf_op jit(solution)/shard_map/pallas_call | solution.py:121
  9.0 0.9 %collective-permute-start.2 = (bf16[192,640]{1,0:T(8,128)(2,1)S(1)}, bf16[192,640]{1,0:T(8,128)(2,1)S(1)}, u32[]{:S(2)}, u32[]{:S(2)}) collective-permute-start(bf16[192,640]{1,0:T(8,128)(2,1)S(1)} %get-tuple-element.39), channel_id=1, source_target_pairs={{0,8},{2,10},{4,12},{6,14},{8,0},{10,2},{12,4},{14,6},{1,9},{3,11}... | collective-permute-start | bytes 737288 | tf_op jit(solution)/shard_map/ppermute | solution.py:100
  9.8 2.0 %collective-permute-start.3 = (bf16[192,640]{1,0:T(8,128)(2,1)S(1)}, bf16[192,640]{1,0:T(8,128)(2,1)S(1)}, u32[]{:S(2)}, u32[]{:S(2)}) collective-permute-start(bf16[192,640]{1,0:T(8,128)(2,1)S(1)} %get-tuple-element.40), channel_id=1, source_target_pairs={{0,10},{2,8},{4,14},{6,12},{8,2},{10,0},{12,6},{14,4},{1,11},{3,9}... | collective-permute-start | bytes 737288 | tf_op jit(solution)/shard_map/ppermute | solution.py:100
  11.8 1.4 %collective-permute-start.4 = (bf16[192,640]{1,0:T(8,128)(2,1)S(1)}, bf16[192,640]{1,0:T(8,128)(2,1)S(1)}, u32[]{:S(2)}, u32[]{:S(2)}) collective-permute-start(bf16[192,640]{1,0:T(8,128)(2,1)S(1)} %get-tuple-element.41), channel_id=1, source_target_pairs={{0,4},{2,6},{4,0},{6,2},{8,12},{10,14},{12,8},{14,10},{1,5},{3,7},... | collective-permute-start | bytes 737288 | tf_op jit(solution)/shard_map/ppermute | solution.py:100
  13.2 17.1 %collective-permute-start.5 = (bf16[192,640]{1,0:T(8,128)(2,1)S(1)}, bf16[192,640]{1,0:T(8,128)(2,1)S(1)}, u32[]{:S(2)}, u32[]{:S(2)}) collective-permute-start(bf16[192,640]{1,0:T(8,128)(2,1)S(1)} %get-tuple-element.42), channel_id=1, source_target_pairs={{0,6},{2,4},{4,2},{6,0},{8,14},{10,12},{12,10},{14,8},{1,7},{3,5},... | collective-permute-start | bytes 737288 | tf_op jit(solution)/shard_map/ppermute | solution.py:100
  31.0 6.8 %collective-permute-done.2.refs_2_.refs_0_ = bf16[192,640]{1,0:T(8,128)(2,1)S(1)} collective-permute-done((bf16[192,640]{1,0:T(8,128)(2,1)S(1)}, bf16[192,640]{1,0:T(8,128)(2,1)S(1)}, u32[]{:S(2)}, u32[]{:S(2)}) %collective-permute-start.2) | collective-permute-done | bytes 245792 | tf_op jit(solution)/shard_map/ppermute | solution.py:100
  37.8 4.4 %collective-permute-done.3.refs_3_.refs_1_ = bf16[192,640]{1,0:T(8,128)(2,1)S(1)} collective-permute-done((bf16[192,640]{1,0:T(8,128)(2,1)S(1)}, bf16[192,640]{1,0:T(8,128)(2,1)S(1)}, u32[]{:S(2)}, u32[]{:S(2)}) %collective-permute-start.3) | collective-permute-done | bytes 245792 | tf_op jit(solution)/shard_map/ppermute | solution.py:100
  42.2 3.2 %collective-permute-done.5.refs_5_.refs_1_ = bf16[192,640]{1,0:T(8,128)(2,1)S(1)} collective-permute-done((bf16[192,640]{1,0:T(8,128)(2,1)S(1)}, bf16[192,640]{1,0:T(8,128)(2,1)S(1)}, u32[]{:S(2)}, u32[]{:S(2)}) %collective-permute-start.5) | collective-permute-done | bytes 245792 | tf_op jit(solution)/shard_map/ppermute | solution.py:100
  45.8 1.3 %collective-permute-start.8 = (bf16[64,640]{1,0:T(8,128)(2,1)S(1)}, bf16[64,640]{1,0:T(8,128)(2,1)S(1)}, u32[]{:S(2)}, u32[]{:S(2)}) collective-permute-start(bf16[64,640]{1,0:T(8,128)(2,1)S(1)} %get-tuple-element.45), channel_id=1, source_target_pairs={{0,12},{2,14},{4,8},{6,10},{8,4},{10,6},{12,0},{14,2},{1,13},{3,15... | collective-permute-start | bytes 245768 | tf_op jit(solution)/shard_map/ppermute | solution.py:100
  47.1 2.1 %collective-permute-start.9 = (bf16[64,640]{1,0:T(8,128)(2,1)S(1)}, bf16[64,640]{1,0:T(8,128)(2,1)S(1)}, u32[]{:S(2)}, u32[]{:S(2)}) collective-permute-start(bf16[64,640]{1,0:T(8,128)(2,1)S(1)} %get-tuple-element.46), channel_id=1, source_target_pairs={{0,14},{2,12},{4,10},{6,8},{8,6},{10,4},{12,2},{14,0},{1,15},{3,13... | collective-permute-start | bytes 245768 | tf_op jit(solution)/shard_map/ppermute | solution.py:100
  49.3 1.2 %shard_map.40 = (bf16[64,640]{1,0:T(8,128)(2,1)S(1)}, bf16[64,640]{1,0:T(8,128)(2,1)S(1)}) custom-call(bf16[2,512,640]{2,1,0:T(8,128)(2,1)S(1)} %shard_map.39.own, bf16[2,512,640]{2,1,0:T(8,128)(2,1)S(1)} %collective-permute-done.7.other, bf16[192,640]{1,0:T(8,128)(2,1)S(1)} %collective-permute-done.2.refs_2_.refs_0_, ...), custom_call_target="tpu_custom_call" | custom-call | tf_op jit(solution)/shard_map/pallas_call | solution.py:146
  50.5 2.0 %shard_map.41 = (bf16[64,640]{1,0:T(8,128)(2,1)S(1)}, bf16[64,640]{1,0:T(8,128)(2,1)S(1)}, bf16[64,640]{1,0:T(8,128)(2,1)S(1)}, bf16[64,640]{1,0:T(8,128)(2,1)S(1)}) custom-call(bf16[2,512,640]{2,1,0:T(8,128)(2,1)S(1)} %shard_map.39.own, bf16[2,512,640]{2,1,0:T(8,128)(2,1)S(1)} %collective-permute-done.7.other, ...), custom_call_target="tpu_custom_call" | custom-call | tf_op jit(solution)/shard_map/pallas_call | solution.py:146
  52.5 2.0 %collective-permute-start.16 = (bf16[64,640]{1,0:T(8,128)(2,1)S(1)}, bf16[64,640]{1,0:T(8,128)(2,1)S(1)}, u32[]{:S(2)}, u32[]{:S(2)}) collective-permute-start(bf16[64,640]{1,0:T(8,128)(2,1)S(1)} %get-tuple-element.62), channel_id=1, source_target_pairs={{0,2},{2,0},{4,6},{6,4},{8,10},{10,8},{12,14},{14,12},{1,3},{3,1},... | collective-permute-start | bytes 245768 | tf_op jit(solution)/shard_map/ppermute | solution.py:100
  54.5 2.5 %collective-permute-start.15 = (bf16[64,640]{1,0:T(8,128)(2,1)S(1)}, bf16[64,640]{1,0:T(8,128)(2,1)S(1)}, u32[]{:S(2)}, u32[]{:S(2)}) collective-permute-start(bf16[64,640]{1,0:T(8,128)(2,1)S(1)} %get-tuple-element.47), channel_id=1, source_target_pairs={{0,8},{2,10},{4,12},{6,14},{8,0},{10,2},{12,4},{14,6},{1,9},{3,11}... | collective-permute-start | bytes 245768 | tf_op jit(solution)/shard_map/ppermute | solution.py:100
  57.0 1.2 %shard_map.42 = (bf16[64,640]{1,0:T(8,128)(2,1)S(1)}, bf16[64,640]{1,0:T(8,128)(2,1)S(1)}) custom-call(bf16[2,512,640]{2,1,0:T(8,128)(2,1)S(1)} %shard_map.39.own, bf16[2,512,640]{2,1,0:T(8,128)(2,1)S(1)} %collective-permute-done.7.other, bf16[64,640]{1,0:T(8,128)(2,1)S(1)} %collective-permute-done.8.refs_0_, bf16[64,640]{1,0:T(8,128)(2,1)S(1)} %collective-permute-done.9.refs_1_), custom_call_target="tpu_custom_call" | custom-call | tf_op jit(solution)/shard_map/pallas_call | solution.py:146
  58.1 2.2 %collective-permute-start.10 = (bf16[64,640]{1,0:T(8,128)(2,1)S(1)}, bf16[64,640]{1,0:T(8,128)(2,1)S(1)}, u32[]{:S(2)}, u32[]{:S(2)}) collective-permute-start(bf16[64,640]{1,0:T(8,128)(2,1)S(1)} %get-tuple-element.55), channel_id=1, source_target_pairs={{0,12},{2,14},{4,8},{6,10},{8,4},{10,6},{12,0},{14,2},{1,13},{3,15... | collective-permute-start | bytes 245768 | tf_op jit(solution)/shard_map/ppermute | solution.py:100
  60.4 3.0 %collective-permute-start.11 = (bf16[64,640]{1,0:T(8,128)(2,1)S(1)}, bf16[64,640]{1,0:T(8,128)(2,1)S(1)}, u32[]{:S(2)}, u32[]{:S(2)}) collective-permute-start(bf16[64,640]{1,0:T(8,128)(2,1)S(1)} %get-tuple-element.56), channel_id=1, source_target_pairs={{0,14},{2,12},{4,10},{6,8},{8,6},{10,4},{12,2},{14,0},{1,15},{3,13... | collective-permute-start | bytes 245768 | tf_op jit(solution)/shard_map/ppermute | solution.py:100
  63.4 0.7 collective-permute-start.13
  64.1 0.8 %shard_map.43.refs_4_ = bf16[64,5120]{1,0:T(8,128)(2,1)} custom-call(s32[1]{0:T(128)} %bitcast.chip_ref, bf16[64,640]{1,0:T(8,128)(2,1)S(1)} %get-tuple-element.52.refs_0_, bf16[64,640]{1,0:T(8,128)(2,1)S(1)} %collective-permute-done.15.refs_1_, bf16[64,640]{1,0:T(8,128)(2,1)S(1)} %collective-permute-done.12.refs_2_, ...), custom_call_target="tpu_custom_call" | custom-call | tf_op jit(solution)/shard_map/pallas_call | solution.py:160
  64.8 2.8 %collective-permute-done.14.refs_3_ = bf16[64,640]{1,0:T(8,128)(2,1)S(1)} collective-permute-done((bf16[64,640]{1,0:T(8,128)(2,1)S(1)}, bf16[64,640]{1,0:T(8,128)(2,1)S(1)}, u32[]{:S(2)}, u32[]{:S(2)}) %collective-permute-start.14) | collective-permute-done | bytes 81952 | tf_op jit(solution)/shard_map/ppermute | solution.py:100
  67.6 1.7 %collective-permute-done.11.refs_1_ = bf16[64,640]{1,0:T(8,128)(2,1)S(1)} collective-permute-done((bf16[64,640]{1,0:T(8,128)(2,1)S(1)}, bf16[64,640]{1,0:T(8,128)(2,1)S(1)}, u32[]{:S(2)}, u32[]{:S(2)}) %collective-permute-start.11) | collective-permute-done | bytes 81952 | tf_op jit(solution)/shard_map/ppermute | solution.py:100
  69.6 0.8 %shard_map.44 = bf16[64,5120]{1,0:T(8,128)(2,1)} custom-call(s32[1]{0:T(128)} %bitcast.chip_ref, bf16[64,640]{1,0:T(8,128)(2,1)S(1)} %collective-permute-done.10.refs_0_, bf16[64,640]{1,0:T(8,128)(2,1)S(1)} %collective-permute-done.11.refs_1_, bf16[64,640]{1,0:T(8,128)(2,1)S(1)} %collective-permute-done.13.refs_2_, ...), custom_call_target="tpu_custom_call", output_to_operand_aliasing={{}: (5, {})} | custom-call | tf_op jit(solution)/shard_map/pallas_call | solution.py:160
  (18 shorter events, 1.7 us)
Async XLA Ops:
  1.0 12.2 %collective-permute-start.1 = (bf16[128,640]{1,0:T(8,128)(2,1)S(1)}, bf16[128,640]{1,0:T(8,128)(2,1)S(1)}, u32[]{:S(2)}, u32[]{:S(2)}) collective-permute-start(bf16[128,640]{1,0:T(8,128)(2,1)S(1)} %get-tuple-element.35), channel_id=1, source_target_pairs={{0,14},{2,12},{4,10},{6,8},{8,6},{10,4},{12,2},{14,0},{1,15},{3,13... | collective-permute-start | bytes 491528 | tf_op jit(solution)/shard_map/ppermute | solution.py:100
  7.1 23.3 %collective-permute-start = (bf16[128,640]{1,0:T(8,128)(2,1)S(1)}, bf16[128,640]{1,0:T(8,128)(2,1)S(1)}, u32[]{:S(2)}, u32[]{:S(2)}) collective-permute-start(bf16[128,640]{1,0:T(8,128)(2,1)S(1)} %get-tuple-element.34), channel_id=1, source_target_pairs={{0,12},{2,14},{4,8},{6,10},{8,4},{10,6},{12,0},{14,2},{1,13},{3,15... | collective-permute-start | bytes 491528 | tf_op jit(solution)/shard_map/ppermute | solution.py:100
  9.0 28.8 %collective-permute-start.2 = (bf16[192,640]{1,0:T(8,128)(2,1)S(1)}, bf16[192,640]{1,0:T(8,128)(2,1)S(1)}, u32[]{:S(2)}, u32[]{:S(2)}) collective-permute-start(bf16[192,640]{1,0:T(8,128)(2,1)S(1)} %get-tuple-element.39), channel_id=1, source_target_pairs={{0,8},{2,10},{4,12},{6,14},{8,0},{10,2},{12,4},{14,6},{1,9},{3,11}... | collective-permute-start | bytes 737288 | tf_op jit(solution)/shard_map/ppermute | solution.py:100
  9.8 32.4 %collective-permute-start.3 = (bf16[192,640]{1,0:T(8,128)(2,1)S(1)}, bf16[192,640]{1,0:T(8,128)(2,1)S(1)}, u32[]{:S(2)}, u32[]{:S(2)}) collective-permute-start(bf16[192,640]{1,0:T(8,128)(2,1)S(1)} %get-tuple-element.40), channel_id=1, source_target_pairs={{0,10},{2,8},{4,14},{6,12},{8,2},{10,0},{12,6},{14,4},{1,11},{3,9}... | collective-permute-start | bytes 737288 | tf_op jit(solution)/shard_map/ppermute | solution.py:100
  11.8 30.4 %collective-permute-start.4 = (bf16[192,640]{1,0:T(8,128)(2,1)S(1)}, bf16[192,640]{1,0:T(8,128)(2,1)S(1)}, u32[]{:S(2)}, u32[]{:S(2)}) collective-permute-start(bf16[192,640]{1,0:T(8,128)(2,1)S(1)} %get-tuple-element.41), channel_id=1, source_target_pairs={{0,4},{2,6},{4,0},{6,2},{8,12},{10,14},{12,8},{14,10},{1,5},{3,7},... | collective-permute-start | bytes 737288 | tf_op jit(solution)/shard_map/ppermute | solution.py:100
  13.2 32.2 %collective-permute-start.5 = (bf16[192,640]{1,0:T(8,128)(2,1)S(1)}, bf16[192,640]{1,0:T(8,128)(2,1)S(1)}, u32[]{:S(2)}, u32[]{:S(2)}) collective-permute-start(bf16[192,640]{1,0:T(8,128)(2,1)S(1)} %get-tuple-element.42), channel_id=1, source_target_pairs={{0,6},{2,4},{4,2},{6,0},{8,14},{10,12},{12,10},{14,8},{1,7},{3,5},... | collective-permute-start | bytes 737288 | tf_op jit(solution)/shard_map/ppermute | solution.py:100
  30.4 15.2 %collective-permute-start.6 = (bf16[192,640]{1,0:T(8,128)(2,1)S(1)}, bf16[192,640]{1,0:T(8,128)(2,1)S(1)}, u32[]{:S(2)}, u32[]{:S(2)}) collective-permute-start(bf16[192,640]{1,0:T(8,128)(2,1)S(1)} %get-tuple-element.43), channel_id=1, source_target_pairs={{0,2},{2,0},{4,6},{6,4},{8,10},{10,8},{12,14},{14,12},{1,3},{3,1},... | collective-permute-start | bytes 737288 | tf_op jit(solution)/shard_map/ppermute | solution.py:100
  45.7 3.5 %collective-permute-start.7 = (bf16[2,512,640]{2,1,0:T(8,128)(2,1)S(1)}, bf16[2,512,640]{2,1,0:T(8,128)(2,1)S(1)}, u32[]{:S(2)}, u32[]{:S(2)}) collective-permute-start(bf16[2,512,640]{2,1,0:T(8,128)(2,1)S(1)} %shard_map.39.own), channel_id=1, source_target_pairs={{0,1},{1,0},{2,3},{3,2},{4,5},{5,4},{6,7},{7,6},{8,9},{9,8},{10,11... | collective-permute-start | bytes 3932168 | tf_op jit(solution)/shard_map/ppermute | solution.py:139
  45.8 11.1 %collective-permute-start.8 = (bf16[64,640]{1,0:T(8,128)(2,1)S(1)}, bf16[64,640]{1,0:T(8,128)(2,1)S(1)}, u32[]{:S(2)}, u32[]{:S(2)}) collective-permute-start(bf16[64,640]{1,0:T(8,128)(2,1)S(1)} %get-tuple-element.45), channel_id=1, source_target_pairs={{0,12},{2,14},{4,8},{6,10},{8,4},{10,6},{12,0},{14,2},{1,13},{3,15... | collective-permute-start | bytes 245768 | tf_op jit(solution)/shard_map/ppermute | solution.py:100
  47.1 9.8 %collective-permute-start.9 = (bf16[64,640]{1,0:T(8,128)(2,1)S(1)}, bf16[64,640]{1,0:T(8,128)(2,1)S(1)}, u32[]{:S(2)}, u32[]{:S(2)}) collective-permute-start(bf16[64,640]{1,0:T(8,128)(2,1)S(1)} %get-tuple-element.46), channel_id=1, source_target_pairs={{0,14},{2,12},{4,10},{6,8},{8,6},{10,4},{12,2},{14,0},{1,15},{3,13... | collective-permute-start | bytes 245768 | tf_op jit(solution)/shard_map/ppermute | solution.py:100
  50.4 9.9 %collective-permute-start.12 = (bf16[64,640]{1,0:T(8,128)(2,1)S(1)}, bf16[64,640]{1,0:T(8,128)(2,1)S(1)}, u32[]{:S(2)}, u32[]{:S(2)}) collective-permute-start(bf16[64,640]{1,0:T(8,128)(2,1)S(1)} %get-tuple-element.58), channel_id=1, source_target_pairs={{0,10},{2,8},{4,14},{6,12},{8,2},{10,0},{12,6},{14,4},{1,11},{3,9}... | collective-permute-start | bytes 245768 | tf_op jit(solution)/shard_map/ppermute | solution.py:100
  52.5 10.9 %collective-permute-start.16 = (bf16[64,640]{1,0:T(8,128)(2,1)S(1)}, bf16[64,640]{1,0:T(8,128)(2,1)S(1)}, u32[]{:S(2)}, u32[]{:S(2)}) collective-permute-start(bf16[64,640]{1,0:T(8,128)(2,1)S(1)} %get-tuple-element.62), channel_id=1, source_target_pairs={{0,2},{2,0},{4,6},{6,4},{8,10},{10,8},{12,14},{14,12},{1,3},{3,1},... | collective-permute-start | bytes 245768 | tf_op jit(solution)/shard_map/ppermute | solution.py:100
  54.5 9.6 %collective-permute-start.15 = (bf16[64,640]{1,0:T(8,128)(2,1)S(1)}, bf16[64,640]{1,0:T(8,128)(2,1)S(1)}, u32[]{:S(2)}, u32[]{:S(2)}) collective-permute-start(bf16[64,640]{1,0:T(8,128)(2,1)S(1)} %get-tuple-element.47), channel_id=1, source_target_pairs={{0,8},{2,10},{4,12},{6,14},{8,0},{10,2},{12,4},{14,6},{1,9},{3,11}... | collective-permute-start | bytes 245768 | tf_op jit(solution)/shard_map/ppermute | solution.py:100
  58.1 11.2 %collective-permute-start.10 = (bf16[64,640]{1,0:T(8,128)(2,1)S(1)}, bf16[64,640]{1,0:T(8,128)(2,1)S(1)}, u32[]{:S(2)}, u32[]{:S(2)}) collective-permute-start(bf16[64,640]{1,0:T(8,128)(2,1)S(1)} %get-tuple-element.55), channel_id=1, source_target_pairs={{0,12},{2,14},{4,8},{6,10},{8,4},{10,6},{12,0},{14,2},{1,13},{3,15... | collective-permute-start | bytes 245768 | tf_op jit(solution)/shard_map/ppermute | solution.py:100
  60.4 7.3 %collective-permute-start.14 = (bf16[64,640]{1,0:T(8,128)(2,1)S(1)}, bf16[64,640]{1,0:T(8,128)(2,1)S(1)}, u32[]{:S(2)}, u32[]{:S(2)}) collective-permute-start(bf16[64,640]{1,0:T(8,128)(2,1)S(1)} %get-tuple-element.61), channel_id=1, source_target_pairs={{0,4},{2,6},{4,0},{6,2},{8,12},{10,14},{12,8},{14,10},{1,5},{3,7},... | collective-permute-start | bytes 245768 | tf_op jit(solution)/shard_map/ppermute | solution.py:100
  60.4 8.9 %collective-permute-start.11 = (bf16[64,640]{1,0:T(8,128)(2,1)S(1)}, bf16[64,640]{1,0:T(8,128)(2,1)S(1)}, u32[]{:S(2)}, u32[]{:S(2)}) collective-permute-start(bf16[64,640]{1,0:T(8,128)(2,1)S(1)} %get-tuple-element.56), channel_id=1, source_target_pairs={{0,14},{2,12},{4,10},{6,8},{8,6},{10,4},{12,2},{14,0},{1,15},{3,13... | collective-permute-start | bytes 245768 | tf_op jit(solution)/shard_map/ppermute | solution.py:100
  63.4 6.3 %collective-permute-start.13 = (bf16[64,640]{1,0:T(8,128)(2,1)S(1)}, bf16[64,640]{1,0:T(8,128)(2,1)S(1)}, u32[]{:S(2)}, u32[]{:S(2)}) collective-permute-start(bf16[64,640]{1,0:T(8,128)(2,1)S(1)} %get-tuple-element.59), channel_id=1, source_target_pairs={{0,6},{2,4},{4,2},{6,0},{8,14},{10,12},{12,10},{14,8},{1,7},{3,5},... | collective-permute-start | bytes 245768 | tf_op jit(solution)/shard_map/ppermute | solution.py:100
